TPU v7x, 128 devices: a whole 4x4x4 slice. The times are simulated.
128 devices in a mesh: ctx: 32 (over x_lo, z, y), tp: 4 (over x_hi, core).
Axes of the slice: x: 4 (x_hi: 2, x_lo: 2; x = x_hi * 2 + x_lo), y: 4, z: 4, core: 2. Of those that a mesh axis runs over, the one named last changes fastest.
Arguments:
- tokens: bfloat16 [8192, 768], P('ctx'), may hold values from -6 to 6
- block_order: int32 [64], replicated, may hold values from 0 to 63, each once
- cotangent: bfloat16 [8192, 768], P('ctx'), may hold values from -20 to 20
- w_qkv: bfloat16 [768, 2304], P(None, 'tp'), may hold values from -0.3125 to 0.3125
- b_qkv: float32 [2304], P('tp'), may hold values from -3 to 3
- w_dense: bfloat16 [768, 768], P('tp'), may hold values from -0.75 to 0.75
- b_dense: float32 [768], replicated, may hold values from -3 to 3
- w_up: bfloat16 [768, 3072], P(None, 'tp'), may hold values from -0.21875 to 0.21875
- b_up: float32 [3072], P('tp'), may hold values from -3 to 3
- w_down: bfloat16 [3072, 768], P('tp'), may hold values from -0.109375 to 0.109375
- b_down: float32 [768], replicated, may hold values from -3 to 3
- gain_attn: float32 [768], replicated, may hold values from 0.25 to 1.75
- shift_attn: float32 [768], replicated, may hold values from -3 to 3
- gain_mlp: float32 [768], replicated, may hold values from 0.25 to 1.75
- shift_mlp: float32 [768], replicated, may hold values from -3 to 3
Outputs:
- output: bfloat16 [8192, 768], P('ctx')
- grad_tokens: bfloat16 [8192, 768], P('ctx')
- grad_w_qkv: float32 [768, 2304], P(None, 'tp')
- grad_b_qkv: float32 [2304], P('tp')
- grad_w_dense: float32 [768, 768], P('tp')
- grad_b_dense: float32 [768], replicated
- grad_w_up: float32 [768, 3072], P(None, 'tp')
- grad_b_up: float32 [3072], P('tp')
- grad_w_down: float32 [3072, 768], P('tp')
- grad_b_down: float32 [768], replicated
- grad_gain_attn: float32 [768], replicated
- grad_shift_attn: float32 [768], replicated
- grad_gain_mlp: float32 [768], replicated
- grad_shift_mlp: float32 [768], replicated
Inputs may be any that keep to these rules, and one draw needn't show every extreme that they name: A permutation: storage block s, rows s * 128 to (s + 1) * 128 - 1, holds the sequence block block_order[s].
All inputs are finite; a program needn't handle non-finite values.
Results may differ from a plain program's by a relative error of at most 0.028.
Values may be sent and summed in bfloat16 or wider, within the bound.
No kernel may reach another device: no remote copies, remote signals or barrier semaphores. Data moves between devices by JAX's collectives and lax.ppermute only.
A program may use at most 128 MiB of HBM per device.

v0:
```python
import math

import jax
import jax.numpy as jnp
from jax import lax
from jax.sharding import PartitionSpec as P

HEAD = 64
ROT = 16


EPSILON = 1e-05
MASKED = -1e30


def layer_norm(values, gain_vector, shift_vector):
    row_mean = jnp.mean(values, axis=-1, keepdims=True)
    centred = values - row_mean
    spread = jnp.mean(centred * centred, axis=-1, keepdims=True)
    return centred * lax.rsqrt(spread + EPSILON) * gain_vector + shift_vector


def norm_grads(values, gain_vector, shift_vector, upstream):
    unused, pullback = jax.vjp(layer_norm, values, gain_vector, shift_vector)
    return pullback(upstream)


def gelu_exact(preact):
    return jax.nn.gelu(preact, approximate=False)


def positions(block_order, first_row, row_count, half_rows):
    row_index = first_row + lax.iota(jnp.int32, row_count)
    slot_index = row_index // half_rows
    slot_table = lax.iota(jnp.int32, block_order.shape[0])
    picked = jnp.sum(
        jnp.where(slot_index[:, None] == slot_table[None, :], block_order[None, :], 0), axis=1
    )
    return picked * half_rows + row_index % half_rows


def rotary_tables(places):
    half_rot = ROT // 2
    frequency = jnp.exp(-math.log(10000.0) * (2.0 * jnp.arange(half_rot, dtype=jnp.float32)) / ROT)
    angles = places.astype(jnp.float32)[:, None] * frequency[None, :]
    angles = jnp.concatenate([angles, angles], axis=1)
    return (jnp.cos(angles), jnp.sin(angles))


def rotate(heads_part, cosine_table, sine_table):
    half_rot = ROT // 2
    turned_part = heads_part[..., :ROT]
    turned = jnp.concatenate([-turned_part[..., half_rot:], turned_part[..., :half_rot]], axis=-1)
    spun_part = turned_part * cosine_table[:, None, :] + turned * sine_table[:, None, :]
    return jnp.concatenate([spun_part, heads_part[..., ROT:]], axis=-1)


def score_block(query_heads, keys_block, query_places, key_places, scale_factor):
    scores = (
        jnp.einsum("qhd,khd->hqk", query_heads, keys_block, preferred_element_type=jnp.float32)
        * scale_factor
    )
    visible = key_places[None, None, :] <= query_places[None, :, None]
    return (scores, visible)


def score_grads(
    query_heads,
    grad_heads,
    log_total,
    delta_rows,
    query_places,
    keys_block,
    values_block,
    key_places,
    scale_factor,
):
    scores, visible = score_block(query_heads, keys_block, query_places, key_places, scale_factor)
    weights = jnp.where(visible, jnp.exp(scores - log_total[:, :, None]), 0.0)
    d_weights = jnp.einsum(
        "qhd,khd->hqk", grad_heads, values_block, preferred_element_type=jnp.float32
    )
    d_scores = (weights * (d_weights - delta_rows[:, :, None])).astype(jnp.bfloat16)
    return (weights.astype(jnp.bfloat16), d_scores)


def on_device(
    tokens,
    block_order,
    cotangent,
    w_qkv,
    b_qkv,
    w_dense,
    b_dense,
    w_up,
    b_up,
    w_down,
    b_down,
    gain_attn,
    shift_attn,
    gain_mlp,
    shift_mlp,
):
    local_rows = tokens.shape[0]
    half_rows = local_rows // 2
    local_heads = w_qkv.shape[1] // (3 * HEAD)
    head_cols = local_heads * HEAD
    scale_factor = 1.0 / math.sqrt(HEAD)
    first_row = lax.axis_index("ctx") * local_rows
    local_places = positions(block_order, first_row, local_rows, half_rows)
    cosine_table, sine_table = rotary_tables(local_places)

    def rotate_local(heads_part):
        return rotate(heads_part, cosine_table, sine_table)

    inputs = tokens.astype(jnp.float32)
    ln_attn = layer_norm(inputs, gain_attn, shift_attn).astype(jnp.bfloat16)
    ln_mlp = layer_norm(inputs, gain_mlp, shift_mlp).astype(jnp.bfloat16)
    joined_proj = jnp.dot(ln_attn, w_qkv, preferred_element_type=jnp.float32) + b_qkv
    joined_proj = joined_proj.reshape(local_rows, local_heads, 3, HEAD)
    queries = rotate_local(joined_proj[:, :, 0]).astype(jnp.bfloat16)
    keys_local = rotate_local(joined_proj[:, :, 1]).astype(jnp.bfloat16)
    values_local = joined_proj[:, :, 2].astype(jnp.bfloat16)
    key_value = jnp.concatenate(
        [keys_local.reshape(local_rows, head_cols), values_local.reshape(local_rows, head_cols)],
        axis=1,
    )
    gathered = lax.all_gather(key_value, "ctx", axis=0, tiled=True)
    seq_rows = gathered.shape[0]
    block_rows = 512
    block_count = seq_rows // block_rows
    key_blocks = gathered[:, :head_cols].reshape(block_count, block_rows, local_heads, HEAD)
    value_blocks = gathered[:, head_cols:].reshape(block_count, block_rows, local_heads, HEAD)
    all_places = positions(block_order, 0, seq_rows, half_rows).reshape(block_count, block_rows)

    def stats_step(carried, block_pair):
        running_max, running_sum = carried
        keys_block, places_block = block_pair
        scores, visible = score_block(queries, keys_block, local_places, places_block, scale_factor)
        masked_scores = jnp.where(visible, scores, MASKED)
        new_max = jnp.maximum(running_max, jnp.max(masked_scores, axis=-1))
        kept_terms = jnp.where(visible, jnp.exp(masked_scores - new_max[:, :, None]), 0.0)
        running_sum = running_sum * jnp.exp(running_max - new_max) + jnp.sum(kept_terms, axis=-1)
        return ((new_max, running_sum), None)

    start_max = jnp.full((local_heads, local_rows), MASKED, jnp.float32)
    (final_max, final_sum), unused = lax.scan(
        stats_step, (start_max, jnp.zeros_like(start_max)), (key_blocks, all_places)
    )
    log_total = final_max + jnp.log(final_sum)

    def output_step(carried, block_pair):
        keys_block, values_block, places_block = block_pair
        scores, visible = score_block(queries, keys_block, local_places, places_block, scale_factor)
        weights_low = jnp.where(visible, jnp.exp(scores - log_total[:, :, None]), 0.0).astype(
            jnp.bfloat16
        )
        return (
            carried
            + jnp.einsum(
                "hqk,khd->qhd", weights_low, values_block, preferred_element_type=jnp.float32
            ),
            None,
        )

    head_zeros = jnp.zeros((local_rows, local_heads, HEAD), jnp.float32)
    attended, unused = lax.scan(output_step, head_zeros, (key_blocks, value_blocks, all_places))
    attended_low = attended.reshape(local_rows, head_cols).astype(jnp.bfloat16)
    upward = jnp.dot(ln_mlp, w_up, preferred_element_type=jnp.float32) + b_up
    hidden = gelu_exact(upward).astype(jnp.bfloat16)
    partial_value = jnp.dot(attended_low, w_dense, preferred_element_type=jnp.float32) + jnp.dot(
        hidden, w_down, preferred_element_type=jnp.float32
    )
    branches = lax.psum(partial_value.astype(jnp.bfloat16), "tp").astype(jnp.float32)
    output = (inputs + branches + b_dense + b_down).astype(jnp.bfloat16)
    upstream = cotangent.astype(jnp.float32)
    grad_bias = jnp.sum(upstream, axis=0)
    grad_w_dense = jnp.dot(attended_low.T, cotangent, preferred_element_type=jnp.float32)
    grad_w_down = jnp.dot(hidden.T, cotangent, preferred_element_type=jnp.float32)
    d_attended = jnp.dot(cotangent, w_dense.T, preferred_element_type=jnp.float32).astype(
        jnp.bfloat16
    )
    d_hidden = jnp.dot(cotangent, w_down.T, preferred_element_type=jnp.float32)
    unused, gelu_back = jax.vjp(gelu_exact, upward)
    d_upward = gelu_back(d_hidden)[0].astype(jnp.bfloat16)
    grad_w_up = jnp.dot(ln_mlp.T, d_upward, preferred_element_type=jnp.float32)
    grad_b_up = jnp.sum(d_upward.astype(jnp.float32), axis=0)
    d_ln_mlp = jnp.dot(d_upward, w_up.T, preferred_element_type=jnp.float32)
    d_heads = d_attended.reshape(local_rows, local_heads, HEAD)
    delta_rows = jnp.einsum("qhd,qhd->hq", d_heads.astype(jnp.float32), attended)

    def back_step(carried, block_pair):
        keys_block, values_block, places_block = block_pair
        weights_low, d_scores = score_grads(
            queries,
            d_heads,
            log_total,
            delta_rows,
            local_places,
            keys_block,
            values_block,
            places_block,
            scale_factor,
        )
        d_query = (
            carried
            + jnp.einsum("hqk,khd->qhd", d_scores, keys_block, preferred_element_type=jnp.float32)
            * scale_factor
        )
        d_key = (
            jnp.einsum("hqk,qhd->khd", d_scores, queries, preferred_element_type=jnp.float32)
            * scale_factor
        )
        d_value = jnp.einsum(
            "hqk,qhd->khd", weights_low, d_heads, preferred_element_type=jnp.float32
        )
        key_term = jnp.concatenate(
            [d_key.reshape(block_rows, head_cols), d_value.reshape(block_rows, head_cols)], axis=1
        )
        return (d_query, key_term)

    d_queries, key_terms = lax.scan(back_step, head_zeros, (key_blocks, value_blocks, all_places))
    key_grads = lax.psum_scatter(
        key_terms.reshape(seq_rows, 2 * head_cols).astype(jnp.bfloat16),
        "ctx",
        scatter_dimension=0,
        tiled=True,
    ).astype(jnp.float32)
    d_keys = key_grads[:, :head_cols].reshape(local_rows, local_heads, HEAD)
    d_values = key_grads[:, head_cols:].reshape(local_rows, local_heads, HEAD)
    unused, rotate_back = jax.vjp(rotate_local, joined_proj[:, :, 0])
    d_joined = jnp.stack([rotate_back(d_queries)[0], rotate_back(d_keys)[0], d_values], axis=2)
    d_joined = d_joined.reshape(local_rows, 3 * head_cols).astype(jnp.bfloat16)
    grad_w_qkv = jnp.dot(ln_attn.T, d_joined, preferred_element_type=jnp.float32)
    grad_b_qkv = jnp.sum(d_joined.astype(jnp.float32), axis=0)
    d_ln_attn = jnp.dot(d_joined, w_qkv.T, preferred_element_type=jnp.float32)
    d_ln_attn, d_ln_mlp = (
        lax.psum(d_ln_attn.astype(jnp.bfloat16), "tp").astype(jnp.float32),
        lax.psum(d_ln_mlp.astype(jnp.bfloat16), "tp").astype(jnp.float32),
    )
    d_in_attn, grad_gain_attn, grad_shift_attn = norm_grads(
        inputs, gain_attn, shift_attn, d_ln_attn
    )
    d_in_mlp, grad_gain_mlp, grad_shift_mlp = norm_grads(inputs, gain_mlp, shift_mlp, d_ln_mlp)
    grad_tokens = (upstream + d_in_attn + d_in_mlp).astype(jnp.bfloat16)
    summed = (
        lax.psum(grad_w_qkv.astype(jnp.bfloat16), "ctx").astype(jnp.float32),
        lax.psum(grad_b_qkv.astype(jnp.bfloat16), "ctx").astype(jnp.float32),
        lax.psum(grad_w_dense.astype(jnp.bfloat16), "ctx").astype(jnp.float32),
        lax.psum(grad_bias.astype(jnp.bfloat16), "ctx").astype(jnp.float32),
        lax.psum(grad_w_up.astype(jnp.bfloat16), "ctx").astype(jnp.float32),
        lax.psum(grad_b_up.astype(jnp.bfloat16), "ctx").astype(jnp.float32),
        lax.psum(grad_w_down.astype(jnp.bfloat16), "ctx").astype(jnp.float32),
        lax.psum(grad_gain_attn.astype(jnp.bfloat16), "ctx").astype(jnp.float32),
        lax.psum(grad_shift_attn.astype(jnp.bfloat16), "ctx").astype(jnp.float32),
        lax.psum(grad_gain_mlp.astype(jnp.bfloat16), "ctx").astype(jnp.float32),
        lax.psum(grad_shift_mlp.astype(jnp.bfloat16), "ctx").astype(jnp.float32),
    )
    return (
        output,
        grad_tokens,
        summed[0],
        summed[1],
        summed[2],
        summed[3],
        summed[4],
        summed[5],
        summed[6],
        summed[3],
        summed[7],
        summed[8],
        summed[9],
        summed[10],
    )


def solution(mesh):
    return jax.shard_map(
        on_device,
        mesh=mesh,
        in_specs=(
            P("ctx", None),
            P(),
            P("ctx", None),
            P(None, "tp"),
            P("tp"),
            P("tp", None),
            P(),
            P(None, "tp"),
            P("tp"),
            P("tp", None),
            P(),
            P(),
            P(),
            P(),
            P(),
        ),
        out_specs=(
            P("ctx", None),
            P("ctx", None),
            P(None, "tp"),
            P("tp"),
            P("tp", None),
            P(),
            P(None, "tp"),
            P("tp"),
            P("tp", None),
            P(),
            P(),
            P(),
            P(),
            P(),
        ),
        check_vma=False,
    )
```

profile of v0, /device:TPU:0, one launch (start us, length us, event | category | flops | bytes accessed | tf_op | source)
XLA Modules:
  0.0 952.1 jit_solution(8385135150578801432)
XLA Ops:
  10.8 1.8 convolution_add_fusion.2
  15.4 153.0 %all-gather.2.cloned.1.call-done = bf16[8192,384]{0,1:T(8,128)(2,1)} async-done(((bf16[256,384]{0,1:T(8,128)(2,1)}), bf16[8192,384]{0,1:T(8,128)(2,1)}) %all-gather.2.cloned.1.call-update) | async-done | bytes 6291472 | tf_op jit(solution)/shard_map/all_gather | solution.py:128
  168.4 5.1 fusion.94
  174.7 3.5 copy.106
  178.2 42.7 %while.37 = (s32[]{:T(128)}, f32[3,256]{1,0:T(4,128)S(1)}, f32[3,256]{1,0:T(4,128)S(1)}, s32[16,512]{1,0:T(8,128)}, s32[256]{0:T(256)S(1)}, /*index=5*/bf16[16,5...) while((s32[]{:T(128)}, f32[3,256]{1,0:T(4,128)S(1)}, ...), condition=%wide.region_7.8_spmd.clone, body=%wide.region_4.7_spmd.clone.sunk | while | flops 52825856 | bytes 3881580 | solution.py:147
  220.9 3.2 copy.145
  224.1 3.4 copy.105
  227.6 41.5 %while.38 = (s32[]{:T(128)}, f32[256,3,64]{0,2,1:T(8,128)S(1)}, bf16[16,512,3,64]{1,3,2,0:T(8,128)(2,1)}, s32[16,512]{1,0:T(8,128)}, s32[256]{0:T(256)S(1)}, /*i...) while((s32[]{:T(128)}, f32[256,3,64]{0,2,1:T(8,128)S(1)}, ...), condition=%wide.region_9.10_spmd.clone, body=%wide.region_8.9_spmd.clone.sunk | while | flops 102465536 | bytes 1158259 | solution.py:167
  228.5 1.7 fusion.152
  231.0 1.7 fusion.152
  233.6 1.7 fusion.152
  236.2 1.7 fusion.152
  238.8 1.7 fusion.152
  241.4 1.7 fusion.152
  244.0 1.7 fusion.152
  246.6 1.7 fusion.152
  249.2 1.7 fusion.152
  251.8 1.7 fusion.152
  254.4 1.7 fusion.152
  257.0 1.7 fusion.152
  259.6 1.7 fusion.152
  262.2 1.7 fusion.152
  264.8 1.7 fusion.152
  267.4 1.7 fusion.152
  269.7 119.5 %while.39 = (s32[]{:T(128)}, f32[256,3,64]{0,2,1:T(8,128)}, bf16[16,512,384]{2,1,0:T(8,128)(2,1)}, bf16[16,512,3,64]{1,3,2,0:T(8,128)(2,1)}, s32[16,512]{1,0:T(8...) while((s32[]{:T(128)}, f32[256,3,64]{0,2,1:T(8,128)}, ...), condition=%wide.region_12.13_spmd.clone, body=%wide.region_11.12_spmd.clone.sunk | while | flops 255672320 | bytes 11484299 | solution.py:222
  275.2 1.9 fusion.164
  282.6 2.0 fusion.164
  290.1 2.0 fusion.164
  297.6 2.0 fusion.164
  305.0 2.0 fusion.164
  312.5 2.0 fusion.164
  319.9 2.0 fusion.164
  327.4 2.0 fusion.164
  334.9 2.0 fusion.164
  342.4 2.0 fusion.164
  349.9 2.0 fusion.164
  357.3 2.0 fusion.164
  364.8 2.0 fusion.164
  372.3 2.0 fusion.164
  379.8 2.0 fusion.164
  387.3 2.0 fusion.164
  391.2 3.0 fusion.88
  398.4 166.4 %reduce-scatter.2.cloned.1.call-done = bf16[256,384]{1,0:T(8,128)(2,1)} async-done(((bf16[8192,384]{1,0:T(8,128)(2,1)}), bf16[256,384]{1,0:T(8,128)(2,1)}) %reduce-scatter.2.cloned.1.call-update) | async-done | bytes 196624 | tf_op jit(solution)/shard_map/reduce_scatter | solution.py:223
  572.5 1.7 convolution_convert_fusion.1
  576.8 36.4 %all-reduce.16.cloned.1.call-done = (bf16[256,768]{1,0:T(8,128)(2,1)}, bf16[256,768]{1,0:T(8,128)(2,1)}, bf16[256,768]{1,0:T(8,128)(2,1)}) async-done(((bf16[256,768]{1,0:T(8,128)(2,1)}, bf16[256,768]{1,0:T(8,128)(2,1)}, bf16[256,768]{1,0:T(8,128)(2,1)}), (bf16[256,768]{1,0:T(8,128)(2,1)}, bf16[256,768]{1,0:T(8,128)(2,1)}, bf16[256,768]{1,0:T(8,128)(2,1)})) %all-reduce.16.cloned.1.call-update) | async-done | bytes 1179664 | tf_op jit(solution)/shard_map/psum | solution.py:174
  618.0 157.3 %all-reduce.8 = (bf16[576]{0:T(1024)(128)(2,1)S(1)}, bf16[768]{0:T(1024)(128)(2,1)S(1)}, bf16[768]{0:T(1024)(128)(2,1)S(1)}, bf16[768]{0:T(1024)(128)(2,1)S(1)},...) all-reduce(bf16[576]{0:T(1024)(128)(2,1)S(1)} %reduce_sum.185, ...), channel_id=1, replica_groups=mesh['ctx'=32,'tp'=4] {'ctx'}, use_global_device_ids=true, to_apply=%region_22.23 | all-reduce | flops 5184 | bytes 20736 | tf_op jit(solution)/shard_map/psum | solution.py:248
  780.4 157.8 %all-reduce.14.cloned.1.call-done = (bf16[768,576]{0,1:T(8,128)(2,1)}, bf16[192,768]{1,0:T(8,128)(2,1)}, bf16[768,768]{1,0:T(8,128)(2,1)}, bf16[768,768]{1,0:T(8,128)(2,1)}) async-done(((bf16[768,576]{0,1:T(8,128)(2,1)}, bf16[192,768]{1,0:T(8,128)(2,1)}, bf16[768,768]{1,0:T(8,128)(2,1)}, bf16[768,768]{1,0:T(8,128)(2,1)}), (bf16[768,576]{0,1:T(8,128)(2,1)}, bf16[192,768]{1,0:T(8,128)(2,1)}, ...) | async-done | bytes 3538960 | tf_op jit(solution)/shard_map/psum | solution.py:247
  938.2 2.9 convert_element_type.185
  (458 shorter events, 181.8 us)
Async XLA Ops:
  7.2 384.0 %copy-start = (bf16[768,768]{1,0:T(8,128)(2,1)S(1)}, bf16[768,768]{1,0:T(8,128)(2,1)}, u32[]{:S(2)}) copy-start(bf16[768,768]{1,0:T(8,128)(2,1)} %param.30) | copy-start | bytes 3538948
  7.2 161.2 %all-gather.2.cloned.1.call-start = ((), (), s32[]{:S(2)}) async-start(), calls=%async_computation.1 | async-start | bytes 6488064 | tf_op jit(solution)/shard_map/all_gather | solution.py:128
  9.7 0.6 copy-start.30
  10.3 0.6 copy-start.27
  10.8 2.0 copy-start.34
  12.7 2.4 copy-start.2
  12.7 2.4 copy-start.7
  13.1 160.3 %copy-start.20 = (f32[256,16]{0,1:T(8,128)}, f32[256,16]{0,1:T(8,128)S(1)}, u32[]{:S(2)}) copy-start(f32[256,16]{0,1:T(8,128)S(1)} %get-tuple-element.487) | copy-start | bytes 49156
  13.1 160.3 %copy-start.22 = (f32[256,16]{0,1:T(8,128)}, f32[256,16]{0,1:T(8,128)S(1)}, u32[]{:S(2)}) copy-start(f32[256,16]{0,1:T(8,128)S(1)} %get-tuple-element.488) | copy-start | bytes 49156
  13.9 551.0 %reduce-scatter.2.cloned.1.call-start = ((), (), s32[]{:S(2)}) async-start(), calls=%async_computation.2 | async-start | bytes 6488064 | tf_op jit(solution)/shard_map/reduce_scatter | solution.py:223
  224.1 3.4 copy-start.12
  269.1 0.7 copy-start.13
  389.2 1.0 copy-start.1
  389.2 1.4 copy-start.9
  389.2 1.4 copy-start.25
  389.2 1.4 copy-start.28
  389.2 1.4 copy-start.37
  389.2 1.4 copy-start.38
  389.3 224.0 %all-reduce.16.cloned.1.call-start = ((), (), s32[]{:S(2)}) async-start(), calls=%async_computation.4 | async-start | bytes 2359296 | tf_op jit(solution)/shard_map/psum | solution.py:174
  394.2 2.7 copy-start.17
  394.2 1.4 copy-start.10
  394.2 2.7 copy-start.14
  394.3 2.6 copy-start.3
  394.3 2.6 copy-start.8
  397.2 168.8 %copy-start.23 = (f32[256,16]{0,1:T(8,128)S(1)}, f32[256,16]{0,1:T(8,128)}, u32[]{:S(2)}) copy-start(f32[256,16]{0,1:T(8,128)} %copy-done.22) | copy-start | bytes 49156
  398.4 170.0 %copy-start.21 = (f32[256,16]{0,1:T(8,128)S(1)}, f32[256,16]{0,1:T(8,128)}, u32[]{:S(2)}) copy-start(f32[256,16]{0,1:T(8,128)} %copy-done.20) | copy-start | bytes 49156
  564.9 1.8 copy-start.15
  568.4 1.2 copy-start.36
  570.9 1.6 copy-start.18
  570.9 1.6 copy-start.29
  570.9 1.6 copy-start.39
  570.9 367.4 %all-reduce.14.cloned.1.call-start = ((), (), s32[]{:S(2)}) async-start(), calls=%async_computation.3 | async-start | bytes 7077888 | tf_op jit(solution)/shard_map/psum | solution.py:247
  572.5 2.7 copy-start.24
  572.5 2.7 copy-start.40
  576.6 40.5 %copy-start.31 = (f32[256]{0:T(256)S(1)}, f32[256]{0:T(256)}, u32[]{:S(2)}) copy-start(f32[256]{0:T(256)} %copy-done.30) | copy-start | bytes 3076
  613.3 3.9 copy-start.4
  613.3 3.9 copy-start.5
  613.3 4.7 copy-start.35
  613.3 165.7 %copy-start.16 = (bf16[256,768]{1,0:T(8,128)(2,1)S(1)}, bf16[256,768]{1,0:T(8,128)(2,1)}, u32[]{:S(2)}) copy-start(bf16[256,768]{1,0:T(8,128)(2,1)} %get-tuple-element.453) | copy-start | bytes 1179652
  613.3 165.7 %copy-start.32 = (f32[768]{0:T(1024)S(1)}, f32[768]{0:T(1024)}, u32[]{:S(2)}) copy-start(f32[768]{0:T(1024)} %param.31) | copy-start | bytes 9220
  613.3 165.7 %copy-start.33 = (f32[768]{0:T(1024)S(1)}, f32[768]{0:T(1024)}, u32[]{:S(2)}) copy-start(f32[768]{0:T(1024)} %param.27) | copy-start | bytes 9220
  775.4 169.6 %copy-start.26 = (f32[768]{0:T(1024)}, f32[768]{0:T(1024)S(1)}, u32[]{:S(2)}) copy-start(f32[768]{0:T(1024)S(1)} %convert_element_type.183) | copy-start | bytes 9220
  938.2 2.9 copy-start.6
  941.2 1.6 copy-start.11
  942.8 1.3 copy-start.19
Sparse Core Ops, SparseCore 0:
  14.0 154.3 all-gather.1
  389.4 175.4 reduce-scatter.1
  571.0 42.2 all-reduce.15
  617.1 321.1 all-reduce.13
where the time goes:
time: 957 us; the launch traced here: 952 us
  waiting for transfers between devices  514 us (54%)
  blocking collectives  157 us (16%)
  matrix products  153 us (16%)
  local copies, waits for them, and re-layouts  75.5 us (8%)
  other arithmetic  35.4 us (4%)
  between operations  14.4 us (2%)
    reduce_scatter x1, waiting for transfers between devices, on_device(): lax.psum_scatter(key_terms.reshape(seq_rows, 2 * head_cols).astype(jnp.bf...  166 us
    psum x1, waiting for transfers between devices, on_device(): lax.psum(grad_w_qkv.astype(jnp.bfloat16), 'ctx').astype(jnp.float32)  158 us
    psum x1, blocking collectives, on_device(): lax.psum(grad_b_qkv.astype(jnp.bfloat16), 'ctx').astype(jnp.float32)  157 us
    all_gather x1, waiting for transfers between devices, on_device(): gathered = lax.all_gather(key_value, 'ctx', axis=0, tiled=True)  153 us
    dot_general x32, matrix products, score_block(): jnp.einsum('qhd,khd->hqk', query_heads, keys_block, preferred_element_typ...  46.5 us
    psum x1, waiting for transfers between devices, on_device(): lax.psum(partial_value.astype(jnp.bfloat16), 'tp').astype(jnp.float32)  36.4 us
    dynamic_slice x48, local copies, waits for them, and re-layouts, on_device(): lax.scan(stats_step, (start_max, jnp.zeros_like(start_max)), (key_blocks,...  34.8 us
    dot_general x16, matrix products, back_step(): jnp.einsum('hqk,khd->qhd', d_scores, keys_block, preferred_element_type=j...  31.3 us
  transfers between devices with their start and end apart: 4, of which 4 were waited for; matrix products, arithmetic and copies ran while one was open for 2% of the time, Pallas kernels for 0%

commit v1 on v0

v1 whole, which is shorter than its diff:
```python
import functools
import math

import jax
import jax.numpy as jnp
import numpy as np
from jax import lax
from jax.experimental import pallas as pl
from jax.experimental.pallas import tpu as pltpu
from jax.sharding import Mesh
from jax.sharding import PartitionSpec as P

HEAD = 64
ROT = 16
HEADS = 3
EPSILON = 1e-05
MASKED = -1e30
CTX = ("xl", "z", "y")
TP = ("xh", "c")
F32 = jnp.float32
BF = jnp.bfloat16
LOG2E = math.log2(math.e)
SCALE = 1.0 / math.sqrt(HEAD)
SCORE = SCALE * LOG2E
NT = (((1,), (1,)), ((), ()))
TN = (((0,), (0,)), ((), ()))


def mm(a, b):
    return jnp.dot(a, b, preferred_element_type=F32)


def mm_nt(a, b):
    return lax.dot_general(a, b, NT, preferred_element_type=F32)


def mm_tn(a, b):
    return lax.dot_general(a, b, TN, preferred_element_type=F32)


def lane_table():
    lane = np.arange(128) % HEAD
    table = np.zeros((8, 128), np.float32)
    table[0] = np.where(lane < ROT, 10000.0 ** (-2.0 * (lane % 8) / ROT), 0.0)
    table[1] = lane < 8
    table[2] = (lane >= 8) & (lane < ROT)
    return table


def spin_tables(coords, order, table):
    shard = (coords[0] * 4 + coords[1]) * 4 + coords[2]
    step = lax.broadcasted_iota(jnp.int32, (128, 128), 0)
    places = jnp.concatenate(
        [step + order[2 * shard] * 128, step + order[2 * shard + 1] * 128], axis=0
    )
    angles = places.astype(F32) * table[0:1, :]
    sine = jnp.sin(angles)
    return jnp.cos(angles), sine * -table[1:2, :], sine * table[2:3, :]


def normed(tokens):
    values = tokens.astype(F32)
    centred = values - jnp.mean(values, axis=-1, keepdims=True)
    rstd = lax.rsqrt(jnp.mean(centred * centred, axis=-1, keepdims=True) + EPSILON)
    return centred * rstd, rstd


def front_kernel(
    coords, order, table, tok, cot, wqkv, bqkv, wd, ga, sa, gm, sm, qdo, kv, lna, lnm
):
    xhat, _ = normed(tok[...])
    ln = (xhat * ga[...] + sa[...]).astype(BF)
    lna[...] = ln
    lnm[...] = (xhat * gm[...] + sm[...]).astype(BF)
    joined = mm(ln, wqkv[...]) + bqkv[...]
    cosine, left_sine, right_sine = spin_tables(coords, order, table)
    half = lax.broadcasted_iota(jnp.int32, (256, 128), 1) < HEAD
    tiles = []
    for t in range(4):
        x = joined[:, 128 * t : 128 * t + 128]
        spun = (
            x * cosine + pltpu.roll(x, 120, 1) * left_sine + pltpu.roll(x, 8, 1) * right_sine
        )
        if t == 1:
            spun = jnp.where(half, x, spun)
        if t == 2:
            spun = jnp.where(half, spun, x)
        tiles.append(spun)
    pieces = []
    for t in range(4):
        pieces += [tiles[t][:, :HEAD], tiles[t][:, HEAD:]]
    pieces.append(joined[:, 512:576])
    d_att = mm_nt(cot[...], wd[...])
    qdo[...] = jnp.concatenate(
        [pieces[0], pieces[3], pieces[6], d_att], axis=1
    ).astype(BF)
    kv[...] = jnp.concatenate([pieces[i] for i in (1, 4, 7, 2, 5, 8)], axis=1).astype(BF)


def mlp_kernel(ln, cot, wu, bu, wdn, gw, small, part, d_ln):
    up = mm(ln[...], wu[...]) + bu[...]
    phi = 0.5 * (1.0 + lax.erf(up * math.sqrt(0.5)))
    hid = (up * phi).astype(BF)
    slope = phi + up * (jnp.exp(up * up * -0.5) * (1.0 / math.sqrt(2.0 * math.pi)))
    d_up = (mm_nt(cot[...], wdn[...]) * slope).astype(BF)
    gw[0:768, :] = mm_tn(ln[...], d_up).astype(BF)
    gw[768:1536, :] = mm_tn(hid, cot[...]).astype(BF)
    part[...] = mm(hid, wdn[...])
    d_ln[...] = mm_nt(d_up, wu[...])
    small[0:1, :] = jnp.sum(d_up.astype(F32), axis=0, keepdims=True)
    small[1:2, :] = jnp.sum(cot[...].astype(F32), axis=0, keepdims=True)
    small[2:8, :] = jnp.zeros((6, 768), F32)


def mask_tile(scores, gap, q_places, k_places):
    rows = []
    for kb in range(2):
        cells = []
        for qb in range(2):
            cell = scores[128 * kb : 128 * kb + 128, 128 * qb : 128 * qb + 128]
            cells.append(jnp.where(gap <= (q_places[qb] - k_places[kb]) * 128, cell, MASKED))
        rows.append(jnp.concatenate(cells, axis=1))
    return jnp.concatenate(rows, axis=0)


def gap_table():
    return lax.broadcasted_iota(jnp.int32, (128, 128), 0) - lax.broadcasted_iota(
        jnp.int32, (128, 128), 1
    )


def query_places(coords, order, slot):
    shard = (coords[0] * 4 + coords[1]) * 4 + (coords[2] + slot) % 4
    return order[2 * shard], order[2 * shard + 1]


def key_places(coords, order, tile):
    shard = ((coords[0] + tile % 2) % 2 * 4 + (coords[1] + tile // 2) % 4) * 4 + coords[2]
    return order[2 * shard], order[2 * shard + 1]


def forward_kernel(
    coords, order, q0, q1, q2, q3, k0, k1, k2, k3, o0, o1, o2, o3, stats, qs, os
):
    for j, ref in enumerate((q0, q1, q2, q3)):
        qs[j] = ref[...]
    keys = (k0, k1, k2, k3)
    gap = gap_table()

    def slot_step(j, carry):
        q_places = query_places(coords, order, j)
        for h in range(HEADS):
            query = qs[j, :, HEAD * h : HEAD * h + HEAD]
            d_att = qs[j, :, 192 + HEAD * h : 256 + HEAD * h]
            tiles, tops = [], []
            for t in range(8):
                key = keys[t // 2][t % 2, :, HEAD * h : HEAD * h + HEAD]
                scores = mask_tile(
                    mm_nt(key, query), gap, q_places, key_places(coords, order, t)
                )
                tiles.append(scores)
                tops.append(jnp.max(scores, axis=0, keepdims=True))
            top = functools.reduce(jnp.maximum, tops) * SCORE
            total = jnp.zeros((1, 256), F32)
            out = jnp.zeros((HEAD, 256), F32)
            for t in range(8):
                weights = jnp.exp2(tiles[t] * SCORE - top)
                total = total + jnp.sum(weights, axis=0, keepdims=True)
                value = keys[t // 2][t % 2, :, 192 + HEAD * h : 256 + HEAD * h]
                out = out + mm(value.T, weights.astype(BF))
            out = out / total
            os[j, HEAD * h : HEAD * h + HEAD, :] = out.astype(BF)
            stats[j, h : h + 1, :] = top + jnp.log2(total)
            stats[j, 3 + h : 4 + h, :] = jnp.sum(
                d_att.astype(F32).T * out, axis=0, keepdims=True
            )
        stats[j, 6:8, :] = jnp.zeros((2, 256), F32)
        return carry

    lax.fori_loop(0, 4, slot_step, 0)
    for j, ref in enumerate((o0, o1, o2, o3)):
        ref[...] = os[j]


def merge_kernel(s0, s1, s2, s3, o0, o1, o2, o3, wd, part, att, branch):
    stats = [ref[-step % 4] for step, ref in enumerate((s0, s1, s2, s3))]
    outs = [o0, o3, o2, o1]
    rows = []
    for h in range(HEADS):
        logs = [s[h : h + 1, :] for s in stats]
        top = functools.reduce(jnp.maximum, logs)
        shares = [jnp.exp2(v - top) for v in logs]
        total = functools.reduce(jnp.add, shares)
        mixed = functools.reduce(
            jnp.add,
            [
                share * ref[HEAD * h : HEAD * h + HEAD, :].astype(F32)
                for share, ref in zip(shares, outs, strict=True)
            ],
        )
        rows.append(mixed / total)
    att_low = jnp.concatenate(rows, axis=0).T.astype(BF)
    att[...] = att_low
    branch[...] = (mm(att_low, wd[...]) + part[...]).astype(BF)


def backward_kernel(
    coords, order, s0, s1, s2, s3, q0, q1, q2, q3, k0, k1, k2, k3,
    dq0, dq1, dq2, dq3, dk0, dk1, dk2, dk3, ks, dks, dqs, st,
):
    queries = (q0, q1, q2, q3)
    for b, ref in enumerate((k0, k1, k2, k3)):
        ks[2 * b : 2 * b + 2] = ref[...]
    dqs[...] = jnp.zeros_like(dqs)
    for j in range(4):
        parts = [ref[(j - step) % 4] for step, ref in enumerate((s0, s1, s2, s3))]
        logs = [p[0:3, :] for p in parts]
        top = functools.reduce(jnp.maximum, logs)
        total = functools.reduce(jnp.add, [jnp.exp2(v - top) for v in logs])
        whole = top + jnp.log2(total)
        st[j, 0:3, :] = whole
        st[j, 3:6, :] = functools.reduce(
            jnp.add, [jnp.exp2(p[0:3, :] - whole) * p[3:6, :] for p in parts]
        )
    gap = gap_table()

    def tile_step(t, carry):
        k_places = key_places(coords, order, t)
        for h in range(HEADS):
            key = ks[t, :, HEAD * h : HEAD * h + HEAD]
            value = ks[t, :, 192 + HEAD * h : 256 + HEAD * h]
            key_turned = key.T
            d_key = jnp.zeros((256, HEAD), F32)
            d_value = jnp.zeros((256, HEAD), F32)
            for j in range(4):
                query = queries[j][:, HEAD * h : HEAD * h + HEAD]
                d_att = queries[j][:, 192 + HEAD * h : 256 + HEAD * h]
                scores = mask_tile(
                    mm_nt(key, query), gap, query_places(coords, order, j), k_places
                )
                weights = jnp.exp2(scores * SCORE - st[j, h : h + 1, :])
                d_weights = mm_nt(value, d_att)
                d_scores = (weights * (d_weights - st[j, 3 + h : 4 + h, :])).astype(BF)
                d_value = d_value + mm(weights.astype(BF), d_att)
                d_key = d_key + mm(d_scores, query)
                dqs[j, HEAD * h : HEAD * h + HEAD, :] += mm(key_turned, d_scores)
            dks[t, :, HEAD * h : HEAD * h + HEAD] = (d_key * SCALE).astype(BF)
            dks[t, :, 192 + HEAD * h : 256 + HEAD * h] = d_value.astype(BF)
        return carry

    lax.fori_loop(0, 8, tile_step, 0)
    for j, ref in enumerate((dq0, dq1, dq2, dq3)):
        ref[...] = (dqs[j] * SCALE).astype(BF)
    for b, ref in enumerate((dk0, dk1, dk2, dk3)):
        ref[...] = dks[2 * b : 2 * b + 2]


def tail_kernel(
    coords, order, table, tok, cot, lna, wqkv, ga, gm, dq0, dq1, dq2, dq3, dkv0, dkv1,
    att, d_ln_mlp, small_in, g0, g1, g2, g3, upstream, small,
):
    d_query = (
        dq0[...].astype(F32) + dq1[...].astype(F32) + dq2[...].astype(F32) + dq3[...].astype(F32)
    ).T
    d_kv = dkv0[...].astype(F32) + dkv1[...].astype(F32)
    both = jnp.concatenate([d_query, d_kv[:, :192]], axis=1)
    cosine, left_sine, right_sine = spin_tables(coords, order, table)
    pieces = []
    for t in range(3):
        x = both[:, 128 * t : 128 * t + 128]
        back = (
            x * cosine
            + pltpu.roll(x * left_sine, 8, 1)
            + pltpu.roll(x * right_sine, 120, 1)
        )
        pieces += [back[:, :HEAD], back[:, HEAD:]]
    cols = []
    for h in range(HEADS):
        cols += [pieces[h], pieces[3 + h], d_kv[:, 192 + HEAD * h : 256 + HEAD * h]]
    d_joined = jnp.concatenate(cols, axis=1).astype(BF)
    grads = jnp.concatenate(
        [mm_tn(lna[...], d_joined), mm_tn(cot[...], att[...])], axis=1
    ).astype(BF)
    y = coords[2]
    for slot, ref in enumerate((g0, g1, g2, g3)):
        pass
    for piece in range(4):
        for slot, ref in enumerate((g0, g1, g2, g3)):

            @pl.when((y + slot) % 4 == piece)
            def _(ref=ref, piece=piece):
                ref[...] = grads[192 * piece : 192 * piece + 192, :]

    d_attn = mm_nt(d_joined, wqkv[...])
    d_mlp = d_ln_mlp[...]
    xhat, _ = normed(tok[...])
    upstream[...] = (d_attn * ga[...] + d_mlp * gm[...]).astype(BF)
    small[0:2, :] = small_in[0:2, :]
    small[2:3, :] = jnp.sum(d_attn * xhat, axis=0, keepdims=True)
    small[3:4, :] = jnp.sum(d_attn, axis=0, keepdims=True)
    small[4:5, :] = jnp.sum(d_mlp * xhat, axis=0, keepdims=True)
    small[5:6, :] = jnp.sum(d_mlp, axis=0, keepdims=True)
    small[6:7, 0:576] = jnp.sum(d_joined.astype(F32), axis=0, keepdims=True)
    small[6:7, 576:768] = jnp.zeros((1, 192), F32)
    small[7:8, :] = jnp.zeros((1, 768), F32)


def token_kernel(tok, cot, e0, e1, out):
    xhat, rstd = normed(tok[...])
    e = e0[...].astype(F32) + e1[...].astype(F32)
    inner = e - jnp.mean(e, axis=-1, keepdims=True)
    inner = inner - xhat * jnp.mean(e * xhat, axis=-1, keepdims=True)
    out[...] = (cot[...].astype(F32) + rstd * inner).astype(BF)


def assemble_kernel(coords, p0, p1, p2, p3, gq, gd, whole):
    for slot, ref in enumerate((p0, p1, p2, p3)):
        whole[(coords[2] + slot) % 4] = ref[...].astype(F32)
    for piece in range(4):
        gq[192 * piece : 192 * piece + 192, :] = whole[piece, :, 0:576]
        gd[:, 192 * piece : 192 * piece + 192] = whole[piece, :, 576:768].T


def call(kernel, outs, args, scalars, scratch=(), flops=0, mib=48):
    smem = pl.BlockSpec(memory_space=pltpu.SMEM)
    vmem = pl.BlockSpec(memory_space=pltpu.VMEM)
    shapes = [jax.ShapeDtypeStruct(s, d) for s, d in outs]
    moved = sum(math.prod(s) * np.dtype(d).itemsize for s, d in outs) + sum(
        a.size * a.dtype.itemsize for a in args
    )
    return pl.pallas_call(
        kernel,
        out_shape=shapes,
        in_specs=[smem] * scalars + [vmem] * (len(args) - scalars),
        out_specs=[vmem] * len(shapes),
        scratch_shapes=list(scratch),
        compiler_params=pltpu.CompilerParams(vmem_limit_bytes=mib << 20),
        cost_estimate=pl.CostEstimate(flops=flops, bytes_accessed=moved, transcendentals=0),
    )(*args)


def hop(x, axis, step):
    n = lax.axis_size(axis)
    return lax.ppermute(x, axis, [(i, (i + step) % n) for i in range(n)])


def add(*parts):
    return functools.reduce(jnp.add, [p.astype(F32) for p in parts])


def on_device(
    tokens,
    block_order,
    cotangent,
    w_qkv,
    b_qkv,
    w_dense,
    b_dense,
    w_up,
    b_up,
    w_down,
    b_down,
    gain_attn,
    shift_attn,
    gain_mlp,
    shift_mlp,
):
    coords = jnp.stack([lax.axis_index(a) for a in CTX]).astype(jnp.int32)
    table = jnp.asarray(lane_table())

    def row(v):
        return v.reshape(1, -1)

    qdo, kv, ln_attn, ln_mlp = call(
        front_kernel,
        [((256, 384), BF), ((256, 384), BF), ((256, 768), BF), ((256, 768), BF)],
        (coords, block_order, table, tokens, cotangent, w_qkv, row(b_qkv), w_dense,
         row(gain_attn), row(shift_attn), row(gain_mlp), row(shift_mlp)),
        2,
        flops=8 * 10**8,
    )
    kv0 = jnp.stack([kv, hop(kv, "xl", 1)])
    kvs = [kv0] + [hop(kv0, "z", -b) for b in (1, 3, 2)]
    kvs = [kvs[0], kvs[1], kvs[3], kvs[2]]
    qdos = [qdo] + [hop(qdo, "y", -j) for j in (1, 2, 3)]

    grads_mlp, small_mlp, part_mlp, d_ln_mlp = call(
        mlp_kernel,
        [((1536, 768), BF), ((8, 768), F32), ((256, 768), F32), ((256, 768), F32)],
        (ln_mlp, cotangent, w_up, row(b_up), w_down),
        0,
        flops=24 * 10**8,
    )
    grads_mlp = lax.psum_scatter(grads_mlp, ("z", "y"), scatter_dimension=0, tiled=True)
    grads_mlp = lax.psum(grads_mlp, "xl")
    grads_mlp = lax.all_gather(grads_mlp, ("z", "y"), axis=0, tiled=True)

    *outs, stats = call(
        forward_kernel,
        [((192, 256), BF)] * 4 + [((4, 8, 256), F32)],
        (coords, block_order, *qdos, *kvs),
        2,
        scratch=[pltpu.VMEM((4, 256, 384), BF), pltpu.VMEM((4, 192, 256), BF)],
        flops=64 * 10**8,
    )
    stats_all = [stats] + [hop(stats, "y", -j) for j in (1, 2, 3)]
    outs = [outs[0]] + [hop(outs[j], "y", j) for j in (1, 2, 3)]
    att, branch = call(
        merge_kernel,
        [((256, 192), BF), ((256, 768), BF)],
        (*stats_all, *outs, w_dense, part_mlp),
        0,
        flops=10**8,
    )
    branch = add(branch, hop(branch, "c", 1)).astype(BF)
    branch = add(branch, hop(branch, "xh", 1))
    output = (tokens.astype(F32) + branch + b_dense + b_down).astype(BF)

    grads = call(
        backward_kernel,
        [((192, 256), BF)] * 4 + [((2, 256, 384), BF)] * 4,
        (coords, block_order, *stats_all, *qdos, *kvs),
        2,
        scratch=[
            pltpu.VMEM((8, 256, 384), BF),
            pltpu.VMEM((8, 256, 384), BF),
            pltpu.VMEM((4, 192, 256), F32),
            pltpu.VMEM((4, 8, 256), F32),
        ],
        flops=160 * 10**8,
    )
    d_kvs = [grads[4]] + [hop(grads[4 + b], "z", b) for b in (1, 3, 2)]
    d_queries = [grads[0]] + [hop(grads[j], "y", j) for j in (1, 2, 3)]
    d_kv_own = add(*[d[0] for d in d_kvs]).astype(BF)
    d_kv_other = hop(add(*[d[1] for d in d_kvs]).astype(BF), "xl", 1)
    *pieces, upstream, small = call(
        tail_kernel,
        [((192, 768), BF)] * 4 + [((256, 768), BF), ((8, 768), F32)],
        (coords, block_order, table, tokens, cotangent, ln_attn, w_qkv, row(gain_attn),
         row(gain_mlp), *d_queries, d_kv_own, d_kv_other, att, d_ln_mlp, small_mlp),
        2,
        flops=8 * 10**8,
    )

    piece = add(pieces[0], *[hop(pieces[j], "y", j) for j in (1, 2, 3)])
    piece = piece.astype(BF).reshape(4, 48, 768)
    z = lax.axis_index("z")

    def block(j):
        return lax.dynamic_index_in_dim(piece, (z + j) % 4, 0, keepdims=False)

    third = add(block(0), *[hop(block(j), "z", j) for j in (1, 2, 3)]).astype(BF)
    third = add(third, hop(third, "xl", 1)).astype(BF)
    quarter = jnp.zeros((4, 48, 768), BF)
    for j, part in enumerate([third] + [hop(third, "z", -j) for j in (1, 2, 3)]):
        quarter = lax.dynamic_update_index_in_dim(quarter, part, (z + j) % 4, 0)
    quarter = quarter.reshape(192, 768)
    grad_w_qkv, grad_w_dense = call(
        assemble_kernel,
        [((768, 576), F32), ((192, 768), F32)],
        (coords, quarter, *[hop(quarter, "y", -j) for j in (1, 2, 3)]),
        1,
        scratch=[pltpu.VMEM((4, 192, 768), F32)],
    )

    upstream = add(upstream, hop(upstream, "c", 1)).astype(BF)
    (grad_tokens,) = call(
        token_kernel,
        [((256, 768), BF)],
        (tokens, cotangent, upstream, hop(upstream, "xh", 1)),
        0,
    )

    gains = small[2:6]
    gains = gains + hop(gains, "c", 1)
    gains = gains + hop(gains, "xh", 1)
    small = jnp.concatenate([small[0:2], gains, small[6:8]], axis=0)
    small = small + hop(small, "xl", 1)
    for axis in ("y", "z"):
        small = add(small, *[hop(small, axis, j) for j in (1, 2, 3)])

    return (
        output,
        grad_tokens,
        grad_w_qkv,
        small[6, :576],
        grad_w_dense,
        small[1],
        grads_mlp[:768].astype(F32),
        small[0],
        grads_mlp[768:].astype(F32),
        small[1],
        small[2],
        small[3],
        small[4],
        small[5],
    )


def solution(mesh):
    fine = Mesh(mesh.devices.reshape(2, 4, 4, 2, 2), CTX + TP)
    rows, cols = P(CTX, None), P(None, TP)
    return jax.shard_map(
        on_device,
        mesh=fine,
        in_specs=(
            rows, P(), rows, cols, P(TP), P(TP, None), P(), cols, P(TP), P(TP, None),
            P(), P(), P(), P(), P(),
        ),
        out_specs=(
            rows, rows, cols, P(TP), P(TP, None), P(), cols, P(TP), P(TP, None),
            P(), P(), P(), P(), P(),
        ),
        check_vma=False,
    )
```

time: 957 us -> 268 us (0.28)
  waiting for transfers between devices: 514 us -> 97.2 us
  blocking collectives: 157 us -> 0 us
  matrix products: 153 us -> 0 us
  starting transfers between devices: 0.34 us -> 65.5 us
  Pallas kernels: 0 us -> 53.8 us
  local copies, waits for them, and re-layouts: 75.5 us -> 27.6 us
  other arithmetic: 35.4 us -> 8.35 us
    reduce_scatter x1, waiting for transfers between devices: 166 us -> 0.01 us  [on_device(): lax.psum_scatter(grads_mlp, ('z', 'y'), scatter_dimension=0, tiled=True)]
    psum x2 -> x1, waiting for transfers between devices: 194 us -> 31.7 us  [on_device(): grads_mlp = lax.psum(grads_mlp, 'xl')]
    psum x1 -> x0, blocking collectives: 157 us -> none  [on_device(): lax.psum(grad_b_qkv.astype(jnp.bfloat16), 'ctx').astype(jnp.float32)]
    dot_general x124 -> x0, matrix products: 153 us -> none  [the longest x32 46.5 us: score_block(): jnp.einsum('qhd,khd->hqk', query_heads, keys_block, preferred_element_typ...]
    all_gather x1, waiting for transfers between devices: 153 us -> 0.01 us  [on_device(): grads_mlp = lax.all_gather(grads_mlp, ('z', 'y'), axis=0, tiled=True)]
    ppermute x0 -> x46, waiting for transfers between devices: none -> 65.4 us  [hop(): return lax.ppermute(x, axis, [(i, (i + step) % n) for i in range(n)])]
    ppermute x0 -> x46, starting transfers between devices: none -> 65.3 us  [hop(): return lax.ppermute(x, axis, [(i, (i + step) % n) for i in range(n)])]
    pallas_call x0 -> x8, Pallas kernels: none -> 53.8 us  [call(): pl.pallas_call(kernel, out_shape=shapes, in_specs=[smem] * scalars + [vme...]
  transfers between devices with their start and end apart: 4 -> 49, of which waited for: 4 -> 24; matrix products, arithmetic and copies ran while one was open for 2% -> 3% of each run, Pallas kernels for 0% -> 18%
where the time goes in v1:
time: 268 us; the launch traced here: 267 us
  waiting for transfers between devices  97.2 us (36%)
  starting transfers between devices  65.5 us (24%)
  Pallas kernels  53.8 us (20%)
  local copies, waits for them, and re-layouts  27.6 us (10%)
  between operations  14.1 us (5%)
  other arithmetic  8.35 us (3%)
    ppermute x46, waiting for transfers between devices, hop(): return lax.ppermute(x, axis, [(i, (i + step) % n) for i in range(n)])  65.4 us
    ppermute x46, starting transfers between devices, hop(): return lax.ppermute(x, axis, [(i, (i + step) % n) for i in range(n)])  65.3 us
    pallas_call x8, Pallas kernels, call(): pl.pallas_call(kernel, out_shape=shapes, in_specs=[smem] * scalars + [vme...  53.8 us
    psum x1, waiting for transfers between devices, on_device(): grads_mlp = lax.psum(grads_mlp, 'xl')  31.7 us
    unnamed x79, local copies, waits for them, and re-layouts  22.2 us
  transfers between devices with their start and end apart: 49, of which 24 were waited for; matrix products, arithmetic and copies ran while one was open for 3% of the time, Pallas kernels for 18%

profile of v1, /device:TPU:0, one launch (start us, length us, event | category | flops | bytes accessed | tf_op | source)
XLA Modules:
  0.0 266.6 jit_solution(2636815790238394288)
XLA Ops:
  7.2 1.6 copy.30.wqkv
  17.4 2.6 shard_map.263
  20.7 1.3 copy-done.24
  22.0 1.3 copy-done.25
  23.3 3.0 %shard_map.265 = (bf16[1536,768]{1,0:T(8,128)(2,1)}, f32[8,768]{1,0:T(8,128)S(1)}, f32[256,768]{1,0:T(8,128)S(1)}, f32[256,768]{1,0:T(8,128)S(1)}) custom-call(bf16[256,768]{1,0:T(8,128)(2,1)S(1)} %get-tuple-element.52.ln, bf16[256,768]{1,0:T(8,128)(2,1)S(1)} %copy-done.3, bf16[768,768]{1,0:T(8,128)(2,1)S(1)} %copy-done.24, f32[1,768]{1,0:T(1,128)S(1)} %reshape.79.bu, ...), custom_call_target="tpu_custom_call" | custom-call | flops 2400000000 | bytes 7105536 | tf_op jit(solution)/shard_map/pallas_call | solution.py:331
  26.9 1.7 collective-permute-start.3
  28.6 3.0 %collective-permute-start = (bf16[256,384]{1,0:T(8,128)(2,1)}, bf16[256,384]{1,0:T(8,128)(2,1)S(1)}, u32[]{:S(2)}, u32[]{:S(2)}) collective-permute-start(bf16[256,384]{1,0:T(8,128)(2,1)} %get-tuple-element.45.q0), channel_id=1, source_target_pairs={{0,12},{4,0},{8,4},{12,8},{1,13},{5,1},{9,5},{13,9},{2,14},{6,2},{... | collective-permute-start | bytes 589832 | tf_op jit(solution)/shard_map/ppermute | solution.py:344
  31.6 1.9 collective-permute-done.3
  33.6 4.4 %collective-permute-start.4 = (bf16[2,256,384]{2,1,0:T(8,128)(2,1)S(1)}, bf16[2,256,384]{2,1,0:T(8,128)(2,1)S(1)}, u32[]{:S(2)}, u32[]{:S(2)}) collective-permute-start(bf16[2,256,384]{2,1,0:T(8,128)(2,1)S(1)} %pad_maximum_fusion.k0), channel_id=1, source_target_pairs={{0,48},{16,0},{32,16},{48,32},{1,49},{17,1},{33,17},{49,33},{2,50}... | collective-permute-start | bytes 1179656 | tf_op jit(solution)/shard_map/ppermute | solution.py:344
  37.9 1.3 collective-permute-start.6
  39.2 3.2 %collective-permute-start.1 = (bf16[256,384]{1,0:T(8,128)(2,1)}, bf16[256,384]{1,0:T(8,128)(2,1)S(1)}, u32[]{:S(2)}, u32[]{:S(2)}) collective-permute-start(bf16[256,384]{1,0:T(8,128)(2,1)} %get-tuple-element.45.q0), channel_id=1, source_target_pairs={{0,8},{4,12},{8,0},{12,4},{1,9},{5,13},{9,1},{13,5},{2,10},{6,14},... | collective-permute-start | bytes 589832 | tf_op jit(solution)/shard_map/ppermute | solution.py:344
  43.0 5.9 %collective-permute-done.1.q2 = bf16[256,384]{1,0:T(8,128)(2,1)S(1)} collective-permute-done((bf16[256,384]{1,0:T(8,128)(2,1)}, bf16[256,384]{1,0:T(8,128)(2,1)S(1)}, u32[]{:S(2)}, u32[]{:S(2)}) %collective-permute-start.1) | collective-permute-done | bytes 196640 | tf_op jit(solution)/shard_map/ppermute | solution.py:344
  48.9 2.3 collective-permute-done.2.q3
  51.2 5.1 %collective-permute-done.4.k1 = bf16[2,256,384]{2,1,0:T(8,128)(2,1)S(1)} collective-permute-done((bf16[2,256,384]{2,1,0:T(8,128)(2,1)S(1)}, bf16[2,256,384]{2,1,0:T(8,128)(2,1)S(1)}, u32[]{:S(2)}, u32[]{:S(2)}) %collective-permute-start.4) | collective-permute-done | bytes 393248 | tf_op jit(solution)/shard_map/ppermute | solution.py:344
  56.3 3.2 %collective-permute-done.6.k3 = bf16[2,256,384]{2,1,0:T(8,128)(2,1)S(1)} collective-permute-done((bf16[2,256,384]{2,1,0:T(8,128)(2,1)S(1)}, bf16[2,256,384]{2,1,0:T(8,128)(2,1)S(1)}, u32[]{:S(2)}, u32[]{:S(2)}) %collective-permute-start.6) | collective-permute-done | bytes 393248 | tf_op jit(solution)/shard_map/ppermute | solution.py:344
  59.5 13.6 %shard_map.264 = (bf16[192,256]{1,0:T(8,128)(2,1)S(1)}, bf16[192,256]{1,0:T(8,128)(2,1)S(1)}, bf16[192,256]{1,0:T(8,128)(2,1)S(1)}, bf16[192,256]{1,0:T(8,128)(2,1)S(1)}, f32[4,8,256]{2,1,0:T(8,128)S(1)}) custom-call(s32[3]{0:T(128)S(1)} %pad_add_fusion.coords, s32[64]{0:T(128)S(1)} %copy-done.22, bf16[256,384]{1,0:T(8,128)(2,1)} %get-tuple-element.45.q0, ...), custom_call_target="tpu_custom_call" | custom-call | flops 6400000000 | bytes 2785548 | tf_op jit(solution)/shard_map/pallas_call | solution.py:331
  73.7 3.0 %collective-permute-start.7 = (f32[4,8,256]{2,1,0:T(8,128)S(1)}, f32[4,8,256]{2,1,0:T(8,128)S(1)}, u32[]{:S(2)}, u32[]{:S(2)}) collective-permute-start(f32[4,8,256]{2,1,0:T(8,128)S(1)} %get-tuple-element.47.s0), channel_id=1, source_target_pairs={{0,12},{4,0},{8,4},{12,8},{1,13},{5,1},{9,5},{13,9},{2,14},{6,2},{... | collective-permute-start | bytes 98312 | tf_op jit(solution)/shard_map/ppermute | solution.py:344
  78.4 3.8 %collective-permute-done.8.s2 = f32[4,8,256]{2,1,0:T(8,128)S(1)} collective-permute-done((f32[4,8,256]{2,1,0:T(8,128)S(1)}, f32[4,8,256]{2,1,0:T(8,128)S(1)}, u32[]{:S(2)}, u32[]{:S(2)}) %collective-permute-start.8) | collective-permute-done | bytes 32800 | tf_op jit(solution)/shard_map/ppermute | solution.py:344
  82.9 27.0 %shard_map.267 = (bf16[192,256]{1,0:T(8,128)(2,1)S(1)}, bf16[192,256]{1,0:T(8,128)(2,1)S(1)}, bf16[192,256]{1,0:T(8,128)(2,1)S(1)}, bf16[192,256]{1,0:T(8,128)(2...) custom-call(s32[3]{0:T(128)S(1)} %pad_add_fusion.coords, ...), custom_call_target="tpu_custom_call" | custom-call | flops 16000000000 | bytes 4456716 | tf_op jit(solution)/shard_map/pallas_call | solution.py:331
  115.6 31.7 %all-reduce.2.cloned.1.call-done = bf16[96,768]{1,0:T(8,128)(2,1)} async-done(((bf16[96,768]{1,0:T(8,128)(2,1)}), bf16[96,768]{1,0:T(8,128)(2,1)}) %all-reduce.2.cloned.1.call-update) | async-done | bytes 147472 | tf_op jit(solution)/shard_map/psum | solution.py:395
  147.4 1.6 collective-permute-start.10
  148.9 2.7 %collective-permute-start.11 = (bf16[192,256]{1,0:T(8,128)(2,1)}, bf16[192,256]{1,0:T(8,128)(2,1)S(1)}, u32[]{:S(2)}, u32[]{:S(2)}) collective-permute-start(bf16[192,256]{1,0:T(8,128)(2,1)} %copy-done.31), channel_id=1, source_target_pairs={{0,8},{4,12},{8,0},{12,4},{1,9},{5,13},{9,1},{13,5},{2,10},{6,14},... | collective-permute-start | bytes 294920 | tf_op jit(solution)/shard_map/ppermute | solution.py:344
  151.6 1.7 fusion.1
  153.9 1.4 collective-permute-start.12
  156.8 1.8 collective-permute-start.17
  165.3 3.0 %shard_map.268 = (bf16[192,768]{1,0:T(8,128)(2,1)S(1)}, bf16[192,768]{1,0:T(8,128)(2,1)S(1)}, bf16[192,768]{1,0:T(8,128)(2,1)S(1)}, bf16[192,768]{1,0:T(8,128)(2...) custom-call(s32[3]{0:T(128)S(1)} %pad_add_fusion.coords, s32[64]{0:T(128)S(1)} %copy-done.23, ...), custom_call_target="tpu_custom_call" | custom-call | flops 800000000 | bytes 5368076 | tf_op jit(solution)/shard_map/pallas_call | solution.py:331
  171.6 3.1 %collective-permute-start.38 = (f32[4,768]{1,0:T(4,128)S(1)}, f32[4,768]{1,0:T(4,128)S(1)}, u32[]{:S(2)}, u32[]{:S(2)}) collective-permute-start(f32[4,768]{1,0:T(4,128)S(1)} %slice_add_fusion), channel_id=1, source_target_pairs={{0,2},{2,0},{1,3},{3,1},{4,6},{6,4},{5,7},{7,5},{8,10},{10,8},{9,1... | collective-permute-start | bytes 36872 | tf_op jit(solution)/shard_map/ppermute | solution.py:344
  174.7 2.2 collective-permute-done.38
  176.9 1.5 collective-permute-start.39
  178.5 2.4 collective-permute-done.39
  180.8 3.8 %collective-permute-start.42 = (f32[8,768]{1,0:T(8,128)S(1)}, f32[8,768]{1,0:T(8,128)S(1)}, u32[]{:S(2)}, u32[]{:S(2)}) collective-permute-start(f32[8,768]{1,0:T(8,128)S(1)} %fusion.5), channel_id=1, source_target_pairs={{0,12},{4,0},{8,4},{12,8},{1,13},{5,1},{9,5},{13,9},{2,14},{6,2},{... | collective-permute-start | bytes 73736 | tf_op jit(solution)/shard_map/ppermute | solution.py:344
  185.0 1.7 collective-permute-start.24
  186.7 4.1 %collective-permute-start.41 = (f32[8,768]{1,0:T(8,128)S(1)}, f32[8,768]{1,0:T(8,128)S(1)}, u32[]{:S(2)}, u32[]{:S(2)}) collective-permute-start(f32[8,768]{1,0:T(8,128)S(1)} %fusion.5), channel_id=1, source_target_pairs={{0,8},{4,12},{8,0},{12,4},{1,9},{5,13},{9,1},{13,5},{2,10},{6,14},... | collective-permute-start | bytes 73736 | tf_op jit(solution)/shard_map/ppermute | solution.py:344
  191.9 15.2 %collective-permute-done.41 = f32[8,768]{1,0:T(8,128)S(1)} collective-permute-done((f32[8,768]{1,0:T(8,128)S(1)}, f32[8,768]{1,0:T(8,128)S(1)}, u32[]{:S(2)}, u32[]{:S(2)}) %collective-permute-start.41) | collective-permute-done | bytes 24608 | tf_op jit(solution)/shard_map/ppermute | solution.py:344
  207.1 3.0 %collective-permute-start.14 = (bf16[256,768]{1,0:T(8,128)(2,1)S(1)}, bf16[256,768]{1,0:T(8,128)(2,1)S(1)}, u32[]{:S(2)}, u32[]{:S(2)}) collective-permute-start(bf16[256,768]{1,0:T(8,128)(2,1)S(1)} %add_convert_fusion.2), channel_id=1, source_target_pairs={{0,2},{2,0},{1,3},{3,1},{4,6},{6,4},{5,7},{7,5},{8,10},{10,8},{9,1... | collective-permute-start | bytes 1179656 | tf_op jit(solution)/shard_map/ppermute | solution.py:344
  210.1 2.9 %collective-permute-start.45 = (f32[8,768]{1,0:T(8,128)S(1)}, f32[8,768]{1,0:T(8,128)S(1)}, u32[]{:S(2)}, u32[]{:S(2)}) collective-permute-start(f32[8,768]{1,0:T(8,128)S(1)} %add_add_fusion.1), channel_id=1, source_target_pairs={{0,48},{16,0},{32,16},{48,32},{1,49},{17,1},{33,17},{49,33},{2,50}... | collective-permute-start | bytes 73736 | tf_op jit(solution)/shard_map/ppermute | solution.py:344
  214.8 3.2 %collective-permute-start.29 = (bf16[48,768]{1,0:T(8,128)(2,1)S(1)}, bf16[48,768]{1,0:T(8,128)(2,1)S(1)}, u32[]{:S(2)}, u32[]{:S(2)}) collective-permute-start(bf16[48,768]{1,0:T(8,128)(2,1)S(1)} %get-tuple-element.103), channel_id=1, source_target_pairs={{0,48},{16,0},{32,16},{48,32},{1,49},{17,1},{33,17},{49,33},{2,50}... | collective-permute-start | bytes 221192 | tf_op jit(solution)/shard_map/ppermute | solution.py:344
  220.5 3.7 %collective-permute-done.28 = bf16[48,768]{1,0:T(8,128)(2,1)S(1)} collective-permute-done((bf16[48,768]{1,0:T(8,128)(2,1)S(1)}, bf16[48,768]{1,0:T(8,128)(2,1)S(1)}, u32[]{:S(2)}, u32[]{:S(2)}) %collective-permute-start.28) | collective-permute-done | bytes 73760 | tf_op jit(solution)/shard_map/ppermute | solution.py:344
  226.3 3.1 %collective-permute-done.30 = bf16[48,768]{1,0:T(8,128)(2,1)S(1)} collective-permute-done((bf16[48,768]{1,0:T(8,128)(2,1)S(1)}, bf16[48,768]{1,0:T(8,128)(2,1)S(1)}, u32[]{:S(2)}, u32[]{:S(2)}) %collective-permute-start.30) | collective-permute-done | bytes 73760 | tf_op jit(solution)/shard_map/ppermute | solution.py:344
  234.0 2.9 %collective-permute-done.32 = bf16[48,768]{1,0:T(8,128)(2,1)S(1)} collective-permute-done((bf16[48,768]{1,0:T(8,128)(2,1)S(1)}, bf16[48,768]{1,0:T(8,128)(2,1)S(1)}, u32[]{:S(2)}, u32[]{:S(2)}) %collective-permute-start.32) | collective-permute-done | bytes 73760 | tf_op jit(solution)/shard_map/ppermute | solution.py:344
  237.6 1.3 collective-permute-start.34
  241.7 1.3 shard_map.269
  243.0 2.7 %collective-permute-done.34.p1 = bf16[192,768]{1,0:T(8,128)(2,1)S(1)} collective-permute-done((bf16[192,768]{1,0:T(8,128)(2,1)S(1)}, bf16[192,768]{1,0:T(8,128)(2,1)S(1)}, u32[]{:S(2)}, u32[]{:S(2)}) %collective-permute-start.34) | collective-permute-done | bytes 294944 | tf_op jit(solution)/shard_map/ppermute | solution.py:344
  245.7 2.6 collective-permute-done.35.p2
  248.3 3.0 %collective-permute-done.36.p3 = bf16[192,768]{1,0:T(8,128)(2,1)S(1)} collective-permute-done((bf16[192,768]{1,0:T(8,128)(2,1)S(1)}, bf16[192,768]{1,0:T(8,128)(2,1)S(1)}, u32[]{:S(2)}, u32[]{:S(2)}) %collective-permute-start.36) | collective-permute-done | bytes 294944 | tf_op jit(solution)/shard_map/ppermute | solution.py:344
  251.3 2.2 shard_map.270
  253.6 1.7 copy.32
  255.3 4.2 %slice_convert_fusion = (f32[768,768]{1,0:T(8,128)}, f32[768,768]{1,0:T(8,128)}) fusion(bf16[1536,768]{1,0:T(8,128)(2,1)} %all-gather.2.cloned.1.call-done), kind=kLoop, calls=%fused_computation | loop fusion | flops 1179648 | bytes 7077888 | tf_op jit(solution)/shard_map/convert_element_type | solution.py:491
  (171 shorter events, 47.8 us)
Async XLA Ops:
  7.2 108.3 %reduce-scatter.2.cloned.1.call-start = ((), (), s32[]{:S(2)}) async-start(), calls=%async_computation.1 | async-start | bytes 2506752 | tf_op jit(solution)/shard_map/reduce_scatter | solution.py:394
  26.9 120.4 %all-reduce.2.cloned.1.call-start = ((), (), s32[]{:S(2)}) async-start(), calls=%async_computation.2 | async-start | bytes 294912 | tf_op jit(solution)/shard_map/psum | solution.py:395
  26.9 6.6 %collective-permute-start.3 = (bf16[256,384]{1,0:T(8,128)(2,1)S(1)}, bf16[256,384]{1,0:T(8,128)(2,1)S(1)}, u32[]{:S(2)}, u32[]{:S(2)}) collective-permute-start(bf16[256,384]{1,0:T(8,128)(2,1)S(1)} %get-tuple-element.46), channel_id=1, source_target_pairs={{0,64},{64,0},{1,65},{65,1},{2,66},{66,2},{3,67},{67,3},{4,68},{68... | collective-permute-start | bytes 589832 | tf_op jit(solution)/shard_map/ppermute | solution.py:344
  28.6 13.8 %collective-permute-start = (bf16[256,384]{1,0:T(8,128)(2,1)}, bf16[256,384]{1,0:T(8,128)(2,1)S(1)}, u32[]{:S(2)}, u32[]{:S(2)}) collective-permute-start(bf16[256,384]{1,0:T(8,128)(2,1)} %get-tuple-element.45.q0), channel_id=1, source_target_pairs={{0,12},{4,0},{8,4},{12,8},{1,13},{5,1},{9,5},{13,9},{2,14},{6,2},{... | collective-permute-start | bytes 589832 | tf_op jit(solution)/shard_map/ppermute | solution.py:344
  33.6 22.8 %collective-permute-start.4 = (bf16[2,256,384]{2,1,0:T(8,128)(2,1)S(1)}, bf16[2,256,384]{2,1,0:T(8,128)(2,1)S(1)}, u32[]{:S(2)}, u32[]{:S(2)}) collective-permute-start(bf16[2,256,384]{2,1,0:T(8,128)(2,1)S(1)} %pad_maximum_fusion.k0), channel_id=1, source_target_pairs={{0,48},{16,0},{32,16},{48,32},{1,49},{17,1},{33,17},{49,33},{2,50}... | collective-permute-start | bytes 1179656 | tf_op jit(solution)/shard_map/ppermute | solution.py:344
  37.9 18.4 %collective-permute-start.5 = (bf16[2,256,384]{2,1,0:T(8,128)(2,1)S(1)}, bf16[2,256,384]{2,1,0:T(8,128)(2,1)S(1)}, u32[]{:S(2)}, u32[]{:S(2)}) collective-permute-start(bf16[2,256,384]{2,1,0:T(8,128)(2,1)S(1)} %pad_maximum_fusion.k0), channel_id=1, source_target_pairs={{0,32},{16,48},{32,0},{48,16},{1,33},{17,49},{33,1},{49,17},{2,34}... | collective-permute-start | bytes 1179656 | tf_op jit(solution)/shard_map/ppermute | solution.py:344
  37.9 21.6 %collective-permute-start.6 = (bf16[2,256,384]{2,1,0:T(8,128)(2,1)S(1)}, bf16[2,256,384]{2,1,0:T(8,128)(2,1)S(1)}, u32[]{:S(2)}, u32[]{:S(2)}) collective-permute-start(bf16[2,256,384]{2,1,0:T(8,128)(2,1)S(1)} %pad_maximum_fusion.k0), channel_id=1, source_target_pairs={{0,16},{16,32},{32,48},{48,0},{1,17},{17,33},{33,49},{49,1},{2,18}... | collective-permute-start | bytes 1179656 | tf_op jit(solution)/shard_map/ppermute | solution.py:344
  39.2 9.7 %collective-permute-start.1 = (bf16[256,384]{1,0:T(8,128)(2,1)}, bf16[256,384]{1,0:T(8,128)(2,1)S(1)}, u32[]{:S(2)}, u32[]{:S(2)}) collective-permute-start(bf16[256,384]{1,0:T(8,128)(2,1)} %get-tuple-element.45.q0), channel_id=1, source_target_pairs={{0,8},{4,12},{8,0},{12,4},{1,9},{5,13},{9,1},{13,5},{2,10},{6,14},... | collective-permute-start | bytes 589832 | tf_op jit(solution)/shard_map/ppermute | solution.py:344
  42.4 8.8 %collective-permute-start.2 = (bf16[256,384]{1,0:T(8,128)(2,1)}, bf16[256,384]{1,0:T(8,128)(2,1)S(1)}, u32[]{:S(2)}, u32[]{:S(2)}) collective-permute-start(bf16[256,384]{1,0:T(8,128)(2,1)} %get-tuple-element.45.q0), channel_id=1, source_target_pairs={{0,4},{4,8},{8,12},{12,0},{1,5},{5,9},{9,13},{13,1},{2,6},{6,10},{... | collective-permute-start | bytes 589832 | tf_op jit(solution)/shard_map/ppermute | solution.py:344
  73.7 4.6 %collective-permute-start.7 = (f32[4,8,256]{2,1,0:T(8,128)S(1)}, f32[4,8,256]{2,1,0:T(8,128)S(1)}, u32[]{:S(2)}, u32[]{:S(2)}) collective-permute-start(f32[4,8,256]{2,1,0:T(8,128)S(1)} %get-tuple-element.47.s0), channel_id=1, source_target_pairs={{0,12},{4,0},{8,4},{12,8},{1,13},{5,1},{9,5},{13,9},{2,14},{6,2},{... | collective-permute-start | bytes 98312 | tf_op jit(solution)/shard_map/ppermute | solution.py:344
  76.8 5.4 %collective-permute-start.8 = (f32[4,8,256]{2,1,0:T(8,128)S(1)}, f32[4,8,256]{2,1,0:T(8,128)S(1)}, u32[]{:S(2)}, u32[]{:S(2)}) collective-permute-start(f32[4,8,256]{2,1,0:T(8,128)S(1)} %get-tuple-element.47.s0), channel_id=1, source_target_pairs={{0,8},{4,12},{8,0},{12,4},{1,9},{5,13},{9,1},{13,5},{2,10},{6,14},... | collective-permute-start | bytes 98312 | tf_op jit(solution)/shard_map/ppermute | solution.py:344
  77.4 5.5 %collective-permute-start.9 = (f32[4,8,256]{2,1,0:T(8,128)S(1)}, f32[4,8,256]{2,1,0:T(8,128)S(1)}, u32[]{:S(2)}, u32[]{:S(2)}) collective-permute-start(f32[4,8,256]{2,1,0:T(8,128)S(1)} %get-tuple-element.47.s0), channel_id=1, source_target_pairs={{0,4},{4,8},{8,12},{12,0},{1,5},{5,9},{9,13},{13,1},{2,6},{6,10},{... | collective-permute-start | bytes 98312 | tf_op jit(solution)/shard_map/ppermute | solution.py:344
  112.6 39.0 %collective-permute-start.20 = (bf16[2,256,384]{2,1,0:T(8,128)(2,1)}, bf16[2,256,384]{2,1,0:T(8,128)(2,1)}, u32[]{:S(2)}, u32[]{:S(2)}) collective-permute-start(bf16[2,256,384]{2,1,0:T(8,128)(2,1)} %get-tuple-element.63), channel_id=1, source_target_pairs={{0,32},{16,48},{32,0},{48,16},{1,33},{17,49},{33,1},{49,17},{2,34}... | collective-permute-start | bytes 1179656 | tf_op jit(solution)/shard_map/ppermute | solution.py:344
  113.5 38.2 %collective-permute-start.19 = (bf16[2,256,384]{2,1,0:T(8,128)(2,1)}, bf16[2,256,384]{2,1,0:T(8,128)(2,1)}, u32[]{:S(2)}, u32[]{:S(2)}) collective-permute-start(bf16[2,256,384]{2,1,0:T(8,128)(2,1)} %get-tuple-element.62), channel_id=1, source_target_pairs={{0,48},{16,0},{32,16},{48,32},{1,49},{17,1},{33,17},{49,33},{2,50}... | collective-permute-start | bytes 1179656 | tf_op jit(solution)/shard_map/ppermute | solution.py:344
  114.6 37.0 %collective-permute-start.18 = (bf16[2,256,384]{2,1,0:T(8,128)(2,1)}, bf16[2,256,384]{2,1,0:T(8,128)(2,1)}, u32[]{:S(2)}, u32[]{:S(2)}) collective-permute-start(bf16[2,256,384]{2,1,0:T(8,128)(2,1)} %get-tuple-element.61), channel_id=1, source_target_pairs={{0,16},{16,32},{32,48},{48,0},{1,17},{17,33},{33,49},{49,1},{2,18}... | collective-permute-start | bytes 1179656 | tf_op jit(solution)/shard_map/ppermute | solution.py:344
  115.5 139.7 %all-gather.2.cloned.1.call-start = ((), (), s32[]{:S(2)}) async-start(), calls=%async_computation.3 | async-start | bytes 2506752 | tf_op jit(solution)/shard_map/all_gather | solution.py:396
  147.4 8.6 %collective-permute-start.10 = (bf16[192,256]{1,0:T(8,128)(2,1)}, bf16[192,256]{1,0:T(8,128)(2,1)S(1)}, u32[]{:S(2)}, u32[]{:S(2)}) collective-permute-start(bf16[192,256]{1,0:T(8,128)(2,1)} %copy-done.34), channel_id=1, source_target_pairs={{0,4},{4,8},{8,12},{12,0},{1,5},{5,9},{9,13},{13,1},{2,6},{6,10},{... | collective-permute-start | bytes 294920 | tf_op jit(solution)/shard_map/ppermute | solution.py:344
  148.9 7.9 %collective-permute-start.11 = (bf16[192,256]{1,0:T(8,128)(2,1)}, bf16[192,256]{1,0:T(8,128)(2,1)S(1)}, u32[]{:S(2)}, u32[]{:S(2)}) collective-permute-start(bf16[192,256]{1,0:T(8,128)(2,1)} %copy-done.31), channel_id=1, source_target_pairs={{0,8},{4,12},{8,0},{12,4},{1,9},{5,13},{9,1},{13,5},{2,10},{6,14},... | collective-permute-start | bytes 294920 | tf_op jit(solution)/shard_map/ppermute | solution.py:344
  153.3 11.3 %collective-permute-start.21 = (bf16[256,384]{1,0:T(8,128)(2,1)S(1)}, bf16[256,384]{1,0:T(8,128)(2,1)S(1)}, u32[]{:S(2)}, u32[]{:S(2)}) collective-permute-start(bf16[256,384]{1,0:T(8,128)(2,1)S(1)} %get-tuple-element.100), channel_id=1, source_target_pairs={{0,64},{64,0},{1,65},{65,1},{2,66},{66,2},{3,67},{67,3},{4,68},{68... | collective-permute-start | bytes 589832 | tf_op jit(solution)/shard_map/ppermute | solution.py:344
  153.9 5.5 %collective-permute-start.12 = (bf16[192,256]{1,0:T(8,128)(2,1)}, bf16[192,256]{1,0:T(8,128)(2,1)S(1)}, u32[]{:S(2)}, u32[]{:S(2)}) collective-permute-start(bf16[192,256]{1,0:T(8,128)(2,1)} %copy-done.29), channel_id=1, source_target_pairs={{0,12},{4,0},{8,4},{12,8},{1,13},{5,1},{9,5},{13,9},{2,14},{6,2},{... | collective-permute-start | bytes 294920 | tf_op jit(solution)/shard_map/ppermute | solution.py:344
  155.4 9.2 %collective-permute-start.15 = (bf16[192,256]{1,0:T(8,128)(2,1)}, bf16[192,256]{1,0:T(8,128)(2,1)S(1)}, u32[]{:S(2)}, u32[]{:S(2)}) collective-permute-start(bf16[192,256]{1,0:T(8,128)(2,1)} %copy-done.33), channel_id=1, source_target_pairs={{0,4},{4,8},{8,12},{12,0},{1,5},{5,9},{9,13},{13,1},{2,6},{6,10},{... | collective-permute-start | bytes 294920 | tf_op jit(solution)/shard_map/ppermute | solution.py:344
  156.0 8.6 %collective-permute-start.16 = (bf16[192,256]{1,0:T(8,128)(2,1)}, bf16[192,256]{1,0:T(8,128)(2,1)S(1)}, u32[]{:S(2)}, u32[]{:S(2)}) collective-permute-start(bf16[192,256]{1,0:T(8,128)(2,1)} %copy-done.32), channel_id=1, source_target_pairs={{0,8},{4,12},{8,0},{12,4},{1,9},{5,13},{9,1},{13,5},{2,10},{6,14},... | collective-permute-start | bytes 294920 | tf_op jit(solution)/shard_map/ppermute | solution.py:344
  156.8 7.7 %collective-permute-start.17 = (bf16[192,256]{1,0:T(8,128)(2,1)}, bf16[192,256]{1,0:T(8,128)(2,1)S(1)}, u32[]{:S(2)}, u32[]{:S(2)}) collective-permute-start(bf16[192,256]{1,0:T(8,128)(2,1)} %copy-done.30), channel_id=1, source_target_pairs={{0,12},{4,0},{8,4},{12,8},{1,13},{5,1},{9,5},{13,9},{2,14},{6,2},{... | collective-permute-start | bytes 294920 | tf_op jit(solution)/shard_map/ppermute | solution.py:344
  170.4 16.2 %collective-permute-start.13 = (bf16[256,768]{1,0:T(8,128)(2,1)}, bf16[256,768]{1,0:T(8,128)(2,1)S(1)}, u32[]{:S(2)}, u32[]{:S(2)}) collective-permute-start(bf16[256,768]{1,0:T(8,128)(2,1)} %get-tuple-element.54), channel_id=1, source_target_pairs={{0,1},{1,0},{2,3},{3,2},{4,5},{5,4},{6,7},{7,6},{8,9},{9,8},{10,11... | collective-permute-start | bytes 1179656 | tf_op jit(solution)/shard_map/ppermute | solution.py:344
  171.6 5.3 %collective-permute-start.38 = (f32[4,768]{1,0:T(4,128)S(1)}, f32[4,768]{1,0:T(4,128)S(1)}, u32[]{:S(2)}, u32[]{:S(2)}) collective-permute-start(f32[4,768]{1,0:T(4,128)S(1)} %slice_add_fusion), channel_id=1, source_target_pairs={{0,2},{2,0},{1,3},{3,1},{4,6},{6,4},{5,7},{7,5},{8,10},{10,8},{9,1... | collective-permute-start | bytes 36872 | tf_op jit(solution)/shard_map/ppermute | solution.py:344
  176.9 3.9 %collective-permute-start.39 = (f32[8,768]{1,0:T(8,128)S(1)}, f32[8,768]{1,0:T(8,128)S(1)}, u32[]{:S(2)}, u32[]{:S(2)}) collective-permute-start(f32[8,768]{1,0:T(8,128)S(1)} %pad_maximum_fusion.1), channel_id=1, source_target_pairs={{0,64},{64,0},{1,65},{65,1},{2,66},{66,2},{3,67},{67,3},{4,68},{68... | collective-permute-start | bytes 73736 | tf_op jit(solution)/shard_map/ppermute | solution.py:344
  180.8 10.0 %collective-permute-start.42 = (f32[8,768]{1,0:T(8,128)S(1)}, f32[8,768]{1,0:T(8,128)S(1)}, u32[]{:S(2)}, u32[]{:S(2)}) collective-permute-start(f32[8,768]{1,0:T(8,128)S(1)} %fusion.5), channel_id=1, source_target_pairs={{0,12},{4,0},{8,4},{12,8},{1,13},{5,1},{9,5},{13,9},{2,14},{6,2},{... | collective-permute-start | bytes 73736 | tf_op jit(solution)/shard_map/ppermute | solution.py:344
  184.6 25.5 %collective-permute-start.26 = (bf16[192,768]{1,0:T(8,128)(2,1)}, bf16[192,768]{1,0:T(8,128)(2,1)S(1)}, u32[]{:S(2)}, u32[]{:S(2)}) collective-permute-start(bf16[192,768]{1,0:T(8,128)(2,1)} %copy-done.28), channel_id=1, source_target_pairs={{0,12},{4,0},{8,4},{12,8},{1,13},{5,1},{9,5},{13,9},{2,14},{6,2},{... | collective-permute-start | bytes 884744 | tf_op jit(solution)/shard_map/ppermute | solution.py:344
  184.8 28.2 %collective-permute-start.25 = (bf16[192,768]{1,0:T(8,128)(2,1)}, bf16[192,768]{1,0:T(8,128)(2,1)S(1)}, u32[]{:S(2)}, u32[]{:S(2)}) collective-permute-start(bf16[192,768]{1,0:T(8,128)(2,1)} %copy-done.27), channel_id=1, source_target_pairs={{0,8},{4,12},{8,0},{12,4},{1,9},{5,13},{9,1},{13,5},{2,10},{6,14},... | collective-permute-start | bytes 884744 | tf_op jit(solution)/shard_map/ppermute | solution.py:344
  185.0 28.7 %collective-permute-start.24 = (bf16[192,768]{1,0:T(8,128)(2,1)}, bf16[192,768]{1,0:T(8,128)(2,1)S(1)}, u32[]{:S(2)}, u32[]{:S(2)}) collective-permute-start(bf16[192,768]{1,0:T(8,128)(2,1)} %copy-done.26), channel_id=1, source_target_pairs={{0,4},{4,8},{8,12},{12,0},{1,5},{5,9},{9,13},{13,1},{2,6},{6,10},{... | collective-permute-start | bytes 884744 | tf_op jit(solution)/shard_map/ppermute | solution.py:344
  186.7 20.4 %collective-permute-start.41 = (f32[8,768]{1,0:T(8,128)S(1)}, f32[8,768]{1,0:T(8,128)S(1)}, u32[]{:S(2)}, u32[]{:S(2)}) collective-permute-start(f32[8,768]{1,0:T(8,128)S(1)} %fusion.5), channel_id=1, source_target_pairs={{0,8},{4,12},{8,0},{12,4},{1,9},{5,13},{9,1},{13,5},{2,10},{6,14},... | collective-permute-start | bytes 73736 | tf_op jit(solution)/shard_map/ppermute | solution.py:344
  190.8 19.2 %collective-permute-start.40 = (f32[8,768]{1,0:T(8,128)S(1)}, f32[8,768]{1,0:T(8,128)S(1)}, u32[]{:S(2)}, u32[]{:S(2)}) collective-permute-start(f32[8,768]{1,0:T(8,128)S(1)} %fusion.5), channel_id=1, source_target_pairs={{0,4},{4,8},{8,12},{12,0},{1,5},{5,9},{9,13},{13,1},{2,6},{6,10},{... | collective-permute-start | bytes 73736 | tf_op jit(solution)/shard_map/ppermute | solution.py:344
  207.1 33.7 %collective-permute-start.14 = (bf16[256,768]{1,0:T(8,128)(2,1)S(1)}, bf16[256,768]{1,0:T(8,128)(2,1)S(1)}, u32[]{:S(2)}, u32[]{:S(2)}) collective-permute-start(bf16[256,768]{1,0:T(8,128)(2,1)S(1)} %add_convert_fusion.2), channel_id=1, source_target_pairs={{0,2},{2,0},{1,3},{3,1},{4,6},{6,4},{5,7},{7,5},{8,10},{10,8},{9,1... | collective-permute-start | bytes 1179656 | tf_op jit(solution)/shard_map/ppermute | solution.py:344
  210.1 20.1 %collective-permute-start.22 = (bf16[256,768]{1,0:T(8,128)(2,1)S(1)}, bf16[256,768]{1,0:T(8,128)(2,1)S(1)}, u32[]{:S(2)}, u32[]{:S(2)}) collective-permute-start(bf16[256,768]{1,0:T(8,128)(2,1)S(1)} %get-tuple-element.67), channel_id=1, source_target_pairs={{0,1},{1,0},{2,3},{3,2},{4,5},{5,4},{6,7},{7,6},{8,9},{9,8},{10,11... | collective-permute-start | bytes 1179656 | tf_op jit(solution)/shard_map/ppermute | solution.py:344
  210.1 4.7 %collective-permute-start.45 = (f32[8,768]{1,0:T(8,128)S(1)}, f32[8,768]{1,0:T(8,128)S(1)}, u32[]{:S(2)}, u32[]{:S(2)}) collective-permute-start(f32[8,768]{1,0:T(8,128)S(1)} %add_add_fusion.1), channel_id=1, source_target_pairs={{0,48},{16,0},{32,16},{48,32},{1,49},{17,1},{33,17},{49,33},{2,50}... | collective-permute-start | bytes 73736 | tf_op jit(solution)/shard_map/ppermute | solution.py:344
  213.0 5.3 %collective-permute-start.44 = (f32[8,768]{1,0:T(8,128)S(1)}, f32[8,768]{1,0:T(8,128)S(1)}, u32[]{:S(2)}, u32[]{:S(2)}) collective-permute-start(f32[8,768]{1,0:T(8,128)S(1)} %add_add_fusion.1), channel_id=1, source_target_pairs={{0,32},{16,48},{32,0},{48,16},{1,33},{17,49},{33,1},{49,17},{2,34}... | collective-permute-start | bytes 73736 | tf_op jit(solution)/shard_map/ppermute | solution.py:344
  213.7 5.6 %collective-permute-start.43 = (f32[8,768]{1,0:T(8,128)S(1)}, f32[8,768]{1,0:T(8,128)S(1)}, u32[]{:S(2)}, u32[]{:S(2)}) collective-permute-start(f32[8,768]{1,0:T(8,128)S(1)} %add_add_fusion.1), channel_id=1, source_target_pairs={{0,16},{16,32},{32,48},{48,0},{1,17},{17,33},{33,49},{49,1},{2,18}... | collective-permute-start | bytes 73736 | tf_op jit(solution)/shard_map/ppermute | solution.py:344
  214.8 5.7 %collective-permute-start.29 = (bf16[48,768]{1,0:T(8,128)(2,1)S(1)}, bf16[48,768]{1,0:T(8,128)(2,1)S(1)}, u32[]{:S(2)}, u32[]{:S(2)}) collective-permute-start(bf16[48,768]{1,0:T(8,128)(2,1)S(1)} %get-tuple-element.103), channel_id=1, source_target_pairs={{0,48},{16,0},{32,16},{48,32},{1,49},{17,1},{33,17},{49,33},{2,50}... | collective-permute-start | bytes 221192 | tf_op jit(solution)/shard_map/ppermute | solution.py:344
  218.3 5.9 %collective-permute-start.28 = (bf16[48,768]{1,0:T(8,128)(2,1)S(1)}, bf16[48,768]{1,0:T(8,128)(2,1)S(1)}, u32[]{:S(2)}, u32[]{:S(2)}) collective-permute-start(bf16[48,768]{1,0:T(8,128)(2,1)S(1)} %get-tuple-element.104), channel_id=1, source_target_pairs={{0,32},{16,48},{32,0},{48,16},{1,33},{17,49},{33,1},{49,17},{2,34}... | collective-permute-start | bytes 221192 | tf_op jit(solution)/shard_map/ppermute | solution.py:344
  219.3 5.7 %collective-permute-start.27 = (bf16[48,768]{1,0:T(8,128)(2,1)S(1)}, bf16[48,768]{1,0:T(8,128)(2,1)S(1)}, u32[]{:S(2)}, u32[]{:S(2)}) collective-permute-start(bf16[48,768]{1,0:T(8,128)(2,1)S(1)} %get-tuple-element.102), channel_id=1, source_target_pairs={{0,16},{16,32},{32,48},{48,0},{1,17},{17,33},{33,49},{49,1},{2,18}... | collective-permute-start | bytes 221192 | tf_op jit(solution)/shard_map/ppermute | solution.py:344
  225.0 4.4 %collective-permute-start.30 = (bf16[48,768]{1,0:T(8,128)(2,1)S(1)}, bf16[48,768]{1,0:T(8,128)(2,1)S(1)}, u32[]{:S(2)}, u32[]{:S(2)}) collective-permute-start(bf16[48,768]{1,0:T(8,128)(2,1)S(1)} %fusion.4), channel_id=1, source_target_pairs={{0,64},{64,0},{1,65},{65,1},{2,66},{66,2},{3,67},{67,3},{4,68},{68... | collective-permute-start | bytes 221192 | tf_op jit(solution)/shard_map/ppermute | solution.py:344
  229.5 4.4 %collective-permute-start.31 = (bf16[48,768]{1,0:T(8,128)(2,1)S(1)}, bf16[48,768]{1,0:T(8,128)(2,1)S(1)}, u32[]{:S(2)}, u32[]{:S(2)}) collective-permute-start(bf16[48,768]{1,0:T(8,128)(2,1)S(1)} %get-tuple-element.97), channel_id=1, source_target_pairs={{0,48},{16,0},{32,16},{48,32},{1,49},{17,1},{33,17},{49,33},{2,50}... | collective-permute-start | bytes 221192 | tf_op jit(solution)/shard_map/ppermute | solution.py:344
  230.3 11.5 %collective-permute-start.23 = (bf16[256,768]{1,0:T(8,128)(2,1)S(1)}, bf16[256,768]{1,0:T(8,128)(2,1)S(1)}, u32[]{:S(2)}, u32[]{:S(2)}) collective-permute-start(bf16[256,768]{1,0:T(8,128)(2,1)S(1)} %add_convert_fusion.e0), channel_id=1, source_target_pairs={{0,2},{2,0},{1,3},{3,1},{4,6},{6,4},{5,7},{7,5},{8,10},{10,8},{9,1... | collective-permute-start | bytes 1179656 | tf_op jit(solution)/shard_map/ppermute | solution.py:344
  231.0 5.9 %collective-permute-start.32 = (bf16[48,768]{1,0:T(8,128)(2,1)S(1)}, bf16[48,768]{1,0:T(8,128)(2,1)S(1)}, u32[]{:S(2)}, u32[]{:S(2)}) collective-permute-start(bf16[48,768]{1,0:T(8,128)(2,1)S(1)} %get-tuple-element.97), channel_id=1, source_target_pairs={{0,32},{16,48},{32,0},{48,16},{1,33},{17,49},{33,1},{49,17},{2,34}... | collective-permute-start | bytes 221192 | tf_op jit(solution)/shard_map/ppermute | solution.py:344
  231.9 5.7 %collective-permute-start.33 = (bf16[48,768]{1,0:T(8,128)(2,1)S(1)}, bf16[48,768]{1,0:T(8,128)(2,1)S(1)}, u32[]{:S(2)}, u32[]{:S(2)}) collective-permute-start(bf16[48,768]{1,0:T(8,128)(2,1)S(1)} %get-tuple-element.97), channel_id=1, source_target_pairs={{0,16},{16,32},{32,48},{48,0},{1,17},{17,33},{33,49},{49,1},{2,18}... | collective-permute-start | bytes 221192 | tf_op jit(solution)/shard_map/ppermute | solution.py:344
  237.6 8.1 %collective-permute-start.34 = (bf16[192,768]{1,0:T(8,128)(2,1)S(1)}, bf16[192,768]{1,0:T(8,128)(2,1)S(1)}, u32[]{:S(2)}, u32[]{:S(2)}) collective-permute-start(bf16[192,768]{1,0:T(8,128)(2,1)S(1)} %bitcast.28), channel_id=1, source_target_pairs={{0,12},{4,0},{8,4},{12,8},{1,13},{5,1},{9,5},{13,9},{2,14},{6,2},{... | collective-permute-start | bytes 884744 | tf_op jit(solution)/shard_map/ppermute | solution.py:344
  238.9 9.4 %collective-permute-start.35 = (bf16[192,768]{1,0:T(8,128)(2,1)S(1)}, bf16[192,768]{1,0:T(8,128)(2,1)S(1)}, u32[]{:S(2)}, u32[]{:S(2)}) collective-permute-start(bf16[192,768]{1,0:T(8,128)(2,1)S(1)} %bitcast.29), channel_id=1, source_target_pairs={{0,8},{4,12},{8,0},{12,4},{1,9},{5,13},{9,1},{13,5},{2,10},{6,14},... | collective-permute-start | bytes 884744 | tf_op jit(solution)/shard_map/ppermute | solution.py:344
  240.2 11.2 %collective-permute-start.36 = (bf16[192,768]{1,0:T(8,128)(2,1)S(1)}, bf16[192,768]{1,0:T(8,128)(2,1)S(1)}, u32[]{:S(2)}, u32[]{:S(2)}) collective-permute-start(bf16[192,768]{1,0:T(8,128)(2,1)S(1)} %bitcast.30), channel_id=1, source_target_pairs={{0,4},{4,8},{8,12},{12,0},{1,5},{5,9},{9,13},{13,1},{2,6},{6,10},{... | collective-permute-start | bytes 884744 | tf_op jit(solution)/shard_map/ppermute | solution.py:344
  (39 other events, 439.4 us)
Sparse Core Ops, SparseCore 0:
  27.0 86.8 reduce-scatter.1
  116.3 30.9 all-reduce.1
  149.4 57.3 all-gather.1

commit v2 on v1

v2 whole, which is shorter than its diff:
```python
import functools
import math

import jax
import jax.numpy as jnp
import numpy as np
from jax import lax
from jax.experimental import pallas as pl
from jax.experimental.pallas import tpu as pltpu
from jax.sharding import Mesh
from jax.sharding import PartitionSpec as P

HEAD = 64
ROT = 16
HEADS = 3
EPSILON = 1e-05
MASKED = -1e30
CTX = ("xl", "z", "y")
TP = ("xh", "c")
F32 = jnp.float32
BF = jnp.bfloat16
LOG2E = math.log2(math.e)
SCALE = 1.0 / math.sqrt(HEAD)
SCORE = SCALE * LOG2E
NT = (((1,), (1,)), ((), ()))
TN = (((0,), (0,)), ((), ()))


def mm(a, b):
    return jnp.dot(a, b, preferred_element_type=F32)


def mm_nt(a, b):
    return lax.dot_general(a, b, NT, preferred_element_type=F32)


def mm_tn(a, b):
    return lax.dot_general(a, b, TN, preferred_element_type=F32)


def lane_table():
    lane = np.arange(128) % HEAD
    table = np.zeros((8, 128), np.float32)
    table[0] = np.where(lane < ROT, 10000.0 ** (-2.0 * (lane % 8) / ROT), 0.0)
    table[1] = lane < 8
    table[2] = (lane >= 8) & (lane < ROT)
    return table


def spin_tables(coords, order, table):
    shard = (coords[0] * 4 + coords[1]) * 4 + coords[2]
    step = lax.broadcasted_iota(jnp.int32, (128, 128), 0)
    places = jnp.concatenate(
        [step + order[2 * shard] * 128, step + order[2 * shard + 1] * 128], axis=0
    )
    angles = places.astype(F32) * table[0:1, :]
    sine = jnp.sin(angles)
    return jnp.cos(angles), sine * -table[1:2, :], sine * table[2:3, :]


def row(ref):
    return ref[...].reshape(1, -1)


def keep_kernel(x, after, out):
    out[...] = x[...]


def widen_kernel(x, after, up, down):
    up[...] = x[0:768, :].astype(F32)
    down[...] = x[768:1536, :].astype(F32)


def normed(tokens):
    values = tokens.astype(F32)
    centred = values - jnp.mean(values, axis=-1, keepdims=True)
    rstd = lax.rsqrt(jnp.mean(centred * centred, axis=-1, keepdims=True) + EPSILON)
    return centred * rstd, rstd


def front_kernel(
    coords, order, table, tok, cot, wqkv, wd, ga, sa, gm, sm, bqkv, qdo, kv, lna, lnm
):
    xhat, _ = normed(tok[...])
    ln = (xhat * row(ga) + row(sa)).astype(BF)
    lna[...] = ln
    lnm[...] = (xhat * row(gm) + row(sm)).astype(BF)
    joined = mm_nt(ln, wqkv[...]) + row(bqkv)
    cosine, left_sine, right_sine = spin_tables(coords, order, table)
    half = lax.broadcasted_iota(jnp.int32, (256, 128), 1) < HEAD
    tiles = []
    for t in range(4):
        x = joined[:, 128 * t : 128 * t + 128]
        spun = (
            x * cosine + pltpu.roll(x, 120, 1) * left_sine + pltpu.roll(x, 8, 1) * right_sine
        )
        if t == 1:
            spun = jnp.where(half, x, spun)
        if t == 2:
            spun = jnp.where(half, spun, x)
        tiles.append(spun)
    pieces = []
    for t in range(4):
        pieces += [tiles[t][:, :HEAD], tiles[t][:, HEAD:]]
    pieces.append(joined[:, 512:576])
    d_att = mm_nt(cot[...], wd[...])
    qdo[...] = jnp.concatenate(
        [pieces[0], pieces[3], pieces[6], d_att], axis=1
    ).astype(BF)
    kv[...] = jnp.concatenate([pieces[i] for i in (1, 4, 7, 2, 5, 8)], axis=1).astype(BF)


def mlp_kernel(ln, cot, wu, bu, wdn, after, gw, small, part, d_ln):
    up = mm(ln[...], wu[...]) + row(bu)
    phi = 0.5 * (1.0 + lax.erf(up * math.sqrt(0.5)))
    hid = (up * phi).astype(BF)
    slope = phi + up * (jnp.exp(up * up * -0.5) * (1.0 / math.sqrt(2.0 * math.pi)))
    d_up = (mm_nt(cot[...], wdn[...]) * slope).astype(BF)
    gw[0:768, :] = mm_tn(ln[...], d_up).astype(BF)
    gw[768:1536, :] = mm_tn(hid, cot[...]).astype(BF)
    part[...] = mm(hid, wdn[...])
    d_ln[...] = mm_nt(d_up, wu[...])
    small[0:1, :] = jnp.sum(d_up.astype(F32), axis=0, keepdims=True)
    small[1:2, :] = jnp.sum(cot[...].astype(F32), axis=0, keepdims=True)
    small[2:8, :] = jnp.zeros((6, 768), F32)


def mask_tile(scores, gap, q_places, k_places):
    rows = []
    for kb in range(2):
        cells = []
        for qb in range(2):
            cell = scores[128 * kb : 128 * kb + 128, 128 * qb : 128 * qb + 128]
            cells.append(jnp.where(gap <= (q_places[qb] - k_places[kb]) * 128, cell, MASKED))
        rows.append(jnp.concatenate(cells, axis=1))
    return jnp.concatenate(rows, axis=0)


def gap_table():
    return lax.broadcasted_iota(jnp.int32, (128, 128), 0) - lax.broadcasted_iota(
        jnp.int32, (128, 128), 1
    )


def query_places(coords, order, slot):
    shard = (coords[0] * 4 + coords[1]) * 4 + (coords[2] + slot) % 4
    return order[2 * shard], order[2 * shard + 1]


def key_places(coords, order, tile):
    shard = ((coords[0] + tile % 2) % 2 * 4 + (coords[1] + tile // 2) % 4) * 4 + coords[2]
    return order[2 * shard], order[2 * shard + 1]


def forward_kernel(coords, order, *refs):
    queries, keys = refs[0:4], refs[4:12]
    outs, stats, qs, os = refs[12:16], refs[16], refs[17], refs[18]
    for j, ref in enumerate(queries):
        qs[j] = ref[...]
    gap = gap_table()

    def slot_step(j, carry):
        q_places = query_places(coords, order, j)
        for h in range(HEADS):
            query = qs[j, :, HEAD * h : HEAD * h + HEAD]
            d_att = qs[j, :, 192 + HEAD * h : 256 + HEAD * h]
            tiles, tops = [], []
            for t in range(8):
                key = keys[t][:, HEAD * h : HEAD * h + HEAD]
                scores = mask_tile(
                    mm_nt(key, query), gap, q_places, key_places(coords, order, t)
                )
                tiles.append(scores)
                tops.append(jnp.max(scores, axis=0, keepdims=True))
            top = functools.reduce(jnp.maximum, tops) * SCORE
            total = jnp.zeros((1, 256), F32)
            out = jnp.zeros((HEAD, 256), F32)
            for t in range(8):
                weights = jnp.exp2(tiles[t] * SCORE - top)
                total = total + jnp.sum(weights, axis=0, keepdims=True)
                value = keys[t][:, 192 + HEAD * h : 256 + HEAD * h]
                out = out + mm(value.T, weights.astype(BF))
            out = out / total
            os[j, HEAD * h : HEAD * h + HEAD, :] = out.astype(BF)
            stats[j, h : h + 1, :] = top + jnp.log2(total)
            stats[j, 3 + h : 4 + h, :] = jnp.sum(
                d_att.astype(F32).T * out, axis=0, keepdims=True
            )
        stats[j, 6:8, :] = jnp.zeros((2, 256), F32)
        return carry

    lax.fori_loop(0, 4, slot_step, 0)
    for j, ref in enumerate(outs):
        ref[...] = os[j]


def merge_kernel(s0, s1, s2, s3, o0, o1, o2, o3, wd, part, att, branch):
    stats = [ref[-step % 4] for step, ref in enumerate((s0, s1, s2, s3))]
    outs = [o0, o3, o2, o1]
    rows = []
    for h in range(HEADS):
        logs = [s[h : h + 1, :] for s in stats]
        top = functools.reduce(jnp.maximum, logs)
        shares = [jnp.exp2(v - top) for v in logs]
        total = functools.reduce(jnp.add, shares)
        mixed = functools.reduce(
            jnp.add,
            [
                share * ref[HEAD * h : HEAD * h + HEAD, :].astype(F32)
                for share, ref in zip(shares, outs, strict=True)
            ],
        )
        rows.append(mixed / total)
    att_low = jnp.concatenate(rows, axis=0).T.astype(BF)
    att[...] = att_low
    branch[...] = (mm(att_low, wd[...]) + part[...]).astype(BF)


def backward_kernel(tiles, first, last, unread, coords, order, *refs):
    n = len(tiles)
    refs = list(refs)

    def take(count):
        taken = refs[:count]
        del refs[:count]
        return taken

    stats = take(4 if first else 1)
    queries, keys = take(4), take(n)
    d_before = None if first else take(1)[0]
    take(unread)
    if first:
        (st,) = take(1)
    else:
        (st,) = stats
    d_keys = take(n // 2)
    d_queries = take(4 if last else 1)
    ks, dks = take(2)
    dqs = take(1)[0] if last else d_queries[0]
    for i, ref in enumerate(keys):
        ks[i] = ref[...]
    dqs[...] = jnp.zeros_like(dqs) if first else d_before[...]
    for j in range(4 if first else 0):
        parts = [ref[(j - step) % 4] for step, ref in enumerate(stats)]
        logs = [p[0:3, :] for p in parts]
        top = functools.reduce(jnp.maximum, logs)
        total = functools.reduce(jnp.add, [jnp.exp2(v - top) for v in logs])
        whole = top + jnp.log2(total)
        st[j, 0:3, :] = whole
        st[j, 3:6, :] = functools.reduce(
            jnp.add, [jnp.exp2(p[0:3, :] - whole) * p[3:6, :] for p in parts]
        )
        st[j, 6:8, :] = jnp.zeros((2, 256), F32)
    gap = gap_table()

    def tile_step(i, carry):
        step = tiles[2] - tiles[0] if n > 2 else 0
        k_places = key_places(coords, order, tiles[0] + i % 2 + i // 2 * step)
        for h in range(HEADS):
            key = ks[i, :, HEAD * h : HEAD * h + HEAD]
            value = ks[i, :, 192 + HEAD * h : 256 + HEAD * h]
            key_turned = key.T
            d_key = jnp.zeros((256, HEAD), F32)
            d_value = jnp.zeros((256, HEAD), F32)
            for j in range(4):
                query = queries[j][:, HEAD * h : HEAD * h + HEAD]
                d_att = queries[j][:, 192 + HEAD * h : 256 + HEAD * h]
                scores = mask_tile(
                    mm_nt(key, query), gap, query_places(coords, order, j), k_places
                )
                weights = jnp.exp2(scores * SCORE - st[j, h : h + 1, :])
                d_weights = mm_nt(value, d_att)
                d_scores = (weights * (d_weights - st[j, 3 + h : 4 + h, :])).astype(BF)
                d_value = d_value + mm(weights.astype(BF), d_att)
                d_key = d_key + mm(d_scores, query)
                dqs[j, HEAD * h : HEAD * h + HEAD, :] += mm(key_turned, d_scores)
            dks[i, :, HEAD * h : HEAD * h + HEAD] = (d_key * SCALE).astype(BF)
            dks[i, :, 192 + HEAD * h : 256 + HEAD * h] = d_value.astype(BF)
        return carry

    lax.fori_loop(0, n, tile_step, 0)
    for i, ref in enumerate(d_keys):
        ref[...] = dks[2 * i : 2 * i + 2]
    if last:
        for j, ref in enumerate(d_queries):
            ref[...] = (dqs[j] * SCALE).astype(BF)


def tail_kernel(
    coords, order, table, tok, cot, lna, wqkv, ga, gm, dq0, dq1, dq2, dq3, dkv0, dkv1,
    att, d_ln_mlp, small_in, g0, g1, g2, g3, upstream, grads,
):
    d_query = (
        dq0[...].astype(F32) + dq1[...].astype(F32) + dq2[...].astype(F32) + dq3[...].astype(F32)
    ).T
    d_kv = dkv0[...].astype(F32) + dkv1[...].astype(F32)
    both = jnp.concatenate([d_query, d_kv[:, :192]], axis=1)
    cosine, left_sine, right_sine = spin_tables(coords, order, table)
    pieces = []
    for t in range(3):
        x = both[:, 128 * t : 128 * t + 128]
        back = (
            x * cosine
            + pltpu.roll(x * left_sine, 8, 1)
            + pltpu.roll(x * right_sine, 120, 1)
        )
        pieces += [back[:, :HEAD], back[:, HEAD:]]
    cols = []
    for h in range(HEADS):
        cols += [pieces[h], pieces[3 + h], d_kv[:, 192 + HEAD * h : 256 + HEAD * h]]
    d_joined = jnp.concatenate(cols, axis=1).astype(BF)
    turned = mm_tn(d_joined, lna[...]).astype(BF)
    for piece in range(3):
        grads[piece] = turned[192 * piece : 192 * piece + 192, :]
    grads[3] = mm_tn(att[...], cot[...]).astype(BF)
    for slot, ref in enumerate((g0, g1, g2, g3)):
        ref[0:192, :] = grads[(coords[2] + slot) % 4]
    d_attn = mm(d_joined, wqkv[...])
    d_mlp = d_ln_mlp[...]
    xhat, _ = normed(tok[...])
    upstream[...] = (d_attn * row(ga) + d_mlp * row(gm)).astype(BF)
    sums = [
        jnp.sum(v, axis=0, keepdims=True) for v in (d_attn * xhat, d_attn, d_mlp * xhat, d_mlp)
    ]
    bias = jnp.sum(d_joined.astype(F32), axis=0, keepdims=True)
    bias = jnp.concatenate([bias, jnp.zeros((1, 192), F32)], axis=1)
    small = jnp.concatenate([*sums, small_in[0:2, :], bias, jnp.zeros((9, 768), F32)], axis=0)
    for ref in (g0, g1, g2, g3):
        ref[192:208, :] = small.astype(BF)


def first_sum_kernel(coords, p0, p1, p2, p3, b0, b1, b2, b3, order, total):
    for slot, ref in enumerate((p0, p1, p2, p3)):
        order[(coords[2] + 4 - slot) % 4] = ref[...].astype(F32)
    rows = ((order[0] + order[1]) + (order[2] + order[3])).astype(BF)
    for block in range(4):
        total[block] = rows[48 * block : 48 * block + 48, :]
    for slot, ref in enumerate((b0, b1, b2, b3)):
        ref[0:48, :] = total[(coords[1] + slot) % 4]
        ref[48:64, :] = rows[192:208, :]


def second_sum_kernel(coords, b0, b1, b2, b3, out, order):
    for slot, ref in enumerate((b0, b1, b2, b3)):
        order[(coords[1] + 4 - slot) % 4] = ref[...].astype(F32)
    out[...] = ((order[0] + order[1]) + (order[2] + order[3])).astype(BF)


def token_kernel(tok, cot, e0, e1, out):
    xhat, rstd = normed(tok[...])
    e = e0[...].astype(F32) + e1[...].astype(F32)
    inner = e - jnp.mean(e, axis=-1, keepdims=True)
    inner = inner - xhat * jnp.mean(e * xhat, axis=-1, keepdims=True)
    out[...] = (cot[...].astype(F32) + rstd * inner).astype(BF)


def quarter_kernel(coords, b0, b1, b2, b3, out):
    for slot, ref in enumerate((b0, b1, b2, b3)):
        out[(coords[1] + slot) % 4] = ref[...]


def assemble_kernel(coords, p0, p1, p2, p3, gq, gd, whole):
    for slot, ref in enumerate((p0, p1, p2, p3)):
        whole[(coords[2] + slot) % 4] = ref[...].astype(F32)
    for block in range(12):
        gq[48 * block : 48 * block + 48, :] = whole[block // 4, block % 4]
    for block in range(4):
        gd[48 * block : 48 * block + 48, :] = whole[3, block]


def call(kernel, outs, args, scalars, scratch=(), mib=48, unread=0):
    smem = pl.BlockSpec(memory_space=pltpu.SMEM)
    vmem = pl.BlockSpec(memory_space=pltpu.VMEM)
    shapes = [jax.ShapeDtypeStruct(s, d) for s, d in outs]
    return pl.pallas_call(
        kernel,
        out_shape=shapes,
        in_specs=[smem] * scalars
        + [vmem] * (len(args) - scalars - unread)
        + [pl.BlockSpec(memory_space=pl.ANY)] * unread,
        out_specs=[vmem] * len(shapes),
        scratch_shapes=list(scratch),
        compiler_params=pltpu.CompilerParams(vmem_limit_bytes=mib << 20),
        cost_estimate=pl.CostEstimate(flops=0, bytes_accessed=1024, transcendentals=0),
    )(*args)


def hop(x, axis, step):
    n = lax.axis_size(axis)
    return lax.ppermute(x, axis, [(i, (i + step) % n) for i in range(n)])


def add(*parts):
    return functools.reduce(jnp.add, [p.astype(F32) for p in parts])


def on_device(
    tokens,
    block_order,
    cotangent,
    w_qkv,
    b_qkv,
    w_dense,
    b_dense,
    w_up,
    b_up,
    w_down,
    b_down,
    gain_attn,
    shift_attn,
    gain_mlp,
    shift_mlp,
):
    coords = jnp.stack([lax.axis_index(a) for a in CTX]).astype(jnp.int32)
    table = jnp.asarray(lane_table())
    w_turned = w_qkv.T

    qdo, kv, ln_attn, ln_mlp = call(
        front_kernel,
        [((256, 384), BF), ((256, 384), BF), ((256, 768), BF), ((256, 768), BF)],
        (coords, block_order, table, tokens, cotangent, w_turned, w_dense,
         gain_attn, shift_attn, gain_mlp, shift_mlp, b_qkv),
        2,
        mib=60,
    )
    kv_x = hop(kv, "xl", 1)
    down, up = hop(kv, "z", 1), hop(kv, "z", -1)
    down_x, up_x = hop(kv_x, "z", 1), hop(kv_x, "z", -1)
    kvs = [kv, kv_x, up, up_x, hop(down, "z", 1), hop(up_x, "z", -1), down, down_x]
    qdos = [qdo] + [hop(qdo, "y", -j) for j in (1, 2, 3)]

    grads_mlp, small_mlp, part_mlp, d_ln_mlp = call(
        mlp_kernel,
        [((1536, 768), BF), ((8, 768), F32), ((256, 768), F32), ((256, 768), F32)],
        (ln_mlp, cotangent, w_up, b_up, w_down, kv_x),
        0,
        unread=1,
    )
    grads_mlp = lax.psum_scatter(grads_mlp, ("z", "y"), scatter_dimension=0, tiled=True)
    *outs, stats = call(
        forward_kernel,
        [((192, 256), BF)] * 4 + [((4, 8, 256), F32)],
        (coords, block_order, *qdos, *kvs),
        2,
        scratch=[pltpu.VMEM((4, 256, 384), BF), pltpu.VMEM((4, 192, 256), BF)],
    )
    stats_all = [stats] + [hop(stats, "y", -j) for j in (1, 2, 3)]
    outs = [outs[0]] + [hop(outs[j], "y", j) for j in (1, 2, 3)]
    att, branch = call(
        merge_kernel,
        [((256, 192), BF), ((256, 768), BF)],
        (*stats_all, *outs, w_dense, part_mlp),
        0,
    )
    branch = add(branch, hop(branch, "c", 1)).astype(BF)
    branch = add(branch, hop(branch, "xh", 1))
    output = (tokens.astype(F32) + branch + b_dense + b_down).astype(BF)

    def backward(tiles, stats_in, before, last, after=()):
        first = before is None
        n = len(tiles)
        kept = [((4, 8, 256), F32)] if first else []
        d_out = [((192, 256), BF)] * 4 if last else [((4, 192, 256), F32)]
        scratch = [pltpu.VMEM((n, 256, 384), BF)] * 2
        if last:
            scratch.append(pltpu.VMEM((4, 192, 256), F32))
        return call(
            functools.partial(backward_kernel, tiles, first, last, len(after)),
            kept + [((2, 256, 384), BF)] * (n // 2) + d_out,
            (coords, block_order, *stats_in, *qdos, *[kvs[t] for t in tiles])
            + (() if first else (before,))
            + tuple(after),
            2,
            unread=len(after),
            scratch=scratch,
        )

    whole, d_far, d_q = backward((4, 5), stats_all, None, False)
    far = hop(d_far, "z", 2)
    d_up, d_down, d_q = backward((2, 3, 6, 7), [whole], d_q, False)
    near = [hop(d_up, "z", 1), hop(d_down, "z", -1)]
    d_kv, *d_qs = backward((0, 1), [whole], d_q, True, (far,))
    (grads_mlp,) = call(
        keep_kernel, [(grads_mlp.shape, BF)], (grads_mlp, d_kv), 0, unread=1
    )
    grads_mlp = add(grads_mlp, hop(grads_mlp, "xl", 1)).astype(BF)
    grads_mlp = lax.all_gather(grads_mlp, ("z", "y"), axis=0, tiled=True)
    d_queries = [d_qs[0]] + [hop(d_qs[j], "y", j) for j in (1, 2, 3)]
    d_kv_other = hop(add(d_kv[1], far[1], near[0][1], near[1][1]).astype(BF), "xl", 1)
    d_kv_own = add(d_kv[0], far[0], near[0][0], near[1][0]).astype(BF)
    *pieces, upstream = call(
        tail_kernel,
        [((208, 768), BF)] * 4 + [((256, 768), BF)],
        (coords, block_order, table, tokens, cotangent, ln_attn, w_turned, gain_attn, gain_mlp,
         *d_queries, d_kv_own, d_kv_other, att, d_ln_mlp, small_mlp),
        2,
        scratch=[pltpu.VMEM((4, 192, 768), BF)],
    )

    pieces = [pieces[0]] + [hop(pieces[j], "y", j) for j in (1, 2, 3)]
    upstream = add(upstream, hop(upstream, "c", 1)).astype(BF)
    upstream_far = hop(upstream, "xh", 1)
    blocks = call(
        first_sum_kernel,
        [((64, 768), BF)] * 4,
        (coords, *pieces),
        1,
        scratch=[pltpu.VMEM((4, 208, 768), F32), pltpu.VMEM((4, 48, 768), BF)],
    )
    (block,) = call(
        second_sum_kernel,
        [((64, 768), BF)],
        (coords, blocks[0], *[hop(blocks[j], "z", j) for j in (1, 2, 3)]),
        1,
        scratch=[pltpu.VMEM((4, 64, 768), F32)],
    )
    block = add(block, hop(block, "xl", 1))
    small = block[48:56]
    gains = small + hop(small, "c", 1)
    gains = gains + hop(gains, "xh", 1)
    block = block[0:48].astype(BF)
    (quarter,) = call(
        quarter_kernel,
        [((4, 48, 768), BF)],
        (coords, block, *[hop(block, "z", -j) for j in (1, 2, 3)]),
        1,
    )
    grad_turned, grad_w_dense = call(
        assemble_kernel,
        [((576, 768), F32), ((192, 768), F32)],
        (coords, quarter, *[hop(quarter, "y", -j) for j in (1, 2, 3)]),
        1,
        scratch=[pltpu.VMEM((4, 4, 48, 768), F32)],
    )
    (grad_tokens,) = call(
        token_kernel, [((256, 768), BF)], (tokens, cotangent, upstream, upstream_far), 0
    )

    grad_w_up, grad_w_down = call(
        widen_kernel, [((768, 768), F32)] * 2, (grads_mlp, quarter), 0, unread=1
    )
    return (
        output,
        grad_tokens,
        grad_turned.T,
        small[6, :576],
        grad_w_dense,
        small[5],
        grad_w_up,
        small[4],
        grad_w_down,
        small[5],
        gains[0],
        gains[1],
        gains[2],
        gains[3],
    )


def solution(mesh):
    fine = Mesh(mesh.devices.reshape(2, 4, 4, 2, 2), CTX + TP)
    rows, cols = P(CTX, None), P(None, TP)
    return jax.shard_map(
        on_device,
        mesh=fine,
        in_specs=(
            rows, P(), rows, cols, P(TP), P(TP, None), P(), cols, P(TP), P(TP, None),
            P(), P(), P(), P(), P(),
        ),
        out_specs=(
            rows, rows, cols, P(TP), P(TP, None), P(), cols, P(TP), P(TP, None),
            P(), P(), P(), P(), P(),
        ),
        check_vma=False,
    )
```

time: 268 us -> 225 us (0.84)
  waiting for transfers between devices: 97.2 us -> 71.7 us
  local copies, waits for them, and re-layouts: 27.6 us -> 14.9 us
  other arithmetic: 8.35 us -> 2.66 us
  Pallas kernels: 53.8 us -> 57.1 us
    psum x1 -> x0, waiting for transfers between devices: 31.7 us -> none  [on_device(): grads_mlp = lax.psum(grads_mlp, 'xl')]
    unnamed x79 -> x65, local copies, waits for them, and re-layouts: 22.2 us -> 13.1 us
    reshape x6 -> x0, local copies, waits for them, and re-layouts: 4.14 us -> none  [row(): return v.reshape(1, -1)]
    convert_element_type x3 -> x1, other arithmetic: 4.36 us -> 0.7 us  [on_device(): grads_mlp = add(grads_mlp, hop(grads_mlp, 'xl', 1)).astype(BF)]
    pallas_call x8 -> x15, Pallas kernels: 53.8 us -> 57.1 us  [call(): pl.pallas_call(kernel, out_shape=shapes, in_specs=[smem] * scalars + [vme...]
    reduce_scatter x1, waiting for transfers between devices: 0.01 us -> 3.24 us  [on_device(): lax.psum_scatter(grads_mlp, ('z', 'y'), scatter_dimension=0, tiled=True)]
    ppermute x46 -> x43, waiting for transfers between devices: 65.4 us -> 68.4 us  [hop(): return lax.ppermute(x, axis, [(i, (i + step) % n) for i in range(n)])]
    ppermute x46 -> x43, starting transfers between devices: 65.3 us -> 63.2 us  [hop(): return lax.ppermute(x, axis, [(i, (i + step) % n) for i in range(n)])]
  transfers between devices with their start and end apart: 49 -> 45, of which waited for: 24 -> 24; matrix products, arithmetic and copies ran while one was open for 3% -> 1% of each run, Pallas kernels for 18% -> 21%
where the time goes in v2:
time: 225 us; the launch traced here: 224 us
  waiting for transfers between devices  71.7 us (32%)
  starting transfers between devices  63.3 us (28%)
  Pallas kernels  57.1 us (25%)
  local copies, waits for them, and re-layouts  14.9 us (7%)
  between operations  14.4 us (6%)
  other arithmetic  2.66 us (1%)
    ppermute x43, waiting for transfers between devices, hop(): return lax.ppermute(x, axis, [(i, (i + step) % n) for i in range(n)])  68.4 us
    ppermute x43, starting transfers between devices, hop(): return lax.ppermute(x, axis, [(i, (i + step) % n) for i in range(n)])  63.2 us
    pallas_call x15, Pallas kernels, call(): pl.pallas_call(kernel, out_shape=shapes, in_specs=[smem] * scalars + [vme...  57.1 us
    unnamed x65, local copies, waits for them, and re-layouts  13.1 us
  transfers between devices with their start and end apart: 45, of which 24 were waited for; matrix products, arithmetic and copies ran while one was open for 1% of the time, Pallas kernels for 21%

profile of v2, /device:TPU:0, one launch (start us, length us, event | category | flops | bytes accessed | tf_op | source)
XLA Modules:
  0.0 224.2 jit_solution(4874551092909996044)
XLA Ops:
  7.8 3.7 %shard_map.263 = (bf16[256,384]{1,0:T(8,128)(2,1)}, bf16[256,384]{1,0:T(8,128)(2,1)}, bf16[256,768]{1,0:T(8,128)(2,1)}, bf16[256,768]{1,0:T(8,128)(2,1)}) custom-call(s32[3]{0:T(128)} %pad_add_fusion.coords, s32[64]{0:T(128)} %order.11, f32[8,128]{1,0:T(8,128)} %constant.17.clone.table, bf16[256,768]{1,0:T(8,128)(2,1)} %tok.5, bf16[256,768]{1,0:T(8,128)(2,1)} %cot.7, ...), custom_call_target="tpu_custom_call" | custom-call | bytes 1024 | tf_op jit(solution)/shard_map/pallas_call | solution.py:375
  11.6 1.6 collective-permute-start.3
  13.1 5.1 %collective-permute-done.3.refs_5_.after.refs_6_ = bf16[256,384]{1,0:T(8,128)(2,1)S(1)} collective-permute-done((bf16[256,384]{1,0:T(8,128)(2,1)}, bf16[256,384]{1,0:T(8,128)(2,1)S(1)}, u32[]{:S(2)}, u32[]{:S(2)}) %collective-permute-start.3) | collective-permute-done | bytes 196640 | tf_op jit(solution)/shard_map/ppermute | solution.py:390
  22.2 3.0 %shard_map.265 = (bf16[1536,768]{1,0:T(8,128)(2,1)}, f32[8,768]{1,0:T(8,128)S(1)}, f32[256,768]{1,0:T(8,128)S(1)}, f32[256,768]{1,0:T(8,128)S(1)}) custom-call(bf16[256,768]{1,0:T(8,128)(2,1)S(1)} %copy-done.11, bf16[256,768]{1,0:T(8,128)(2,1)S(1)} %copy-done, bf16[768,768]{1,0:T(8,128)(2,1)S(1)} %copy-done.7, f32[768]{0:T(1024)S(1)} %copy-done.20, ...), custom_call_target="tpu_custom_call" | custom-call | bytes 1024 | tf_op jit(solution)/shard_map/pallas_call | solution.py:375
  25.3 3.3 %collective-permute-start = (bf16[256,384]{1,0:T(8,128)(2,1)S(1)}, bf16[256,384]{1,0:T(8,128)(2,1)S(1)}, u32[]{:S(2)}, u32[]{:S(2)}) collective-permute-start(bf16[256,384]{1,0:T(8,128)(2,1)S(1)} %copy-done.4), channel_id=1, source_target_pairs={{0,12},{4,0},{8,4},{12,8},{1,13},{5,1},{9,5},{13,9},{2,14},{6,2},{... | collective-permute-start | bytes 589832 | tf_op jit(solution)/shard_map/ppermute | solution.py:390
  29.3 1.9 collective-permute-start.6
  31.2 2.1 collective-permute-start.5
  34.3 1.9 collective-permute-done.refs_1_.refs_5_.refs_2_
  36.1 4.0 %collective-permute-start.4 = (bf16[256,384]{1,0:T(8,128)(2,1)S(1)}, bf16[256,384]{1,0:T(8,128)(2,1)S(1)}, u32[]{:S(2)}, u32[]{:S(2)}) collective-permute-start(bf16[256,384]{1,0:T(8,128)(2,1)S(1)} %copy-done.9), channel_id=1, source_target_pairs={{0,48},{16,0},{32,16},{48,32},{1,49},{17,1},{33,17},{49,33},{2,50}... | collective-permute-start | bytes 589832 | tf_op jit(solution)/shard_map/ppermute | solution.py:390
  40.2 1.4 collective-permute-start.7
  41.6 1.9 collective-permute-start.8
  44.7 3.4 %collective-permute-done.9.refs_11_.refs_8_ = bf16[256,384]{1,0:T(8,128)(2,1)S(1)} collective-permute-done((bf16[256,384]{1,0:T(8,128)(2,1)S(1)}, bf16[256,384]{1,0:T(8,128)(2,1)S(1)}, u32[]{:S(2)}, u32[]{:S(2)}) %collective-permute-start.9) | collective-permute-done | bytes 196640 | tf_op jit(solution)/shard_map/ppermute | solution.py:390
  48.0 2.7 %collective-permute-done.7.refs_8_ = bf16[256,384]{1,0:T(8,128)(2,1)S(1)} collective-permute-done((bf16[256,384]{1,0:T(8,128)(2,1)S(1)}, bf16[256,384]{1,0:T(8,128)(2,1)S(1)}, u32[]{:S(2)}, u32[]{:S(2)}) %collective-permute-start.7) | collective-permute-done | bytes 196640 | tf_op jit(solution)/shard_map/ppermute | solution.py:390
  50.8 13.0 %shard_map.264 = (bf16[192,256]{1,0:T(8,128)(2,1)S(1)}, bf16[192,256]{1,0:T(8,128)(2,1)S(1)}, bf16[192,256]{1,0:T(8,128)(2,1)S(1)}, bf16[192,256]{1,0:T(8,128)(2,1)S(1)}, f32[4,8,256]{2,1,0:T(8,128)S(1)}) custom-call(s32[3]{0:T(128)S(1)} %copy-done.15, s32[64]{0:T(128)S(1)} %copy-done.16, bf16[256,384]{1,0:T(8,128)(2,1)S(1)} %copy-done.4, ...), custom_call_target="tpu_custom_call" | custom-call | bytes 1024 | tf_op jit(solution)/shard_map/pallas_call | solution.py:375
  65.7 4.0 %collective-permute-start.10 = (f32[4,8,256]{2,1,0:T(8,128)S(1)}, f32[4,8,256]{2,1,0:T(8,128)S(1)}, u32[]{:S(2)}, u32[]{:S(2)}) collective-permute-start(f32[4,8,256]{2,1,0:T(8,128)S(1)} %get-tuple-element.55.s0.refs_0_), channel_id=1, source_target_pairs={{0,12},{4,0},{8,4},{12,8},{1,13},{5,1},{9,5},{13,9},{2,14},{6,2},{... | collective-permute-start | bytes 98312 | tf_op jit(solution)/shard_map/ppermute | solution.py:390
  71.2 4.0 %collective-permute-done.11.s2.refs_2_ = f32[4,8,256]{2,1,0:T(8,128)S(1)} collective-permute-done((f32[4,8,256]{2,1,0:T(8,128)S(1)}, f32[4,8,256]{2,1,0:T(8,128)S(1)}, u32[]{:S(2)}, u32[]{:S(2)}) %collective-permute-start.11) | collective-permute-done | bytes 32800 | tf_op jit(solution)/shard_map/ppermute | solution.py:390
  75.3 6.9 %shard_map.267 = (f32[4,8,256]{2,1,0:T(8,128)S(1)}, bf16[2,256,384]{2,1,0:T(8,128)(2,1)S(1)}, f32[4,192,256]{2,1,0:T(8,128)S(1)}) custom-call(s32[3]{0:T(128)S(1)} %copy-done.15, s32[64]{0:T(128)S(1)} %copy-done.16, f32[4,8,256]{2,1,0:T(8,128)S(1)} %get-tuple-element.55.s0.refs_0_, f32[4,8,256]{2,1,0:T(8,128)S(1)} %collective-permute-done.10.s1.refs_1_, ...), custom_call_target="tpu_custom_call" | custom-call | bytes 1024 | tf_op jit(solution)/shard_map/pallas_call | solution.py:375
  82.1 1.6 collective-permute-start.18
  83.8 13.0 %shard_map.268 = (bf16[2,256,384]{2,1,0:T(8,128)(2,1)S(1)}, bf16[2,256,384]{2,1,0:T(8,128)(2,1)S(1)}, f32[4,192,256]{2,1,0:T(8,128)S(1)}) custom-call(s32[3]{0:T(128)S(1)} %copy-done.15, s32[64]{0:T(128)S(1)} %copy-done.16, f32[4,8,256]{2,1,0:T(8,128)S(1)} %get-tuple-element.64.refs_0_, bf16[256,384]{1,0:T(8,128)(2,1)S(1)} %copy-done.4, ...), custom_call_target="tpu_custom_call" | custom-call | bytes 1024 | tf_op jit(solution)/shard_map/pallas_call | solution.py:375
  98.3 6.8 %shard_map.269 = (bf16[2,256,384]{2,1,0:T(8,128)(2,1)S(1)}, bf16[192,256]{1,0:T(8,128)(2,1)S(1)}, bf16[192,256]{1,0:T(8,128)(2,1)S(1)}, bf16[192,256]{1,0:T(8,128)(2,1)S(1)}, bf16[192,256]{1,0:T(8,128)(2,1)S(1)}) custom-call(s32[3]{0:T(128)S(1)} %copy-done.15, s32[64]{0:T(128)S(1)} %copy-done.16, f32[4,8,256]{2,1,0:T(8,128)S(1)} %get-tuple-element.64.refs_0_, ...), custom_call_target="tpu_custom_call" | custom-call | bytes 1024 | tf_op jit(solution)/shard_map/pallas_call | solution.py:375
  107.7 3.2 %reduce-scatter.2.cloned.1.call-done.x = bf16[96,768]{1,0:T(8,128)(2,1)} async-done(((bf16[1536,768]{1,0:T(8,128)(2,1)}), bf16[96,768]{1,0:T(8,128)(2,1)}) %reduce-scatter.2.cloned.1.call-update) | async-done | bytes 147472 | tf_op jit(solution)/shard_map/reduce_scatter | solution.py:439
  111.8 1.6 collective-permute-start.40
  113.4 3.7 %collective-permute-done.40 = bf16[96,768]{1,0:T(8,128)(2,1)S(1)} collective-permute-done((bf16[96,768]{1,0:T(8,128)(2,1)S(1)}, bf16[96,768]{1,0:T(8,128)(2,1)S(1)}, u32[]{:S(2)}, u32[]{:S(2)}) %collective-permute-start.40) | collective-permute-done | bytes 147488 | tf_op jit(solution)/shard_map/ppermute | solution.py:390
  119.0 2.1 collective-permute-start.23
  122.2 2.7 %collective-permute-start.14 = (bf16[192,256]{1,0:T(8,128)(2,1)}, bf16[192,256]{1,0:T(8,128)(2,1)S(1)}, u32[]{:S(2)}, u32[]{:S(2)}) collective-permute-start(bf16[192,256]{1,0:T(8,128)(2,1)} %copy-done.27), channel_id=1, source_target_pairs={{0,8},{4,12},{8,0},{12,4},{1,9},{5,13},{9,1},{13,5},{2,10},{6,14},... | collective-permute-start | bytes 294920 | tf_op jit(solution)/shard_map/ppermute | solution.py:390
  127.1 1.6 collective-permute-done.14.o2
  130.6 1.7 collective-permute-start.24
  133.5 3.6 %collective-permute-start.20 = (bf16[192,256]{1,0:T(8,128)(2,1)}, bf16[192,256]{1,0:T(8,128)(2,1)S(1)}, u32[]{:S(2)}, u32[]{:S(2)}) collective-permute-start(bf16[192,256]{1,0:T(8,128)(2,1)} %copy-done.24), channel_id=1, source_target_pairs={{0,8},{4,12},{8,0},{12,4},{1,9},{5,13},{9,1},{13,5},{2,10},{6,14},... | collective-permute-start | bytes 294920 | tf_op jit(solution)/shard_map/ppermute | solution.py:390
  137.2 2.8 %collective-permute-start.17 = (bf16[256,768]{1,0:T(8,128)(2,1)S(1)}, bf16[256,768]{1,0:T(8,128)(2,1)S(1)}, u32[]{:S(2)}, u32[]{:S(2)}) collective-permute-start(bf16[256,768]{1,0:T(8,128)(2,1)S(1)} %add_convert_fusion.2), channel_id=1, source_target_pairs={{0,2},{2,0},{1,3},{3,1},{4,6},{6,4},{5,7},{7,5},{8,10},{10,8},{9,1... | collective-permute-start | bytes 1179656 | tf_op jit(solution)/shard_map/ppermute | solution.py:390
  140.0 2.8 %collective-permute-done.20.dq2 = bf16[192,256]{1,0:T(8,128)(2,1)S(1)} collective-permute-done((bf16[192,256]{1,0:T(8,128)(2,1)}, bf16[192,256]{1,0:T(8,128)(2,1)S(1)}, u32[]{:S(2)}, u32[]{:S(2)}) %collective-permute-start.20) | collective-permute-done | bytes 98336 | tf_op jit(solution)/shard_map/ppermute | solution.py:390
  142.9 2.3 %shard_map.270 = (bf16[208,768]{1,0:T(8,128)(2,1)S(1)}, bf16[208,768]{1,0:T(8,128)(2,1)S(1)}, bf16[208,768]{1,0:T(8,128)(2,1)S(1)}, bf16[208,768]{1,0:T(8,128)(2,1)S(1)}, bf16[256,768]{1,0:T(8,128)(2,1)S(1)}) custom-call(s32[3]{0:T(128)S(1)} %copy-done.15, s32[64]{0:T(128)S(1)} %copy-done.16, f32[8,128]{1,0:T(8,128)S(1)} %copy-done.19, ...), custom_call_target="tpu_custom_call" | custom-call | bytes 1024 | tf_op jit(solution)/shard_map/pallas_call | solution.py:375
  145.5 3.1 %collective-permute-start.28 = (bf16[208,768]{1,0:T(8,128)(2,1)S(1)}, bf16[208,768]{1,0:T(8,128)(2,1)S(1)}, u32[]{:S(2)}, u32[]{:S(2)}) collective-permute-start(bf16[208,768]{1,0:T(8,128)(2,1)S(1)} %get-tuple-element.81), channel_id=1, source_target_pairs={{0,8},{4,12},{8,0},{12,4},{1,9},{5,13},{9,1},{13,5},{2,10},{6,14},... | collective-permute-start | bytes 958472 | tf_op jit(solution)/shard_map/ppermute | solution.py:390
  148.8 11.4 %collective-permute-done.27.p1 = bf16[208,768]{1,0:T(8,128)(2,1)S(1)} collective-permute-done((bf16[208,768]{1,0:T(8,128)(2,1)S(1)}, bf16[208,768]{1,0:T(8,128)(2,1)S(1)}, u32[]{:S(2)}, u32[]{:S(2)}) %collective-permute-start.27) | collective-permute-done | bytes 319520 | tf_op jit(solution)/shard_map/ppermute | solution.py:390
  160.2 12.2 %collective-permute-done.28.p2 = bf16[208,768]{1,0:T(8,128)(2,1)S(1)} collective-permute-done((bf16[208,768]{1,0:T(8,128)(2,1)S(1)}, bf16[208,768]{1,0:T(8,128)(2,1)S(1)}, u32[]{:S(2)}, u32[]{:S(2)}) %collective-permute-start.28) | collective-permute-done | bytes 319520 | tf_op jit(solution)/shard_map/ppermute | solution.py:390
  173.4 1.6 collective-permute-start.31
  175.0 1.7 collective-permute-start.32
  177.6 2.7 %collective-permute-done.30.b1 = bf16[64,768]{1,0:T(8,128)(2,1)S(1)} collective-permute-done((bf16[64,768]{1,0:T(8,128)(2,1)S(1)}, bf16[64,768]{1,0:T(8,128)(2,1)S(1)}, u32[]{:S(2)}, u32[]{:S(2)}) %collective-permute-start.30) | collective-permute-done | bytes 98336 | tf_op jit(solution)/shard_map/ppermute | solution.py:390
  182.9 3.1 %collective-permute-start.26 = (bf16[256,768]{1,0:T(8,128)(2,1)S(1)}, bf16[256,768]{1,0:T(8,128)(2,1)S(1)}, u32[]{:S(2)}, u32[]{:S(2)}) collective-permute-start(bf16[256,768]{1,0:T(8,128)(2,1)S(1)} %add_convert_fusion.e0), channel_id=1, source_target_pairs={{0,2},{2,0},{1,3},{3,1},{4,6},{6,4},{5,7},{7,5},{8,10},{10,8},{9,1... | collective-permute-start | bytes 1179656 | tf_op jit(solution)/shard_map/ppermute | solution.py:390
  186.0 1.7 collective-permute-done.33
  187.7 2.4 %collective-permute-start.34 = (bf16[48,768]{1,0:T(8,128)(2,1)S(1)}, bf16[48,768]{1,0:T(8,128)(2,1)S(1)}, u32[]{:S(2)}, u32[]{:S(2)}) collective-permute-start(bf16[48,768]{1,0:T(8,128)(2,1)S(1)} %slice.105.b0), channel_id=1, source_target_pairs={{0,48},{16,0},{32,16},{48,32},{1,49},{17,1},{33,17},{49,33},{2,50}... | collective-permute-start | bytes 221192 | tf_op jit(solution)/shard_map/ppermute | solution.py:390
  192.8 3.2 %collective-permute-done.35.b2 = bf16[48,768]{1,0:T(8,128)(2,1)S(1)} collective-permute-done((bf16[48,768]{1,0:T(8,128)(2,1)S(1)}, bf16[48,768]{1,0:T(8,128)(2,1)S(1)}, u32[]{:S(2)}, u32[]{:S(2)}) %collective-permute-start.35) | collective-permute-done | bytes 73760 | tf_op jit(solution)/shard_map/ppermute | solution.py:390
  197.4 1.6 collective-permute-start.38
  199.5 3.0 %collective-permute-start.42 = (f32[8,768]{1,0:T(8,128)S(1)}, f32[8,768]{1,0:T(8,128)S(1)}, u32[]{:S(2)}, u32[]{:S(2)}) collective-permute-start(f32[8,768]{1,0:T(8,128)S(1)} %slice_add_fusion), channel_id=1, source_target_pairs={{0,2},{2,0},{1,3},{3,1},{4,6},{6,4},{5,7},{7,5},{8,10},{10,8},{9,1... | collective-permute-start | bytes 73736 | tf_op jit(solution)/shard_map/ppermute | solution.py:390
  203.1 1.8 collective-permute-done.42
  207.7 2.8 %collective-permute-done.39.p3 = bf16[4,48,768]{2,1,0:T(8,128)(2,1)S(1)} collective-permute-done((bf16[4,48,768]{2,1,0:T(8,128)(2,1)S(1)}, bf16[4,48,768]{2,1,0:T(8,128)(2,1)S(1)}, u32[]{:S(2)}, u32[]{:S(2)}) %collective-permute-start.39) | collective-permute-done | bytes 294944 | tf_op jit(solution)/shard_map/ppermute | solution.py:390
  210.5 2.2 shard_map.275
  212.7 1.7 copy-done.5
  214.4 2.3 %shard_map.277 = (f32[768,768]{1,0:T(8,128)}, f32[768,768]{1,0:T(8,128)}) custom-call(bf16[1536,768]{1,0:T(8,128)(2,1)S(1)} %copy-done.5, bf16[4,48,768]{2,1,0:T(8,128)(2,1)S(1)} %shard_map.274.p0.after), custom_call_target="tpu_custom_call" | custom-call | bytes 1024 | tf_op jit(solution)/shard_map/pallas_call | solution.py:375
  (138 shorter events, 37.8 us)
Async XLA Ops:
  7.2 103.7 %reduce-scatter.2.cloned.1.call-start = ((), (), s32[]{:S(2)}) async-start(), calls=%async_computation.1 | async-start | bytes 2506752 | tf_op jit(solution)/shard_map/reduce_scatter | solution.py:439
  11.6 6.7 %collective-permute-start.3 = (bf16[256,384]{1,0:T(8,128)(2,1)}, bf16[256,384]{1,0:T(8,128)(2,1)S(1)}, u32[]{:S(2)}, u32[]{:S(2)}) collective-permute-start(bf16[256,384]{1,0:T(8,128)(2,1)} %get-tuple-element.54.refs_4_.refs_5_), channel_id=1, source_target_pairs={{0,64},{64,0},{1,65},{65,1},{2,66},{66,2},{3,67},{67,3},{4,68},{68... | collective-permute-start | bytes 589832 | tf_op jit(solution)/shard_map/ppermute | solution.py:390
  25.3 187.5 %all-gather.2.cloned.1.call-start = ((), (), s32[]{:S(2)}) async-start(), calls=%async_computation.2 | async-start | bytes 2506752 | tf_op jit(solution)/shard_map/all_gather | solution.py:487
  25.3 10.8 %collective-permute-start = (bf16[256,384]{1,0:T(8,128)(2,1)S(1)}, bf16[256,384]{1,0:T(8,128)(2,1)S(1)}, u32[]{:S(2)}, u32[]{:S(2)}) collective-permute-start(bf16[256,384]{1,0:T(8,128)(2,1)S(1)} %copy-done.4), channel_id=1, source_target_pairs={{0,12},{4,0},{8,4},{12,8},{1,13},{5,1},{9,5},{13,9},{2,14},{6,2},{... | collective-permute-start | bytes 589832 | tf_op jit(solution)/shard_map/ppermute | solution.py:390
  28.6 11.5 %collective-permute-start.1 = (bf16[256,384]{1,0:T(8,128)(2,1)S(1)}, bf16[256,384]{1,0:T(8,128)(2,1)S(1)}, u32[]{:S(2)}, u32[]{:S(2)}) collective-permute-start(bf16[256,384]{1,0:T(8,128)(2,1)S(1)} %copy-done.4), channel_id=1, source_target_pairs={{0,8},{4,12},{8,0},{12,4},{1,9},{5,13},{9,1},{13,5},{2,10},{6,14},... | collective-permute-start | bytes 589832 | tf_op jit(solution)/shard_map/ppermute | solution.py:390
  29.3 10.9 %collective-permute-start.6 = (bf16[256,384]{1,0:T(8,128)(2,1)S(1)}, bf16[256,384]{1,0:T(8,128)(2,1)S(1)}, u32[]{:S(2)}, u32[]{:S(2)}) collective-permute-start(bf16[256,384]{1,0:T(8,128)(2,1)S(1)} %copy-done.9), channel_id=1, source_target_pairs={{0,16},{16,32},{32,48},{48,0},{1,17},{17,33},{33,49},{49,1},{2,18}... | collective-permute-start | bytes 589832 | tf_op jit(solution)/shard_map/ppermute | solution.py:390
  31.2 10.4 %collective-permute-start.5 = (bf16[256,384]{1,0:T(8,128)(2,1)S(1)}, bf16[256,384]{1,0:T(8,128)(2,1)S(1)}, u32[]{:S(2)}, u32[]{:S(2)}) collective-permute-start(bf16[256,384]{1,0:T(8,128)(2,1)S(1)} %collective-permute-done.3.refs_5_.after.refs_6_), channel_id=1, source_target_pairs={{0,48},{16,0},{32,16},{48,32},{1,49},{17,1},{33,17},{49,33},{2,50}... | collective-permute-start | bytes 589832 | tf_op jit(solution)/shard_map/ppermute | solution.py:390
  33.3 10.2 %collective-permute-start.2 = (bf16[256,384]{1,0:T(8,128)(2,1)S(1)}, bf16[256,384]{1,0:T(8,128)(2,1)S(1)}, u32[]{:S(2)}, u32[]{:S(2)}) collective-permute-start(bf16[256,384]{1,0:T(8,128)(2,1)S(1)} %copy-done.4), channel_id=1, source_target_pairs={{0,4},{4,8},{8,12},{12,0},{1,5},{5,9},{9,13},{13,1},{2,6},{6,10},{... | collective-permute-start | bytes 589832 | tf_op jit(solution)/shard_map/ppermute | solution.py:390
  36.1 8.5 %collective-permute-start.4 = (bf16[256,384]{1,0:T(8,128)(2,1)S(1)}, bf16[256,384]{1,0:T(8,128)(2,1)S(1)}, u32[]{:S(2)}, u32[]{:S(2)}) collective-permute-start(bf16[256,384]{1,0:T(8,128)(2,1)S(1)} %copy-done.9), channel_id=1, source_target_pairs={{0,48},{16,0},{32,16},{48,32},{1,49},{17,1},{33,17},{49,33},{2,50}... | collective-permute-start | bytes 589832 | tf_op jit(solution)/shard_map/ppermute | solution.py:390
  40.2 7.9 %collective-permute-start.9 = (bf16[256,384]{1,0:T(8,128)(2,1)S(1)}, bf16[256,384]{1,0:T(8,128)(2,1)S(1)}, u32[]{:S(2)}, u32[]{:S(2)}) collective-permute-start(bf16[256,384]{1,0:T(8,128)(2,1)S(1)} %collective-permute-done.3.refs_5_.after.refs_6_), channel_id=1, source_target_pairs={{0,16},{16,32},{32,48},{48,0},{1,17},{17,33},{33,49},{49,1},{2,18}... | collective-permute-start | bytes 589832 | tf_op jit(solution)/shard_map/ppermute | solution.py:390
  40.2 10.6 %collective-permute-start.7 = (bf16[256,384]{1,0:T(8,128)(2,1)S(1)}, bf16[256,384]{1,0:T(8,128)(2,1)S(1)}, u32[]{:S(2)}, u32[]{:S(2)}) collective-permute-start(bf16[256,384]{1,0:T(8,128)(2,1)S(1)} %collective-permute-done.6.refs_10_.refs_7_), channel_id=1, source_target_pairs={{0,16},{16,32},{32,48},{48,0},{1,17},{17,33},{33,49},{49,1},{2,18}... | collective-permute-start | bytes 589832 | tf_op jit(solution)/shard_map/ppermute | solution.py:390
  41.6 9.1 %collective-permute-start.8 = (bf16[256,384]{1,0:T(8,128)(2,1)S(1)}, bf16[256,384]{1,0:T(8,128)(2,1)S(1)}, u32[]{:S(2)}, u32[]{:S(2)}) collective-permute-start(bf16[256,384]{1,0:T(8,128)(2,1)S(1)} %collective-permute-done.5.refs_7_.refs_6_), channel_id=1, source_target_pairs={{0,48},{16,0},{32,16},{48,32},{1,49},{17,1},{33,17},{49,33},{2,50}... | collective-permute-start | bytes 589832 | tf_op jit(solution)/shard_map/ppermute | solution.py:390
  65.7 5.6 %collective-permute-start.10 = (f32[4,8,256]{2,1,0:T(8,128)S(1)}, f32[4,8,256]{2,1,0:T(8,128)S(1)}, u32[]{:S(2)}, u32[]{:S(2)}) collective-permute-start(f32[4,8,256]{2,1,0:T(8,128)S(1)} %get-tuple-element.55.s0.refs_0_), channel_id=1, source_target_pairs={{0,12},{4,0},{8,4},{12,8},{1,13},{5,1},{9,5},{13,9},{2,14},{6,2},{... | collective-permute-start | bytes 98312 | tf_op jit(solution)/shard_map/ppermute | solution.py:390
  69.6 5.6 %collective-permute-start.11 = (f32[4,8,256]{2,1,0:T(8,128)S(1)}, f32[4,8,256]{2,1,0:T(8,128)S(1)}, u32[]{:S(2)}, u32[]{:S(2)}) collective-permute-start(f32[4,8,256]{2,1,0:T(8,128)S(1)} %get-tuple-element.55.s0.refs_0_), channel_id=1, source_target_pairs={{0,8},{4,12},{8,0},{12,4},{1,9},{5,13},{9,1},{13,5},{2,10},{6,14},... | collective-permute-start | bytes 98312 | tf_op jit(solution)/shard_map/ppermute | solution.py:390
  69.6 5.6 %collective-permute-start.12 = (f32[4,8,256]{2,1,0:T(8,128)S(1)}, f32[4,8,256]{2,1,0:T(8,128)S(1)}, u32[]{:S(2)}, u32[]{:S(2)}) collective-permute-start(f32[4,8,256]{2,1,0:T(8,128)S(1)} %get-tuple-element.55.s0.refs_0_), channel_id=1, source_target_pairs={{0,4},{4,8},{8,12},{12,0},{1,5},{5,9},{9,13},{13,1},{2,6},{6,10},{... | collective-permute-start | bytes 98312 | tf_op jit(solution)/shard_map/ppermute | solution.py:390
  82.1 16.2 %collective-permute-start.18 = (bf16[2,256,384]{2,1,0:T(8,128)(2,1)S(1)}, bf16[2,256,384]{2,1,0:T(8,128)(2,1)S(1)}, u32[]{:S(2)}, u32[]{:S(2)}) collective-permute-start(bf16[2,256,384]{2,1,0:T(8,128)(2,1)S(1)} %get-tuple-element.67), channel_id=1, source_target_pairs={{0,32},{16,48},{32,0},{48,16},{1,33},{17,49},{33,1},{49,17},{2,34}... | collective-permute-start | bytes 1179656 | tf_op jit(solution)/shard_map/ppermute | solution.py:390
  98.3 31.6 %copy-start.6 = (bf16[192,768]{1,0:T(8,128)(2,1)S(1)}, bf16[192,768]{1,0:T(8,128)(2,1)}, u32[]{:S(2)}) copy-start(bf16[192,768]{1,0:T(8,128)(2,1)} %wd.3) | copy-start | bytes 884740
  111.8 5.2 %collective-permute-start.40 = (bf16[96,768]{1,0:T(8,128)(2,1)S(1)}, bf16[96,768]{1,0:T(8,128)(2,1)S(1)}, u32[]{:S(2)}, u32[]{:S(2)}) collective-permute-start(bf16[96,768]{1,0:T(8,128)(2,1)S(1)} %shard_map.276), channel_id=1, source_target_pairs={{0,64},{64,0},{1,65},{65,1},{2,66},{66,2},{3,67},{67,3},{4,68},{68... | collective-permute-start | bytes 442376 | tf_op jit(solution)/shard_map/ppermute | solution.py:390
  117.8 12.6 %collective-permute-start.22 = (bf16[2,256,384]{2,1,0:T(8,128)(2,1)}, bf16[2,256,384]{2,1,0:T(8,128)(2,1)S(1)}, u32[]{:S(2)}, u32[]{:S(2)}) collective-permute-start(bf16[2,256,384]{2,1,0:T(8,128)(2,1)} %copy-done.22), channel_id=1, source_target_pairs={{0,16},{16,32},{32,48},{48,0},{1,17},{17,33},{33,49},{49,1},{2,18}... | collective-permute-start | bytes 1179656 | tf_op jit(solution)/shard_map/ppermute | solution.py:390
  119.0 11.4 %collective-permute-start.23 = (bf16[2,256,384]{2,1,0:T(8,128)(2,1)}, bf16[2,256,384]{2,1,0:T(8,128)(2,1)S(1)}, u32[]{:S(2)}, u32[]{:S(2)}) collective-permute-start(bf16[2,256,384]{2,1,0:T(8,128)(2,1)} %copy-done.21), channel_id=1, source_target_pairs={{0,48},{16,0},{32,16},{48,32},{1,49},{17,1},{33,17},{49,33},{2,50}... | collective-permute-start | bytes 1179656 | tf_op jit(solution)/shard_map/ppermute | solution.py:390
  121.1 6.0 %collective-permute-start.13 = (bf16[192,256]{1,0:T(8,128)(2,1)}, bf16[192,256]{1,0:T(8,128)(2,1)S(1)}, u32[]{:S(2)}, u32[]{:S(2)}) collective-permute-start(bf16[192,256]{1,0:T(8,128)(2,1)} %copy-done.28), channel_id=1, source_target_pairs={{0,4},{4,8},{8,12},{12,0},{1,5},{5,9},{9,13},{13,1},{2,6},{6,10},{... | collective-permute-start | bytes 294920 | tf_op jit(solution)/shard_map/ppermute | solution.py:390
  122.2 6.5 %collective-permute-start.14 = (bf16[192,256]{1,0:T(8,128)(2,1)}, bf16[192,256]{1,0:T(8,128)(2,1)S(1)}, u32[]{:S(2)}, u32[]{:S(2)}) collective-permute-start(bf16[192,256]{1,0:T(8,128)(2,1)} %copy-done.27), channel_id=1, source_target_pairs={{0,8},{4,12},{8,0},{12,4},{1,9},{5,13},{9,1},{13,5},{2,10},{6,14},... | collective-permute-start | bytes 294920 | tf_op jit(solution)/shard_map/ppermute | solution.py:390
  124.9 4.9 %collective-permute-start.15 = (bf16[192,256]{1,0:T(8,128)(2,1)}, bf16[192,256]{1,0:T(8,128)(2,1)S(1)}, u32[]{:S(2)}, u32[]{:S(2)}) collective-permute-start(bf16[192,256]{1,0:T(8,128)(2,1)} %copy-done.26), channel_id=1, source_target_pairs={{0,12},{4,0},{8,4},{12,8},{1,13},{5,1},{9,5},{13,9},{2,14},{6,2},{... | collective-permute-start | bytes 294920 | tf_op jit(solution)/shard_map/ppermute | solution.py:390
  130.3 6.8 %collective-permute-start.16 = (bf16[256,768]{1,0:T(8,128)(2,1)S(1)}, bf16[256,768]{1,0:T(8,128)(2,1)S(1)}, u32[]{:S(2)}, u32[]{:S(2)}) collective-permute-start(bf16[256,768]{1,0:T(8,128)(2,1)S(1)} %get-tuple-element.62), channel_id=1, source_target_pairs={{0,1},{1,0},{2,3},{3,2},{4,5},{5,4},{6,7},{7,6},{8,9},{9,8},{10,11... | collective-permute-start | bytes 1179656 | tf_op jit(solution)/shard_map/ppermute | solution.py:390
  130.6 12.2 %collective-permute-start.24 = (bf16[256,384]{1,0:T(8,128)(2,1)S(1)}, bf16[256,384]{1,0:T(8,128)(2,1)S(1)}, u32[]{:S(2)}, u32[]{:S(2)}) collective-permute-start(bf16[256,384]{1,0:T(8,128)(2,1)S(1)} %get-tuple-element.98), channel_id=1, source_target_pairs={{0,64},{64,0},{1,65},{65,1},{2,66},{66,2},{3,67},{67,3},{4,68},{68... | collective-permute-start | bytes 589832 | tf_op jit(solution)/shard_map/ppermute | solution.py:390
  132.4 7.7 %collective-permute-start.19 = (bf16[192,256]{1,0:T(8,128)(2,1)}, bf16[192,256]{1,0:T(8,128)(2,1)S(1)}, u32[]{:S(2)}, u32[]{:S(2)}) collective-permute-start(bf16[192,256]{1,0:T(8,128)(2,1)} %copy-done.25), channel_id=1, source_target_pairs={{0,4},{4,8},{8,12},{12,0},{1,5},{5,9},{9,13},{13,1},{2,6},{6,10},{... | collective-permute-start | bytes 294920 | tf_op jit(solution)/shard_map/ppermute | solution.py:390
  133.5 9.3 %collective-permute-start.20 = (bf16[192,256]{1,0:T(8,128)(2,1)}, bf16[192,256]{1,0:T(8,128)(2,1)S(1)}, u32[]{:S(2)}, u32[]{:S(2)}) collective-permute-start(bf16[192,256]{1,0:T(8,128)(2,1)} %copy-done.24), channel_id=1, source_target_pairs={{0,8},{4,12},{8,0},{12,4},{1,9},{5,13},{9,1},{13,5},{2,10},{6,14},... | collective-permute-start | bytes 294920 | tf_op jit(solution)/shard_map/ppermute | solution.py:390
  137.1 5.7 %collective-permute-start.21 = (bf16[192,256]{1,0:T(8,128)(2,1)}, bf16[192,256]{1,0:T(8,128)(2,1)S(1)}, u32[]{:S(2)}, u32[]{:S(2)}) collective-permute-start(bf16[192,256]{1,0:T(8,128)(2,1)} %copy-done.23), channel_id=1, source_target_pairs={{0,12},{4,0},{8,4},{12,8},{1,13},{5,1},{9,5},{13,9},{2,14},{6,2},{... | collective-permute-start | bytes 294920 | tf_op jit(solution)/shard_map/ppermute | solution.py:390
  137.2 39.5 %collective-permute-start.17 = (bf16[256,768]{1,0:T(8,128)(2,1)S(1)}, bf16[256,768]{1,0:T(8,128)(2,1)S(1)}, u32[]{:S(2)}, u32[]{:S(2)}) collective-permute-start(bf16[256,768]{1,0:T(8,128)(2,1)S(1)} %add_convert_fusion.2), channel_id=1, source_target_pairs={{0,2},{2,0},{1,3},{3,1},{4,6},{6,4},{5,7},{7,5},{8,10},{10,8},{9,1... | collective-permute-start | bytes 1179656 | tf_op jit(solution)/shard_map/ppermute | solution.py:390
  142.9 33.8 %copy-start.30 = (f32[768]{0:T(1024)S(1)}, f32[768]{0:T(1024)}, u32[]{:S(2)}) copy-start(f32[768]{0:T(1024)} %param.26) | copy-start | bytes 9220
  142.9 33.8 %copy-start.31 = (f32[768]{0:T(1024)S(1)}, f32[768]{0:T(1024)}, u32[]{:S(2)}) copy-start(f32[768]{0:T(1024)} %param.22) | copy-start | bytes 9220
  145.2 15.0 %collective-permute-start.27 = (bf16[208,768]{1,0:T(8,128)(2,1)S(1)}, bf16[208,768]{1,0:T(8,128)(2,1)S(1)}, u32[]{:S(2)}, u32[]{:S(2)}) collective-permute-start(bf16[208,768]{1,0:T(8,128)(2,1)S(1)} %get-tuple-element.80), channel_id=1, source_target_pairs={{0,4},{4,8},{8,12},{12,0},{1,5},{5,9},{9,13},{13,1},{2,6},{6,10},{... | collective-permute-start | bytes 958472 | tf_op jit(solution)/shard_map/ppermute | solution.py:390
  145.5 26.9 %collective-permute-start.28 = (bf16[208,768]{1,0:T(8,128)(2,1)S(1)}, bf16[208,768]{1,0:T(8,128)(2,1)S(1)}, u32[]{:S(2)}, u32[]{:S(2)}) collective-permute-start(bf16[208,768]{1,0:T(8,128)(2,1)S(1)} %get-tuple-element.81), channel_id=1, source_target_pairs={{0,8},{4,12},{8,0},{12,4},{1,9},{5,13},{9,1},{13,5},{2,10},{6,14},... | collective-permute-start | bytes 958472 | tf_op jit(solution)/shard_map/ppermute | solution.py:390
  148.6 23.8 %collective-permute-start.29 = (bf16[208,768]{1,0:T(8,128)(2,1)S(1)}, bf16[208,768]{1,0:T(8,128)(2,1)S(1)}, u32[]{:S(2)}, u32[]{:S(2)}) collective-permute-start(bf16[208,768]{1,0:T(8,128)(2,1)S(1)} %get-tuple-element.82), channel_id=1, source_target_pairs={{0,12},{4,0},{8,4},{12,8},{1,13},{5,1},{9,5},{13,9},{2,14},{6,2},{... | collective-permute-start | bytes 958472 | tf_op jit(solution)/shard_map/ppermute | solution.py:390
  148.8 33.9 %collective-permute-start.25 = (bf16[256,768]{1,0:T(8,128)(2,1)S(1)}, bf16[256,768]{1,0:T(8,128)(2,1)S(1)}, u32[]{:S(2)}, u32[]{:S(2)}) collective-permute-start(bf16[256,768]{1,0:T(8,128)(2,1)S(1)} %get-tuple-element.78), channel_id=1, source_target_pairs={{0,1},{1,0},{2,3},{3,2},{4,5},{5,4},{6,7},{7,6},{8,9},{9,8},{10,11... | collective-permute-start | bytes 1179656 | tf_op jit(solution)/shard_map/ppermute | solution.py:390
  173.4 7.0 %collective-permute-start.30 = (bf16[64,768]{1,0:T(8,128)(2,1)S(1)}, bf16[64,768]{1,0:T(8,128)(2,1)S(1)}, u32[]{:S(2)}, u32[]{:S(2)}) collective-permute-start(bf16[64,768]{1,0:T(8,128)(2,1)S(1)} %get-tuple-element.84), channel_id=1, source_target_pairs={{0,16},{16,32},{32,48},{48,0},{1,17},{17,33},{33,49},{49,1},{2,18}... | collective-permute-start | bytes 294920 | tf_op jit(solution)/shard_map/ppermute | solution.py:390
  173.4 6.9 %collective-permute-start.31 = (bf16[64,768]{1,0:T(8,128)(2,1)S(1)}, bf16[64,768]{1,0:T(8,128)(2,1)S(1)}, u32[]{:S(2)}, u32[]{:S(2)}) collective-permute-start(bf16[64,768]{1,0:T(8,128)(2,1)S(1)} %get-tuple-element.85), channel_id=1, source_target_pairs={{0,32},{16,48},{32,0},{48,16},{1,33},{17,49},{33,1},{49,17},{2,34}... | collective-permute-start | bytes 294920 | tf_op jit(solution)/shard_map/ppermute | solution.py:390
  175.0 6.2 %collective-permute-start.32 = (bf16[64,768]{1,0:T(8,128)(2,1)S(1)}, bf16[64,768]{1,0:T(8,128)(2,1)S(1)}, u32[]{:S(2)}, u32[]{:S(2)}) collective-permute-start(bf16[64,768]{1,0:T(8,128)(2,1)S(1)} %get-tuple-element.86), channel_id=1, source_target_pairs={{0,48},{16,0},{32,16},{48,32},{1,49},{17,1},{33,17},{49,33},{2,50}... | collective-permute-start | bytes 294920 | tf_op jit(solution)/shard_map/ppermute | solution.py:390
  181.9 5.8 %collective-permute-start.33 = (bf16[64,768]{1,0:T(8,128)(2,1)S(1)}, bf16[64,768]{1,0:T(8,128)(2,1)S(1)}, u32[]{:S(2)}, u32[]{:S(2)}) collective-permute-start(bf16[64,768]{1,0:T(8,128)(2,1)S(1)} %shard_map.273), channel_id=1, source_target_pairs={{0,64},{64,0},{1,65},{65,1},{2,66},{66,2},{3,67},{67,3},{4,68},{68... | collective-permute-start | bytes 294920 | tf_op jit(solution)/shard_map/ppermute | solution.py:390
  182.9 22.7 %collective-permute-start.26 = (bf16[256,768]{1,0:T(8,128)(2,1)S(1)}, bf16[256,768]{1,0:T(8,128)(2,1)S(1)}, u32[]{:S(2)}, u32[]{:S(2)}) collective-permute-start(bf16[256,768]{1,0:T(8,128)(2,1)S(1)} %add_convert_fusion.e0), channel_id=1, source_target_pairs={{0,2},{2,0},{1,3},{3,1},{4,6},{6,4},{5,7},{7,5},{8,10},{10,8},{9,1... | collective-permute-start | bytes 1179656 | tf_op jit(solution)/shard_map/ppermute | solution.py:390
  187.7 5.1 %collective-permute-start.34 = (bf16[48,768]{1,0:T(8,128)(2,1)S(1)}, bf16[48,768]{1,0:T(8,128)(2,1)S(1)}, u32[]{:S(2)}, u32[]{:S(2)}) collective-permute-start(bf16[48,768]{1,0:T(8,128)(2,1)S(1)} %slice.105.b0), channel_id=1, source_target_pairs={{0,48},{16,0},{32,16},{48,32},{1,49},{17,1},{33,17},{49,33},{2,50}... | collective-permute-start | bytes 221192 | tf_op jit(solution)/shard_map/ppermute | solution.py:390
  190.1 5.9 %collective-permute-start.35 = (bf16[48,768]{1,0:T(8,128)(2,1)S(1)}, bf16[48,768]{1,0:T(8,128)(2,1)S(1)}, u32[]{:S(2)}, u32[]{:S(2)}) collective-permute-start(bf16[48,768]{1,0:T(8,128)(2,1)S(1)} %slice.105.b0), channel_id=1, source_target_pairs={{0,32},{16,48},{32,0},{48,16},{1,33},{17,49},{33,1},{49,17},{2,34}... | collective-permute-start | bytes 221192 | tf_op jit(solution)/shard_map/ppermute | solution.py:390
  190.8 6.0 %collective-permute-start.36 = (bf16[48,768]{1,0:T(8,128)(2,1)S(1)}, bf16[48,768]{1,0:T(8,128)(2,1)S(1)}, u32[]{:S(2)}, u32[]{:S(2)}) collective-permute-start(bf16[48,768]{1,0:T(8,128)(2,1)S(1)} %slice.105.b0), channel_id=1, source_target_pairs={{0,16},{16,32},{32,48},{48,0},{1,17},{17,33},{33,49},{49,1},{2,18}... | collective-permute-start | bytes 221192 | tf_op jit(solution)/shard_map/ppermute | solution.py:390
  191.1 8.4 %collective-permute-start.41 = (f32[8,768]{1,0:T(8,128)S(1)}, f32[8,768]{1,0:T(8,128)S(1)}, u32[]{:S(2)}, u32[]{:S(2)}) collective-permute-start(f32[8,768]{1,0:T(8,128)S(1)} %slice.83), channel_id=1, source_target_pairs={{0,1},{1,0},{2,3},{3,2},{4,5},{5,4},{6,7},{7,6},{8,9},{9,8},{10,11... | collective-permute-start | bytes 73736 | tf_op jit(solution)/shard_map/ppermute | solution.py:390
  197.4 9.5 %collective-permute-start.37 = (bf16[4,48,768]{2,1,0:T(8,128)(2,1)S(1)}, bf16[4,48,768]{2,1,0:T(8,128)(2,1)S(1)}, u32[]{:S(2)}, u32[]{:S(2)}) collective-permute-start(bf16[4,48,768]{2,1,0:T(8,128)(2,1)S(1)} %shard_map.274.p0.after), channel_id=1, source_target_pairs={{0,12},{4,0},{8,4},{12,8},{1,13},{5,1},{9,5},{13,9},{2,14},{6,2},{... | collective-permute-start | bytes 884744 | tf_op jit(solution)/shard_map/ppermute | solution.py:390
  197.4 10.2 %collective-permute-start.38 = (bf16[4,48,768]{2,1,0:T(8,128)(2,1)S(1)}, bf16[4,48,768]{2,1,0:T(8,128)(2,1)S(1)}, u32[]{:S(2)}, u32[]{:S(2)}) collective-permute-start(bf16[4,48,768]{2,1,0:T(8,128)(2,1)S(1)} %shard_map.274.p0.after), channel_id=1, source_target_pairs={{0,8},{4,12},{8,0},{12,4},{1,9},{5,13},{9,1},{13,5},{2,10},{6,14},... | collective-permute-start | bytes 884744 | tf_op jit(solution)/shard_map/ppermute | solution.py:390
  199.0 11.5 %collective-permute-start.39 = (bf16[4,48,768]{2,1,0:T(8,128)(2,1)S(1)}, bf16[4,48,768]{2,1,0:T(8,128)(2,1)S(1)}, u32[]{:S(2)}, u32[]{:S(2)}) collective-permute-start(bf16[4,48,768]{2,1,0:T(8,128)(2,1)S(1)} %shard_map.274.p0.after), channel_id=1, source_target_pairs={{0,4},{4,8},{8,12},{12,0},{1,5},{5,9},{9,13},{13,1},{2,6},{6,10},{... | collective-permute-start | bytes 884744 | tf_op jit(solution)/shard_map/ppermute | solution.py:390
  199.5 5.4 %collective-permute-start.42 = (f32[8,768]{1,0:T(8,128)S(1)}, f32[8,768]{1,0:T(8,128)S(1)}, u32[]{:S(2)}, u32[]{:S(2)}) collective-permute-start(f32[8,768]{1,0:T(8,128)S(1)} %slice_add_fusion), channel_id=1, source_target_pairs={{0,2},{2,0},{1,3},{3,1},{4,6},{6,4},{5,7},{7,5},{8,10},{10,8},{9,1... | collective-permute-start | bytes 73736 | tf_op jit(solution)/shard_map/ppermute | solution.py:390
  (29 other events, 219.3 us)
Sparse Core Ops, SparseCore 0:
  25.4 85.4 reduce-scatter.1
  117.9 55.3 all-gather.1

commit v3 on v2

--- a/solution.py
+++ b/solution.py
@@ -62,8 +62,8 @@
     return ref[...].reshape(1, -1)
 
 
-def keep_kernel(x, after, out):
-    out[...] = x[...]
+def keep_kernel(x, *refs):
+    refs[-1][...] = x[...]
 
 
 def widen_kernel(x, after, up, down):
@@ -110,7 +110,8 @@
     kv[...] = jnp.concatenate([pieces[i] for i in (1, 4, 7, 2, 5, 8)], axis=1).astype(BF)
 
 
-def mlp_kernel(ln, cot, wu, bu, wdn, after, gw, small, part, d_ln):
+def mlp_kernel(ln, cot, wu, bu, wdn, *refs):
+    gw, small, part, d_ln = refs[-4:]
     up = mm(ln[...], wu[...]) + row(bu)
     phi = 0.5 * (1.0 + lax.erf(up * math.sqrt(0.5)))
     hid = (up * phi).astype(BF)
@@ -359,7 +360,7 @@
         out[(coords[1] + slot) % 4] = ref[...]
 
 
-def assemble_kernel(coords, p0, p1, p2, p3, gq, gd, whole):
+def assemble_kernel(coords, p0, p1, p2, p3, after, gq, gd, whole):
     for slot, ref in enumerate((p0, p1, p2, p3)):
         whole[(coords[2] + slot) % 4] = ref[...].astype(F32)
     for block in range(12):
@@ -432,9 +433,9 @@
     grads_mlp, small_mlp, part_mlp, d_ln_mlp = call(
         mlp_kernel,
         [((1536, 768), BF), ((8, 768), F32), ((256, 768), F32), ((256, 768), F32)],
-        (ln_mlp, cotangent, w_up, b_up, w_down, kv_x),
+        (ln_mlp, cotangent, w_up, b_up, w_down, up_x, down, down_x, *qdos[1:]),
         0,
-        unread=1,
+        unread=6,
     )
     grads_mlp = lax.psum_scatter(grads_mlp, ("z", "y"), scatter_dimension=0, tiled=True)
     *outs, stats = call(
@@ -452,7 +453,8 @@
         (*stats_all, *outs, w_dense, part_mlp),
         0,
     )
-    branch = add(branch, hop(branch, "c", 1)).astype(BF)
+    branch_near = hop(branch, "c", 1)
+    branch = add(branch, branch_near).astype(BF)
     branch = add(branch, hop(branch, "xh", 1))
     output = (tokens.astype(F32) + branch + b_dense + b_down).astype(BF)
 
@@ -479,15 +481,16 @@
     far = hop(d_far, "z", 2)
     d_up, d_down, d_q = backward((2, 3, 6, 7), [whole], d_q, False)
     near = [hop(d_up, "z", 1), hop(d_down, "z", -1)]
-    d_kv, *d_qs = backward((0, 1), [whole], d_q, True, (far,))
+    d_kv, *d_qs = backward((0, 1), [whole], d_q, True, (far, branch_near))
+    d_queries = [d_qs[0]] + [hop(d_qs[j], "y", j) for j in (1, 2, 3)]
+    d_kv_send = add(d_kv[1], far[1], near[0][1], near[1][1]).astype(BF)
+    d_kv_other = hop(d_kv_send, "xl", 1)
+    d_kv_own = add(d_kv[0], far[0], near[0][0], near[1][0]).astype(BF)
     (grads_mlp,) = call(
-        keep_kernel, [(grads_mlp.shape, BF)], (grads_mlp, d_kv), 0, unread=1
+        keep_kernel, [(grads_mlp.shape, BF)], (grads_mlp, d_kv_send, *d_queries[1:]), 0, unread=4
     )
     grads_mlp = add(grads_mlp, hop(grads_mlp, "xl", 1)).astype(BF)
     grads_mlp = lax.all_gather(grads_mlp, ("z", "y"), axis=0, tiled=True)
-    d_queries = [d_qs[0]] + [hop(d_qs[j], "y", j) for j in (1, 2, 3)]
-    d_kv_other = hop(add(d_kv[1], far[1], near[0][1], near[1][1]).astype(BF), "xl", 1)
-    d_kv_own = add(d_kv[0], far[0], near[0][0], near[1][0]).astype(BF)
     *pieces, upstream = call(
         tail_kernel,
         [((208, 768), BF)] * 4 + [((256, 768), BF)],
@@ -525,20 +528,21 @@
         (coords, block, *[hop(block, "z", -j) for j in (1, 2, 3)]),
         1,
     )
+    grad_w_up, grad_w_down = call(
+        widen_kernel, [((768, 768), F32)] * 2, (grads_mlp, quarter), 0, unread=1
+    )
     grad_turned, grad_w_dense = call(
         assemble_kernel,
         [((576, 768), F32), ((192, 768), F32)],
-        (coords, quarter, *[hop(quarter, "y", -j) for j in (1, 2, 3)]),
+        (coords, quarter, *[hop(quarter, "y", -j) for j in (1, 2, 3)], grad_w_up),
         1,
+        unread=1,
         scratch=[pltpu.VMEM((4, 4, 48, 768), F32)],
     )
     (grad_tokens,) = call(
         token_kernel, [((256, 768), BF)], (tokens, cotangent, upstream, upstream_far), 0
     )
 
-    grad_w_up, grad_w_down = call(
-        widen_kernel, [((768, 768), F32)] * 2, (grads_mlp, quarter), 0, unread=1
-    )
     return (
         output,
         grad_tokens,

time: 225 us -> 210 us (0.933)
  waiting for transfers between devices: 71.7 us -> 46.8 us
  starting transfers between devices: 63.3 us -> 68.4 us
  local copies, waits for them, and re-layouts: 14.9 us -> 18.6 us
    ppermute x43, waiting for transfers between devices: 68.4 us -> 45.6 us  [hop(): return lax.ppermute(x, axis, [(i, (i + step) % n) for i in range(n)])]
    ppermute x43, starting transfers between devices: 63.2 us -> 68.4 us  [hop(): return lax.ppermute(x, axis, [(i, (i + step) % n) for i in range(n)])]
    unnamed x65 -> x73, local copies, waits for them, and re-layouts: 13.1 us -> 16.8 us
  transfers between devices with their start and end apart: 45 -> 45, of which waited for: 24 -> 22; matrix products, arithmetic and copies ran while one was open for 1% -> 2% of each run, Pallas kernels for 21% -> 23%
where the time goes in v3:
time: 210 us; the launch traced here: 209 us
  starting transfers between devices  68.4 us (33%)
  Pallas kernels  57.1 us (27%)
  waiting for transfers between devices  46.8 us (22%)
  local copies, waits for them, and re-layouts  18.6 us (9%)
  between operations  14.4 us (7%)
  other arithmetic  3.64 us (2%)
    ppermute x43, starting transfers between devices, hop(): return lax.ppermute(x, axis, [(i, (i + step) % n) for i in range(n)])  68.4 us
    pallas_call x15, Pallas kernels, call(): pl.pallas_call(kernel, out_shape=shapes, in_specs=[smem] * scalars + [vme...  57.1 us
    ppermute x43, waiting for transfers between devices, hop(): return lax.ppermute(x, axis, [(i, (i + step) % n) for i in range(n)])  45.6 us
    unnamed x73, local copies, waits for them, and re-layouts  16.8 us
  transfers between devices with their start and end apart: 45, of which 22 were waited for; matrix products, arithmetic and copies ran while one was open for 2% of the time, Pallas kernels for 23%

profile of v3, /device:TPU:0, one launch (start us, length us, event | category | flops | bytes accessed | tf_op | source)
XLA Modules:
  0.0 209.0 jit_solution(7457895036252911816)
XLA Ops:
  7.8 3.7 %shard_map.263 = (bf16[256,384]{1,0:T(8,128)(2,1)}, bf16[256,384]{1,0:T(8,128)(2,1)}, bf16[256,768]{1,0:T(8,128)(2,1)}, bf16[256,768]{1,0:T(8,128)(2,1)}) custom-call(s32[3]{0:T(128)} %pad_add_fusion.coords, s32[64]{0:T(128)} %order.11, f32[8,128]{1,0:T(8,128)} %constant.17.clone.table, bf16[256,768]{1,0:T(8,128)(2,1)} %tok.5, bf16[256,768]{1,0:T(8,128)(2,1)} %cot.7, ...), custom_call_target="tpu_custom_call" | custom-call | bytes 1024 | tf_op jit(solution)/shard_map/pallas_call | solution.py:376
  11.6 1.6 collective-permute-start.3
  13.1 1.9 collective-permute-start.6
  15.1 1.6 collective-permute-start.2
  16.6 2.9 %collective-permute-start.1 = (bf16[256,384]{1,0:T(8,128)(2,1)}, bf16[256,384]{1,0:T(8,128)(2,1)S(1)}, u32[]{:S(2)}, u32[]{:S(2)}) collective-permute-start(bf16[256,384]{1,0:T(8,128)(2,1)} %get-tuple-element.53.refs_0_.refs_4_.refs_1_), channel_id=1, source_target_pairs={{0,8},{4,12},{8,0},{12,4},{1,9},{5,13},{9,1},{13,5},{2,10},{6,14},... | collective-permute-start | bytes 589832 | tf_op jit(solution)/shard_map/ppermute | solution.py:391
  19.5 1.3 collective-permute-start
  20.9 1.9 collective-permute-start.9
  24.8 3.2 %collective-permute-done.1.refs_2_.refs_4_.refs_6_.refs_3_ = bf16[256,384]{1,0:T(8,128)(2,1)S(1)} collective-permute-done((bf16[256,384]{1,0:T(8,128)(2,1)}, bf16[256,384]{1,0:T(8,128)(2,1)S(1)}, u32[]{:S(2)}, u32[]{:S(2)}) %collective-permute-start.1) | collective-permute-done | bytes 196640 | tf_op jit(solution)/shard_map/ppermute | solution.py:391
  32.4 3.0 %shard_map.265 = (bf16[1536,768]{1,0:T(8,128)(2,1)}, f32[8,768]{1,0:T(8,128)S(1)}, f32[256,768]{1,0:T(8,128)S(1)}, f32[256,768]{1,0:T(8,128)S(1)}) custom-call(bf16[256,768]{1,0:T(8,128)(2,1)S(1)} %copy-done.16, bf16[256,768]{1,0:T(8,128)(2,1)S(1)} %copy-done, bf16[768,768]{1,0:T(8,128)(2,1)S(1)} %copy-done.7, f32[768]{0:T(1024)S(1)} %copy-done.32, ...), custom_call_target="tpu_custom_call" | custom-call | bytes 1024 | tf_op jit(solution)/shard_map/pallas_call | solution.py:376
  37.0 2.6 %collective-permute-start.4 = (bf16[256,384]{1,0:T(8,128)(2,1)S(1)}, bf16[256,384]{1,0:T(8,128)(2,1)S(1)}, u32[]{:S(2)}, u32[]{:S(2)}) collective-permute-start(bf16[256,384]{1,0:T(8,128)(2,1)S(1)} %copy-done.10), channel_id=1, source_target_pairs={{0,48},{16,0},{32,16},{48,32},{1,49},{17,1},{33,17},{49,33},{2,50}... | collective-permute-start | bytes 589832 | tf_op jit(solution)/shard_map/ppermute | solution.py:391
  39.7 3.2 %collective-permute-start.8 = (bf16[256,384]{1,0:T(8,128)(2,1)S(1)}, bf16[256,384]{1,0:T(8,128)(2,1)S(1)}, u32[]{:S(2)}, u32[]{:S(2)}) collective-permute-start(bf16[256,384]{1,0:T(8,128)(2,1)S(1)} %collective-permute-done.5.refs_7_.refs_0_.refs_6_), channel_id=1, source_target_pairs={{0,48},{16,0},{32,16},{48,32},{1,49},{17,1},{33,17},{49,33},{2,50}... | collective-permute-start | bytes 589832 | tf_op jit(solution)/shard_map/ppermute | solution.py:391
  42.9 1.8 collective-permute-done.4.refs_6_.refs_5_
  44.7 1.8 collective-permute-done.7.refs_8_
  47.0 13.0 %shard_map.264 = (bf16[192,256]{1,0:T(8,128)(2,1)S(1)}, bf16[192,256]{1,0:T(8,128)(2,1)S(1)}, bf16[192,256]{1,0:T(8,128)(2,1)S(1)}, bf16[192,256]{1,0:T(8,128)(2,1)S(1)}, f32[4,8,256]{2,1,0:T(8,128)S(1)}) custom-call(s32[3]{0:T(128)S(1)} %copy-done.25, s32[64]{0:T(128)S(1)} %copy-done.28, bf16[256,384]{1,0:T(8,128)(2,1)S(1)} %copy-done.4, ...), custom_call_target="tpu_custom_call" | custom-call | bytes 1024 | tf_op jit(solution)/shard_map/pallas_call | solution.py:376
  61.3 2.8 %collective-permute-start.14 = (bf16[192,256]{1,0:T(8,128)(2,1)S(1)}, bf16[192,256]{1,0:T(8,128)(2,1)S(1)}, u32[]{:S(2)}, u32[]{:S(2)}) collective-permute-start(bf16[192,256]{1,0:T(8,128)(2,1)S(1)} %get-tuple-element.58), channel_id=1, source_target_pairs={{0,8},{4,12},{8,0},{12,4},{1,9},{5,13},{9,1},{13,5},{2,10},{6,14},... | collective-permute-start | bytes 294920 | tf_op jit(solution)/shard_map/ppermute | solution.py:391
  66.9 3.4 %collective-permute-done.12.s3.refs_3_ = f32[4,8,256]{2,1,0:T(8,128)S(1)} collective-permute-done((f32[4,8,256]{2,1,0:T(8,128)S(1)}, f32[4,8,256]{2,1,0:T(8,128)S(1)}, u32[]{:S(2)}, u32[]{:S(2)}) %collective-permute-start.12) | collective-permute-done | bytes 32800 | tf_op jit(solution)/shard_map/ppermute | solution.py:391
  71.6 2.7 %collective-permute-done.10.s1.refs_1_ = f32[4,8,256]{2,1,0:T(8,128)S(1)} collective-permute-done((f32[4,8,256]{2,1,0:T(8,128)S(1)}, f32[4,8,256]{2,1,0:T(8,128)S(1)}, u32[]{:S(2)}, u32[]{:S(2)}) %collective-permute-start.10) | collective-permute-done | bytes 32800 | tf_op jit(solution)/shard_map/ppermute | solution.py:391
  74.3 6.8 %shard_map.267 = (f32[4,8,256]{2,1,0:T(8,128)S(1)}, bf16[2,256,384]{2,1,0:T(8,128)(2,1)S(1)}, f32[4,192,256]{2,1,0:T(8,128)S(1)}) custom-call(s32[3]{0:T(128)S(1)} %copy-done.25, s32[64]{0:T(128)S(1)} %copy-done.28, f32[4,8,256]{2,1,0:T(8,128)S(1)} %get-tuple-element.55.s0.refs_0_, f32[4,8,256]{2,1,0:T(8,128)S(1)} %collective-permute-done.10.s1.refs_1_, ...), custom_call_target="tpu_custom_call" | custom-call | bytes 1024 | tf_op jit(solution)/shard_map/pallas_call | solution.py:376
  81.1 2.6 %collective-permute-start.18 = (bf16[2,256,384]{2,1,0:T(8,128)(2,1)S(1)}, bf16[2,256,384]{2,1,0:T(8,128)(2,1)S(1)}, u32[]{:S(2)}, u32[]{:S(2)}) collective-permute-start(bf16[2,256,384]{2,1,0:T(8,128)(2,1)S(1)} %get-tuple-element.67), channel_id=1, source_target_pairs={{0,32},{16,48},{32,0},{48,16},{1,33},{17,49},{33,1},{49,17},{2,34}... | collective-permute-start | bytes 1179656 | tf_op jit(solution)/shard_map/ppermute | solution.py:391
  84.8 13.0 %shard_map.268 = (bf16[2,256,384]{2,1,0:T(8,128)(2,1)S(1)}, bf16[2,256,384]{2,1,0:T(8,128)(2,1)S(1)}, f32[4,192,256]{2,1,0:T(8,128)S(1)}) custom-call(s32[3]{0:T(128)S(1)} %copy-done.25, s32[64]{0:T(128)S(1)} %copy-done.28, f32[4,8,256]{2,1,0:T(8,128)S(1)} %get-tuple-element.64.refs_0_, bf16[256,384]{1,0:T(8,128)(2,1)S(1)} %copy-done.4, ...), custom_call_target="tpu_custom_call" | custom-call | bytes 1024 | tf_op jit(solution)/shard_map/pallas_call | solution.py:376
  97.8 1.8 collective-permute-start.22
  99.7 1.5 collective-permute-start.23
  101.2 6.9 %shard_map.269 = (bf16[2,256,384]{2,1,0:T(8,128)(2,1)S(1)}, bf16[192,256]{1,0:T(8,128)(2,1)S(1)}, bf16[192,256]{1,0:T(8,128)(2,1)S(1)}, bf16[192,256]{1,0:T(8,128)(2,1)S(1)}, bf16[192,256]{1,0:T(8,128)(2,1)S(1)}) custom-call(s32[3]{0:T(128)S(1)} %copy-done.25, s32[64]{0:T(128)S(1)} %copy-done.28, f32[4,8,256]{2,1,0:T(8,128)S(1)} %get-tuple-element.64.refs_0_, ...), custom_call_target="tpu_custom_call" | custom-call | bytes 1024 | tf_op jit(solution)/shard_map/pallas_call | solution.py:376
  108.4 2.6 %collective-permute-start.20 = (bf16[192,256]{1,0:T(8,128)(2,1)S(1)}, bf16[192,256]{1,0:T(8,128)(2,1)S(1)}, u32[]{:S(2)}, u32[]{:S(2)}) collective-permute-start(bf16[192,256]{1,0:T(8,128)(2,1)S(1)} %get-tuple-element.70), channel_id=1, source_target_pairs={{0,8},{4,12},{8,0},{12,4},{1,9},{5,13},{9,1},{13,5},{2,10},{6,14},... | collective-permute-start | bytes 294920 | tf_op jit(solution)/shard_map/ppermute | solution.py:391
  111.0 1.4 collective-permute-start.21
  112.6 5.1 %collective-permute-done.19.dq1.refs_1_ = bf16[192,256]{1,0:T(8,128)(2,1)S(1)} collective-permute-done((bf16[192,256]{1,0:T(8,128)(2,1)S(1)}, bf16[192,256]{1,0:T(8,128)(2,1)S(1)}, u32[]{:S(2)}, u32[]{:S(2)}) %collective-permute-start.19) | collective-permute-done | bytes 98336 | tf_op jit(solution)/shard_map/ppermute | solution.py:391
  121.0 4.1 %collective-permute-done.40 = bf16[96,768]{1,0:T(8,128)(2,1)S(1)} collective-permute-done((bf16[96,768]{1,0:T(8,128)(2,1)S(1)}, bf16[96,768]{1,0:T(8,128)(2,1)S(1)}, u32[]{:S(2)}, u32[]{:S(2)}) %collective-permute-start.40) | collective-permute-done | bytes 147488 | tf_op jit(solution)/shard_map/ppermute | solution.py:391
  128.0 3.0 %collective-permute-start.17 = (bf16[256,768]{1,0:T(8,128)(2,1)S(1)}, bf16[256,768]{1,0:T(8,128)(2,1)S(1)}, u32[]{:S(2)}, u32[]{:S(2)}) collective-permute-start(bf16[256,768]{1,0:T(8,128)(2,1)S(1)} %add_convert_fusion.2), channel_id=1, source_target_pairs={{0,2},{2,0},{1,3},{3,1},{4,6},{6,4},{5,7},{7,5},{8,10},{10,8},{9,1... | collective-permute-start | bytes 1179656 | tf_op jit(solution)/shard_map/ppermute | solution.py:391
  131.0 1.8 collective-permute-done.24.dkv1
  138.0 2.2 %shard_map.270 = (bf16[208,768]{1,0:T(8,128)(2,1)S(1)}, bf16[208,768]{1,0:T(8,128)(2,1)S(1)}, bf16[208,768]{1,0:T(8,128)(2,1)S(1)}, bf16[208,768]{1,0:T(8,128)(2,1)S(1)}, bf16[256,768]{1,0:T(8,128)(2,1)S(1)}) custom-call(s32[3]{0:T(128)S(1)} %copy-done.25, s32[64]{0:T(128)S(1)} %copy-done.28, f32[8,128]{1,0:T(8,128)S(1)} %copy-done.31, ...), custom_call_target="tpu_custom_call" | custom-call | bytes 1024 | tf_op jit(solution)/shard_map/pallas_call | solution.py:376
  140.2 1.5 collective-permute-start.27
  141.8 3.8 %collective-permute-start.28 = (bf16[208,768]{1,0:T(8,128)(2,1)S(1)}, bf16[208,768]{1,0:T(8,128)(2,1)S(1)}, u32[]{:S(2)}, u32[]{:S(2)}) collective-permute-start(bf16[208,768]{1,0:T(8,128)(2,1)S(1)} %get-tuple-element.81), channel_id=1, source_target_pairs={{0,8},{4,12},{8,0},{12,4},{1,9},{5,13},{9,1},{13,5},{2,10},{6,14},... | collective-permute-start | bytes 958472 | tf_op jit(solution)/shard_map/ppermute | solution.py:391
  145.6 6.7 %collective-permute-done.27.p1 = bf16[208,768]{1,0:T(8,128)(2,1)S(1)} collective-permute-done((bf16[208,768]{1,0:T(8,128)(2,1)S(1)}, bf16[208,768]{1,0:T(8,128)(2,1)S(1)}, u32[]{:S(2)}, u32[]{:S(2)}) %collective-permute-start.27) | collective-permute-done | bytes 319520 | tf_op jit(solution)/shard_map/ppermute | solution.py:391
  152.3 3.4 %collective-permute-done.28.p2 = bf16[208,768]{1,0:T(8,128)(2,1)S(1)} collective-permute-done((bf16[208,768]{1,0:T(8,128)(2,1)S(1)}, bf16[208,768]{1,0:T(8,128)(2,1)S(1)}, u32[]{:S(2)}, u32[]{:S(2)}) %collective-permute-start.28) | collective-permute-done | bytes 319520 | tf_op jit(solution)/shard_map/ppermute | solution.py:391
  157.9 2.5 %collective-permute-start.31 = (bf16[64,768]{1,0:T(8,128)(2,1)S(1)}, bf16[64,768]{1,0:T(8,128)(2,1)S(1)}, u32[]{:S(2)}, u32[]{:S(2)}) collective-permute-start(bf16[64,768]{1,0:T(8,128)(2,1)S(1)} %get-tuple-element.85), channel_id=1, source_target_pairs={{0,32},{16,48},{32,0},{48,16},{1,33},{17,49},{33,1},{49,17},{2,34}... | collective-permute-start | bytes 294920 | tf_op jit(solution)/shard_map/ppermute | solution.py:391
  160.4 1.6 collective-permute-start.32
  164.2 4.0 %collective-permute-done.32.b3 = bf16[64,768]{1,0:T(8,128)(2,1)S(1)} collective-permute-done((bf16[64,768]{1,0:T(8,128)(2,1)S(1)}, bf16[64,768]{1,0:T(8,128)(2,1)S(1)}, u32[]{:S(2)}, u32[]{:S(2)}) %collective-permute-start.32) | collective-permute-done | bytes 98336 | tf_op jit(solution)/shard_map/ppermute | solution.py:391
  168.8 2.1 %collective-permute-start.33 = (bf16[64,768]{1,0:T(8,128)(2,1)S(1)}, bf16[64,768]{1,0:T(8,128)(2,1)S(1)}, u32[]{:S(2)}, u32[]{:S(2)}) collective-permute-start(bf16[64,768]{1,0:T(8,128)(2,1)S(1)} %shard_map.273), channel_id=1, source_target_pairs={{0,64},{64,0},{1,65},{65,1},{2,66},{66,2},{3,67},{67,3},{4,68},{68... | collective-permute-start | bytes 294920 | tf_op jit(solution)/shard_map/ppermute | solution.py:391
  171.0 1.9 collective-permute-start.26
  173.9 2.5 %collective-permute-start.35 = (bf16[48,768]{1,0:T(8,128)(2,1)S(1)}, bf16[48,768]{1,0:T(8,128)(2,1)S(1)}, u32[]{:S(2)}, u32[]{:S(2)}) collective-permute-start(bf16[48,768]{1,0:T(8,128)(2,1)S(1)} %slice.105.b0), channel_id=1, source_target_pairs={{0,32},{16,48},{32,0},{48,16},{1,33},{17,49},{33,1},{49,17},{2,34}... | collective-permute-start | bytes 221192 | tf_op jit(solution)/shard_map/ppermute | solution.py:391
  176.5 2.4 %collective-permute-start.34 = (bf16[48,768]{1,0:T(8,128)(2,1)S(1)}, bf16[48,768]{1,0:T(8,128)(2,1)S(1)}, u32[]{:S(2)}, u32[]{:S(2)}) collective-permute-start(bf16[48,768]{1,0:T(8,128)(2,1)S(1)} %slice.105.b0), channel_id=1, source_target_pairs={{0,48},{16,0},{32,16},{48,32},{1,49},{17,1},{33,17},{49,33},{2,50}... | collective-permute-start | bytes 221192 | tf_op jit(solution)/shard_map/ppermute | solution.py:391
  182.6 3.2 %collective-permute-start.38 = (bf16[4,48,768]{2,1,0:T(8,128)(2,1)S(1)}, bf16[4,48,768]{2,1,0:T(8,128)(2,1)S(1)}, u32[]{:S(2)}, u32[]{:S(2)}) collective-permute-start(bf16[4,48,768]{2,1,0:T(8,128)(2,1)S(1)} %shard_map.274.after.p0), channel_id=1, source_target_pairs={{0,8},{4,12},{8,0},{12,4},{1,9},{5,13},{9,1},{13,5},{2,10},{6,14},... | collective-permute-start | bytes 884744 | tf_op jit(solution)/shard_map/ppermute | solution.py:391
  186.0 3.2 %collective-permute-start.42 = (f32[8,768]{1,0:T(8,128)S(1)}, f32[8,768]{1,0:T(8,128)S(1)}, u32[]{:S(2)}, u32[]{:S(2)}) collective-permute-start(f32[8,768]{1,0:T(8,128)S(1)} %slice_add_fusion), channel_id=1, source_target_pairs={{0,2},{2,0},{1,3},{3,1},{4,6},{6,4},{5,7},{7,5},{8,10},{10,8},{9,1... | collective-permute-start | bytes 73736 | tf_op jit(solution)/shard_map/ppermute | solution.py:391
  189.8 1.6 collective-permute-done.42
  193.3 1.7 copy-done.5
  195.0 2.3 %shard_map.276 = (f32[768,768]{1,0:T(8,128)}, f32[768,768]{1,0:T(8,128)}) custom-call(bf16[1536,768]{1,0:T(8,128)(2,1)S(1)} %copy-done.5, bf16[4,48,768]{2,1,0:T(8,128)(2,1)S(1)} %shard_map.274.after.p0), custom_call_target="tpu_custom_call" | custom-call | bytes 1024 | tf_op jit(solution)/shard_map/pallas_call | solution.py:376
  197.7 1.7 copy-done.6
  199.4 2.2 %shard_map.277 = (f32[576,768]{1,0:T(8,128)}, f32[192,768]{1,0:T(8,128)}) custom-call(s32[3]{0:T(128)S(1)} %copy-done.25, bf16[4,48,768]{2,1,0:T(8,128)(2,1)S(1)} %shard_map.274.after.p0, bf16[4,48,768]{2,1,0:T(8,128)(2,1)S(1)} %collective-permute-done.37.p1, bf16[4,48,768]{2,1,0:T(8,128)(2,1)S(1)} %collective-permute-done.38.p2, ...), custom_call_target="tpu_custom_call" | custom-call | bytes 1024 | tf_op jit(solution)/shard_map/pallas_call | solution.py:376
  (146 shorter events, 40.8 us)
Async XLA Ops:
  7.2 111.8 %reduce-scatter.2.cloned.1.call-start = ((), (), s32[]{:S(2)}) async-start(), calls=%async_computation.1 | async-start | bytes 2506752 | tf_op jit(solution)/shard_map/reduce_scatter | solution.py:440
  11.6 9.3 %collective-permute-start.3 = (bf16[256,384]{1,0:T(8,128)(2,1)}, bf16[256,384]{1,0:T(8,128)(2,1)S(1)}, u32[]{:S(2)}, u32[]{:S(2)}) collective-permute-start(bf16[256,384]{1,0:T(8,128)(2,1)} %get-tuple-element.54.refs_4_.refs_5_), channel_id=1, source_target_pairs={{0,64},{64,0},{1,65},{65,1},{2,66},{66,2},{3,67},{67,3},{4,68},{68... | collective-permute-start | bytes 589832 | tf_op jit(solution)/shard_map/ppermute | solution.py:391
  13.1 9.7 %collective-permute-start.6 = (bf16[256,384]{1,0:T(8,128)(2,1)}, bf16[256,384]{1,0:T(8,128)(2,1)S(1)}, u32[]{:S(2)}, u32[]{:S(2)}) collective-permute-start(bf16[256,384]{1,0:T(8,128)(2,1)} %get-tuple-element.54.refs_4_.refs_5_), channel_id=1, source_target_pairs={{0,16},{16,32},{32,48},{48,0},{1,17},{17,33},{33,49},{49,1},{2,18}... | collective-permute-start | bytes 589832 | tf_op jit(solution)/shard_map/ppermute | solution.py:391
  15.1 9.7 %collective-permute-start.2 = (bf16[256,384]{1,0:T(8,128)(2,1)}, bf16[256,384]{1,0:T(8,128)(2,1)S(1)}, u32[]{:S(2)}, u32[]{:S(2)}) collective-permute-start(bf16[256,384]{1,0:T(8,128)(2,1)} %get-tuple-element.53.refs_0_.refs_4_.refs_1_), channel_id=1, source_target_pairs={{0,4},{4,8},{8,12},{12,0},{1,5},{5,9},{9,13},{13,1},{2,6},{6,10},{... | collective-permute-start | bytes 589832 | tf_op jit(solution)/shard_map/ppermute | solution.py:391
  16.6 11.4 %collective-permute-start.1 = (bf16[256,384]{1,0:T(8,128)(2,1)}, bf16[256,384]{1,0:T(8,128)(2,1)S(1)}, u32[]{:S(2)}, u32[]{:S(2)}) collective-permute-start(bf16[256,384]{1,0:T(8,128)(2,1)} %get-tuple-element.53.refs_0_.refs_4_.refs_1_), channel_id=1, source_target_pairs={{0,8},{4,12},{8,0},{12,4},{1,9},{5,13},{9,1},{13,5},{2,10},{6,14},... | collective-permute-start | bytes 589832 | tf_op jit(solution)/shard_map/ppermute | solution.py:391
  19.5 8.5 %collective-permute-start = (bf16[256,384]{1,0:T(8,128)(2,1)}, bf16[256,384]{1,0:T(8,128)(2,1)S(1)}, u32[]{:S(2)}, u32[]{:S(2)}) collective-permute-start(bf16[256,384]{1,0:T(8,128)(2,1)} %get-tuple-element.53.refs_0_.refs_4_.refs_1_), channel_id=1, source_target_pairs={{0,12},{4,0},{8,4},{12,8},{1,13},{5,1},{9,5},{13,9},{2,14},{6,2},{... | collective-permute-start | bytes 589832 | tf_op jit(solution)/shard_map/ppermute | solution.py:391
  20.9 7.1 %collective-permute-start.9 = (bf16[256,384]{1,0:T(8,128)(2,1)S(1)}, bf16[256,384]{1,0:T(8,128)(2,1)S(1)}, u32[]{:S(2)}, u32[]{:S(2)}) collective-permute-start(bf16[256,384]{1,0:T(8,128)(2,1)S(1)} %collective-permute-done.3.refs_5_.refs_6_), channel_id=1, source_target_pairs={{0,16},{16,32},{32,48},{48,0},{1,17},{17,33},{33,49},{49,1},{2,18}... | collective-permute-start | bytes 589832 | tf_op jit(solution)/shard_map/ppermute | solution.py:391
  22.8 5.7 %collective-permute-start.5 = (bf16[256,384]{1,0:T(8,128)(2,1)S(1)}, bf16[256,384]{1,0:T(8,128)(2,1)S(1)}, u32[]{:S(2)}, u32[]{:S(2)}) collective-permute-start(bf16[256,384]{1,0:T(8,128)(2,1)S(1)} %collective-permute-done.3.refs_5_.refs_6_), channel_id=1, source_target_pairs={{0,48},{16,0},{32,16},{48,32},{1,49},{17,1},{33,17},{49,33},{2,50}... | collective-permute-start | bytes 589832 | tf_op jit(solution)/shard_map/ppermute | solution.py:391
  37.0 46.8 %copy-start.9 = (bf16[192,768]{1,0:T(8,128)(2,1)S(1)}, bf16[192,768]{1,0:T(8,128)(2,1)}, u32[]{:S(2)}) copy-start(bf16[192,768]{1,0:T(8,128)(2,1)} %wd.3) | copy-start | bytes 884740
  37.0 156.3 %all-gather.2.cloned.1.call-start = ((), (), s32[]{:S(2)}) async-start(), calls=%async_computation.2 | async-start | bytes 2506752 | tf_op jit(solution)/shard_map/all_gather | solution.py:493
  37.0 46.7 %copy-start.14 = (f32[256,768]{1,0:T(8,128)S(1)}, f32[256,768]{1,0:T(8,128)}, u32[]{:S(2)}) copy-start(f32[256,768]{1,0:T(8,128)} %copy-done.13) | copy-start | bytes 2359300
  37.0 7.7 %collective-permute-start.4 = (bf16[256,384]{1,0:T(8,128)(2,1)S(1)}, bf16[256,384]{1,0:T(8,128)(2,1)S(1)}, u32[]{:S(2)}, u32[]{:S(2)}) collective-permute-start(bf16[256,384]{1,0:T(8,128)(2,1)S(1)} %copy-done.10), channel_id=1, source_target_pairs={{0,48},{16,0},{32,16},{48,32},{1,49},{17,1},{33,17},{49,33},{2,50}... | collective-permute-start | bytes 589832 | tf_op jit(solution)/shard_map/ppermute | solution.py:391
  39.7 6.9 %collective-permute-start.7 = (bf16[256,384]{1,0:T(8,128)(2,1)S(1)}, bf16[256,384]{1,0:T(8,128)(2,1)S(1)}, u32[]{:S(2)}, u32[]{:S(2)}) collective-permute-start(bf16[256,384]{1,0:T(8,128)(2,1)S(1)} %collective-permute-done.6.refs_10_.refs_1_.refs_7_), channel_id=1, source_target_pairs={{0,16},{16,32},{32,48},{48,0},{1,17},{17,33},{33,49},{49,1},{2,18}... | collective-permute-start | bytes 589832 | tf_op jit(solution)/shard_map/ppermute | solution.py:391
  39.7 7.3 %collective-permute-start.8 = (bf16[256,384]{1,0:T(8,128)(2,1)S(1)}, bf16[256,384]{1,0:T(8,128)(2,1)S(1)}, u32[]{:S(2)}, u32[]{:S(2)}) collective-permute-start(bf16[256,384]{1,0:T(8,128)(2,1)S(1)} %collective-permute-done.5.refs_7_.refs_0_.refs_6_), channel_id=1, source_target_pairs={{0,48},{16,0},{32,16},{48,32},{1,49},{17,1},{33,17},{49,33},{2,50}... | collective-permute-start | bytes 589832 | tf_op jit(solution)/shard_map/ppermute | solution.py:391
  60.0 23.7 %collective-permute-start.13 = (bf16[192,256]{1,0:T(8,128)(2,1)S(1)}, bf16[192,256]{1,0:T(8,128)(2,1)S(1)}, u32[]{:S(2)}, u32[]{:S(2)}) collective-permute-start(bf16[192,256]{1,0:T(8,128)(2,1)S(1)} %get-tuple-element.57), channel_id=1, source_target_pairs={{0,4},{4,8},{8,12},{12,0},{1,5},{5,9},{9,13},{13,1},{2,6},{6,10},{... | collective-permute-start | bytes 294920 | tf_op jit(solution)/shard_map/ppermute | solution.py:391
  61.3 22.4 %collective-permute-start.14 = (bf16[192,256]{1,0:T(8,128)(2,1)S(1)}, bf16[192,256]{1,0:T(8,128)(2,1)S(1)}, u32[]{:S(2)}, u32[]{:S(2)}) collective-permute-start(bf16[192,256]{1,0:T(8,128)(2,1)S(1)} %get-tuple-element.58), channel_id=1, source_target_pairs={{0,8},{4,12},{8,0},{12,4},{1,9},{5,13},{9,1},{13,5},{2,10},{6,14},... | collective-permute-start | bytes 294920 | tf_op jit(solution)/shard_map/ppermute | solution.py:391
  64.1 19.6 %collective-permute-start.15 = (bf16[192,256]{1,0:T(8,128)(2,1)S(1)}, bf16[192,256]{1,0:T(8,128)(2,1)S(1)}, u32[]{:S(2)}, u32[]{:S(2)}) collective-permute-start(bf16[192,256]{1,0:T(8,128)(2,1)S(1)} %get-tuple-element.59), channel_id=1, source_target_pairs={{0,12},{4,0},{8,4},{12,8},{1,13},{5,1},{9,5},{13,9},{2,14},{6,2},{... | collective-permute-start | bytes 294920 | tf_op jit(solution)/shard_map/ppermute | solution.py:391
  65.1 5.2 %collective-permute-start.12 = (f32[4,8,256]{2,1,0:T(8,128)S(1)}, f32[4,8,256]{2,1,0:T(8,128)S(1)}, u32[]{:S(2)}, u32[]{:S(2)}) collective-permute-start(f32[4,8,256]{2,1,0:T(8,128)S(1)} %get-tuple-element.55.s0.refs_0_), channel_id=1, source_target_pairs={{0,4},{4,8},{8,12},{12,0},{1,5},{5,9},{9,13},{13,1},{2,6},{6,10},{... | collective-permute-start | bytes 98312 | tf_op jit(solution)/shard_map/ppermute | solution.py:391
  66.1 5.4 %collective-permute-start.11 = (f32[4,8,256]{2,1,0:T(8,128)S(1)}, f32[4,8,256]{2,1,0:T(8,128)S(1)}, u32[]{:S(2)}, u32[]{:S(2)}) collective-permute-start(f32[4,8,256]{2,1,0:T(8,128)S(1)} %get-tuple-element.55.s0.refs_0_), channel_id=1, source_target_pairs={{0,8},{4,12},{8,0},{12,4},{1,9},{5,13},{9,1},{13,5},{2,10},{6,14},... | collective-permute-start | bytes 98312 | tf_op jit(solution)/shard_map/ppermute | solution.py:391
  70.3 4.0 %collective-permute-start.10 = (f32[4,8,256]{2,1,0:T(8,128)S(1)}, f32[4,8,256]{2,1,0:T(8,128)S(1)}, u32[]{:S(2)}, u32[]{:S(2)}) collective-permute-start(f32[4,8,256]{2,1,0:T(8,128)S(1)} %get-tuple-element.55.s0.refs_0_), channel_id=1, source_target_pairs={{0,12},{4,0},{8,4},{12,8},{1,13},{5,1},{9,5},{13,9},{2,14},{6,2},{... | collective-permute-start | bytes 98312 | tf_op jit(solution)/shard_map/ppermute | solution.py:391
  81.1 20.0 %collective-permute-start.18 = (bf16[2,256,384]{2,1,0:T(8,128)(2,1)S(1)}, bf16[2,256,384]{2,1,0:T(8,128)(2,1)S(1)}, u32[]{:S(2)}, u32[]{:S(2)}) collective-permute-start(bf16[2,256,384]{2,1,0:T(8,128)(2,1)S(1)} %get-tuple-element.67), channel_id=1, source_target_pairs={{0,32},{16,48},{32,0},{48,16},{1,33},{17,49},{33,1},{49,17},{2,34}... | collective-permute-start | bytes 1179656 | tf_op jit(solution)/shard_map/ppermute | solution.py:391
  84.8 16.3 %collective-permute-start.16 = (bf16[256,768]{1,0:T(8,128)(2,1)S(1)}, bf16[256,768]{1,0:T(8,128)(2,1)S(1)}, u32[]{:S(2)}, u32[]{:S(2)}) collective-permute-start(bf16[256,768]{1,0:T(8,128)(2,1)S(1)} %get-tuple-element.62), channel_id=1, source_target_pairs={{0,1},{1,0},{2,3},{3,2},{4,5},{5,4},{6,7},{7,6},{8,9},{9,8},{10,11... | collective-permute-start | bytes 1179656 | tf_op jit(solution)/shard_map/ppermute | solution.py:391
  97.8 14.6 %collective-permute-start.22 = (bf16[2,256,384]{2,1,0:T(8,128)(2,1)S(1)}, bf16[2,256,384]{2,1,0:T(8,128)(2,1)S(1)}, u32[]{:S(2)}, u32[]{:S(2)}) collective-permute-start(bf16[2,256,384]{2,1,0:T(8,128)(2,1)S(1)} %get-tuple-element.73), channel_id=1, source_target_pairs={{0,16},{16,32},{32,48},{48,0},{1,17},{17,33},{33,49},{49,1},{2,18}... | collective-permute-start | bytes 1179656 | tf_op jit(solution)/shard_map/ppermute | solution.py:391
  99.7 12.8 %collective-permute-start.23 = (bf16[2,256,384]{2,1,0:T(8,128)(2,1)S(1)}, bf16[2,256,384]{2,1,0:T(8,128)(2,1)S(1)}, u32[]{:S(2)}, u32[]{:S(2)}) collective-permute-start(bf16[2,256,384]{2,1,0:T(8,128)(2,1)S(1)} %get-tuple-element.74), channel_id=1, source_target_pairs={{0,48},{16,0},{32,16},{48,32},{1,49},{17,1},{33,17},{49,33},{2,50}... | collective-permute-start | bytes 1179656 | tf_op jit(solution)/shard_map/ppermute | solution.py:391
  108.0 24.8 %copy-start.1 = (bf16[256,768]{1,0:T(8,128)(2,1)S(1)}, bf16[256,768]{1,0:T(8,128)(2,1)}, u32[]{:S(2)}) copy-start(bf16[256,768]{1,0:T(8,128)(2,1)} %cot.7) | copy-start | bytes 1179652
  108.1 9.6 %collective-permute-start.19 = (bf16[192,256]{1,0:T(8,128)(2,1)S(1)}, bf16[192,256]{1,0:T(8,128)(2,1)S(1)}, u32[]{:S(2)}, u32[]{:S(2)}) collective-permute-start(bf16[192,256]{1,0:T(8,128)(2,1)S(1)} %get-tuple-element.69), channel_id=1, source_target_pairs={{0,4},{4,8},{8,12},{12,0},{1,5},{5,9},{9,13},{13,1},{2,6},{6,10},{... | collective-permute-start | bytes 294920 | tf_op jit(solution)/shard_map/ppermute | solution.py:391
  108.4 9.3 %collective-permute-start.20 = (bf16[192,256]{1,0:T(8,128)(2,1)S(1)}, bf16[192,256]{1,0:T(8,128)(2,1)S(1)}, u32[]{:S(2)}, u32[]{:S(2)}) collective-permute-start(bf16[192,256]{1,0:T(8,128)(2,1)S(1)} %get-tuple-element.70), channel_id=1, source_target_pairs={{0,8},{4,12},{8,0},{12,4},{1,9},{5,13},{9,1},{13,5},{2,10},{6,14},... | collective-permute-start | bytes 294920 | tf_op jit(solution)/shard_map/ppermute | solution.py:391
  111.0 6.7 %collective-permute-start.21 = (bf16[192,256]{1,0:T(8,128)(2,1)S(1)}, bf16[192,256]{1,0:T(8,128)(2,1)S(1)}, u32[]{:S(2)}, u32[]{:S(2)}) collective-permute-start(bf16[192,256]{1,0:T(8,128)(2,1)S(1)} %get-tuple-element.71), channel_id=1, source_target_pairs={{0,12},{4,0},{8,4},{12,8},{1,13},{5,1},{9,5},{13,9},{2,14},{6,2},{... | collective-permute-start | bytes 294920 | tf_op jit(solution)/shard_map/ppermute | solution.py:391
  119.9 5.2 %collective-permute-start.40 = (bf16[96,768]{1,0:T(8,128)(2,1)S(1)}, bf16[96,768]{1,0:T(8,128)(2,1)S(1)}, u32[]{:S(2)}, u32[]{:S(2)}) collective-permute-start(bf16[96,768]{1,0:T(8,128)(2,1)S(1)} %shard_map.275), channel_id=1, source_target_pairs={{0,64},{64,0},{1,65},{65,1},{2,66},{66,2},{3,67},{67,3},{4,68},{68... | collective-permute-start | bytes 442376 | tf_op jit(solution)/shard_map/ppermute | solution.py:391
  125.8 7.0 %collective-permute-start.24 = (bf16[256,384]{1,0:T(8,128)(2,1)S(1)}, bf16[256,384]{1,0:T(8,128)(2,1)S(1)}, u32[]{:S(2)}, u32[]{:S(2)}) collective-permute-start(bf16[256,384]{1,0:T(8,128)(2,1)S(1)} %get-tuple-element.98.refs_0_), channel_id=1, source_target_pairs={{0,64},{64,0},{1,65},{65,1},{2,66},{66,2},{3,67},{67,3},{4,68},{68... | collective-permute-start | bytes 589832 | tf_op jit(solution)/shard_map/ppermute | solution.py:391
  128.0 34.0 %collective-permute-start.17 = (bf16[256,768]{1,0:T(8,128)(2,1)S(1)}, bf16[256,768]{1,0:T(8,128)(2,1)S(1)}, u32[]{:S(2)}, u32[]{:S(2)}) collective-permute-start(bf16[256,768]{1,0:T(8,128)(2,1)S(1)} %add_convert_fusion.2), channel_id=1, source_target_pairs={{0,2},{2,0},{1,3},{3,1},{4,6},{6,4},{5,7},{7,5},{8,10},{10,8},{9,1... | collective-permute-start | bytes 1179656 | tf_op jit(solution)/shard_map/ppermute | solution.py:391
  140.2 12.1 %collective-permute-start.27 = (bf16[208,768]{1,0:T(8,128)(2,1)S(1)}, bf16[208,768]{1,0:T(8,128)(2,1)S(1)}, u32[]{:S(2)}, u32[]{:S(2)}) collective-permute-start(bf16[208,768]{1,0:T(8,128)(2,1)S(1)} %get-tuple-element.80), channel_id=1, source_target_pairs={{0,4},{4,8},{8,12},{12,0},{1,5},{5,9},{9,13},{13,1},{2,6},{6,10},{... | collective-permute-start | bytes 958472 | tf_op jit(solution)/shard_map/ppermute | solution.py:391
  141.8 14.0 %collective-permute-start.28 = (bf16[208,768]{1,0:T(8,128)(2,1)S(1)}, bf16[208,768]{1,0:T(8,128)(2,1)S(1)}, u32[]{:S(2)}, u32[]{:S(2)}) collective-permute-start(bf16[208,768]{1,0:T(8,128)(2,1)S(1)} %get-tuple-element.81), channel_id=1, source_target_pairs={{0,8},{4,12},{8,0},{12,4},{1,9},{5,13},{9,1},{13,5},{2,10},{6,14},... | collective-permute-start | bytes 958472 | tf_op jit(solution)/shard_map/ppermute | solution.py:391
  145.6 10.3 %collective-permute-start.29 = (bf16[208,768]{1,0:T(8,128)(2,1)S(1)}, bf16[208,768]{1,0:T(8,128)(2,1)S(1)}, u32[]{:S(2)}, u32[]{:S(2)}) collective-permute-start(bf16[208,768]{1,0:T(8,128)(2,1)S(1)} %get-tuple-element.82), channel_id=1, source_target_pairs={{0,12},{4,0},{8,4},{12,8},{1,13},{5,1},{9,5},{13,9},{2,14},{6,2},{... | collective-permute-start | bytes 958472 | tf_op jit(solution)/shard_map/ppermute | solution.py:391
  145.6 25.4 %collective-permute-start.25 = (bf16[256,768]{1,0:T(8,128)(2,1)S(1)}, bf16[256,768]{1,0:T(8,128)(2,1)S(1)}, u32[]{:S(2)}, u32[]{:S(2)}) collective-permute-start(bf16[256,768]{1,0:T(8,128)(2,1)S(1)} %get-tuple-element.78), channel_id=1, source_target_pairs={{0,1},{1,0},{2,3},{3,2},{4,5},{5,4},{6,7},{7,6},{8,9},{9,8},{10,11... | collective-permute-start | bytes 1179656 | tf_op jit(solution)/shard_map/ppermute | solution.py:391
  156.8 6.2 %collective-permute-start.30 = (bf16[64,768]{1,0:T(8,128)(2,1)S(1)}, bf16[64,768]{1,0:T(8,128)(2,1)S(1)}, u32[]{:S(2)}, u32[]{:S(2)}) collective-permute-start(bf16[64,768]{1,0:T(8,128)(2,1)S(1)} %get-tuple-element.84), channel_id=1, source_target_pairs={{0,16},{16,32},{32,48},{48,0},{1,17},{17,33},{33,49},{49,1},{2,18}... | collective-permute-start | bytes 294920 | tf_op jit(solution)/shard_map/ppermute | solution.py:391
  157.9 6.3 %collective-permute-start.31 = (bf16[64,768]{1,0:T(8,128)(2,1)S(1)}, bf16[64,768]{1,0:T(8,128)(2,1)S(1)}, u32[]{:S(2)}, u32[]{:S(2)}) collective-permute-start(bf16[64,768]{1,0:T(8,128)(2,1)S(1)} %get-tuple-element.85), channel_id=1, source_target_pairs={{0,32},{16,48},{32,0},{48,16},{1,33},{17,49},{33,1},{49,17},{2,34}... | collective-permute-start | bytes 294920 | tf_op jit(solution)/shard_map/ppermute | solution.py:391
  160.4 7.8 %collective-permute-start.32 = (bf16[64,768]{1,0:T(8,128)(2,1)S(1)}, bf16[64,768]{1,0:T(8,128)(2,1)S(1)}, u32[]{:S(2)}, u32[]{:S(2)}) collective-permute-start(bf16[64,768]{1,0:T(8,128)(2,1)S(1)} %get-tuple-element.86), channel_id=1, source_target_pairs={{0,48},{16,0},{32,16},{48,32},{1,49},{17,1},{33,17},{49,33},{2,50}... | collective-permute-start | bytes 294920 | tf_op jit(solution)/shard_map/ppermute | solution.py:391
  168.8 4.7 %collective-permute-start.33 = (bf16[64,768]{1,0:T(8,128)(2,1)S(1)}, bf16[64,768]{1,0:T(8,128)(2,1)S(1)}, u32[]{:S(2)}, u32[]{:S(2)}) collective-permute-start(bf16[64,768]{1,0:T(8,128)(2,1)S(1)} %shard_map.273), channel_id=1, source_target_pairs={{0,64},{64,0},{1,65},{65,1},{2,66},{66,2},{3,67},{67,3},{4,68},{68... | collective-permute-start | bytes 294920 | tf_op jit(solution)/shard_map/ppermute | solution.py:391
  171.0 21.0 %collective-permute-start.26 = (bf16[256,768]{1,0:T(8,128)(2,1)S(1)}, bf16[256,768]{1,0:T(8,128)(2,1)S(1)}, u32[]{:S(2)}, u32[]{:S(2)}) collective-permute-start(bf16[256,768]{1,0:T(8,128)(2,1)S(1)} %add_convert_fusion.e0), channel_id=1, source_target_pairs={{0,2},{2,0},{1,3},{3,1},{4,6},{6,4},{5,7},{7,5},{8,10},{10,8},{9,1... | collective-permute-start | bytes 1179656 | tf_op jit(solution)/shard_map/ppermute | solution.py:391
  173.6 6.4 %collective-permute-start.36 = (bf16[48,768]{1,0:T(8,128)(2,1)S(1)}, bf16[48,768]{1,0:T(8,128)(2,1)S(1)}, u32[]{:S(2)}, u32[]{:S(2)}) collective-permute-start(bf16[48,768]{1,0:T(8,128)(2,1)S(1)} %slice.105.b0), channel_id=1, source_target_pairs={{0,16},{16,32},{32,48},{48,0},{1,17},{17,33},{33,49},{49,1},{2,18}... | collective-permute-start | bytes 221192 | tf_op jit(solution)/shard_map/ppermute | solution.py:391
  173.9 6.1 %collective-permute-start.35 = (bf16[48,768]{1,0:T(8,128)(2,1)S(1)}, bf16[48,768]{1,0:T(8,128)(2,1)S(1)}, u32[]{:S(2)}, u32[]{:S(2)}) collective-permute-start(bf16[48,768]{1,0:T(8,128)(2,1)S(1)} %slice.105.b0), channel_id=1, source_target_pairs={{0,32},{16,48},{32,0},{48,16},{1,33},{17,49},{33,1},{49,17},{2,34}... | collective-permute-start | bytes 221192 | tf_op jit(solution)/shard_map/ppermute | solution.py:391
  176.5 4.4 %collective-permute-start.34 = (bf16[48,768]{1,0:T(8,128)(2,1)S(1)}, bf16[48,768]{1,0:T(8,128)(2,1)S(1)}, u32[]{:S(2)}, u32[]{:S(2)}) collective-permute-start(bf16[48,768]{1,0:T(8,128)(2,1)S(1)} %slice.105.b0), channel_id=1, source_target_pairs={{0,48},{16,0},{32,16},{48,32},{1,49},{17,1},{33,17},{49,33},{2,50}... | collective-permute-start | bytes 221192 | tf_op jit(solution)/shard_map/ppermute | solution.py:391
  178.9 7.1 %collective-permute-start.41 = (f32[8,768]{1,0:T(8,128)S(1)}, f32[8,768]{1,0:T(8,128)S(1)}, u32[]{:S(2)}, u32[]{:S(2)}) collective-permute-start(f32[8,768]{1,0:T(8,128)S(1)} %slice.83), channel_id=1, source_target_pairs={{0,1},{1,0},{2,3},{3,2},{4,5},{5,4},{6,7},{7,6},{8,9},{9,8},{10,11... | collective-permute-start | bytes 73736 | tf_op jit(solution)/shard_map/ppermute | solution.py:391
  181.4 15.9 %collective-permute-start.39 = (bf16[4,48,768]{2,1,0:T(8,128)(2,1)S(1)}, bf16[4,48,768]{2,1,0:T(8,128)(2,1)S(1)}, u32[]{:S(2)}, u32[]{:S(2)}) collective-permute-start(bf16[4,48,768]{2,1,0:T(8,128)(2,1)S(1)} %shard_map.274.after.p0), channel_id=1, source_target_pairs={{0,4},{4,8},{8,12},{12,0},{1,5},{5,9},{9,13},{13,1},{2,6},{6,10},{... | collective-permute-start | bytes 884744 | tf_op jit(solution)/shard_map/ppermute | solution.py:391
  182.6 14.7 %collective-permute-start.38 = (bf16[4,48,768]{2,1,0:T(8,128)(2,1)S(1)}, bf16[4,48,768]{2,1,0:T(8,128)(2,1)S(1)}, u32[]{:S(2)}, u32[]{:S(2)}) collective-permute-start(bf16[4,48,768]{2,1,0:T(8,128)(2,1)S(1)} %shard_map.274.after.p0), channel_id=1, source_target_pairs={{0,8},{4,12},{8,0},{12,4},{1,9},{5,13},{9,1},{13,5},{2,10},{6,14},... | collective-permute-start | bytes 884744 | tf_op jit(solution)/shard_map/ppermute | solution.py:391
  185.8 11.9 %collective-permute-start.37 = (bf16[4,48,768]{2,1,0:T(8,128)(2,1)S(1)}, bf16[4,48,768]{2,1,0:T(8,128)(2,1)S(1)}, u32[]{:S(2)}, u32[]{:S(2)}) collective-permute-start(bf16[4,48,768]{2,1,0:T(8,128)(2,1)S(1)} %shard_map.274.after.p0), channel_id=1, source_target_pairs={{0,12},{4,0},{8,4},{12,8},{1,13},{5,1},{9,5},{13,9},{2,14},{6,2},{... | collective-permute-start | bytes 884744 | tf_op jit(solution)/shard_map/ppermute | solution.py:391
  186.0 5.4 %collective-permute-start.42 = (f32[8,768]{1,0:T(8,128)S(1)}, f32[8,768]{1,0:T(8,128)S(1)}, u32[]{:S(2)}, u32[]{:S(2)}) collective-permute-start(f32[8,768]{1,0:T(8,128)S(1)} %slice_add_fusion), channel_id=1, source_target_pairs={{0,2},{2,0},{1,3},{3,1},{4,6},{6,4},{5,7},{7,5},{8,10},{10,8},{9,1... | collective-permute-start | bytes 73736 | tf_op jit(solution)/shard_map/ppermute | solution.py:391
  (33 other events, 313.0 us)
Sparse Core Ops, SparseCore 0:
  37.1 81.8 reduce-scatter.1
  125.9 51.6 all-gather.1

commit v4 on v2

--- a/solution.py
+++ b/solution.py
@@ -62,15 +62,6 @@
     return ref[...].reshape(1, -1)
 
 
-def keep_kernel(x, after, out):
-    out[...] = x[...]
-
-
-def widen_kernel(x, after, up, down):
-    up[...] = x[0:768, :].astype(F32)
-    down[...] = x[768:1536, :].astype(F32)
-
-
 def normed(tokens):
     values = tokens.astype(F32)
     centred = values - jnp.mean(values, axis=-1, keepdims=True)
@@ -79,12 +70,12 @@
 
 
 def front_kernel(
-    coords, order, table, tok, cot, wqkv, wd, ga, sa, gm, sm, bqkv, qdo, kv, lna, lnm
+    coords, order, table, tok, cot, wqkv, wd, ga, sa, gm, sm, bqkv, wu, bu, wdn,
+    qdo, kv, lna, gw, small, part, d_ln,
 ):
     xhat, _ = normed(tok[...])
     ln = (xhat * row(ga) + row(sa)).astype(BF)
     lna[...] = ln
-    lnm[...] = (xhat * row(gm) + row(sm)).astype(BF)
     joined = mm_nt(ln, wqkv[...]) + row(bqkv)
     cosine, left_sine, right_sine = spin_tables(coords, order, table)
     half = lax.broadcasted_iota(jnp.int32, (256, 128), 1) < HEAD
@@ -109,14 +100,13 @@
     ).astype(BF)
     kv[...] = jnp.concatenate([pieces[i] for i in (1, 4, 7, 2, 5, 8)], axis=1).astype(BF)
 
-
-def mlp_kernel(ln, cot, wu, bu, wdn, after, gw, small, part, d_ln):
-    up = mm(ln[...], wu[...]) + row(bu)
+    ln = (xhat * row(gm) + row(sm)).astype(BF)
+    up = mm(ln, wu[...]) + row(bu)
     phi = 0.5 * (1.0 + lax.erf(up * math.sqrt(0.5)))
     hid = (up * phi).astype(BF)
     slope = phi + up * (jnp.exp(up * up * -0.5) * (1.0 / math.sqrt(2.0 * math.pi)))
     d_up = (mm_nt(cot[...], wdn[...]) * slope).astype(BF)
-    gw[0:768, :] = mm_tn(ln[...], d_up).astype(BF)
+    gw[0:768, :] = mm_tn(ln, d_up).astype(BF)
     gw[768:1536, :] = mm_tn(hid, cot[...]).astype(BF)
     part[...] = mm(hid, wdn[...])
     d_ln[...] = mm_nt(d_up, wu[...])
@@ -194,9 +184,8 @@
         ref[...] = os[j]
 
 
-def merge_kernel(s0, s1, s2, s3, o0, o1, o2, o3, wd, part, att, branch):
-    stats = [ref[-step % 4] for step, ref in enumerate((s0, s1, s2, s3))]
-    outs = [o0, o3, o2, o1]
+def merged(stat_refs, out_refs):
+    stats = [ref[-step % 4] for step, ref in enumerate(stat_refs)]
     rows = []
     for h in range(HEADS):
         logs = [s[h : h + 1, :] for s in stats]
@@ -207,13 +196,11 @@
             jnp.add,
             [
                 share * ref[HEAD * h : HEAD * h + HEAD, :].astype(F32)
-                for share, ref in zip(shares, outs, strict=True)
+                for share, ref in zip(shares, out_refs, strict=True)
             ],
         )
         rows.append(mixed / total)
-    att_low = jnp.concatenate(rows, axis=0).T.astype(BF)
-    att[...] = att_low
-    branch[...] = (mm(att_low, wd[...]) + part[...]).astype(BF)
+    return jnp.concatenate(rows, axis=0).T.astype(BF)
 
 
 def backward_kernel(tiles, first, last, unread, coords, order, *refs):
@@ -228,6 +215,7 @@
     stats = take(4 if first else 1)
     queries, keys = take(4), take(n)
     d_before = None if first else take(1)[0]
+    passed = take(3 if last else 0)
     take(unread)
     if first:
         (st,) = take(1)
@@ -283,17 +271,40 @@
         ref[...] = dks[2 * i : 2 * i + 2]
     if last:
         for j, ref in enumerate(d_queries):
-            ref[...] = (dqs[j] * SCALE).astype(BF)
+            ref[0:192, :] = (dqs[j] * SCALE).astype(BF)
+        for source, ref in zip(passed, d_queries[1:], strict=True):
+            ref[192:384, :] = source[...]
+
+
+def key_sum_kernel(own, far, near, near_too, mlp, send, kept):
+    def total(a):
+        parts = [ref[a].astype(F32) for ref in (own, far, near, near_too)]
+        return functools.reduce(jnp.add, parts).astype(BF)
+
+    kept[...] = total(0)
+    send[0:256, :] = total(1)
+    send[256:352, :] = mlp[:, 0:384]
+    send[352:448, :] = mlp[:, 384:768]
 
 
 def tail_kernel(
     coords, order, table, tok, cot, lna, wqkv, ga, gm, dq0, dq1, dq2, dq3, dkv0, dkv1,
-    att, d_ln_mlp, small_in, g0, g1, g2, g3, upstream, grads,
+    s0, s1, s2, s3, o0, wd, part, d_ln_mlp, small_in, mlp, g0, g1, g2, g3, upstream, mlp_sum, grads,
 ):
+    outs = [o0] + [ref.at[192:384] for ref in (dq3, dq2, dq1)]
+    att = merged((s0, s1, s2, s3), outs)
+    upstream[256:512, :] = (mm(att, wd[...]) + part[...]).astype(BF)
     d_query = (
-        dq0[...].astype(F32) + dq1[...].astype(F32) + dq2[...].astype(F32) + dq3[...].astype(F32)
+        dq0[...].astype(F32)
+        + dq1[0:192, :].astype(F32)
+        + dq2[0:192, :].astype(F32)
+        + dq3[0:192, :].astype(F32)
     ).T
-    d_kv = dkv0[...].astype(F32) + dkv1[...].astype(F32)
+    d_kv = dkv0[...].astype(F32) + dkv1[0:256, :].astype(F32)
+    for half in range(2):
+        lanes = slice(384 * half, 384 * half + 384)
+        other = dkv1[256 + 96 * half : 352 + 96 * half, :]
+        mlp_sum[:, lanes] = (mlp[:, lanes].astype(F32) + other.astype(F32)).astype(BF)
     both = jnp.concatenate([d_query, d_kv[:, :192]], axis=1)
     cosine, left_sine, right_sine = spin_tables(coords, order, table)
     pieces = []
@@ -312,13 +323,13 @@
     turned = mm_tn(d_joined, lna[...]).astype(BF)
     for piece in range(3):
         grads[piece] = turned[192 * piece : 192 * piece + 192, :]
-    grads[3] = mm_tn(att[...], cot[...]).astype(BF)
+    grads[3] = mm_tn(att, cot[...]).astype(BF)
     for slot, ref in enumerate((g0, g1, g2, g3)):
         ref[0:192, :] = grads[(coords[2] + slot) % 4]
     d_attn = mm(d_joined, wqkv[...])
     d_mlp = d_ln_mlp[...]
     xhat, _ = normed(tok[...])
-    upstream[...] = (d_attn * row(ga) + d_mlp * row(gm)).astype(BF)
+    upstream[0:256, :] = (d_attn * row(ga) + d_mlp * row(gm)).astype(BF)
     sums = [
         jnp.sum(v, axis=0, keepdims=True) for v in (d_attn * xhat, d_attn, d_mlp * xhat, d_mlp)
     ]
@@ -346,9 +357,11 @@
     out[...] = ((order[0] + order[1]) + (order[2] + order[3])).astype(BF)
 
 
-def token_kernel(tok, cot, e0, e1, out):
+def token_kernel(tok, cot, e0, e1, b_dense, b_down, out, output):
+    branch = e0[256:512, :].astype(F32) + e1[256:512, :].astype(F32)
+    output[...] = (tok[...].astype(F32) + branch + row(b_dense) + row(b_down)).astype(BF)
     xhat, rstd = normed(tok[...])
-    e = e0[...].astype(F32) + e1[...].astype(F32)
+    e = e0[0:256, :].astype(F32) + e1[0:256, :].astype(F32)
     inner = e - jnp.mean(e, axis=-1, keepdims=True)
     inner = inner - xhat * jnp.mean(e * xhat, axis=-1, keepdims=True)
     out[...] = (cot[...].astype(F32) + rstd * inner).astype(BF)
@@ -359,7 +372,9 @@
         out[(coords[1] + slot) % 4] = ref[...]
 
 
-def assemble_kernel(coords, p0, p1, p2, p3, gq, gd, whole):
+def assemble_kernel(coords, p0, p1, p2, p3, mlp, gq, gd, gu, gdn, whole):
+    gu[...] = mlp[0:768, :].astype(F32)
+    gdn[...] = mlp[768:1536, :].astype(F32)
     for slot, ref in enumerate((p0, p1, p2, p3)):
         whole[(coords[2] + slot) % 4] = ref[...].astype(F32)
     for block in range(12):
@@ -415,28 +430,22 @@
     table = jnp.asarray(lane_table())
     w_turned = w_qkv.T
 
-    qdo, kv, ln_attn, ln_mlp = call(
+    qdo, kv, ln_attn, grads_mlp, small_mlp, part_mlp, d_ln_mlp = call(
         front_kernel,
-        [((256, 384), BF), ((256, 384), BF), ((256, 768), BF), ((256, 768), BF)],
+        [((256, 384), BF), ((256, 384), BF), ((256, 768), BF), ((1536, 768), BF),
+         ((8, 768), F32), ((256, 768), F32), ((256, 768), F32)],
         (coords, block_order, table, tokens, cotangent, w_turned, w_dense,
-         gain_attn, shift_attn, gain_mlp, shift_mlp, b_qkv),
+         gain_attn, shift_attn, gain_mlp, shift_mlp, b_qkv, w_up, b_up, w_down),
         2,
         mib=60,
     )
+    grads_mlp = lax.psum_scatter(grads_mlp, ("z", "y"), scatter_dimension=0, tiled=True)
     kv_x = hop(kv, "xl", 1)
     down, up = hop(kv, "z", 1), hop(kv, "z", -1)
     down_x, up_x = hop(kv_x, "z", 1), hop(kv_x, "z", -1)
     kvs = [kv, kv_x, up, up_x, hop(down, "z", 1), hop(up_x, "z", -1), down, down_x]
     qdos = [qdo] + [hop(qdo, "y", -j) for j in (1, 2, 3)]
 
-    grads_mlp, small_mlp, part_mlp, d_ln_mlp = call(
-        mlp_kernel,
-        [((1536, 768), BF), ((8, 768), F32), ((256, 768), F32), ((256, 768), F32)],
-        (ln_mlp, cotangent, w_up, b_up, w_down, kv_x),
-        0,
-        unread=1,
-    )
-    grads_mlp = lax.psum_scatter(grads_mlp, ("z", "y"), scatter_dimension=0, tiled=True)
     *outs, stats = call(
         forward_kernel,
         [((192, 256), BF)] * 4 + [((4, 8, 256), F32)],
@@ -445,22 +454,11 @@
         scratch=[pltpu.VMEM((4, 256, 384), BF), pltpu.VMEM((4, 192, 256), BF)],
     )
     stats_all = [stats] + [hop(stats, "y", -j) for j in (1, 2, 3)]
-    outs = [outs[0]] + [hop(outs[j], "y", j) for j in (1, 2, 3)]
-    att, branch = call(
-        merge_kernel,
-        [((256, 192), BF), ((256, 768), BF)],
-        (*stats_all, *outs, w_dense, part_mlp),
-        0,
-    )
-    branch = add(branch, hop(branch, "c", 1)).astype(BF)
-    branch = add(branch, hop(branch, "xh", 1))
-    output = (tokens.astype(F32) + branch + b_dense + b_down).astype(BF)
-
     def backward(tiles, stats_in, before, last, after=()):
         first = before is None
         n = len(tiles)
         kept = [((4, 8, 256), F32)] if first else []
-        d_out = [((192, 256), BF)] * 4 if last else [((4, 192, 256), F32)]
+        d_out = [((192, 256), BF)] + [((384, 256), BF)] * 3 if last else [((4, 192, 256), F32)]
         scratch = [pltpu.VMEM((n, 256, 384), BF)] * 2
         if last:
             scratch.append(pltpu.VMEM((4, 192, 256), F32))
@@ -469,6 +467,7 @@
             kept + [((2, 256, 384), BF)] * (n // 2) + d_out,
             (coords, block_order, *stats_in, *qdos, *[kvs[t] for t in tiles])
             + (() if first else (before,))
+            + (tuple(outs[1:]) if last else ())
             + tuple(after),
             2,
             unread=len(after),
@@ -480,22 +479,22 @@
     d_up, d_down, d_q = backward((2, 3, 6, 7), [whole], d_q, False)
     near = [hop(d_up, "z", 1), hop(d_down, "z", -1)]
     d_kv, *d_qs = backward((0, 1), [whole], d_q, True, (far,))
-    (grads_mlp,) = call(
-        keep_kernel, [(grads_mlp.shape, BF)], (grads_mlp, d_kv), 0, unread=1
-    )
-    grads_mlp = add(grads_mlp, hop(grads_mlp, "xl", 1)).astype(BF)
-    grads_mlp = lax.all_gather(grads_mlp, ("z", "y"), axis=0, tiled=True)
     d_queries = [d_qs[0]] + [hop(d_qs[j], "y", j) for j in (1, 2, 3)]
-    d_kv_other = hop(add(d_kv[1], far[1], near[0][1], near[1][1]).astype(BF), "xl", 1)
-    d_kv_own = add(d_kv[0], far[0], near[0][0], near[1][0]).astype(BF)
-    *pieces, upstream = call(
+    d_kv_send, d_kv_own = call(
+        key_sum_kernel, [((448, 384), BF), ((256, 384), BF)], (d_kv, far, *near, grads_mlp), 0
+    )
+    d_kv_other = hop(d_kv_send, "xl", 1)
+    *pieces, upstream, grads_mlp = call(
         tail_kernel,
-        [((208, 768), BF)] * 4 + [((256, 768), BF)],
+        [((208, 768), BF)] * 4 + [((512, 768), BF), ((96, 768), BF)],
         (coords, block_order, table, tokens, cotangent, ln_attn, w_turned, gain_attn, gain_mlp,
-         *d_queries, d_kv_own, d_kv_other, att, d_ln_mlp, small_mlp),
+         *d_queries, d_kv_own, d_kv_other, *stats_all, outs[0], w_dense, part_mlp,
+         d_ln_mlp, small_mlp, grads_mlp),
         2,
         scratch=[pltpu.VMEM((4, 192, 768), BF)],
-    )
+        mib=60,
+    )
+    grads_mlp = lax.all_gather(grads_mlp, ("z", "y"), axis=0, tiled=True)
 
     pieces = [pieces[0]] + [hop(pieces[j], "y", j) for j in (1, 2, 3)]
     upstream = add(upstream, hop(upstream, "c", 1)).astype(BF)
@@ -525,19 +524,19 @@
         (coords, block, *[hop(block, "z", -j) for j in (1, 2, 3)]),
         1,
     )
-    grad_turned, grad_w_dense = call(
+    grad_turned, grad_w_dense, grad_w_up, grad_w_down = call(
         assemble_kernel,
-        [((576, 768), F32), ((192, 768), F32)],
-        (coords, quarter, *[hop(quarter, "y", -j) for j in (1, 2, 3)]),
+        [((576, 768), F32), ((192, 768), F32), ((768, 768), F32), ((768, 768), F32)],
+        (coords, quarter, *[hop(quarter, "y", -j) for j in (1, 2, 3)], grads_mlp),
         1,
         scratch=[pltpu.VMEM((4, 4, 48, 768), F32)],
-    )
-    (grad_tokens,) = call(
-        token_kernel, [((256, 768), BF)], (tokens, cotangent, upstream, upstream_far), 0
-    )
-
-    grad_w_up, grad_w_down = call(
-        widen_kernel, [((768, 768), F32)] * 2, (grads_mlp, quarter), 0, unread=1
+        mib=60,
+    )
+    grad_tokens, output = call(
+        token_kernel,
+        [((256, 768), BF)] * 2,
+        (tokens, cotangent, upstream, upstream_far, b_dense, b_down),
+        0,
     )
     return (
         output,

time: 225 us -> 199 us (0.88)
  waiting for transfers between devices: 71.7 us -> 54.4 us
  local copies, waits for them, and re-layouts: 14.9 us -> 8.13 us
  Pallas kernels: 57.1 us -> 62.3 us
  starting transfers between devices: 63.3 us -> 58.6 us
    ppermute x43 -> x37, waiting for transfers between devices: 68.4 us -> 48.2 us  [hop(): return lax.ppermute(x, axis, [(i, (i + step) % n) for i in range(n)])]
    unnamed x65 -> x57, local copies, waits for them, and re-layouts: 13.1 us -> 6.28 us
    pallas_call x15 -> x12, Pallas kernels: 57.1 us -> 62.3 us  [call(): pl.pallas_call(kernel, out_shape=shapes, in_specs=[smem] * scalars + [vme...]
    ppermute x43 -> x37, starting transfers between devices: 63.2 us -> 58.5 us  [hop(): return lax.ppermute(x, axis, [(i, (i + step) % n) for i in range(n)])]
    reduce_scatter x1, waiting for transfers between devices: 3.24 us -> 6.15 us  [on_device(): lax.psum_scatter(grads_mlp, ('z', 'y'), scatter_dimension=0, tiled=True)]
  transfers between devices with their start and end apart: 45 -> 39, of which waited for: 24 -> 18; matrix products, arithmetic and copies ran while one was open for 1% -> 1% of each run, Pallas kernels for 21% -> 22%
where the time goes in v4:
time: 199 us
  Pallas kernels  62.3 us (31%)
  starting transfers between devices  58.6 us (29%)
  waiting for transfers between devices  54.4 us (27%)
  between operations  14.4 us (7%)
  local copies, waits for them, and re-layouts  8.13 us (4%)
    pallas_call x12, Pallas kernels, call(): pl.pallas_call(kernel, out_shape=shapes, in_specs=[smem] * scalars + [vme...  62.3 us
    ppermute x37, starting transfers between devices, hop(): return lax.ppermute(x, axis, [(i, (i + step) % n) for i in range(n)])  58.5 us
    ppermute x37, waiting for transfers between devices, hop(): return lax.ppermute(x, axis, [(i, (i + step) % n) for i in range(n)])  48.2 us
    unnamed x57, local copies, waits for them, and re-layouts  6.28 us
    reduce_scatter x1, waiting for transfers between devices, on_device(): lax.psum_scatter(grads_mlp, ('z', 'y'), scatter_dimension=0, tiled=True)  6.15 us
  transfers between devices with their start and end apart: 39, of which 18 were waited for; matrix products, arithmetic and copies ran while one was open for 1% of the time, Pallas kernels for 22%

profile of v4, /device:TPU:0, one launch (start us, length us, event | category | flops | bytes accessed | tf_op | source)
XLA Modules:
  0.0 198.7 jit_solution(11075364099950271080)
XLA Ops:
  7.8 6.9 %shard_map.263 = (bf16[256,384]{1,0:T(8,128)(2,1)}, bf16[256,384]{1,0:T(8,128)(2,1)}, bf16[256,768]{1,0:T(8,128)(2,1)}, bf16[1536,768]{1,0:T(8,128)(2,1)}, f32[8...) custom-call(s32[3]{0:T(128)} %pad_add_fusion.coords, s32[64]{0:T(128)} %order.11, ...), custom_call_target="tpu_custom_call" | custom-call | bytes 1024 | tf_op jit(solution)/shard_map/pallas_call | solution.py:390
  15.7 1.6 collective-permute-start.3
  17.2 1.9 collective-permute-start.6
  19.1 2.1 %collective-permute-start.4 = (bf16[256,384]{1,0:T(8,128)(2,1)S(1)}, bf16[256,384]{1,0:T(8,128)(2,1)S(1)}, u32[]{:S(2)}, u32[]{:S(2)}) collective-permute-start(bf16[256,384]{1,0:T(8,128)(2,1)S(1)} %copy-done.4), channel_id=1, source_target_pairs={{0,48},{16,0},{32,16},{48,32},{1,49},{17,1},{33,17},{49,33},{2,50}... | collective-permute-start | bytes 589832 | tf_op jit(solution)/shard_map/ppermute | solution.py:405
  21.3 1.6 collective-permute-start.2
  22.9 3.6 %collective-permute-start.5 = (bf16[256,384]{1,0:T(8,128)(2,1)S(1)}, bf16[256,384]{1,0:T(8,128)(2,1)S(1)}, u32[]{:S(2)}, u32[]{:S(2)}) collective-permute-start(bf16[256,384]{1,0:T(8,128)(2,1)S(1)} %collective-permute-done.3.refs_5_.refs_6_), channel_id=1, source_target_pairs={{0,48},{16,0},{32,16},{48,32},{1,49},{17,1},{33,17},{49,33},{2,50}... | collective-permute-start | bytes 589832 | tf_op jit(solution)/shard_map/ppermute | solution.py:405
  26.4 3.2 %collective-permute-start.1 = (bf16[256,384]{1,0:T(8,128)(2,1)S(1)}, bf16[256,384]{1,0:T(8,128)(2,1)S(1)}, u32[]{:S(2)}, u32[]{:S(2)}) collective-permute-start(bf16[256,384]{1,0:T(8,128)(2,1)S(1)} %copy-done.2), channel_id=1, source_target_pairs={{0,8},{4,12},{8,0},{12,4},{1,9},{5,13},{9,1},{13,5},{2,10},{6,14},... | collective-permute-start | bytes 589832 | tf_op jit(solution)/shard_map/ppermute | solution.py:405
  30.8 3.4 %collective-permute-start.8 = (bf16[256,384]{1,0:T(8,128)(2,1)S(1)}, bf16[256,384]{1,0:T(8,128)(2,1)S(1)}, u32[]{:S(2)}, u32[]{:S(2)}) collective-permute-start(bf16[256,384]{1,0:T(8,128)(2,1)S(1)} %collective-permute-done.5.refs_7_.refs_6_), channel_id=1, source_target_pairs={{0,48},{16,0},{32,16},{48,32},{1,49},{17,1},{33,17},{49,33},{2,50}... | collective-permute-start | bytes 589832 | tf_op jit(solution)/shard_map/ppermute | solution.py:405
  35.1 4.5 %collective-permute-done.refs_1_.refs_5_.refs_2_ = bf16[256,384]{1,0:T(8,128)(2,1)S(1)} collective-permute-done((bf16[256,384]{1,0:T(8,128)(2,1)S(1)}, bf16[256,384]{1,0:T(8,128)(2,1)S(1)}, u32[]{:S(2)}, u32[]{:S(2)}) %collective-permute-start) | collective-permute-done | bytes 196640 | tf_op jit(solution)/shard_map/ppermute | solution.py:405
  39.6 3.5 %collective-permute-done.7.refs_8_ = bf16[256,384]{1,0:T(8,128)(2,1)S(1)} collective-permute-done((bf16[256,384]{1,0:T(8,128)(2,1)S(1)}, bf16[256,384]{1,0:T(8,128)(2,1)S(1)}, u32[]{:S(2)}, u32[]{:S(2)}) %collective-permute-start.7) | collective-permute-done | bytes 196640 | tf_op jit(solution)/shard_map/ppermute | solution.py:405
  43.1 13.3 %shard_map.264 = (bf16[192,256]{1,0:T(8,128)(2,1)S(1)}, bf16[192,256]{1,0:T(8,128)(2,1)S(1)}, bf16[192,256]{1,0:T(8,128)(2,1)S(1)}, bf16[192,256]{1,0:T(8,128)(2,1)S(1)}, f32[4,8,256]{2,1,0:T(8,128)S(1)}) custom-call(s32[3]{0:T(128)S(1)} %copy-done.14, s32[64]{0:T(128)S(1)} %copy-done.16, bf16[256,384]{1,0:T(8,128)(2,1)S(1)} %copy-done.2, ...), custom_call_target="tpu_custom_call" | custom-call | bytes 1024 | tf_op jit(solution)/shard_map/pallas_call | solution.py:390
  56.4 1.4 collective-permute-start.12
  58.6 2.3 %collective-permute-start.10 = (f32[4,8,256]{2,1,0:T(8,128)S(1)}, f32[4,8,256]{2,1,0:T(8,128)S(1)}, u32[]{:S(2)}, u32[]{:S(2)}) collective-permute-start(f32[4,8,256]{2,1,0:T(8,128)S(1)} %get-tuple-element.58.refs_0_.s0), channel_id=1, source_target_pairs={{0,12},{4,0},{8,4},{12,8},{1,13},{5,1},{9,5},{13,9},{2,14},{6,2},{... | collective-permute-start | bytes 98312 | tf_op jit(solution)/shard_map/ppermute | solution.py:405
  61.7 1.5 collective-permute-done.11.refs_2_.s2
  63.3 6.9 %shard_map.265 = (f32[4,8,256]{2,1,0:T(8,128)S(1)}, bf16[2,256,384]{2,1,0:T(8,128)(2,1)S(1)}, f32[4,192,256]{2,1,0:T(8,128)S(1)}) custom-call(s32[3]{0:T(128)S(1)} %copy-done.14, s32[64]{0:T(128)S(1)} %copy-done.16, f32[4,8,256]{2,1,0:T(8,128)S(1)} %get-tuple-element.58.refs_0_.s0, f32[4,8,256]{2,1,0:T(8,128)S(1)} %collective-permute-done.10.refs_1_.s1, ...), custom_call_target="tpu_custom_call" | custom-call | bytes 1024 | tf_op jit(solution)/shard_map/pallas_call | solution.py:390
  70.3 13.1 %shard_map.266 = (bf16[2,256,384]{2,1,0:T(8,128)(2,1)S(1)}, bf16[2,256,384]{2,1,0:T(8,128)(2,1)S(1)}, f32[4,192,256]{2,1,0:T(8,128)S(1)}) custom-call(s32[3]{0:T(128)S(1)} %copy-done.14, s32[64]{0:T(128)S(1)} %copy-done.16, f32[4,8,256]{2,1,0:T(8,128)S(1)} %get-tuple-element.59.refs_0_, bf16[256,384]{1,0:T(8,128)(2,1)S(1)} %copy-done.2, ...), custom_call_target="tpu_custom_call" | custom-call | bytes 1024 | tf_op jit(solution)/shard_map/pallas_call | solution.py:390
  83.5 1.7 collective-permute-start.17
  85.2 1.6 collective-permute-start.18
  86.8 6.9 %shard_map.267 = (bf16[2,256,384]{2,1,0:T(8,128)(2,1)S(1)}, bf16[192,256]{1,0:T(8,128)(2,1)S(1)}, bf16[384,256]{1,0:T(8,128)(2,1)S(1)}, bf16[384,256]{1,0:T(8,128)(2,1)S(1)}, bf16[384,256]{1,0:T(8,128)(2,1)S(1)}) custom-call(s32[3]{0:T(128)S(1)} %copy-done.14, s32[64]{0:T(128)S(1)} %copy-done.16, f32[4,8,256]{2,1,0:T(8,128)S(1)} %get-tuple-element.59.refs_0_, ...), custom_call_target="tpu_custom_call" | custom-call | bytes 1024 | tf_op jit(solution)/shard_map/pallas_call | solution.py:390
  94.4 6.2 %reduce-scatter.2.cloned.1.call-done.mlp = bf16[96,768]{1,0:T(8,128)(2,1)} async-done(((bf16[1536,768]{1,0:T(8,128)(2,1)}), bf16[96,768]{1,0:T(8,128)(2,1)}) %reduce-scatter.2.cloned.1.call-update) | async-done | bytes 147472 | tf_op jit(solution)/shard_map/reduce_scatter | solution.py:442
  102.3 1.5 collective-permute-start.19
  103.8 1.2 collective-permute-start.14
  105.0 2.7 %collective-permute-start.15 = (bf16[384,256]{1,0:T(8,128)(2,1)S(1)}, bf16[384,256]{1,0:T(8,128)(2,1)S(1)}, u32[]{:S(2)}, u32[]{:S(2)}) collective-permute-start(bf16[384,256]{1,0:T(8,128)(2,1)S(1)} %get-tuple-element.68), channel_id=1, source_target_pairs={{0,8},{4,12},{8,0},{12,4},{1,9},{5,13},{9,1},{13,5},{2,10},{6,14},... | collective-permute-start | bytes 589832 | tf_op jit(solution)/shard_map/ppermute | solution.py:405
  107.7 1.4 collective-permute-start.16
  109.0 3.7 %collective-permute-done.14.dq1 = bf16[384,256]{1,0:T(8,128)(2,1)S(1)} collective-permute-done((bf16[384,256]{1,0:T(8,128)(2,1)S(1)}, bf16[384,256]{1,0:T(8,128)(2,1)S(1)}, u32[]{:S(2)}, u32[]{:S(2)}) %collective-permute-start.14) | collective-permute-done | bytes 196640 | tf_op jit(solution)/shard_map/ppermute | solution.py:405
  112.8 2.1 %collective-permute-done.15.dq2 = bf16[384,256]{1,0:T(8,128)(2,1)S(1)} collective-permute-done((bf16[384,256]{1,0:T(8,128)(2,1)S(1)}, bf16[384,256]{1,0:T(8,128)(2,1)S(1)}, u32[]{:S(2)}, u32[]{:S(2)}) %collective-permute-start.15) | collective-permute-done | bytes 196640 | tf_op jit(solution)/shard_map/ppermute | solution.py:405
  115.8 5.9 %shard_map.269 = (bf16[208,768]{1,0:T(8,128)(2,1)}, bf16[208,768]{1,0:T(8,128)(2,1)}, bf16[208,768]{1,0:T(8,128)(2,1)}, bf16[208,768]{1,0:T(8,128)(2,1)}, bf16[5...) custom-call(s32[3]{0:T(128)} %pad_add_fusion.coords, s32[64]{0:T(128)} %order.11, f32[8,128]{1,0:T(8,128)} %constant.17.clone.table, ...), custom_call_target="tpu_custom_call" | custom-call | bytes 1024 | tf_op jit(solution)/shard_map/pallas_call | solution.py:390
  121.8 1.8 collective-permute-start.22
  123.5 2.4 %collective-permute-start.23 = (bf16[208,768]{1,0:T(8,128)(2,1)}, bf16[208,768]{1,0:T(8,128)(2,1)S(1)}, u32[]{:S(2)}, u32[]{:S(2)}) collective-permute-start(bf16[208,768]{1,0:T(8,128)(2,1)} %get-tuple-element.85), channel_id=1, source_target_pairs={{0,8},{4,12},{8,0},{12,4},{1,9},{5,13},{9,1},{13,5},{2,10},{6,14},... | collective-permute-start | bytes 958472 | tf_op jit(solution)/shard_map/ppermute | solution.py:405
  127.0 6.2 %collective-permute-done.22.p1 = bf16[208,768]{1,0:T(8,128)(2,1)S(1)} collective-permute-done((bf16[208,768]{1,0:T(8,128)(2,1)}, bf16[208,768]{1,0:T(8,128)(2,1)S(1)}, u32[]{:S(2)}, u32[]{:S(2)}) %collective-permute-start.22) | collective-permute-done | bytes 319520 | tf_op jit(solution)/shard_map/ppermute | solution.py:405
  133.1 9.3 %collective-permute-done.23.p2 = bf16[208,768]{1,0:T(8,128)(2,1)S(1)} collective-permute-done((bf16[208,768]{1,0:T(8,128)(2,1)}, bf16[208,768]{1,0:T(8,128)(2,1)S(1)}, u32[]{:S(2)}, u32[]{:S(2)}) %collective-permute-start.23) | collective-permute-done | bytes 319520 | tf_op jit(solution)/shard_map/ppermute | solution.py:405
  144.4 1.4 collective-permute-start.25
  145.8 2.5 %collective-permute-start.26 = (bf16[64,768]{1,0:T(8,128)(2,1)S(1)}, bf16[64,768]{1,0:T(8,128)(2,1)S(1)}, u32[]{:S(2)}, u32[]{:S(2)}) collective-permute-start(bf16[64,768]{1,0:T(8,128)(2,1)S(1)} %get-tuple-element.89), channel_id=1, source_target_pairs={{0,32},{16,48},{32,0},{48,16},{1,33},{17,49},{33,1},{49,17},{2,34}... | collective-permute-start | bytes 294920 | tf_op jit(solution)/shard_map/ppermute | solution.py:405
  148.8 2.5 %collective-permute-done.25.b1 = bf16[64,768]{1,0:T(8,128)(2,1)S(1)} collective-permute-done((bf16[64,768]{1,0:T(8,128)(2,1)S(1)}, bf16[64,768]{1,0:T(8,128)(2,1)S(1)}, u32[]{:S(2)}, u32[]{:S(2)}) %collective-permute-start.25) | collective-permute-done | bytes 98336 | tf_op jit(solution)/shard_map/ppermute | solution.py:405
  151.3 1.3 collective-permute-done.26.b2
  154.4 3.2 %collective-permute-start.21 = (bf16[512,768]{1,0:T(8,128)(2,1)S(1)}, bf16[512,768]{1,0:T(8,128)(2,1)S(1)}, u32[]{:S(2)}, u32[]{:S(2)}) collective-permute-start(bf16[512,768]{1,0:T(8,128)(2,1)S(1)} %add_convert_fusion.e0), channel_id=1, source_target_pairs={{0,2},{2,0},{1,3},{3,1},{4,6},{6,4},{5,7},{7,5},{8,10},{10,8},{9,1... | collective-permute-start | bytes 2359304 | tf_op jit(solution)/shard_map/ppermute | solution.py:405
  157.6 1.6 collective-permute-done.28
  159.2 1.1 collective-permute-start.31
  160.3 3.0 %collective-permute-start.30 = (bf16[48,768]{1,0:T(8,128)(2,1)S(1)}, bf16[48,768]{1,0:T(8,128)(2,1)S(1)}, u32[]{:S(2)}, u32[]{:S(2)}) collective-permute-start(bf16[48,768]{1,0:T(8,128)(2,1)S(1)} %slice.59.b0), channel_id=1, source_target_pairs={{0,32},{16,48},{32,0},{48,16},{1,33},{17,49},{33,1},{49,17},{2,34}... | collective-permute-start | bytes 221192 | tf_op jit(solution)/shard_map/ppermute | solution.py:405
  164.1 2.2 %collective-permute-done.31.b3 = bf16[48,768]{1,0:T(8,128)(2,1)S(1)} collective-permute-done((bf16[48,768]{1,0:T(8,128)(2,1)S(1)}, bf16[48,768]{1,0:T(8,128)(2,1)S(1)}, u32[]{:S(2)}, u32[]{:S(2)}) %collective-permute-start.31) | collective-permute-done | bytes 73760 | tf_op jit(solution)/shard_map/ppermute | solution.py:405
  166.3 3.2 %collective-permute-done.30.b2 = bf16[48,768]{1,0:T(8,128)(2,1)S(1)} collective-permute-done((bf16[48,768]{1,0:T(8,128)(2,1)S(1)}, bf16[48,768]{1,0:T(8,128)(2,1)S(1)}, u32[]{:S(2)}, u32[]{:S(2)}) %collective-permute-start.30) | collective-permute-done | bytes 73760 | tf_op jit(solution)/shard_map/ppermute | solution.py:405
  170.1 1.6 collective-permute-start.34
  171.7 2.6 %collective-permute-start.33 = (bf16[4,48,768]{2,1,0:T(8,128)(2,1)S(1)}, bf16[4,48,768]{2,1,0:T(8,128)(2,1)S(1)}, u32[]{:S(2)}, u32[]{:S(2)}) collective-permute-start(bf16[4,48,768]{2,1,0:T(8,128)(2,1)S(1)} %shard_map.273.p0), channel_id=1, source_target_pairs={{0,8},{4,12},{8,0},{12,4},{1,9},{5,13},{9,1},{13,5},{2,10},{6,14},... | collective-permute-start | bytes 884744 | tf_op jit(solution)/shard_map/ppermute | solution.py:405
  174.8 3.0 %collective-permute-start.36 = (f32[8,768]{1,0:T(8,128)S(1)}, f32[8,768]{1,0:T(8,128)S(1)}, u32[]{:S(2)}, u32[]{:S(2)}) collective-permute-start(f32[8,768]{1,0:T(8,128)S(1)} %slice_add_fusion), channel_id=1, source_target_pairs={{0,2},{2,0},{1,3},{3,1},{4,6},{6,4},{5,7},{7,5},{8,10},{10,8},{9,1... | collective-permute-start | bytes 73736 | tf_op jit(solution)/shard_map/ppermute | solution.py:405
  178.5 1.8 collective-permute-done.36
  180.9 1.7 shard_map.270
  182.6 2.5 %collective-permute-done.33.p2 = bf16[4,48,768]{2,1,0:T(8,128)(2,1)S(1)} collective-permute-done((bf16[4,48,768]{2,1,0:T(8,128)(2,1)S(1)}, bf16[4,48,768]{2,1,0:T(8,128)(2,1)S(1)}, u32[]{:S(2)}, u32[]{:S(2)}) %collective-permute-start.33) | collective-permute-done | bytes 294944 | tf_op jit(solution)/shard_map/ppermute | solution.py:405
  186.0 5.3 %shard_map.274 = (f32[576,768]{1,0:T(8,128)}, f32[192,768]{1,0:T(8,128)}, f32[768,768]{1,0:T(8,128)}, f32[768,768]{1,0:T(8,128)}) custom-call(s32[3]{0:T(128)} %pad_add_fusion.coords, bf16[4,48,768]{2,1,0:T(8,128)(2,1)} %copy-done.3, bf16[4,48,768]{2,1,0:T(8,128)(2,1)} %copy-done.23, bf16[4,48,768]{2,1,0:T(8,128)(2,1)} %copy-done.22, ...), custom_call_target="tpu_custom_call" | custom-call | bytes 1024 | tf_op jit(solution)/shard_map/pallas_call | solution.py:390
  (111 shorter events, 18.6 us)
Async XLA Ops:
  7.2 93.3 %reduce-scatter.2.cloned.1.call-start = ((), (), s32[]{:S(2)}) async-start(), calls=%async_computation.1 | async-start | bytes 2506752 | tf_op jit(solution)/shard_map/reduce_scatter | solution.py:442
  14.7 28.4 %copy-start.14 = (s32[3]{0:T(128)S(1)}, s32[3]{0:T(128)}, u32[]{:S(2)}) copy-start(s32[3]{0:T(128)} %pad_add_fusion.coords) | copy-start | bytes 40
  14.8 28.3 %copy-start.16 = (s32[64]{0:T(128)S(1)}, s32[64]{0:T(128)}, u32[]{:S(2)}) copy-start(s32[64]{0:T(128)} %order.11) | copy-start | bytes 772
  14.8 170.4 %all-gather.2.cloned.1.call-start = ((), (), s32[]{:S(2)}) async-start(), calls=%async_computation.2 | async-start | bytes 2506752 | tf_op jit(solution)/shard_map/all_gather | solution.py:497
  15.7 7.2 %collective-permute-start.3 = (bf16[256,384]{1,0:T(8,128)(2,1)S(1)}, bf16[256,384]{1,0:T(8,128)(2,1)S(1)}, u32[]{:S(2)}, u32[]{:S(2)}) collective-permute-start(bf16[256,384]{1,0:T(8,128)(2,1)S(1)} %copy-done.4), channel_id=1, source_target_pairs={{0,64},{64,0},{1,65},{65,1},{2,66},{66,2},{3,67},{67,3},{4,68},{68... | collective-permute-start | bytes 589832 | tf_op jit(solution)/shard_map/ppermute | solution.py:405
  17.2 12.4 %collective-permute-start.6 = (bf16[256,384]{1,0:T(8,128)(2,1)S(1)}, bf16[256,384]{1,0:T(8,128)(2,1)S(1)}, u32[]{:S(2)}, u32[]{:S(2)}) collective-permute-start(bf16[256,384]{1,0:T(8,128)(2,1)S(1)} %copy-done.4), channel_id=1, source_target_pairs={{0,16},{16,32},{32,48},{48,0},{1,17},{17,33},{33,49},{49,1},{2,18}... | collective-permute-start | bytes 589832 | tf_op jit(solution)/shard_map/ppermute | solution.py:405
  19.1 11.5 %collective-permute-start.4 = (bf16[256,384]{1,0:T(8,128)(2,1)S(1)}, bf16[256,384]{1,0:T(8,128)(2,1)S(1)}, u32[]{:S(2)}, u32[]{:S(2)}) collective-permute-start(bf16[256,384]{1,0:T(8,128)(2,1)S(1)} %copy-done.4), channel_id=1, source_target_pairs={{0,48},{16,0},{32,16},{48,32},{1,49},{17,1},{33,17},{49,33},{2,50}... | collective-permute-start | bytes 589832 | tf_op jit(solution)/shard_map/ppermute | solution.py:405
  21.3 9.4 %collective-permute-start.2 = (bf16[256,384]{1,0:T(8,128)(2,1)S(1)}, bf16[256,384]{1,0:T(8,128)(2,1)S(1)}, u32[]{:S(2)}, u32[]{:S(2)}) collective-permute-start(bf16[256,384]{1,0:T(8,128)(2,1)S(1)} %copy-done.2), channel_id=1, source_target_pairs={{0,4},{4,8},{8,12},{12,0},{1,5},{5,9},{9,13},{13,1},{2,6},{6,10},{... | collective-permute-start | bytes 589832 | tf_op jit(solution)/shard_map/ppermute | solution.py:405
  22.9 7.9 %collective-permute-start.5 = (bf16[256,384]{1,0:T(8,128)(2,1)S(1)}, bf16[256,384]{1,0:T(8,128)(2,1)S(1)}, u32[]{:S(2)}, u32[]{:S(2)}) collective-permute-start(bf16[256,384]{1,0:T(8,128)(2,1)S(1)} %collective-permute-done.3.refs_5_.refs_6_), channel_id=1, source_target_pairs={{0,48},{16,0},{32,16},{48,32},{1,49},{17,1},{33,17},{49,33},{2,50}... | collective-permute-start | bytes 589832 | tf_op jit(solution)/shard_map/ppermute | solution.py:405
  26.4 8.7 %collective-permute-start.1 = (bf16[256,384]{1,0:T(8,128)(2,1)S(1)}, bf16[256,384]{1,0:T(8,128)(2,1)S(1)}, u32[]{:S(2)}, u32[]{:S(2)}) collective-permute-start(bf16[256,384]{1,0:T(8,128)(2,1)S(1)} %copy-done.2), channel_id=1, source_target_pairs={{0,8},{4,12},{8,0},{12,4},{1,9},{5,13},{9,1},{13,5},{2,10},{6,14},... | collective-permute-start | bytes 589832 | tf_op jit(solution)/shard_map/ppermute | solution.py:405
  29.6 10.0 %collective-permute-start = (bf16[256,384]{1,0:T(8,128)(2,1)S(1)}, bf16[256,384]{1,0:T(8,128)(2,1)S(1)}, u32[]{:S(2)}, u32[]{:S(2)}) collective-permute-start(bf16[256,384]{1,0:T(8,128)(2,1)S(1)} %copy-done.2), channel_id=1, source_target_pairs={{0,12},{4,0},{8,4},{12,8},{1,13},{5,1},{9,5},{13,9},{2,14},{6,2},{... | collective-permute-start | bytes 589832 | tf_op jit(solution)/shard_map/ppermute | solution.py:405
  30.7 12.4 %collective-permute-start.9 = (bf16[256,384]{1,0:T(8,128)(2,1)S(1)}, bf16[256,384]{1,0:T(8,128)(2,1)S(1)}, u32[]{:S(2)}, u32[]{:S(2)}) collective-permute-start(bf16[256,384]{1,0:T(8,128)(2,1)S(1)} %collective-permute-done.3.refs_5_.refs_6_), channel_id=1, source_target_pairs={{0,16},{16,32},{32,48},{48,0},{1,17},{17,33},{33,49},{49,1},{2,18}... | collective-permute-start | bytes 589832 | tf_op jit(solution)/shard_map/ppermute | solution.py:405
  30.7 12.4 %collective-permute-start.7 = (bf16[256,384]{1,0:T(8,128)(2,1)S(1)}, bf16[256,384]{1,0:T(8,128)(2,1)S(1)}, u32[]{:S(2)}, u32[]{:S(2)}) collective-permute-start(bf16[256,384]{1,0:T(8,128)(2,1)S(1)} %collective-permute-done.6.refs_10_.refs_7_), channel_id=1, source_target_pairs={{0,16},{16,32},{32,48},{48,0},{1,17},{17,33},{33,49},{49,1},{2,18}... | collective-permute-start | bytes 589832 | tf_op jit(solution)/shard_map/ppermute | solution.py:405
  30.8 12.3 %collective-permute-start.8 = (bf16[256,384]{1,0:T(8,128)(2,1)S(1)}, bf16[256,384]{1,0:T(8,128)(2,1)S(1)}, u32[]{:S(2)}, u32[]{:S(2)}) collective-permute-start(bf16[256,384]{1,0:T(8,128)(2,1)S(1)} %collective-permute-done.5.refs_7_.refs_6_), channel_id=1, source_target_pairs={{0,48},{16,0},{32,16},{48,32},{1,49},{17,1},{33,17},{49,33},{2,50}... | collective-permute-start | bytes 589832 | tf_op jit(solution)/shard_map/ppermute | solution.py:405
  56.4 27.0 %copy-start.8 = (f32[4,8,256]{2,1,0:T(8,128)}, f32[4,8,256]{2,1,0:T(8,128)S(1)}, u32[]{:S(2)}) copy-start(f32[4,8,256]{2,1,0:T(8,128)S(1)} %get-tuple-element.58.refs_0_.s0) | copy-start | bytes 98308
  56.4 27.0 %copy-start.12 = (bf16[192,256]{1,0:T(8,128)(2,1)}, bf16[192,256]{1,0:T(8,128)(2,1)S(1)}, u32[]{:S(2)}) copy-start(bf16[192,256]{1,0:T(8,128)(2,1)S(1)} %get-tuple-element.76.o0) | copy-start | bytes 294916
  56.4 5.3 %collective-permute-start.12 = (f32[4,8,256]{2,1,0:T(8,128)S(1)}, f32[4,8,256]{2,1,0:T(8,128)S(1)}, u32[]{:S(2)}, u32[]{:S(2)}) collective-permute-start(f32[4,8,256]{2,1,0:T(8,128)S(1)} %get-tuple-element.58.refs_0_.s0), channel_id=1, source_target_pairs={{0,4},{4,8},{8,12},{12,0},{1,5},{5,9},{9,13},{13,1},{2,6},{6,10},{... | collective-permute-start | bytes 98312 | tf_op jit(solution)/shard_map/ppermute | solution.py:405
  57.9 5.4 %collective-permute-start.11 = (f32[4,8,256]{2,1,0:T(8,128)S(1)}, f32[4,8,256]{2,1,0:T(8,128)S(1)}, u32[]{:S(2)}, u32[]{:S(2)}) collective-permute-start(f32[4,8,256]{2,1,0:T(8,128)S(1)} %get-tuple-element.58.refs_0_.s0), channel_id=1, source_target_pairs={{0,8},{4,12},{8,0},{12,4},{1,9},{5,13},{9,1},{13,5},{2,10},{6,14},... | collective-permute-start | bytes 98312 | tf_op jit(solution)/shard_map/ppermute | solution.py:405
  58.6 4.7 %collective-permute-start.10 = (f32[4,8,256]{2,1,0:T(8,128)S(1)}, f32[4,8,256]{2,1,0:T(8,128)S(1)}, u32[]{:S(2)}, u32[]{:S(2)}) collective-permute-start(f32[4,8,256]{2,1,0:T(8,128)S(1)} %get-tuple-element.58.refs_0_.s0), channel_id=1, source_target_pairs={{0,12},{4,0},{8,4},{12,8},{1,13},{5,1},{9,5},{13,9},{2,14},{6,2},{... | collective-permute-start | bytes 98312 | tf_op jit(solution)/shard_map/ppermute | solution.py:405
  70.2 16.6 %collective-permute-start.13 = (bf16[2,256,384]{2,1,0:T(8,128)(2,1)S(1)}, bf16[2,256,384]{2,1,0:T(8,128)(2,1)S(1)}, u32[]{:S(2)}, u32[]{:S(2)}) collective-permute-start(bf16[2,256,384]{2,1,0:T(8,128)(2,1)S(1)} %get-tuple-element.65), channel_id=1, source_target_pairs={{0,32},{16,48},{32,0},{48,16},{1,33},{17,49},{33,1},{49,17},{2,34}... | collective-permute-start | bytes 1179656 | tf_op jit(solution)/shard_map/ppermute | solution.py:405
  83.5 10.9 %collective-permute-start.17 = (bf16[2,256,384]{2,1,0:T(8,128)(2,1)S(1)}, bf16[2,256,384]{2,1,0:T(8,128)(2,1)S(1)}, u32[]{:S(2)}, u32[]{:S(2)}) collective-permute-start(bf16[2,256,384]{2,1,0:T(8,128)(2,1)S(1)} %get-tuple-element.71), channel_id=1, source_target_pairs={{0,16},{16,32},{32,48},{48,0},{1,17},{17,33},{33,49},{49,1},{2,18}... | collective-permute-start | bytes 1179656 | tf_op jit(solution)/shard_map/ppermute | solution.py:405
  85.2 9.2 %collective-permute-start.18 = (bf16[2,256,384]{2,1,0:T(8,128)(2,1)S(1)}, bf16[2,256,384]{2,1,0:T(8,128)(2,1)S(1)}, u32[]{:S(2)}, u32[]{:S(2)}) collective-permute-start(bf16[2,256,384]{2,1,0:T(8,128)(2,1)S(1)} %get-tuple-element.72), channel_id=1, source_target_pairs={{0,48},{16,0},{32,16},{48,32},{1,49},{17,1},{33,17},{49,33},{2,50}... | collective-permute-start | bytes 1179656 | tf_op jit(solution)/shard_map/ppermute | solution.py:405
  102.3 12.6 %collective-permute-start.19 = (bf16[448,384]{1,0:T(8,128)(2,1)S(1)}, bf16[448,384]{1,0:T(8,128)(2,1)S(1)}, u32[]{:S(2)}, u32[]{:S(2)}) collective-permute-start(bf16[448,384]{1,0:T(8,128)(2,1)S(1)} %get-tuple-element.75), channel_id=1, source_target_pairs={{0,64},{64,0},{1,65},{65,1},{2,66},{66,2},{3,67},{67,3},{4,68},{68... | collective-permute-start | bytes 1032200 | tf_op jit(solution)/shard_map/ppermute | solution.py:405
  103.8 9.0 %collective-permute-start.14 = (bf16[384,256]{1,0:T(8,128)(2,1)S(1)}, bf16[384,256]{1,0:T(8,128)(2,1)S(1)}, u32[]{:S(2)}, u32[]{:S(2)}) collective-permute-start(bf16[384,256]{1,0:T(8,128)(2,1)S(1)} %get-tuple-element.67), channel_id=1, source_target_pairs={{0,4},{4,8},{8,12},{12,0},{1,5},{5,9},{9,13},{13,1},{2,6},{6,10},{... | collective-permute-start | bytes 589832 | tf_op jit(solution)/shard_map/ppermute | solution.py:405
  105.0 9.9 %collective-permute-start.15 = (bf16[384,256]{1,0:T(8,128)(2,1)S(1)}, bf16[384,256]{1,0:T(8,128)(2,1)S(1)}, u32[]{:S(2)}, u32[]{:S(2)}) collective-permute-start(bf16[384,256]{1,0:T(8,128)(2,1)S(1)} %get-tuple-element.68), channel_id=1, source_target_pairs={{0,8},{4,12},{8,0},{12,4},{1,9},{5,13},{9,1},{13,5},{2,10},{6,14},... | collective-permute-start | bytes 589832 | tf_op jit(solution)/shard_map/ppermute | solution.py:405
  107.7 7.2 %collective-permute-start.16 = (bf16[384,256]{1,0:T(8,128)(2,1)S(1)}, bf16[384,256]{1,0:T(8,128)(2,1)S(1)}, u32[]{:S(2)}, u32[]{:S(2)}) collective-permute-start(bf16[384,256]{1,0:T(8,128)(2,1)S(1)} %get-tuple-element.69), channel_id=1, source_target_pairs={{0,12},{4,0},{8,4},{12,8},{1,13},{5,1},{9,5},{13,9},{2,14},{6,2},{... | collective-permute-start | bytes 589832 | tf_op jit(solution)/shard_map/ppermute | solution.py:405
  121.7 32.5 %collective-permute-start.20 = (bf16[512,768]{1,0:T(8,128)(2,1)}, bf16[512,768]{1,0:T(8,128)(2,1)S(1)}, u32[]{:S(2)}, u32[]{:S(2)}) collective-permute-start(bf16[512,768]{1,0:T(8,128)(2,1)} %get-tuple-element.80), channel_id=1, source_target_pairs={{0,1},{1,0},{2,3},{3,2},{4,5},{5,4},{6,7},{7,6},{8,9},{9,8},{10,11... | collective-permute-start | bytes 2359304 | tf_op jit(solution)/shard_map/ppermute | solution.py:405
  121.8 11.4 %collective-permute-start.22 = (bf16[208,768]{1,0:T(8,128)(2,1)}, bf16[208,768]{1,0:T(8,128)(2,1)S(1)}, u32[]{:S(2)}, u32[]{:S(2)}) collective-permute-start(bf16[208,768]{1,0:T(8,128)(2,1)} %get-tuple-element.84), channel_id=1, source_target_pairs={{0,4},{4,8},{8,12},{12,0},{1,5},{5,9},{9,13},{13,1},{2,6},{6,10},{... | collective-permute-start | bytes 958472 | tf_op jit(solution)/shard_map/ppermute | solution.py:405
  123.5 18.9 %collective-permute-start.23 = (bf16[208,768]{1,0:T(8,128)(2,1)}, bf16[208,768]{1,0:T(8,128)(2,1)S(1)}, u32[]{:S(2)}, u32[]{:S(2)}) collective-permute-start(bf16[208,768]{1,0:T(8,128)(2,1)} %get-tuple-element.85), channel_id=1, source_target_pairs={{0,8},{4,12},{8,0},{12,4},{1,9},{5,13},{9,1},{13,5},{2,10},{6,14},... | collective-permute-start | bytes 958472 | tf_op jit(solution)/shard_map/ppermute | solution.py:405
  125.9 16.5 %collective-permute-start.24 = (bf16[208,768]{1,0:T(8,128)(2,1)}, bf16[208,768]{1,0:T(8,128)(2,1)S(1)}, u32[]{:S(2)}, u32[]{:S(2)}) collective-permute-start(bf16[208,768]{1,0:T(8,128)(2,1)} %get-tuple-element.86), channel_id=1, source_target_pairs={{0,12},{4,0},{8,4},{12,8},{1,13},{5,1},{9,5},{13,9},{2,14},{6,2},{... | collective-permute-start | bytes 958472 | tf_op jit(solution)/shard_map/ppermute | solution.py:405
  144.4 7.0 %collective-permute-start.25 = (bf16[64,768]{1,0:T(8,128)(2,1)S(1)}, bf16[64,768]{1,0:T(8,128)(2,1)S(1)}, u32[]{:S(2)}, u32[]{:S(2)}) collective-permute-start(bf16[64,768]{1,0:T(8,128)(2,1)S(1)} %get-tuple-element.88), channel_id=1, source_target_pairs={{0,16},{16,32},{32,48},{48,0},{1,17},{17,33},{33,49},{49,1},{2,18}... | collective-permute-start | bytes 294920 | tf_op jit(solution)/shard_map/ppermute | solution.py:405
  145.8 6.8 %collective-permute-start.26 = (bf16[64,768]{1,0:T(8,128)(2,1)S(1)}, bf16[64,768]{1,0:T(8,128)(2,1)S(1)}, u32[]{:S(2)}, u32[]{:S(2)}) collective-permute-start(bf16[64,768]{1,0:T(8,128)(2,1)S(1)} %get-tuple-element.89), channel_id=1, source_target_pairs={{0,32},{16,48},{32,0},{48,16},{1,33},{17,49},{33,1},{49,17},{2,34}... | collective-permute-start | bytes 294920 | tf_op jit(solution)/shard_map/ppermute | solution.py:405
  148.3 4.8 %collective-permute-start.27 = (bf16[64,768]{1,0:T(8,128)(2,1)S(1)}, bf16[64,768]{1,0:T(8,128)(2,1)S(1)}, u32[]{:S(2)}, u32[]{:S(2)}) collective-permute-start(bf16[64,768]{1,0:T(8,128)(2,1)S(1)} %get-tuple-element.90), channel_id=1, source_target_pairs={{0,48},{16,0},{32,16},{48,32},{1,49},{17,1},{33,17},{49,33},{2,50}... | collective-permute-start | bytes 294920 | tf_op jit(solution)/shard_map/ppermute | solution.py:405
  153.7 27.2 %copy-start = (bf16[256,768]{1,0:T(8,128)(2,1)S(1)}, bf16[256,768]{1,0:T(8,128)(2,1)}, u32[]{:S(2)}) copy-start(bf16[256,768]{1,0:T(8,128)(2,1)} %tok.5) | copy-start | bytes 1179652
  153.7 27.2 %copy-start.1 = (bf16[256,768]{1,0:T(8,128)(2,1)S(1)}, bf16[256,768]{1,0:T(8,128)(2,1)}, u32[]{:S(2)}) copy-start(bf16[256,768]{1,0:T(8,128)(2,1)} %cot.5) | copy-start | bytes 1179652
  153.7 27.2 %copy-start.17 = (f32[768]{0:T(1024)S(1)}, f32[768]{0:T(1024)}, u32[]{:S(2)}) copy-start(f32[768]{0:T(1024)} %b_dense.1) | copy-start | bytes 9220
  153.7 27.2 %copy-start.18 = (f32[768]{0:T(1024)S(1)}, f32[768]{0:T(1024)}, u32[]{:S(2)}) copy-start(f32[768]{0:T(1024)} %b_down.1) | copy-start | bytes 9220
  153.7 5.4 %collective-permute-start.28 = (bf16[64,768]{1,0:T(8,128)(2,1)S(1)}, bf16[64,768]{1,0:T(8,128)(2,1)S(1)}, u32[]{:S(2)}, u32[]{:S(2)}) collective-permute-start(bf16[64,768]{1,0:T(8,128)(2,1)S(1)} %shard_map.272), channel_id=1, source_target_pairs={{0,64},{64,0},{1,65},{65,1},{2,66},{66,2},{3,67},{67,3},{4,68},{68... | collective-permute-start | bytes 294920 | tf_op jit(solution)/shard_map/ppermute | solution.py:405
  154.4 26.5 %collective-permute-start.21 = (bf16[512,768]{1,0:T(8,128)(2,1)S(1)}, bf16[512,768]{1,0:T(8,128)(2,1)S(1)}, u32[]{:S(2)}, u32[]{:S(2)}) collective-permute-start(bf16[512,768]{1,0:T(8,128)(2,1)S(1)} %add_convert_fusion.e0), channel_id=1, source_target_pairs={{0,2},{2,0},{1,3},{3,1},{4,6},{6,4},{5,7},{7,5},{8,10},{10,8},{9,1... | collective-permute-start | bytes 2359304 | tf_op jit(solution)/shard_map/ppermute | solution.py:405
  159.2 7.1 %collective-permute-start.31 = (bf16[48,768]{1,0:T(8,128)(2,1)S(1)}, bf16[48,768]{1,0:T(8,128)(2,1)S(1)}, u32[]{:S(2)}, u32[]{:S(2)}) collective-permute-start(bf16[48,768]{1,0:T(8,128)(2,1)S(1)} %slice.59.b0), channel_id=1, source_target_pairs={{0,16},{16,32},{32,48},{48,0},{1,17},{17,33},{33,49},{49,1},{2,18}... | collective-permute-start | bytes 221192 | tf_op jit(solution)/shard_map/ppermute | solution.py:405
  160.3 9.2 %collective-permute-start.30 = (bf16[48,768]{1,0:T(8,128)(2,1)S(1)}, bf16[48,768]{1,0:T(8,128)(2,1)S(1)}, u32[]{:S(2)}, u32[]{:S(2)}) collective-permute-start(bf16[48,768]{1,0:T(8,128)(2,1)S(1)} %slice.59.b0), channel_id=1, source_target_pairs={{0,32},{16,48},{32,0},{48,16},{1,33},{17,49},{33,1},{49,17},{2,34}... | collective-permute-start | bytes 221192 | tf_op jit(solution)/shard_map/ppermute | solution.py:405
  163.3 6.2 %collective-permute-start.29 = (bf16[48,768]{1,0:T(8,128)(2,1)S(1)}, bf16[48,768]{1,0:T(8,128)(2,1)S(1)}, u32[]{:S(2)}, u32[]{:S(2)}) collective-permute-start(bf16[48,768]{1,0:T(8,128)(2,1)S(1)} %slice.59.b0), channel_id=1, source_target_pairs={{0,48},{16,0},{32,16},{48,32},{1,49},{17,1},{33,17},{49,33},{2,50}... | collective-permute-start | bytes 221192 | tf_op jit(solution)/shard_map/ppermute | solution.py:405
  163.5 11.3 %collective-permute-start.35 = (f32[8,768]{1,0:T(8,128)S(1)}, f32[8,768]{1,0:T(8,128)S(1)}, u32[]{:S(2)}, u32[]{:S(2)}) collective-permute-start(f32[8,768]{1,0:T(8,128)S(1)} %slice.45), channel_id=1, source_target_pairs={{0,1},{1,0},{2,3},{3,2},{4,5},{5,4},{6,7},{7,6},{8,9},{9,8},{10,11... | collective-permute-start | bytes 73736 | tf_op jit(solution)/shard_map/ppermute | solution.py:405
  164.1 27.1 %copy-start.27 = (f32[768]{0:T(1024)}, f32[768]{0:T(1024)S(1)}, u32[]{:S(2)}) copy-start(f32[768]{0:T(1024)S(1)} %get-tuple-element.125) | copy-start | bytes 9220
  170.1 12.5 %collective-permute-start.34 = (bf16[4,48,768]{2,1,0:T(8,128)(2,1)S(1)}, bf16[4,48,768]{2,1,0:T(8,128)(2,1)S(1)}, u32[]{:S(2)}, u32[]{:S(2)}) collective-permute-start(bf16[4,48,768]{2,1,0:T(8,128)(2,1)S(1)} %shard_map.273.p0), channel_id=1, source_target_pairs={{0,4},{4,8},{8,12},{12,0},{1,5},{5,9},{9,13},{13,1},{2,6},{6,10},{... | collective-permute-start | bytes 884744 | tf_op jit(solution)/shard_map/ppermute | solution.py:405
  171.7 13.5 %collective-permute-start.33 = (bf16[4,48,768]{2,1,0:T(8,128)(2,1)S(1)}, bf16[4,48,768]{2,1,0:T(8,128)(2,1)S(1)}, u32[]{:S(2)}, u32[]{:S(2)}) collective-permute-start(bf16[4,48,768]{2,1,0:T(8,128)(2,1)S(1)} %shard_map.273.p0), channel_id=1, source_target_pairs={{0,8},{4,12},{8,0},{12,4},{1,9},{5,13},{9,1},{13,5},{2,10},{6,14},... | collective-permute-start | bytes 884744 | tf_op jit(solution)/shard_map/ppermute | solution.py:405
  174.2 10.9 %collective-permute-start.32 = (bf16[4,48,768]{2,1,0:T(8,128)(2,1)S(1)}, bf16[4,48,768]{2,1,0:T(8,128)(2,1)S(1)}, u32[]{:S(2)}, u32[]{:S(2)}) collective-permute-start(bf16[4,48,768]{2,1,0:T(8,128)(2,1)S(1)} %shard_map.273.p0), channel_id=1, source_target_pairs={{0,12},{4,0},{8,4},{12,8},{1,13},{5,1},{9,5},{13,9},{2,14},{6,2},{... | collective-permute-start | bytes 884744 | tf_op jit(solution)/shard_map/ppermute | solution.py:405
  174.8 5.4 %collective-permute-start.36 = (f32[8,768]{1,0:T(8,128)S(1)}, f32[8,768]{1,0:T(8,128)S(1)}, u32[]{:S(2)}, u32[]{:S(2)}) collective-permute-start(f32[8,768]{1,0:T(8,128)S(1)} %slice_add_fusion), channel_id=1, source_target_pairs={{0,2},{2,0},{1,3},{3,1},{4,6},{6,4},{5,7},{7,5},{8,10},{10,8},{9,1... | collective-permute-start | bytes 73736 | tf_op jit(solution)/shard_map/ppermute | solution.py:405
  (19 other events, 133.8 us)
Sparse Core Ops, SparseCore 0:
  14.9 85.5 reduce-scatter.1
  121.8 49.3 all-gather.1

commit v5 on v4

--- a/solution.py
+++ b/solution.py
@@ -276,20 +276,26 @@
             ref[192:384, :] = source[...]
 
 
-def key_sum_kernel(own, far, near, near_too, mlp, send, kept):
+def key_sum_kernel(own, far, near, near_too, send, kept):
     def total(a):
         parts = [ref[a].astype(F32) for ref in (own, far, near, near_too)]
         return functools.reduce(jnp.add, parts).astype(BF)
 
     kept[...] = total(0)
-    send[0:256, :] = total(1)
-    send[256:352, :] = mlp[:, 0:384]
-    send[352:448, :] = mlp[:, 384:768]
+    send[...] = total(1)
+
+
+def keep_kernel(x, after, out):
+    out[...] = x[...]
+
+
+def pair_kernel(x, y, after, out):
+    out[...] = (x[...].astype(F32) + y[...].astype(F32)).astype(BF)
 
 
 def tail_kernel(
     coords, order, table, tok, cot, lna, wqkv, ga, gm, dq0, dq1, dq2, dq3, dkv0, dkv1,
-    s0, s1, s2, s3, o0, wd, part, d_ln_mlp, small_in, mlp, g0, g1, g2, g3, upstream, mlp_sum, grads,
+    s0, s1, s2, s3, o0, wd, part, d_ln_mlp, small_in, g0, g1, g2, g3, upstream, grads,
 ):
     outs = [o0] + [ref.at[192:384] for ref in (dq3, dq2, dq1)]
     att = merged((s0, s1, s2, s3), outs)
@@ -300,11 +306,7 @@
         + dq2[0:192, :].astype(F32)
         + dq3[0:192, :].astype(F32)
     ).T
-    d_kv = dkv0[...].astype(F32) + dkv1[0:256, :].astype(F32)
-    for half in range(2):
-        lanes = slice(384 * half, 384 * half + 384)
-        other = dkv1[256 + 96 * half : 352 + 96 * half, :]
-        mlp_sum[:, lanes] = (mlp[:, lanes].astype(F32) + other.astype(F32)).astype(BF)
+    d_kv = dkv0[...].astype(F32) + dkv1[...].astype(F32)
     both = jnp.concatenate([d_query, d_kv[:, :192]], axis=1)
     cosine, left_sine, right_sine = spin_tables(coords, order, table)
     pieces = []
@@ -481,18 +483,23 @@
     d_kv, *d_qs = backward((0, 1), [whole], d_q, True, (far,))
     d_queries = [d_qs[0]] + [hop(d_qs[j], "y", j) for j in (1, 2, 3)]
     d_kv_send, d_kv_own = call(
-        key_sum_kernel, [((448, 384), BF), ((256, 384), BF)], (d_kv, far, *near, grads_mlp), 0
+        key_sum_kernel, [((256, 384), BF), ((256, 384), BF)], (d_kv, far, *near), 0
     )
     d_kv_other = hop(d_kv_send, "xl", 1)
-    *pieces, upstream, grads_mlp = call(
+    (grads_mlp,) = call(keep_kernel, [((96, 768), BF)], (grads_mlp, d_kv_other), 0, unread=1)
+    mlp_other = hop(grads_mlp, "xl", 1)
+    *pieces, upstream = call(
         tail_kernel,
-        [((208, 768), BF)] * 4 + [((512, 768), BF), ((96, 768), BF)],
+        [((208, 768), BF)] * 4 + [((512, 768), BF)],
         (coords, block_order, table, tokens, cotangent, ln_attn, w_turned, gain_attn, gain_mlp,
          *d_queries, d_kv_own, d_kv_other, *stats_all, outs[0], w_dense, part_mlp,
-         d_ln_mlp, small_mlp, grads_mlp),
+         d_ln_mlp, small_mlp),
         2,
         scratch=[pltpu.VMEM((4, 192, 768), BF)],
         mib=60,
+    )
+    (grads_mlp,) = call(
+        pair_kernel, [((96, 768), BF)], (grads_mlp, mlp_other, upstream), 0, unread=1
     )
     grads_mlp = lax.all_gather(grads_mlp, ("z", "y"), axis=0, tiled=True)
 

time: 199 us -> 193 us (0.970)
  waiting for transfers between devices: 54.4 us -> 45.9 us
    reduce_scatter x1, waiting for transfers between devices: 6.15 us -> 0.02 us  [on_device(): lax.psum_scatter(grads_mlp, ('z', 'y'), scatter_dimension=0, tiled=True)]
    ppermute x37 -> x38, waiting for transfers between devices: 48.2 us -> 45.8 us  [hop(): return lax.ppermute(x, axis, [(i, (i + step) % n) for i in range(n)])]
    ppermute x37 -> x38, starting transfers between devices: 58.5 us -> 59.9 us  [hop(): return lax.ppermute(x, axis, [(i, (i + step) % n) for i in range(n)])]
    unnamed x57 -> x59, local copies, waits for them, and re-layouts: 6.28 us -> 6.73 us
    pallas_call x12 -> x14, Pallas kernels: 62.3 us -> 62.7 us  [call(): pl.pallas_call(kernel, out_shape=shapes, in_specs=[smem] * scalars + [vme...]
  transfers between devices with their start and end apart: 39 -> 40, of which waited for: 18 -> 17; matrix products, arithmetic and copies ran while one was open for 1% -> 1% of each run, Pallas kernels for 22% -> 26%
where the time goes in v5:
time: 193 us; the launch traced here: 192 us
  Pallas kernels  62.7 us (32%)
  starting transfers between devices  60 us (31%)
  waiting for transfers between devices  45.9 us (24%)
  between operations  14.5 us (8%)
  local copies, waits for them, and re-layouts  8.59 us (4%)
    pallas_call x14, Pallas kernels, call(): pl.pallas_call(kernel, out_shape=shapes, in_specs=[smem] * scalars + [vme...  62.7 us
    ppermute x38, starting transfers between devices, hop(): return lax.ppermute(x, axis, [(i, (i + step) % n) for i in range(n)])  59.9 us
    ppermute x38, waiting for transfers between devices, hop(): return lax.ppermute(x, axis, [(i, (i + step) % n) for i in range(n)])  45.8 us
    unnamed x59, local copies, waits for them, and re-layouts  6.73 us
  transfers between devices with their start and end apart: 40, of which 17 were waited for; matrix products, arithmetic and copies ran while one was open for 1% of the time, Pallas kernels for 26%

profile of v5, /device:TPU:0, one launch (start us, length us, event | category | flops | bytes accessed | tf_op | source)
XLA Modules:
  0.0 192.5 jit_solution(12680818718775939370)
XLA Ops:
  7.8 6.9 %shard_map.263 = (bf16[256,384]{1,0:T(8,128)(2,1)}, bf16[256,384]{1,0:T(8,128)(2,1)}, bf16[256,768]{1,0:T(8,128)(2,1)}, bf16[1536,768]{1,0:T(8,128)(2,1)}, f32[8...) custom-call(s32[3]{0:T(128)} %pad_add_fusion.coords, s32[64]{0:T(128)} %order.11, ...), custom_call_target="tpu_custom_call" | custom-call | bytes 1024 | tf_op jit(solution)/shard_map/pallas_call | solution.py:392
  15.7 1.6 collective-permute-start.3
  17.2 1.9 collective-permute-start.6
  19.1 2.1 %collective-permute-start.4 = (bf16[256,384]{1,0:T(8,128)(2,1)S(1)}, bf16[256,384]{1,0:T(8,128)(2,1)S(1)}, u32[]{:S(2)}, u32[]{:S(2)}) collective-permute-start(bf16[256,384]{1,0:T(8,128)(2,1)S(1)} %copy-done.7), channel_id=1, source_target_pairs={{0,48},{16,0},{32,16},{48,32},{1,49},{17,1},{33,17},{49,33},{2,50}... | collective-permute-start | bytes 589832 | tf_op jit(solution)/shard_map/ppermute | solution.py:407
  21.3 1.6 collective-permute-start.2
  22.9 3.6 %collective-permute-start.5 = (bf16[256,384]{1,0:T(8,128)(2,1)S(1)}, bf16[256,384]{1,0:T(8,128)(2,1)S(1)}, u32[]{:S(2)}, u32[]{:S(2)}) collective-permute-start(bf16[256,384]{1,0:T(8,128)(2,1)S(1)} %collective-permute-done.3.refs_5_.refs_6_), channel_id=1, source_target_pairs={{0,48},{16,0},{32,16},{48,32},{1,49},{17,1},{33,17},{49,33},{2,50}... | collective-permute-start | bytes 589832 | tf_op jit(solution)/shard_map/ppermute | solution.py:407
  26.4 3.2 %collective-permute-start.1 = (bf16[256,384]{1,0:T(8,128)(2,1)S(1)}, bf16[256,384]{1,0:T(8,128)(2,1)S(1)}, u32[]{:S(2)}, u32[]{:S(2)}) collective-permute-start(bf16[256,384]{1,0:T(8,128)(2,1)S(1)} %copy-done.2), channel_id=1, source_target_pairs={{0,8},{4,12},{8,0},{12,4},{1,9},{5,13},{9,1},{13,5},{2,10},{6,14},... | collective-permute-start | bytes 589832 | tf_op jit(solution)/shard_map/ppermute | solution.py:407
  29.6 1.1 collective-permute-start
  30.8 3.4 %collective-permute-start.8 = (bf16[256,384]{1,0:T(8,128)(2,1)S(1)}, bf16[256,384]{1,0:T(8,128)(2,1)S(1)}, u32[]{:S(2)}, u32[]{:S(2)}) collective-permute-start(bf16[256,384]{1,0:T(8,128)(2,1)S(1)} %collective-permute-done.5.refs_7_.refs_6_), channel_id=1, source_target_pairs={{0,48},{16,0},{32,16},{48,32},{1,49},{17,1},{33,17},{49,33},{2,50}... | collective-permute-start | bytes 589832 | tf_op jit(solution)/shard_map/ppermute | solution.py:407
  35.1 4.5 %collective-permute-done.refs_1_.refs_5_.refs_2_ = bf16[256,384]{1,0:T(8,128)(2,1)S(1)} collective-permute-done((bf16[256,384]{1,0:T(8,128)(2,1)S(1)}, bf16[256,384]{1,0:T(8,128)(2,1)S(1)}, u32[]{:S(2)}, u32[]{:S(2)}) %collective-permute-start) | collective-permute-done | bytes 196640 | tf_op jit(solution)/shard_map/ppermute | solution.py:407
  39.6 3.5 %collective-permute-done.7.refs_8_ = bf16[256,384]{1,0:T(8,128)(2,1)S(1)} collective-permute-done((bf16[256,384]{1,0:T(8,128)(2,1)S(1)}, bf16[256,384]{1,0:T(8,128)(2,1)S(1)}, u32[]{:S(2)}, u32[]{:S(2)}) %collective-permute-start.7) | collective-permute-done | bytes 196640 | tf_op jit(solution)/shard_map/ppermute | solution.py:407
  43.1 13.2 %shard_map.264 = (bf16[192,256]{1,0:T(8,128)(2,1)S(1)}, bf16[192,256]{1,0:T(8,128)(2,1)S(1)}, bf16[192,256]{1,0:T(8,128)(2,1)S(1)}, bf16[192,256]{1,0:T(8,128)(2,1)S(1)}, f32[4,8,256]{2,1,0:T(8,128)S(1)}) custom-call(s32[3]{0:T(128)S(1)} %copy-done.17, s32[64]{0:T(128)S(1)} %copy-done.19, bf16[256,384]{1,0:T(8,128)(2,1)S(1)} %copy-done.2, ...), custom_call_target="tpu_custom_call" | custom-call | bytes 1024 | tf_op jit(solution)/shard_map/pallas_call | solution.py:392
  56.3 1.4 collective-permute-start.12
  58.5 2.3 %collective-permute-start.10 = (f32[4,8,256]{2,1,0:T(8,128)S(1)}, f32[4,8,256]{2,1,0:T(8,128)S(1)}, u32[]{:S(2)}, u32[]{:S(2)}) collective-permute-start(f32[4,8,256]{2,1,0:T(8,128)S(1)} %get-tuple-element.57.refs_0_.s0), channel_id=1, source_target_pairs={{0,12},{4,0},{8,4},{12,8},{1,13},{5,1},{9,5},{13,9},{2,14},{6,2},{... | collective-permute-start | bytes 98312 | tf_op jit(solution)/shard_map/ppermute | solution.py:407
  61.6 1.6 collective-permute-done.11.refs_2_.s2
  63.2 6.9 %shard_map.265 = (f32[4,8,256]{2,1,0:T(8,128)S(1)}, bf16[2,256,384]{2,1,0:T(8,128)(2,1)S(1)}, f32[4,192,256]{2,1,0:T(8,128)S(1)}) custom-call(s32[3]{0:T(128)S(1)} %copy-done.17, s32[64]{0:T(128)S(1)} %copy-done.19, f32[4,8,256]{2,1,0:T(8,128)S(1)} %get-tuple-element.57.refs_0_.s0, f32[4,8,256]{2,1,0:T(8,128)S(1)} %collective-permute-done.10.refs_1_.s1, ...), custom_call_target="tpu_custom_call" | custom-call | bytes 1024 | tf_op jit(solution)/shard_map/pallas_call | solution.py:392
  70.2 13.1 %shard_map.266 = (bf16[2,256,384]{2,1,0:T(8,128)(2,1)S(1)}, bf16[2,256,384]{2,1,0:T(8,128)(2,1)S(1)}, f32[4,192,256]{2,1,0:T(8,128)S(1)}) custom-call(s32[3]{0:T(128)S(1)} %copy-done.17, s32[64]{0:T(128)S(1)} %copy-done.19, f32[4,8,256]{2,1,0:T(8,128)S(1)} %get-tuple-element.58.refs_0_, bf16[256,384]{1,0:T(8,128)(2,1)S(1)} %copy-done.2, ...), custom_call_target="tpu_custom_call" | custom-call | bytes 1024 | tf_op jit(solution)/shard_map/pallas_call | solution.py:392
  83.3 1.7 collective-permute-start.17
  85.0 1.6 collective-permute-start.18
  86.6 6.9 %shard_map.267 = (bf16[2,256,384]{2,1,0:T(8,128)(2,1)S(1)}, bf16[192,256]{1,0:T(8,128)(2,1)S(1)}, bf16[384,256]{1,0:T(8,128)(2,1)S(1)}, bf16[384,256]{1,0:T(8,128)(2,1)S(1)}, bf16[384,256]{1,0:T(8,128)(2,1)S(1)}) custom-call(s32[3]{0:T(128)S(1)} %copy-done.17, s32[64]{0:T(128)S(1)} %copy-done.19, f32[4,8,256]{2,1,0:T(8,128)S(1)} %get-tuple-element.58.refs_0_, ...), custom_call_target="tpu_custom_call" | custom-call | bytes 1024 | tf_op jit(solution)/shard_map/pallas_call | solution.py:392
  94.8 1.2 collective-permute-start.19
  96.0 1.8 collective-permute-start.14
  97.8 3.1 %collective-permute-start.15 = (bf16[384,256]{1,0:T(8,128)(2,1)S(1)}, bf16[384,256]{1,0:T(8,128)(2,1)S(1)}, u32[]{:S(2)}, u32[]{:S(2)}) collective-permute-start(bf16[384,256]{1,0:T(8,128)(2,1)S(1)} %get-tuple-element.67), channel_id=1, source_target_pairs={{0,8},{4,12},{8,0},{12,4},{1,9},{5,13},{9,1},{13,5},{2,10},{6,14},... | collective-permute-start | bytes 589832 | tf_op jit(solution)/shard_map/ppermute | solution.py:407
  101.9 2.3 %collective-permute-start.35 = (bf16[96,768]{1,0:T(8,128)(2,1)S(1)}, bf16[96,768]{1,0:T(8,128)(2,1)S(1)}, u32[]{:S(2)}, u32[]{:S(2)}) collective-permute-start(bf16[96,768]{1,0:T(8,128)(2,1)S(1)} %shard_map.274.x), channel_id=1, source_target_pairs={{0,64},{64,0},{1,65},{65,1},{2,66},{66,2},{3,67},{67,3},{4,68},{68... | collective-permute-start | bytes 442376 | tf_op jit(solution)/shard_map/ppermute | solution.py:407
  104.3 2.4 %collective-permute-done.15.dq2 = bf16[384,256]{1,0:T(8,128)(2,1)S(1)} collective-permute-done((bf16[384,256]{1,0:T(8,128)(2,1)S(1)}, bf16[384,256]{1,0:T(8,128)(2,1)S(1)}, u32[]{:S(2)}, u32[]{:S(2)}) %collective-permute-start.15) | collective-permute-done | bytes 196640 | tf_op jit(solution)/shard_map/ppermute | solution.py:407
  107.4 5.8 %shard_map.269 = (bf16[208,768]{1,0:T(8,128)(2,1)}, bf16[208,768]{1,0:T(8,128)(2,1)}, bf16[208,768]{1,0:T(8,128)(2,1)}, bf16[208,768]{1,0:T(8,128)(2,1)}, bf16[512,768]{1,0:T(8,128)(2,1)}) custom-call(s32[3]{0:T(128)} %pad_add_fusion.coords, s32[64]{0:T(128)} %order.11, f32[8,128]{1,0:T(8,128)} %constant.17.clone.table, bf16[256,768]{1,0:T(8,128)(2,1)} %tok.5, ...), custom_call_target="tpu_custom_call" | custom-call | bytes 1024 | tf_op jit(solution)/shard_map/pallas_call | solution.py:392
  113.2 1.1 copy-done.3
  115.6 3.1 %collective-permute-start.23 = (bf16[208,768]{1,0:T(8,128)(2,1)}, bf16[208,768]{1,0:T(8,128)(2,1)S(1)}, u32[]{:S(2)}, u32[]{:S(2)}) collective-permute-start(bf16[208,768]{1,0:T(8,128)(2,1)} %get-tuple-element.83), channel_id=1, source_target_pairs={{0,8},{4,12},{8,0},{12,4},{1,9},{5,13},{9,1},{13,5},{2,10},{6,14},... | collective-permute-start | bytes 958472 | tf_op jit(solution)/shard_map/ppermute | solution.py:407
  119.3 7.5 %collective-permute-done.22.p1 = bf16[208,768]{1,0:T(8,128)(2,1)S(1)} collective-permute-done((bf16[208,768]{1,0:T(8,128)(2,1)}, bf16[208,768]{1,0:T(8,128)(2,1)S(1)}, u32[]{:S(2)}, u32[]{:S(2)}) %collective-permute-start.22) | collective-permute-done | bytes 319520 | tf_op jit(solution)/shard_map/ppermute | solution.py:407
  126.8 8.4 %collective-permute-done.23.p2 = bf16[208,768]{1,0:T(8,128)(2,1)S(1)} collective-permute-done((bf16[208,768]{1,0:T(8,128)(2,1)}, bf16[208,768]{1,0:T(8,128)(2,1)S(1)}, u32[]{:S(2)}, u32[]{:S(2)}) %collective-permute-start.23) | collective-permute-done | bytes 319520 | tf_op jit(solution)/shard_map/ppermute | solution.py:407
  137.8 2.5 %collective-permute-start.25 = (bf16[64,768]{1,0:T(8,128)(2,1)S(1)}, bf16[64,768]{1,0:T(8,128)(2,1)S(1)}, u32[]{:S(2)}, u32[]{:S(2)}) collective-permute-start(bf16[64,768]{1,0:T(8,128)(2,1)S(1)} %get-tuple-element.86), channel_id=1, source_target_pairs={{0,16},{16,32},{32,48},{48,0},{1,17},{17,33},{33,49},{49,1},{2,18}... | collective-permute-start | bytes 294920 | tf_op jit(solution)/shard_map/ppermute | solution.py:407
  140.3 1.3 collective-permute-start.26
  141.6 1.4 collective-permute-start.27
  143.1 1.1 collective-permute-done.25.b1
  144.2 2.2 %collective-permute-done.26.b2 = bf16[64,768]{1,0:T(8,128)(2,1)S(1)} collective-permute-done((bf16[64,768]{1,0:T(8,128)(2,1)S(1)}, bf16[64,768]{1,0:T(8,128)(2,1)S(1)}, u32[]{:S(2)}, u32[]{:S(2)}) %collective-permute-start.26) | collective-permute-done | bytes 98336 | tf_op jit(solution)/shard_map/ppermute | solution.py:407
  147.9 3.2 %collective-permute-start.21 = (bf16[512,768]{1,0:T(8,128)(2,1)S(1)}, bf16[512,768]{1,0:T(8,128)(2,1)S(1)}, u32[]{:S(2)}, u32[]{:S(2)}) collective-permute-start(bf16[512,768]{1,0:T(8,128)(2,1)S(1)} %add_convert_fusion.e0), channel_id=1, source_target_pairs={{0,2},{2,0},{1,3},{3,1},{4,6},{6,4},{5,7},{7,5},{8,10},{10,8},{9,1... | collective-permute-start | bytes 2359304 | tf_op jit(solution)/shard_map/ppermute | solution.py:407
  151.1 1.8 collective-permute-done.28
  152.9 1.3 collective-permute-start.31
  154.2 2.9 %collective-permute-start.30 = (bf16[48,768]{1,0:T(8,128)(2,1)S(1)}, bf16[48,768]{1,0:T(8,128)(2,1)S(1)}, u32[]{:S(2)}, u32[]{:S(2)}) collective-permute-start(bf16[48,768]{1,0:T(8,128)(2,1)S(1)} %slice.59.b0), channel_id=1, source_target_pairs={{0,32},{16,48},{32,0},{48,16},{1,33},{17,49},{33,1},{49,17},{2,34}... | collective-permute-start | bytes 221192 | tf_op jit(solution)/shard_map/ppermute | solution.py:407
  158.2 1.9 collective-permute-done.31.b3
  160.1 2.8 %collective-permute-done.30.b2 = bf16[48,768]{1,0:T(8,128)(2,1)S(1)} collective-permute-done((bf16[48,768]{1,0:T(8,128)(2,1)S(1)}, bf16[48,768]{1,0:T(8,128)(2,1)S(1)}, u32[]{:S(2)}, u32[]{:S(2)}) %collective-permute-start.30) | collective-permute-done | bytes 73760 | tf_op jit(solution)/shard_map/ppermute | solution.py:407
  163.5 1.2 collective-permute-start.34
  164.8 3.1 %collective-permute-start.33 = (bf16[4,48,768]{2,1,0:T(8,128)(2,1)S(1)}, bf16[4,48,768]{2,1,0:T(8,128)(2,1)S(1)}, u32[]{:S(2)}, u32[]{:S(2)}) collective-permute-start(bf16[4,48,768]{2,1,0:T(8,128)(2,1)S(1)} %shard_map.273.p0), channel_id=1, source_target_pairs={{0,8},{4,12},{8,0},{12,4},{1,9},{5,13},{9,1},{13,5},{2,10},{6,14},... | collective-permute-start | bytes 884744 | tf_op jit(solution)/shard_map/ppermute | solution.py:407
  167.9 3.0 %collective-permute-start.37 = (f32[8,768]{1,0:T(8,128)S(1)}, f32[8,768]{1,0:T(8,128)S(1)}, u32[]{:S(2)}, u32[]{:S(2)}) collective-permute-start(f32[8,768]{1,0:T(8,128)S(1)} %slice_add_fusion), channel_id=1, source_target_pairs={{0,2},{2,0},{1,3},{3,1},{4,6},{6,4},{5,7},{7,5},{8,10},{10,8},{9,1... | collective-permute-start | bytes 73736 | tf_op jit(solution)/shard_map/ppermute | solution.py:407
  171.5 1.8 collective-permute-done.37
  174.0 1.7 shard_map.270
  175.6 3.3 %collective-permute-done.33.p2 = bf16[4,48,768]{2,1,0:T(8,128)(2,1)S(1)} collective-permute-done((bf16[4,48,768]{2,1,0:T(8,128)(2,1)S(1)}, bf16[4,48,768]{2,1,0:T(8,128)(2,1)S(1)}, u32[]{:S(2)}, u32[]{:S(2)}) %collective-permute-start.33) | collective-permute-done | bytes 294944 | tf_op jit(solution)/shard_map/ppermute | solution.py:407
  179.8 5.3 %shard_map.276 = (f32[576,768]{1,0:T(8,128)}, f32[192,768]{1,0:T(8,128)}, f32[768,768]{1,0:T(8,128)}, f32[768,768]{1,0:T(8,128)}) custom-call(s32[3]{0:T(128)} %pad_add_fusion.coords, bf16[4,48,768]{2,1,0:T(8,128)(2,1)} %copy-done.5, bf16[4,48,768]{2,1,0:T(8,128)(2,1)} %copy-done.24, bf16[4,48,768]{2,1,0:T(8,128)(2,1)} %copy-done.23, ...), custom_call_target="tpu_custom_call" | custom-call | bytes 1024 | tf_op jit(solution)/shard_map/pallas_call | solution.py:392
  (117 shorter events, 17.5 us)
Async XLA Ops:
  7.2 93.8 %reduce-scatter.2.cloned.1.call-start = ((), (), s32[]{:S(2)}) async-start(), calls=%async_computation.1 | async-start | bytes 2506752 | tf_op jit(solution)/shard_map/reduce_scatter | solution.py:444
  14.7 28.4 %copy-start.17 = (s32[3]{0:T(128)S(1)}, s32[3]{0:T(128)}, u32[]{:S(2)}) copy-start(s32[3]{0:T(128)} %pad_add_fusion.coords) | copy-start | bytes 40
  14.8 28.3 %copy-start.19 = (s32[64]{0:T(128)S(1)}, s32[64]{0:T(128)}, u32[]{:S(2)}) copy-start(s32[64]{0:T(128)} %order.11) | copy-start | bytes 772
  14.8 164.2 %all-gather.2.cloned.1.call-start = ((), (), s32[]{:S(2)}) async-start(), calls=%async_computation.2 | async-start | bytes 2506752 | tf_op jit(solution)/shard_map/all_gather | solution.py:504
  15.7 7.2 %collective-permute-start.3 = (bf16[256,384]{1,0:T(8,128)(2,1)S(1)}, bf16[256,384]{1,0:T(8,128)(2,1)S(1)}, u32[]{:S(2)}, u32[]{:S(2)}) collective-permute-start(bf16[256,384]{1,0:T(8,128)(2,1)S(1)} %copy-done.7), channel_id=1, source_target_pairs={{0,64},{64,0},{1,65},{65,1},{2,66},{66,2},{3,67},{67,3},{4,68},{68... | collective-permute-start | bytes 589832 | tf_op jit(solution)/shard_map/ppermute | solution.py:407
  17.2 12.4 %collective-permute-start.6 = (bf16[256,384]{1,0:T(8,128)(2,1)S(1)}, bf16[256,384]{1,0:T(8,128)(2,1)S(1)}, u32[]{:S(2)}, u32[]{:S(2)}) collective-permute-start(bf16[256,384]{1,0:T(8,128)(2,1)S(1)} %copy-done.7), channel_id=1, source_target_pairs={{0,16},{16,32},{32,48},{48,0},{1,17},{17,33},{33,49},{49,1},{2,18}... | collective-permute-start | bytes 589832 | tf_op jit(solution)/shard_map/ppermute | solution.py:407
  19.1 11.5 %collective-permute-start.4 = (bf16[256,384]{1,0:T(8,128)(2,1)S(1)}, bf16[256,384]{1,0:T(8,128)(2,1)S(1)}, u32[]{:S(2)}, u32[]{:S(2)}) collective-permute-start(bf16[256,384]{1,0:T(8,128)(2,1)S(1)} %copy-done.7), channel_id=1, source_target_pairs={{0,48},{16,0},{32,16},{48,32},{1,49},{17,1},{33,17},{49,33},{2,50}... | collective-permute-start | bytes 589832 | tf_op jit(solution)/shard_map/ppermute | solution.py:407
  21.3 9.4 %collective-permute-start.2 = (bf16[256,384]{1,0:T(8,128)(2,1)S(1)}, bf16[256,384]{1,0:T(8,128)(2,1)S(1)}, u32[]{:S(2)}, u32[]{:S(2)}) collective-permute-start(bf16[256,384]{1,0:T(8,128)(2,1)S(1)} %copy-done.2), channel_id=1, source_target_pairs={{0,4},{4,8},{8,12},{12,0},{1,5},{5,9},{9,13},{13,1},{2,6},{6,10},{... | collective-permute-start | bytes 589832 | tf_op jit(solution)/shard_map/ppermute | solution.py:407
  22.9 7.9 %collective-permute-start.5 = (bf16[256,384]{1,0:T(8,128)(2,1)S(1)}, bf16[256,384]{1,0:T(8,128)(2,1)S(1)}, u32[]{:S(2)}, u32[]{:S(2)}) collective-permute-start(bf16[256,384]{1,0:T(8,128)(2,1)S(1)} %collective-permute-done.3.refs_5_.refs_6_), channel_id=1, source_target_pairs={{0,48},{16,0},{32,16},{48,32},{1,49},{17,1},{33,17},{49,33},{2,50}... | collective-permute-start | bytes 589832 | tf_op jit(solution)/shard_map/ppermute | solution.py:407
  26.4 8.7 %collective-permute-start.1 = (bf16[256,384]{1,0:T(8,128)(2,1)S(1)}, bf16[256,384]{1,0:T(8,128)(2,1)S(1)}, u32[]{:S(2)}, u32[]{:S(2)}) collective-permute-start(bf16[256,384]{1,0:T(8,128)(2,1)S(1)} %copy-done.2), channel_id=1, source_target_pairs={{0,8},{4,12},{8,0},{12,4},{1,9},{5,13},{9,1},{13,5},{2,10},{6,14},... | collective-permute-start | bytes 589832 | tf_op jit(solution)/shard_map/ppermute | solution.py:407
  29.6 10.0 %collective-permute-start = (bf16[256,384]{1,0:T(8,128)(2,1)S(1)}, bf16[256,384]{1,0:T(8,128)(2,1)S(1)}, u32[]{:S(2)}, u32[]{:S(2)}) collective-permute-start(bf16[256,384]{1,0:T(8,128)(2,1)S(1)} %copy-done.2), channel_id=1, source_target_pairs={{0,12},{4,0},{8,4},{12,8},{1,13},{5,1},{9,5},{13,9},{2,14},{6,2},{... | collective-permute-start | bytes 589832 | tf_op jit(solution)/shard_map/ppermute | solution.py:407
  30.7 12.4 %collective-permute-start.9 = (bf16[256,384]{1,0:T(8,128)(2,1)S(1)}, bf16[256,384]{1,0:T(8,128)(2,1)S(1)}, u32[]{:S(2)}, u32[]{:S(2)}) collective-permute-start(bf16[256,384]{1,0:T(8,128)(2,1)S(1)} %collective-permute-done.3.refs_5_.refs_6_), channel_id=1, source_target_pairs={{0,16},{16,32},{32,48},{48,0},{1,17},{17,33},{33,49},{49,1},{2,18}... | collective-permute-start | bytes 589832 | tf_op jit(solution)/shard_map/ppermute | solution.py:407
  30.7 12.4 %collective-permute-start.7 = (bf16[256,384]{1,0:T(8,128)(2,1)S(1)}, bf16[256,384]{1,0:T(8,128)(2,1)S(1)}, u32[]{:S(2)}, u32[]{:S(2)}) collective-permute-start(bf16[256,384]{1,0:T(8,128)(2,1)S(1)} %collective-permute-done.6.refs_10_.refs_7_), channel_id=1, source_target_pairs={{0,16},{16,32},{32,48},{48,0},{1,17},{17,33},{33,49},{49,1},{2,18}... | collective-permute-start | bytes 589832 | tf_op jit(solution)/shard_map/ppermute | solution.py:407
  30.8 12.3 %collective-permute-start.8 = (bf16[256,384]{1,0:T(8,128)(2,1)S(1)}, bf16[256,384]{1,0:T(8,128)(2,1)S(1)}, u32[]{:S(2)}, u32[]{:S(2)}) collective-permute-start(bf16[256,384]{1,0:T(8,128)(2,1)S(1)} %collective-permute-done.5.refs_7_.refs_6_), channel_id=1, source_target_pairs={{0,48},{16,0},{32,16},{48,32},{1,49},{17,1},{33,17},{49,33},{2,50}... | collective-permute-start | bytes 589832 | tf_op jit(solution)/shard_map/ppermute | solution.py:407
  56.3 26.9 %copy-start.11 = (f32[4,8,256]{2,1,0:T(8,128)}, f32[4,8,256]{2,1,0:T(8,128)S(1)}, u32[]{:S(2)}) copy-start(f32[4,8,256]{2,1,0:T(8,128)S(1)} %get-tuple-element.57.refs_0_.s0) | copy-start | bytes 98308
  56.3 5.3 %collective-permute-start.12 = (f32[4,8,256]{2,1,0:T(8,128)S(1)}, f32[4,8,256]{2,1,0:T(8,128)S(1)}, u32[]{:S(2)}, u32[]{:S(2)}) collective-permute-start(f32[4,8,256]{2,1,0:T(8,128)S(1)} %get-tuple-element.57.refs_0_.s0), channel_id=1, source_target_pairs={{0,4},{4,8},{8,12},{12,0},{1,5},{5,9},{9,13},{13,1},{2,6},{6,10},{... | collective-permute-start | bytes 98312 | tf_op jit(solution)/shard_map/ppermute | solution.py:407
  57.8 5.4 %collective-permute-start.11 = (f32[4,8,256]{2,1,0:T(8,128)S(1)}, f32[4,8,256]{2,1,0:T(8,128)S(1)}, u32[]{:S(2)}, u32[]{:S(2)}) collective-permute-start(f32[4,8,256]{2,1,0:T(8,128)S(1)} %get-tuple-element.57.refs_0_.s0), channel_id=1, source_target_pairs={{0,8},{4,12},{8,0},{12,4},{1,9},{5,13},{9,1},{13,5},{2,10},{6,14},... | collective-permute-start | bytes 98312 | tf_op jit(solution)/shard_map/ppermute | solution.py:407
  58.5 4.7 %collective-permute-start.10 = (f32[4,8,256]{2,1,0:T(8,128)S(1)}, f32[4,8,256]{2,1,0:T(8,128)S(1)}, u32[]{:S(2)}, u32[]{:S(2)}) collective-permute-start(f32[4,8,256]{2,1,0:T(8,128)S(1)} %get-tuple-element.57.refs_0_.s0), channel_id=1, source_target_pairs={{0,12},{4,0},{8,4},{12,8},{1,13},{5,1},{9,5},{13,9},{2,14},{6,2},{... | collective-permute-start | bytes 98312 | tf_op jit(solution)/shard_map/ppermute | solution.py:407
  70.1 16.5 %collective-permute-start.13 = (bf16[2,256,384]{2,1,0:T(8,128)(2,1)S(1)}, bf16[2,256,384]{2,1,0:T(8,128)(2,1)S(1)}, u32[]{:S(2)}, u32[]{:S(2)}) collective-permute-start(bf16[2,256,384]{2,1,0:T(8,128)(2,1)S(1)} %get-tuple-element.64), channel_id=1, source_target_pairs={{0,32},{16,48},{32,0},{48,16},{1,33},{17,49},{33,1},{49,17},{2,34}... | collective-permute-start | bytes 1179656 | tf_op jit(solution)/shard_map/ppermute | solution.py:407
  83.3 10.2 %collective-permute-start.17 = (bf16[2,256,384]{2,1,0:T(8,128)(2,1)S(1)}, bf16[2,256,384]{2,1,0:T(8,128)(2,1)S(1)}, u32[]{:S(2)}, u32[]{:S(2)}) collective-permute-start(bf16[2,256,384]{2,1,0:T(8,128)(2,1)S(1)} %get-tuple-element.70), channel_id=1, source_target_pairs={{0,16},{16,32},{32,48},{48,0},{1,17},{17,33},{33,49},{49,1},{2,18}... | collective-permute-start | bytes 1179656 | tf_op jit(solution)/shard_map/ppermute | solution.py:407
  85.0 9.0 %collective-permute-start.18 = (bf16[2,256,384]{2,1,0:T(8,128)(2,1)S(1)}, bf16[2,256,384]{2,1,0:T(8,128)(2,1)S(1)}, u32[]{:S(2)}, u32[]{:S(2)}) collective-permute-start(bf16[2,256,384]{2,1,0:T(8,128)(2,1)S(1)} %get-tuple-element.71), channel_id=1, source_target_pairs={{0,48},{16,0},{32,16},{48,32},{1,49},{17,1},{33,17},{49,33},{2,50}... | collective-permute-start | bytes 1179656 | tf_op jit(solution)/shard_map/ppermute | solution.py:407
  94.8 6.1 %collective-permute-start.19 = (bf16[256,384]{1,0:T(8,128)(2,1)S(1)}, bf16[256,384]{1,0:T(8,128)(2,1)S(1)}, u32[]{:S(2)}, u32[]{:S(2)}) collective-permute-start(bf16[256,384]{1,0:T(8,128)(2,1)S(1)} %get-tuple-element.73), channel_id=1, source_target_pairs={{0,64},{64,0},{1,65},{65,1},{2,66},{66,2},{3,67},{67,3},{4,68},{68... | collective-permute-start | bytes 589832 | tf_op jit(solution)/shard_map/ppermute | solution.py:407
  96.0 8.3 %collective-permute-start.14 = (bf16[384,256]{1,0:T(8,128)(2,1)S(1)}, bf16[384,256]{1,0:T(8,128)(2,1)S(1)}, u32[]{:S(2)}, u32[]{:S(2)}) collective-permute-start(bf16[384,256]{1,0:T(8,128)(2,1)S(1)} %get-tuple-element.66), channel_id=1, source_target_pairs={{0,4},{4,8},{8,12},{12,0},{1,5},{5,9},{9,13},{13,1},{2,6},{6,10},{... | collective-permute-start | bytes 589832 | tf_op jit(solution)/shard_map/ppermute | solution.py:407
  97.8 8.8 %collective-permute-start.15 = (bf16[384,256]{1,0:T(8,128)(2,1)S(1)}, bf16[384,256]{1,0:T(8,128)(2,1)S(1)}, u32[]{:S(2)}, u32[]{:S(2)}) collective-permute-start(bf16[384,256]{1,0:T(8,128)(2,1)S(1)} %get-tuple-element.67), channel_id=1, source_target_pairs={{0,8},{4,12},{8,0},{12,4},{1,9},{5,13},{9,1},{13,5},{2,10},{6,14},... | collective-permute-start | bytes 589832 | tf_op jit(solution)/shard_map/ppermute | solution.py:407
  100.9 5.8 %collective-permute-start.16 = (bf16[384,256]{1,0:T(8,128)(2,1)S(1)}, bf16[384,256]{1,0:T(8,128)(2,1)S(1)}, u32[]{:S(2)}, u32[]{:S(2)}) collective-permute-start(bf16[384,256]{1,0:T(8,128)(2,1)S(1)} %get-tuple-element.68), channel_id=1, source_target_pairs={{0,12},{4,0},{8,4},{12,8},{1,13},{5,1},{9,5},{13,9},{2,14},{6,2},{... | collective-permute-start | bytes 589832 | tf_op jit(solution)/shard_map/ppermute | solution.py:407
  101.9 11.3 %collective-permute-start.35 = (bf16[96,768]{1,0:T(8,128)(2,1)S(1)}, bf16[96,768]{1,0:T(8,128)(2,1)S(1)}, u32[]{:S(2)}, u32[]{:S(2)}) collective-permute-start(bf16[96,768]{1,0:T(8,128)(2,1)S(1)} %shard_map.274.x), channel_id=1, source_target_pairs={{0,64},{64,0},{1,65},{65,1},{2,66},{66,2},{3,67},{67,3},{4,68},{68... | collective-permute-start | bytes 442376 | tf_op jit(solution)/shard_map/ppermute | solution.py:407
  107.4 28.5 %copy-start.18 = (s32[3]{0:T(128)S(1)}, s32[3]{0:T(128)}, u32[]{:S(2)}) copy-start(s32[3]{0:T(128)} %pad_add_fusion.coords) | copy-start | bytes 40
  114.4 33.3 %copy-start.4 = (bf16[512,768]{1,0:T(8,128)(2,1)S(1)}, bf16[512,768]{1,0:T(8,128)(2,1)}, u32[]{:S(2)}) copy-start(bf16[512,768]{1,0:T(8,128)(2,1)} %get-tuple-element.78.after) | copy-start | bytes 2359300
  115.1 32.6 %collective-permute-start.20 = (bf16[512,768]{1,0:T(8,128)(2,1)}, bf16[512,768]{1,0:T(8,128)(2,1)S(1)}, u32[]{:S(2)}, u32[]{:S(2)}) collective-permute-start(bf16[512,768]{1,0:T(8,128)(2,1)} %get-tuple-element.78.after), channel_id=1, source_target_pairs={{0,1},{1,0},{2,3},{3,2},{4,5},{5,4},{6,7},{7,6},{8,9},{9,8},{10,11... | collective-permute-start | bytes 2359304 | tf_op jit(solution)/shard_map/ppermute | solution.py:407
  115.2 11.6 %collective-permute-start.22 = (bf16[208,768]{1,0:T(8,128)(2,1)}, bf16[208,768]{1,0:T(8,128)(2,1)S(1)}, u32[]{:S(2)}, u32[]{:S(2)}) collective-permute-start(bf16[208,768]{1,0:T(8,128)(2,1)} %get-tuple-element.82), channel_id=1, source_target_pairs={{0,4},{4,8},{8,12},{12,0},{1,5},{5,9},{9,13},{13,1},{2,6},{6,10},{... | collective-permute-start | bytes 958472 | tf_op jit(solution)/shard_map/ppermute | solution.py:407
  115.6 19.6 %collective-permute-start.23 = (bf16[208,768]{1,0:T(8,128)(2,1)}, bf16[208,768]{1,0:T(8,128)(2,1)S(1)}, u32[]{:S(2)}, u32[]{:S(2)}) collective-permute-start(bf16[208,768]{1,0:T(8,128)(2,1)} %get-tuple-element.83), channel_id=1, source_target_pairs={{0,8},{4,12},{8,0},{12,4},{1,9},{5,13},{9,1},{13,5},{2,10},{6,14},... | collective-permute-start | bytes 958472 | tf_op jit(solution)/shard_map/ppermute | solution.py:407
  118.7 17.2 %collective-permute-start.24 = (bf16[208,768]{1,0:T(8,128)(2,1)}, bf16[208,768]{1,0:T(8,128)(2,1)S(1)}, u32[]{:S(2)}, u32[]{:S(2)}) collective-permute-start(bf16[208,768]{1,0:T(8,128)(2,1)} %get-tuple-element.84), channel_id=1, source_target_pairs={{0,12},{4,0},{8,4},{12,8},{1,13},{5,1},{9,5},{13,9},{2,14},{6,2},{... | collective-permute-start | bytes 958472 | tf_op jit(solution)/shard_map/ppermute | solution.py:407
  137.8 6.4 %collective-permute-start.25 = (bf16[64,768]{1,0:T(8,128)(2,1)S(1)}, bf16[64,768]{1,0:T(8,128)(2,1)S(1)}, u32[]{:S(2)}, u32[]{:S(2)}) collective-permute-start(bf16[64,768]{1,0:T(8,128)(2,1)S(1)} %get-tuple-element.86), channel_id=1, source_target_pairs={{0,16},{16,32},{32,48},{48,0},{1,17},{17,33},{33,49},{49,1},{2,18}... | collective-permute-start | bytes 294920 | tf_op jit(solution)/shard_map/ppermute | solution.py:407
  140.3 6.1 %collective-permute-start.26 = (bf16[64,768]{1,0:T(8,128)(2,1)S(1)}, bf16[64,768]{1,0:T(8,128)(2,1)S(1)}, u32[]{:S(2)}, u32[]{:S(2)}) collective-permute-start(bf16[64,768]{1,0:T(8,128)(2,1)S(1)} %get-tuple-element.87), channel_id=1, source_target_pairs={{0,32},{16,48},{32,0},{48,16},{1,33},{17,49},{33,1},{49,17},{2,34}... | collective-permute-start | bytes 294920 | tf_op jit(solution)/shard_map/ppermute | solution.py:407
  141.6 4.8 %collective-permute-start.27 = (bf16[64,768]{1,0:T(8,128)(2,1)S(1)}, bf16[64,768]{1,0:T(8,128)(2,1)S(1)}, u32[]{:S(2)}, u32[]{:S(2)}) collective-permute-start(bf16[64,768]{1,0:T(8,128)(2,1)S(1)} %get-tuple-element.88), channel_id=1, source_target_pairs={{0,48},{16,0},{32,16},{48,32},{1,49},{17,1},{33,17},{49,33},{2,50}... | collective-permute-start | bytes 294920 | tf_op jit(solution)/shard_map/ppermute | solution.py:407
  147.1 26.8 %copy-start = (bf16[256,768]{1,0:T(8,128)(2,1)S(1)}, bf16[256,768]{1,0:T(8,128)(2,1)}, u32[]{:S(2)}) copy-start(bf16[256,768]{1,0:T(8,128)(2,1)} %tok.5) | copy-start | bytes 1179652
  147.1 26.8 %copy-start.1 = (bf16[256,768]{1,0:T(8,128)(2,1)S(1)}, bf16[256,768]{1,0:T(8,128)(2,1)}, u32[]{:S(2)}) copy-start(bf16[256,768]{1,0:T(8,128)(2,1)} %cot.5) | copy-start | bytes 1179652
  147.1 26.8 %copy-start.20 = (f32[768]{0:T(1024)S(1)}, f32[768]{0:T(1024)}, u32[]{:S(2)}) copy-start(f32[768]{0:T(1024)} %b_dense.1) | copy-start | bytes 9220
  147.1 5.7 %collective-permute-start.28 = (bf16[64,768]{1,0:T(8,128)(2,1)S(1)}, bf16[64,768]{1,0:T(8,128)(2,1)S(1)}, u32[]{:S(2)}, u32[]{:S(2)}) collective-permute-start(bf16[64,768]{1,0:T(8,128)(2,1)S(1)} %shard_map.272), channel_id=1, source_target_pairs={{0,64},{64,0},{1,65},{65,1},{2,66},{66,2},{3,67},{67,3},{4,68},{68... | collective-permute-start | bytes 294920 | tf_op jit(solution)/shard_map/ppermute | solution.py:407
  147.9 26.1 %collective-permute-start.21 = (bf16[512,768]{1,0:T(8,128)(2,1)S(1)}, bf16[512,768]{1,0:T(8,128)(2,1)S(1)}, u32[]{:S(2)}, u32[]{:S(2)}) collective-permute-start(bf16[512,768]{1,0:T(8,128)(2,1)S(1)} %add_convert_fusion.e0), channel_id=1, source_target_pairs={{0,2},{2,0},{1,3},{3,1},{4,6},{6,4},{5,7},{7,5},{8,10},{10,8},{9,1... | collective-permute-start | bytes 2359304 | tf_op jit(solution)/shard_map/ppermute | solution.py:407
  152.9 7.2 %collective-permute-start.31 = (bf16[48,768]{1,0:T(8,128)(2,1)S(1)}, bf16[48,768]{1,0:T(8,128)(2,1)S(1)}, u32[]{:S(2)}, u32[]{:S(2)}) collective-permute-start(bf16[48,768]{1,0:T(8,128)(2,1)S(1)} %slice.59.b0), channel_id=1, source_target_pairs={{0,16},{16,32},{32,48},{48,0},{1,17},{17,33},{33,49},{49,1},{2,18}... | collective-permute-start | bytes 221192 | tf_op jit(solution)/shard_map/ppermute | solution.py:407
  154.2 8.7 %collective-permute-start.30 = (bf16[48,768]{1,0:T(8,128)(2,1)S(1)}, bf16[48,768]{1,0:T(8,128)(2,1)S(1)}, u32[]{:S(2)}, u32[]{:S(2)}) collective-permute-start(bf16[48,768]{1,0:T(8,128)(2,1)S(1)} %slice.59.b0), channel_id=1, source_target_pairs={{0,32},{16,48},{32,0},{48,16},{1,33},{17,49},{33,1},{49,17},{2,34}... | collective-permute-start | bytes 221192 | tf_op jit(solution)/shard_map/ppermute | solution.py:407
  157.1 5.9 %collective-permute-start.29 = (bf16[48,768]{1,0:T(8,128)(2,1)S(1)}, bf16[48,768]{1,0:T(8,128)(2,1)S(1)}, u32[]{:S(2)}, u32[]{:S(2)}) collective-permute-start(bf16[48,768]{1,0:T(8,128)(2,1)S(1)} %slice.59.b0), channel_id=1, source_target_pairs={{0,48},{16,0},{32,16},{48,32},{1,49},{17,1},{33,17},{49,33},{2,50}... | collective-permute-start | bytes 221192 | tf_op jit(solution)/shard_map/ppermute | solution.py:407
  157.6 10.3 %collective-permute-start.36 = (f32[8,768]{1,0:T(8,128)S(1)}, f32[8,768]{1,0:T(8,128)S(1)}, u32[]{:S(2)}, u32[]{:S(2)}) collective-permute-start(f32[8,768]{1,0:T(8,128)S(1)} %slice.45), channel_id=1, source_target_pairs={{0,1},{1,0},{2,3},{3,2},{4,5},{5,4},{6,7},{7,6},{8,9},{9,8},{10,11... | collective-permute-start | bytes 73736 | tf_op jit(solution)/shard_map/ppermute | solution.py:407
  163.5 12.1 %collective-permute-start.34 = (bf16[4,48,768]{2,1,0:T(8,128)(2,1)S(1)}, bf16[4,48,768]{2,1,0:T(8,128)(2,1)S(1)}, u32[]{:S(2)}, u32[]{:S(2)}) collective-permute-start(bf16[4,48,768]{2,1,0:T(8,128)(2,1)S(1)} %shard_map.273.p0), channel_id=1, source_target_pairs={{0,4},{4,8},{8,12},{12,0},{1,5},{5,9},{9,13},{13,1},{2,6},{6,10},{... | collective-permute-start | bytes 884744 | tf_op jit(solution)/shard_map/ppermute | solution.py:407
  164.8 14.1 %collective-permute-start.33 = (bf16[4,48,768]{2,1,0:T(8,128)(2,1)S(1)}, bf16[4,48,768]{2,1,0:T(8,128)(2,1)S(1)}, u32[]{:S(2)}, u32[]{:S(2)}) collective-permute-start(bf16[4,48,768]{2,1,0:T(8,128)(2,1)S(1)} %shard_map.273.p0), channel_id=1, source_target_pairs={{0,8},{4,12},{8,0},{12,4},{1,9},{5,13},{9,1},{13,5},{2,10},{6,14},... | collective-permute-start | bytes 884744 | tf_op jit(solution)/shard_map/ppermute | solution.py:407
  167.9 11.1 %collective-permute-start.32 = (bf16[4,48,768]{2,1,0:T(8,128)(2,1)S(1)}, bf16[4,48,768]{2,1,0:T(8,128)(2,1)S(1)}, u32[]{:S(2)}, u32[]{:S(2)}) collective-permute-start(bf16[4,48,768]{2,1,0:T(8,128)(2,1)S(1)} %shard_map.273.p0), channel_id=1, source_target_pairs={{0,12},{4,0},{8,4},{12,8},{1,13},{5,1},{9,5},{13,9},{2,14},{6,2},{... | collective-permute-start | bytes 884744 | tf_op jit(solution)/shard_map/ppermute | solution.py:407
  167.9 5.4 %collective-permute-start.37 = (f32[8,768]{1,0:T(8,128)S(1)}, f32[8,768]{1,0:T(8,128)S(1)}, u32[]{:S(2)}, u32[]{:S(2)}) collective-permute-start(f32[8,768]{1,0:T(8,128)S(1)} %slice_add_fusion), channel_id=1, source_target_pairs={{0,2},{2,0},{1,3},{3,1},{4,6},{6,4},{5,7},{7,5},{8,10},{10,8},{9,1... | collective-permute-start | bytes 73736 | tf_op jit(solution)/shard_map/ppermute | solution.py:407
  (21 other events, 177.8 us)
Sparse Core Ops, SparseCore 0:
  14.9 85.5 reduce-scatter.1
  115.2 48.2 all-gather.1

commit v6 on v5

--- a/solution.py
+++ b/solution.py
@@ -40,22 +40,32 @@
 
 def lane_table():
     lane = np.arange(128) % HEAD
-    table = np.zeros((8, 128), np.float32)
-    table[0] = np.where(lane < ROT, 10000.0 ** (-2.0 * (lane % 8) / ROT), 0.0)
-    table[1] = lane < 8
-    table[2] = (lane >= 8) & (lane < ROT)
+    table = np.zeros((32, 256), np.float32)
+    for j in range(8):
+        table[j] = 10000.0 ** (-2.0 * j / ROT)
+        table[8 + j, :128] = (lane == j) | (lane == j + 8)
+        table[16 + j, :128] = -1.0 * (lane == j)
+        table[16 + j, 128:] = lane == j + 8
+    table[24, :128] = lane >= ROT
     return table
 
 
 def spin_tables(coords, order, table):
     shard = (coords[0] * 4 + coords[1]) * 4 + coords[2]
-    step = lax.broadcasted_iota(jnp.int32, (128, 128), 0)
-    places = jnp.concatenate(
-        [step + order[2 * shard] * 128, step + order[2 * shard + 1] * 128], axis=0
-    )
-    angles = places.astype(F32) * table[0:1, :]
-    sine = jnp.sin(angles)
-    return jnp.cos(angles), sine * -table[1:2, :], sine * table[2:3, :]
+    lane = lax.broadcasted_iota(jnp.int32, (8, 256), 1)
+    places = lane + jnp.where(
+        lane < 128, order[2 * shard] * 128, order[2 * shard + 1] * 128 - 128
+    )
+    angles = places.astype(F32) * table[0:8, :]
+
+    def spread(values, lanes):
+        return lax.dot_general(
+            values, lanes, TN, precision=lax.Precision.HIGHEST, preferred_element_type=F32
+        )
+
+    cosine = spread(jnp.cos(angles), table[8:16, 0:128]) + table[24:25, 0:128]
+    sines = spread(jnp.sin(angles), table[16:24, :])
+    return cosine, sines[:, 0:128], sines[:, 128:256]
 
 
 def row(ref):
@@ -71,13 +81,15 @@
 
 def front_kernel(
     coords, order, table, tok, cot, wqkv, wd, ga, sa, gm, sm, bqkv, wu, bu, wdn,
-    qdo, kv, lna, gw, small, part, d_ln,
+    qdo, kv, lna, gw, small, part, d_ln, spin,
 ):
     xhat, _ = normed(tok[...])
     ln = (xhat * row(ga) + row(sa)).astype(BF)
     lna[...] = ln
     joined = mm_nt(ln, wqkv[...]) + row(bqkv)
     cosine, left_sine, right_sine = spin_tables(coords, order, table)
+    for i, values in enumerate((cosine, left_sine, right_sine)):
+        spin[i] = values
     half = lax.broadcasted_iota(jnp.int32, (256, 128), 1) < HEAD
     tiles = []
     for t in range(4):
@@ -294,7 +306,7 @@
 
 
 def tail_kernel(
-    coords, order, table, tok, cot, lna, wqkv, ga, gm, dq0, dq1, dq2, dq3, dkv0, dkv1,
+    coords, tok, cot, lna, wqkv, ga, gm, spin, dq0, dq1, dq2, dq3, dkv0, dkv1,
     s0, s1, s2, s3, o0, wd, part, d_ln_mlp, small_in, g0, g1, g2, g3, upstream, grads,
 ):
     outs = [o0] + [ref.at[192:384] for ref in (dq3, dq2, dq1)]
@@ -308,7 +320,7 @@
     ).T
     d_kv = dkv0[...].astype(F32) + dkv1[...].astype(F32)
     both = jnp.concatenate([d_query, d_kv[:, :192]], axis=1)
-    cosine, left_sine, right_sine = spin_tables(coords, order, table)
+    cosine, left_sine, right_sine = spin[0], spin[1], spin[2]
     pieces = []
     for t in range(3):
         x = both[:, 128 * t : 128 * t + 128]
@@ -374,15 +386,21 @@
         out[(coords[1] + slot) % 4] = ref[...]
 
 
-def assemble_kernel(coords, p0, p1, p2, p3, mlp, gq, gd, gu, gdn, whole):
+def assemble_kernel(coords, p0, p1, p2, p3, mlp, gq, gd, gu, gdn):
     gu[...] = mlp[0:768, :].astype(F32)
     gdn[...] = mlp[768:1536, :].astype(F32)
     for slot, ref in enumerate((p0, p1, p2, p3)):
-        whole[(coords[2] + slot) % 4] = ref[...].astype(F32)
-    for block in range(12):
-        gq[48 * block : 48 * block + 48, :] = whole[block // 4, block % 4]
-    for block in range(4):
-        gd[48 * block : 48 * block + 48, :] = whole[3, block]
+        piece = (coords[2] + slot) % 4
+
+        @pl.when(piece < 3)
+        def _(ref=ref, piece=piece):
+            for block in range(4):
+                gq[piece, 48 * block : 48 * block + 48, :] = ref[block].astype(F32)
+
+        @pl.when(piece == 3)
+        def _(ref=ref):
+            for block in range(4):
+                gd[48 * block : 48 * block + 48, :] = ref[block].astype(F32)
 
 
 def call(kernel, outs, args, scalars, scratch=(), mib=48, unread=0):
@@ -432,10 +450,10 @@
     table = jnp.asarray(lane_table())
     w_turned = w_qkv.T
 
-    qdo, kv, ln_attn, grads_mlp, small_mlp, part_mlp, d_ln_mlp = call(
+    qdo, kv, ln_attn, grads_mlp, small_mlp, part_mlp, d_ln_mlp, spin = call(
         front_kernel,
         [((256, 384), BF), ((256, 384), BF), ((256, 768), BF), ((1536, 768), BF),
-         ((8, 768), F32), ((256, 768), F32), ((256, 768), F32)],
+         ((8, 768), F32), ((256, 768), F32), ((256, 768), F32), ((3, 256, 128), F32)],
         (coords, block_order, table, tokens, cotangent, w_turned, w_dense,
          gain_attn, shift_attn, gain_mlp, shift_mlp, b_qkv, w_up, b_up, w_down),
         2,
@@ -491,19 +509,19 @@
     *pieces, upstream = call(
         tail_kernel,
         [((208, 768), BF)] * 4 + [((512, 768), BF)],
-        (coords, block_order, table, tokens, cotangent, ln_attn, w_turned, gain_attn, gain_mlp,
+        (coords, tokens, cotangent, ln_attn, w_turned, gain_attn, gain_mlp, spin,
          *d_queries, d_kv_own, d_kv_other, *stats_all, outs[0], w_dense, part_mlp,
          d_ln_mlp, small_mlp),
-        2,
+        1,
         scratch=[pltpu.VMEM((4, 192, 768), BF)],
         mib=60,
     )
+
+    pieces = [pieces[0]] + [hop(pieces[j], "y", j) for j in (1, 2, 3)]
     (grads_mlp,) = call(
         pair_kernel, [((96, 768), BF)], (grads_mlp, mlp_other, upstream), 0, unread=1
     )
     grads_mlp = lax.all_gather(grads_mlp, ("z", "y"), axis=0, tiled=True)
-
-    pieces = [pieces[0]] + [hop(pieces[j], "y", j) for j in (1, 2, 3)]
     upstream = add(upstream, hop(upstream, "c", 1)).astype(BF)
     upstream_far = hop(upstream, "xh", 1)
     blocks = call(
@@ -533,10 +551,9 @@
     )
     grad_turned, grad_w_dense, grad_w_up, grad_w_down = call(
         assemble_kernel,
-        [((576, 768), F32), ((192, 768), F32), ((768, 768), F32), ((768, 768), F32)],
+        [((3, 192, 768), F32), ((192, 768), F32), ((768, 768), F32), ((768, 768), F32)],
         (coords, quarter, *[hop(quarter, "y", -j) for j in (1, 2, 3)], grads_mlp),
         1,
-        scratch=[pltpu.VMEM((4, 4, 48, 768), F32)],
         mib=60,
     )
     grad_tokens, output = call(
@@ -548,7 +565,7 @@
     return (
         output,
         grad_tokens,
-        grad_turned.T,
+        grad_turned.reshape(576, 768).T,
         small[6, :576],
         grad_w_dense,
         small[5],

time: 193 us -> 193 us (level)
  no operation moved by 1% of the time
where the time goes in v6:
time: 193 us; the launch traced here: 192 us
  Pallas kernels  63 us (33%)
  starting transfers between devices  59.4 us (31%)
  waiting for transfers between devices  45.9 us (24%)
  between operations  14.5 us (8%)
  local copies, waits for them, and re-layouts  8.58 us (4%)
    pallas_call x14, Pallas kernels, call(): pl.pallas_call(kernel, out_shape=shapes, in_specs=[smem] * scalars + [vme...  63 us
    ppermute x38, starting transfers between devices, hop(): return lax.ppermute(x, axis, [(i, (i + step) % n) for i in range(n)])  59.3 us
    ppermute x38, waiting for transfers between devices, hop(): return lax.ppermute(x, axis, [(i, (i + step) % n) for i in range(n)])  45.9 us
    unnamed x59, local copies, waits for them, and re-layouts  6.73 us
  transfers between devices with their start and end apart: 40, of which 17 were waited for; matrix products, arithmetic and copies ran while one was open for 1% of the time, Pallas kernels for 26%

profile of v6, /device:TPU:0, one launch (start us, length us, event | category | flops | bytes accessed | tf_op | source)
XLA Modules:
  0.0 192.3 jit_solution(7117735481249818298)
XLA Ops:
  7.8 7.2 %shard_map.263 = (bf16[256,384]{1,0:T(8,128)(2,1)}, bf16[256,384]{1,0:T(8,128)(2,1)}, bf16[256,768]{1,0:T(8,128)(2,1)}, bf16[1536,768]{1,0:T(8,128)(2,1)}, f32[8...) custom-call(s32[3]{0:T(128)} %pad_add_fusion.coords, s32[64]{0:T(128)} %order.9, ...), custom_call_target="tpu_custom_call" | custom-call | bytes 1024 | tf_op jit(solution)/shard_map/pallas_call | solution.py:410
  16.0 1.6 collective-permute-start.3
  17.6 1.9 collective-permute-start.6
  19.5 2.1 %collective-permute-start.4 = (bf16[256,384]{1,0:T(8,128)(2,1)S(1)}, bf16[256,384]{1,0:T(8,128)(2,1)S(1)}, u32[]{:S(2)}, u32[]{:S(2)}) collective-permute-start(bf16[256,384]{1,0:T(8,128)(2,1)S(1)} %copy-done.7), channel_id=1, source_target_pairs={{0,48},{16,0},{32,16},{48,32},{1,49},{17,1},{33,17},{49,33},{2,50}... | collective-permute-start | bytes 589832 | tf_op jit(solution)/shard_map/ppermute | solution.py:425
  21.6 1.6 collective-permute-start.2
  23.2 3.6 %collective-permute-start.5 = (bf16[256,384]{1,0:T(8,128)(2,1)S(1)}, bf16[256,384]{1,0:T(8,128)(2,1)S(1)}, u32[]{:S(2)}, u32[]{:S(2)}) collective-permute-start(bf16[256,384]{1,0:T(8,128)(2,1)S(1)} %collective-permute-done.3.refs_5_.refs_6_), channel_id=1, source_target_pairs={{0,48},{16,0},{32,16},{48,32},{1,49},{17,1},{33,17},{49,33},{2,50}... | collective-permute-start | bytes 589832 | tf_op jit(solution)/shard_map/ppermute | solution.py:425
  26.7 3.2 %collective-permute-start.1 = (bf16[256,384]{1,0:T(8,128)(2,1)S(1)}, bf16[256,384]{1,0:T(8,128)(2,1)S(1)}, u32[]{:S(2)}, u32[]{:S(2)}) collective-permute-start(bf16[256,384]{1,0:T(8,128)(2,1)S(1)} %copy-done.2), channel_id=1, source_target_pairs={{0,8},{4,12},{8,0},{12,4},{1,9},{5,13},{9,1},{13,5},{2,10},{6,14},... | collective-permute-start | bytes 589832 | tf_op jit(solution)/shard_map/ppermute | solution.py:425
  29.9 1.0 collective-permute-start
  31.1 3.4 %collective-permute-start.8 = (bf16[256,384]{1,0:T(8,128)(2,1)S(1)}, bf16[256,384]{1,0:T(8,128)(2,1)S(1)}, u32[]{:S(2)}, u32[]{:S(2)}) collective-permute-start(bf16[256,384]{1,0:T(8,128)(2,1)S(1)} %collective-permute-done.5.refs_7_.refs_6_), channel_id=1, source_target_pairs={{0,48},{16,0},{32,16},{48,32},{1,49},{17,1},{33,17},{49,33},{2,50}... | collective-permute-start | bytes 589832 | tf_op jit(solution)/shard_map/ppermute | solution.py:425
  35.4 4.6 %collective-permute-done.refs_1_.refs_5_.refs_2_ = bf16[256,384]{1,0:T(8,128)(2,1)S(1)} collective-permute-done((bf16[256,384]{1,0:T(8,128)(2,1)S(1)}, bf16[256,384]{1,0:T(8,128)(2,1)S(1)}, u32[]{:S(2)}, u32[]{:S(2)}) %collective-permute-start) | collective-permute-done | bytes 196640 | tf_op jit(solution)/shard_map/ppermute | solution.py:425
  40.0 3.4 %collective-permute-done.7.refs_8_ = bf16[256,384]{1,0:T(8,128)(2,1)S(1)} collective-permute-done((bf16[256,384]{1,0:T(8,128)(2,1)S(1)}, bf16[256,384]{1,0:T(8,128)(2,1)S(1)}, u32[]{:S(2)}, u32[]{:S(2)}) %collective-permute-start.7) | collective-permute-done | bytes 196640 | tf_op jit(solution)/shard_map/ppermute | solution.py:425
  43.4 13.2 %shard_map.264 = (bf16[192,256]{1,0:T(8,128)(2,1)S(1)}, bf16[192,256]{1,0:T(8,128)(2,1)S(1)}, bf16[192,256]{1,0:T(8,128)(2,1)S(1)}, bf16[192,256]{1,0:T(8,128)(2,1)S(1)}, f32[4,8,256]{2,1,0:T(8,128)S(1)}) custom-call(s32[3]{0:T(128)S(1)} %copy-done.17, s32[64]{0:T(128)S(1)} %copy-done.19, bf16[256,384]{1,0:T(8,128)(2,1)S(1)} %copy-done.2, ...), custom_call_target="tpu_custom_call" | custom-call | bytes 1024 | tf_op jit(solution)/shard_map/pallas_call | solution.py:410
  56.6 1.5 collective-permute-start.12
  58.8 2.4 %collective-permute-start.10 = (f32[4,8,256]{2,1,0:T(8,128)S(1)}, f32[4,8,256]{2,1,0:T(8,128)S(1)}, u32[]{:S(2)}, u32[]{:S(2)}) collective-permute-start(f32[4,8,256]{2,1,0:T(8,128)S(1)} %get-tuple-element.59.refs_0_.s0), channel_id=1, source_target_pairs={{0,12},{4,0},{8,4},{12,8},{1,13},{5,1},{9,5},{13,9},{2,14},{6,2},{... | collective-permute-start | bytes 98312 | tf_op jit(solution)/shard_map/ppermute | solution.py:425
  61.9 1.7 collective-permute-done.11.refs_2_.s2
  63.6 6.9 %shard_map.265 = (f32[4,8,256]{2,1,0:T(8,128)S(1)}, bf16[2,256,384]{2,1,0:T(8,128)(2,1)S(1)}, f32[4,192,256]{2,1,0:T(8,128)S(1)}) custom-call(s32[3]{0:T(128)S(1)} %copy-done.17, s32[64]{0:T(128)S(1)} %copy-done.19, f32[4,8,256]{2,1,0:T(8,128)S(1)} %get-tuple-element.59.refs_0_.s0, f32[4,8,256]{2,1,0:T(8,128)S(1)} %collective-permute-done.10.refs_1_.s1, ...), custom_call_target="tpu_custom_call" | custom-call | bytes 1024 | tf_op jit(solution)/shard_map/pallas_call | solution.py:410
  70.6 13.1 %shard_map.266 = (bf16[2,256,384]{2,1,0:T(8,128)(2,1)S(1)}, bf16[2,256,384]{2,1,0:T(8,128)(2,1)S(1)}, f32[4,192,256]{2,1,0:T(8,128)S(1)}) custom-call(s32[3]{0:T(128)S(1)} %copy-done.17, s32[64]{0:T(128)S(1)} %copy-done.19, f32[4,8,256]{2,1,0:T(8,128)S(1)} %get-tuple-element.60.refs_0_, bf16[256,384]{1,0:T(8,128)(2,1)S(1)} %copy-done.2, ...), custom_call_target="tpu_custom_call" | custom-call | bytes 1024 | tf_op jit(solution)/shard_map/pallas_call | solution.py:410
  83.7 1.6 collective-permute-start.17
  85.3 1.7 collective-permute-start.18
  87.0 6.9 %shard_map.267 = (bf16[2,256,384]{2,1,0:T(8,128)(2,1)S(1)}, bf16[192,256]{1,0:T(8,128)(2,1)S(1)}, bf16[384,256]{1,0:T(8,128)(2,1)S(1)}, bf16[384,256]{1,0:T(8,128)(2,1)S(1)}, bf16[384,256]{1,0:T(8,128)(2,1)S(1)}) custom-call(s32[3]{0:T(128)S(1)} %copy-done.17, s32[64]{0:T(128)S(1)} %copy-done.19, f32[4,8,256]{2,1,0:T(8,128)S(1)} %get-tuple-element.60.refs_0_, ...), custom_call_target="tpu_custom_call" | custom-call | bytes 1024 | tf_op jit(solution)/shard_map/pallas_call | solution.py:410
  95.2 1.0 collective-permute-start.19
  96.2 1.9 %collective-permute-start.14 = (bf16[384,256]{1,0:T(8,128)(2,1)S(1)}, bf16[384,256]{1,0:T(8,128)(2,1)S(1)}, u32[]{:S(2)}, u32[]{:S(2)}) collective-permute-start(bf16[384,256]{1,0:T(8,128)(2,1)S(1)} %get-tuple-element.68), channel_id=1, source_target_pairs={{0,4},{4,8},{8,12},{12,0},{1,5},{5,9},{9,13},{13,1},{2,6},{6,10},{... | collective-permute-start | bytes 589832 | tf_op jit(solution)/shard_map/ppermute | solution.py:425
  98.2 3.0 %collective-permute-start.15 = (bf16[384,256]{1,0:T(8,128)(2,1)S(1)}, bf16[384,256]{1,0:T(8,128)(2,1)S(1)}, u32[]{:S(2)}, u32[]{:S(2)}) collective-permute-start(bf16[384,256]{1,0:T(8,128)(2,1)S(1)} %get-tuple-element.69), channel_id=1, source_target_pairs={{0,8},{4,12},{8,0},{12,4},{1,9},{5,13},{9,1},{13,5},{2,10},{6,14},... | collective-permute-start | bytes 589832 | tf_op jit(solution)/shard_map/ppermute | solution.py:425
  102.2 2.0 %collective-permute-start.35 = (bf16[96,768]{1,0:T(8,128)(2,1)S(1)}, bf16[96,768]{1,0:T(8,128)(2,1)S(1)}, u32[]{:S(2)}, u32[]{:S(2)}) collective-permute-start(bf16[96,768]{1,0:T(8,128)(2,1)S(1)} %shard_map.274.x), channel_id=1, source_target_pairs={{0,64},{64,0},{1,65},{65,1},{2,66},{66,2},{3,67},{67,3},{4,68},{68... | collective-permute-start | bytes 442376 | tf_op jit(solution)/shard_map/ppermute | solution.py:425
  104.2 2.8 %collective-permute-done.15.dq2 = bf16[384,256]{1,0:T(8,128)(2,1)S(1)} collective-permute-done((bf16[384,256]{1,0:T(8,128)(2,1)S(1)}, bf16[384,256]{1,0:T(8,128)(2,1)S(1)}, u32[]{:S(2)}, u32[]{:S(2)}) %collective-permute-start.15) | collective-permute-done | bytes 196640 | tf_op jit(solution)/shard_map/ppermute | solution.py:425
  107.7 5.6 %shard_map.269 = (bf16[208,768]{1,0:T(8,128)(2,1)}, bf16[208,768]{1,0:T(8,128)(2,1)}, bf16[208,768]{1,0:T(8,128)(2,1)}, bf16[208,768]{1,0:T(8,128)(2,1)}, bf16[512,768]{1,0:T(8,128)(2,1)}) custom-call(s32[3]{0:T(128)} %pad_add_fusion.coords, bf16[256,768]{1,0:T(8,128)(2,1)} %tok.5, bf16[256,768]{1,0:T(8,128)(2,1)} %cot.5, ...), custom_call_target="tpu_custom_call" | custom-call | bytes 1024 | tf_op jit(solution)/shard_map/pallas_call | solution.py:410
  113.3 1.1 copy-done.3
  115.7 3.0 %collective-permute-start.23 = (bf16[208,768]{1,0:T(8,128)(2,1)}, bf16[208,768]{1,0:T(8,128)(2,1)S(1)}, u32[]{:S(2)}, u32[]{:S(2)}) collective-permute-start(bf16[208,768]{1,0:T(8,128)(2,1)} %get-tuple-element.85), channel_id=1, source_target_pairs={{0,8},{4,12},{8,0},{12,4},{1,9},{5,13},{9,1},{13,5},{2,10},{6,14},... | collective-permute-start | bytes 958472 | tf_op jit(solution)/shard_map/ppermute | solution.py:425
  119.4 7.5 %collective-permute-done.22.p1 = bf16[208,768]{1,0:T(8,128)(2,1)S(1)} collective-permute-done((bf16[208,768]{1,0:T(8,128)(2,1)}, bf16[208,768]{1,0:T(8,128)(2,1)S(1)}, u32[]{:S(2)}, u32[]{:S(2)}) %collective-permute-start.22) | collective-permute-done | bytes 319520 | tf_op jit(solution)/shard_map/ppermute | solution.py:425
  126.9 8.4 %collective-permute-done.23.p2 = bf16[208,768]{1,0:T(8,128)(2,1)S(1)} collective-permute-done((bf16[208,768]{1,0:T(8,128)(2,1)}, bf16[208,768]{1,0:T(8,128)(2,1)S(1)}, u32[]{:S(2)}, u32[]{:S(2)}) %collective-permute-start.23) | collective-permute-done | bytes 319520 | tf_op jit(solution)/shard_map/ppermute | solution.py:425
  137.9 2.5 %collective-permute-start.25 = (bf16[64,768]{1,0:T(8,128)(2,1)S(1)}, bf16[64,768]{1,0:T(8,128)(2,1)S(1)}, u32[]{:S(2)}, u32[]{:S(2)}) collective-permute-start(bf16[64,768]{1,0:T(8,128)(2,1)S(1)} %get-tuple-element.88), channel_id=1, source_target_pairs={{0,16},{16,32},{32,48},{48,0},{1,17},{17,33},{33,49},{49,1},{2,18}... | collective-permute-start | bytes 294920 | tf_op jit(solution)/shard_map/ppermute | solution.py:425
  140.4 1.4 collective-permute-start.26
  141.8 1.4 collective-permute-start.27
  143.2 1.1 collective-permute-done.25.b1
  144.3 2.2 %collective-permute-done.26.b2 = bf16[64,768]{1,0:T(8,128)(2,1)S(1)} collective-permute-done((bf16[64,768]{1,0:T(8,128)(2,1)S(1)}, bf16[64,768]{1,0:T(8,128)(2,1)S(1)}, u32[]{:S(2)}, u32[]{:S(2)}) %collective-permute-start.26) | collective-permute-done | bytes 98336 | tf_op jit(solution)/shard_map/ppermute | solution.py:425
  147.9 3.1 %collective-permute-start.21 = (bf16[512,768]{1,0:T(8,128)(2,1)S(1)}, bf16[512,768]{1,0:T(8,128)(2,1)S(1)}, u32[]{:S(2)}, u32[]{:S(2)}) collective-permute-start(bf16[512,768]{1,0:T(8,128)(2,1)S(1)} %add_convert_fusion.e0), channel_id=1, source_target_pairs={{0,2},{2,0},{1,3},{3,1},{4,6},{6,4},{5,7},{7,5},{8,10},{10,8},{9,1... | collective-permute-start | bytes 2359304 | tf_op jit(solution)/shard_map/ppermute | solution.py:425
  151.1 1.9 %collective-permute-done.28 = bf16[64,768]{1,0:T(8,128)(2,1)S(1)} collective-permute-done((bf16[64,768]{1,0:T(8,128)(2,1)S(1)}, bf16[64,768]{1,0:T(8,128)(2,1)S(1)}, u32[]{:S(2)}, u32[]{:S(2)}) %collective-permute-start.28) | collective-permute-done | bytes 98336 | tf_op jit(solution)/shard_map/ppermute | solution.py:425
  153.1 1.2 collective-permute-start.31
  154.3 2.9 %collective-permute-start.30 = (bf16[48,768]{1,0:T(8,128)(2,1)S(1)}, bf16[48,768]{1,0:T(8,128)(2,1)S(1)}, u32[]{:S(2)}, u32[]{:S(2)}) collective-permute-start(bf16[48,768]{1,0:T(8,128)(2,1)S(1)} %slice.59.b0), channel_id=1, source_target_pairs={{0,32},{16,48},{32,0},{48,16},{1,33},{17,49},{33,1},{49,17},{2,34}... | collective-permute-start | bytes 221192 | tf_op jit(solution)/shard_map/ppermute | solution.py:425
  158.3 2.0 %collective-permute-done.31.b3 = bf16[48,768]{1,0:T(8,128)(2,1)S(1)} collective-permute-done((bf16[48,768]{1,0:T(8,128)(2,1)S(1)}, bf16[48,768]{1,0:T(8,128)(2,1)S(1)}, u32[]{:S(2)}, u32[]{:S(2)}) %collective-permute-start.31) | collective-permute-done | bytes 73760 | tf_op jit(solution)/shard_map/ppermute | solution.py:425
  160.3 2.7 %collective-permute-done.30.b2 = bf16[48,768]{1,0:T(8,128)(2,1)S(1)} collective-permute-done((bf16[48,768]{1,0:T(8,128)(2,1)S(1)}, bf16[48,768]{1,0:T(8,128)(2,1)S(1)}, u32[]{:S(2)}, u32[]{:S(2)}) %collective-permute-start.30) | collective-permute-done | bytes 73760 | tf_op jit(solution)/shard_map/ppermute | solution.py:425
  163.6 1.3 collective-permute-start.34
  164.9 2.9 %collective-permute-start.33 = (bf16[4,48,768]{2,1,0:T(8,128)(2,1)S(1)}, bf16[4,48,768]{2,1,0:T(8,128)(2,1)S(1)}, u32[]{:S(2)}, u32[]{:S(2)}) collective-permute-start(bf16[4,48,768]{2,1,0:T(8,128)(2,1)S(1)} %shard_map.273.p0), channel_id=1, source_target_pairs={{0,8},{4,12},{8,0},{12,4},{1,9},{5,13},{9,1},{13,5},{2,10},{6,14},... | collective-permute-start | bytes 884744 | tf_op jit(solution)/shard_map/ppermute | solution.py:425
  167.9 3.1 %collective-permute-start.37 = (f32[8,768]{1,0:T(8,128)S(1)}, f32[8,768]{1,0:T(8,128)S(1)}, u32[]{:S(2)}, u32[]{:S(2)}) collective-permute-start(f32[8,768]{1,0:T(8,128)S(1)} %slice_add_fusion), channel_id=1, source_target_pairs={{0,2},{2,0},{1,3},{3,1},{4,6},{6,4},{5,7},{7,5},{8,10},{10,8},{9,1... | collective-permute-start | bytes 73736 | tf_op jit(solution)/shard_map/ppermute | solution.py:425
  171.5 1.7 collective-permute-done.37
  173.9 1.7 shard_map.270
  175.6 2.9 %collective-permute-done.33.p2 = bf16[4,48,768]{2,1,0:T(8,128)(2,1)S(1)} collective-permute-done((bf16[4,48,768]{2,1,0:T(8,128)(2,1)S(1)}, bf16[4,48,768]{2,1,0:T(8,128)(2,1)S(1)}, u32[]{:S(2)}, u32[]{:S(2)}) %collective-permute-start.33) | collective-permute-done | bytes 294944 | tf_op jit(solution)/shard_map/ppermute | solution.py:425
  179.3 5.5 %shard_map.276 = (f32[3,192,768]{2,1,0:T(8,128)}, f32[192,768]{1,0:T(8,128)}, f32[768,768]{1,0:T(8,128)}, f32[768,768]{1,0:T(8,128)}) custom-call(s32[3]{0:T(128)} %pad_add_fusion.coords, bf16[4,48,768]{2,1,0:T(8,128)(2,1)} %copy-done.5, bf16[4,48,768]{2,1,0:T(8,128)(2,1)} %copy-done.24, bf16[4,48,768]{2,1,0:T(8,128)(2,1)} %copy-done.23, ...), custom_call_target="tpu_custom_call" | custom-call | bytes 1024 | tf_op jit(solution)/shard_map/pallas_call | solution.py:410
  (117 shorter events, 17.4 us)
Async XLA Ops:
  7.2 94.1 %reduce-scatter.2.cloned.1.call-start = ((), (), s32[]{:S(2)}) async-start(), calls=%async_computation.1 | async-start | bytes 2506752 | tf_op jit(solution)/shard_map/reduce_scatter | solution.py:462
  15.1 28.3 %copy-start.17 = (s32[3]{0:T(128)S(1)}, s32[3]{0:T(128)}, u32[]{:S(2)}) copy-start(s32[3]{0:T(128)} %pad_add_fusion.coords) | copy-start | bytes 40
  15.1 28.3 %copy-start.19 = (s32[64]{0:T(128)S(1)}, s32[64]{0:T(128)}, u32[]{:S(2)}) copy-start(s32[64]{0:T(128)} %order.9) | copy-start | bytes 772
  15.1 163.4 %all-gather.2.cloned.1.call-start = ((), (), s32[]{:S(2)}) async-start(), calls=%async_computation.2 | async-start | bytes 2506752 | tf_op jit(solution)/shard_map/all_gather | solution.py:524
  16.0 7.2 %collective-permute-start.3 = (bf16[256,384]{1,0:T(8,128)(2,1)S(1)}, bf16[256,384]{1,0:T(8,128)(2,1)S(1)}, u32[]{:S(2)}, u32[]{:S(2)}) collective-permute-start(bf16[256,384]{1,0:T(8,128)(2,1)S(1)} %copy-done.7), channel_id=1, source_target_pairs={{0,64},{64,0},{1,65},{65,1},{2,66},{66,2},{3,67},{67,3},{4,68},{68... | collective-permute-start | bytes 589832 | tf_op jit(solution)/shard_map/ppermute | solution.py:425
  17.6 12.4 %collective-permute-start.6 = (bf16[256,384]{1,0:T(8,128)(2,1)S(1)}, bf16[256,384]{1,0:T(8,128)(2,1)S(1)}, u32[]{:S(2)}, u32[]{:S(2)}) collective-permute-start(bf16[256,384]{1,0:T(8,128)(2,1)S(1)} %copy-done.7), channel_id=1, source_target_pairs={{0,16},{16,32},{32,48},{48,0},{1,17},{17,33},{33,49},{49,1},{2,18}... | collective-permute-start | bytes 589832 | tf_op jit(solution)/shard_map/ppermute | solution.py:425
  19.5 11.5 %collective-permute-start.4 = (bf16[256,384]{1,0:T(8,128)(2,1)S(1)}, bf16[256,384]{1,0:T(8,128)(2,1)S(1)}, u32[]{:S(2)}, u32[]{:S(2)}) collective-permute-start(bf16[256,384]{1,0:T(8,128)(2,1)S(1)} %copy-done.7), channel_id=1, source_target_pairs={{0,48},{16,0},{32,16},{48,32},{1,49},{17,1},{33,17},{49,33},{2,50}... | collective-permute-start | bytes 589832 | tf_op jit(solution)/shard_map/ppermute | solution.py:425
  21.6 9.4 %collective-permute-start.2 = (bf16[256,384]{1,0:T(8,128)(2,1)S(1)}, bf16[256,384]{1,0:T(8,128)(2,1)S(1)}, u32[]{:S(2)}, u32[]{:S(2)}) collective-permute-start(bf16[256,384]{1,0:T(8,128)(2,1)S(1)} %copy-done.2), channel_id=1, source_target_pairs={{0,4},{4,8},{8,12},{12,0},{1,5},{5,9},{9,13},{13,1},{2,6},{6,10},{... | collective-permute-start | bytes 589832 | tf_op jit(solution)/shard_map/ppermute | solution.py:425
  23.2 7.9 %collective-permute-start.5 = (bf16[256,384]{1,0:T(8,128)(2,1)S(1)}, bf16[256,384]{1,0:T(8,128)(2,1)S(1)}, u32[]{:S(2)}, u32[]{:S(2)}) collective-permute-start(bf16[256,384]{1,0:T(8,128)(2,1)S(1)} %collective-permute-done.3.refs_5_.refs_6_), channel_id=1, source_target_pairs={{0,48},{16,0},{32,16},{48,32},{1,49},{17,1},{33,17},{49,33},{2,50}... | collective-permute-start | bytes 589832 | tf_op jit(solution)/shard_map/ppermute | solution.py:425
  26.7 8.7 %collective-permute-start.1 = (bf16[256,384]{1,0:T(8,128)(2,1)S(1)}, bf16[256,384]{1,0:T(8,128)(2,1)S(1)}, u32[]{:S(2)}, u32[]{:S(2)}) collective-permute-start(bf16[256,384]{1,0:T(8,128)(2,1)S(1)} %copy-done.2), channel_id=1, source_target_pairs={{0,8},{4,12},{8,0},{12,4},{1,9},{5,13},{9,1},{13,5},{2,10},{6,14},... | collective-permute-start | bytes 589832 | tf_op jit(solution)/shard_map/ppermute | solution.py:425
  29.9 10.0 %collective-permute-start = (bf16[256,384]{1,0:T(8,128)(2,1)S(1)}, bf16[256,384]{1,0:T(8,128)(2,1)S(1)}, u32[]{:S(2)}, u32[]{:S(2)}) collective-permute-start(bf16[256,384]{1,0:T(8,128)(2,1)S(1)} %copy-done.2), channel_id=1, source_target_pairs={{0,12},{4,0},{8,4},{12,8},{1,13},{5,1},{9,5},{13,9},{2,14},{6,2},{... | collective-permute-start | bytes 589832 | tf_op jit(solution)/shard_map/ppermute | solution.py:425
  31.0 12.4 %collective-permute-start.9 = (bf16[256,384]{1,0:T(8,128)(2,1)S(1)}, bf16[256,384]{1,0:T(8,128)(2,1)S(1)}, u32[]{:S(2)}, u32[]{:S(2)}) collective-permute-start(bf16[256,384]{1,0:T(8,128)(2,1)S(1)} %collective-permute-done.3.refs_5_.refs_6_), channel_id=1, source_target_pairs={{0,16},{16,32},{32,48},{48,0},{1,17},{17,33},{33,49},{49,1},{2,18}... | collective-permute-start | bytes 589832 | tf_op jit(solution)/shard_map/ppermute | solution.py:425
  31.0 12.4 %collective-permute-start.7 = (bf16[256,384]{1,0:T(8,128)(2,1)S(1)}, bf16[256,384]{1,0:T(8,128)(2,1)S(1)}, u32[]{:S(2)}, u32[]{:S(2)}) collective-permute-start(bf16[256,384]{1,0:T(8,128)(2,1)S(1)} %collective-permute-done.6.refs_10_.refs_7_), channel_id=1, source_target_pairs={{0,16},{16,32},{32,48},{48,0},{1,17},{17,33},{33,49},{49,1},{2,18}... | collective-permute-start | bytes 589832 | tf_op jit(solution)/shard_map/ppermute | solution.py:425
  31.1 12.3 %collective-permute-start.8 = (bf16[256,384]{1,0:T(8,128)(2,1)S(1)}, bf16[256,384]{1,0:T(8,128)(2,1)S(1)}, u32[]{:S(2)}, u32[]{:S(2)}) collective-permute-start(bf16[256,384]{1,0:T(8,128)(2,1)S(1)} %collective-permute-done.5.refs_7_.refs_6_), channel_id=1, source_target_pairs={{0,48},{16,0},{32,16},{48,32},{1,49},{17,1},{33,17},{49,33},{2,50}... | collective-permute-start | bytes 589832 | tf_op jit(solution)/shard_map/ppermute | solution.py:425
  56.6 27.1 %copy-start.11 = (f32[4,8,256]{2,1,0:T(8,128)}, f32[4,8,256]{2,1,0:T(8,128)S(1)}, u32[]{:S(2)}) copy-start(f32[4,8,256]{2,1,0:T(8,128)S(1)} %get-tuple-element.59.refs_0_.s0) | copy-start | bytes 98308
  56.6 5.3 %collective-permute-start.12 = (f32[4,8,256]{2,1,0:T(8,128)S(1)}, f32[4,8,256]{2,1,0:T(8,128)S(1)}, u32[]{:S(2)}, u32[]{:S(2)}) collective-permute-start(f32[4,8,256]{2,1,0:T(8,128)S(1)} %get-tuple-element.59.refs_0_.s0), channel_id=1, source_target_pairs={{0,4},{4,8},{8,12},{12,0},{1,5},{5,9},{9,13},{13,1},{2,6},{6,10},{... | collective-permute-start | bytes 98312 | tf_op jit(solution)/shard_map/ppermute | solution.py:425
  58.1 5.5 %collective-permute-start.11 = (f32[4,8,256]{2,1,0:T(8,128)S(1)}, f32[4,8,256]{2,1,0:T(8,128)S(1)}, u32[]{:S(2)}, u32[]{:S(2)}) collective-permute-start(f32[4,8,256]{2,1,0:T(8,128)S(1)} %get-tuple-element.59.refs_0_.s0), channel_id=1, source_target_pairs={{0,8},{4,12},{8,0},{12,4},{1,9},{5,13},{9,1},{13,5},{2,10},{6,14},... | collective-permute-start | bytes 98312 | tf_op jit(solution)/shard_map/ppermute | solution.py:425
  58.8 4.9 %collective-permute-start.10 = (f32[4,8,256]{2,1,0:T(8,128)S(1)}, f32[4,8,256]{2,1,0:T(8,128)S(1)}, u32[]{:S(2)}, u32[]{:S(2)}) collective-permute-start(f32[4,8,256]{2,1,0:T(8,128)S(1)} %get-tuple-element.59.refs_0_.s0), channel_id=1, source_target_pairs={{0,12},{4,0},{8,4},{12,8},{1,13},{5,1},{9,5},{13,9},{2,14},{6,2},{... | collective-permute-start | bytes 98312 | tf_op jit(solution)/shard_map/ppermute | solution.py:425
  70.5 16.5 %collective-permute-start.13 = (bf16[2,256,384]{2,1,0:T(8,128)(2,1)S(1)}, bf16[2,256,384]{2,1,0:T(8,128)(2,1)S(1)}, u32[]{:S(2)}, u32[]{:S(2)}) collective-permute-start(bf16[2,256,384]{2,1,0:T(8,128)(2,1)S(1)} %get-tuple-element.66), channel_id=1, source_target_pairs={{0,32},{16,48},{32,0},{48,16},{1,33},{17,49},{33,1},{49,17},{2,34}... | collective-permute-start | bytes 1179656 | tf_op jit(solution)/shard_map/ppermute | solution.py:425
  83.7 10.2 %collective-permute-start.17 = (bf16[2,256,384]{2,1,0:T(8,128)(2,1)S(1)}, bf16[2,256,384]{2,1,0:T(8,128)(2,1)S(1)}, u32[]{:S(2)}, u32[]{:S(2)}) collective-permute-start(bf16[2,256,384]{2,1,0:T(8,128)(2,1)S(1)} %get-tuple-element.72), channel_id=1, source_target_pairs={{0,16},{16,32},{32,48},{48,0},{1,17},{17,33},{33,49},{49,1},{2,18}... | collective-permute-start | bytes 1179656 | tf_op jit(solution)/shard_map/ppermute | solution.py:425
  85.3 9.0 %collective-permute-start.18 = (bf16[2,256,384]{2,1,0:T(8,128)(2,1)S(1)}, bf16[2,256,384]{2,1,0:T(8,128)(2,1)S(1)}, u32[]{:S(2)}, u32[]{:S(2)}) collective-permute-start(bf16[2,256,384]{2,1,0:T(8,128)(2,1)S(1)} %get-tuple-element.73), channel_id=1, source_target_pairs={{0,48},{16,0},{32,16},{48,32},{1,49},{17,1},{33,17},{49,33},{2,50}... | collective-permute-start | bytes 1179656 | tf_op jit(solution)/shard_map/ppermute | solution.py:425
  95.2 6.0 %collective-permute-start.19 = (bf16[256,384]{1,0:T(8,128)(2,1)S(1)}, bf16[256,384]{1,0:T(8,128)(2,1)S(1)}, u32[]{:S(2)}, u32[]{:S(2)}) collective-permute-start(bf16[256,384]{1,0:T(8,128)(2,1)S(1)} %get-tuple-element.75), channel_id=1, source_target_pairs={{0,64},{64,0},{1,65},{65,1},{2,66},{66,2},{3,67},{67,3},{4,68},{68... | collective-permute-start | bytes 589832 | tf_op jit(solution)/shard_map/ppermute | solution.py:425
  96.2 8.0 %collective-permute-start.14 = (bf16[384,256]{1,0:T(8,128)(2,1)S(1)}, bf16[384,256]{1,0:T(8,128)(2,1)S(1)}, u32[]{:S(2)}, u32[]{:S(2)}) collective-permute-start(bf16[384,256]{1,0:T(8,128)(2,1)S(1)} %get-tuple-element.68), channel_id=1, source_target_pairs={{0,4},{4,8},{8,12},{12,0},{1,5},{5,9},{9,13},{13,1},{2,6},{6,10},{... | collective-permute-start | bytes 589832 | tf_op jit(solution)/shard_map/ppermute | solution.py:425
  98.2 8.8 %collective-permute-start.15 = (bf16[384,256]{1,0:T(8,128)(2,1)S(1)}, bf16[384,256]{1,0:T(8,128)(2,1)S(1)}, u32[]{:S(2)}, u32[]{:S(2)}) collective-permute-start(bf16[384,256]{1,0:T(8,128)(2,1)S(1)} %get-tuple-element.69), channel_id=1, source_target_pairs={{0,8},{4,12},{8,0},{12,4},{1,9},{5,13},{9,1},{13,5},{2,10},{6,14},... | collective-permute-start | bytes 589832 | tf_op jit(solution)/shard_map/ppermute | solution.py:425
  101.2 5.8 %collective-permute-start.16 = (bf16[384,256]{1,0:T(8,128)(2,1)S(1)}, bf16[384,256]{1,0:T(8,128)(2,1)S(1)}, u32[]{:S(2)}, u32[]{:S(2)}) collective-permute-start(bf16[384,256]{1,0:T(8,128)(2,1)S(1)} %get-tuple-element.70), channel_id=1, source_target_pairs={{0,12},{4,0},{8,4},{12,8},{1,13},{5,1},{9,5},{13,9},{2,14},{6,2},{... | collective-permute-start | bytes 589832 | tf_op jit(solution)/shard_map/ppermute | solution.py:425
  102.2 11.0 %collective-permute-start.35 = (bf16[96,768]{1,0:T(8,128)(2,1)S(1)}, bf16[96,768]{1,0:T(8,128)(2,1)S(1)}, u32[]{:S(2)}, u32[]{:S(2)}) collective-permute-start(bf16[96,768]{1,0:T(8,128)(2,1)S(1)} %shard_map.274.x), channel_id=1, source_target_pairs={{0,64},{64,0},{1,65},{65,1},{2,66},{66,2},{3,67},{67,3},{4,68},{68... | collective-permute-start | bytes 442376 | tf_op jit(solution)/shard_map/ppermute | solution.py:425
  107.7 28.3 %copy-start.18 = (s32[3]{0:T(128)S(1)}, s32[3]{0:T(128)}, u32[]{:S(2)}) copy-start(s32[3]{0:T(128)} %pad_add_fusion.coords) | copy-start | bytes 40
  114.4 33.3 %copy-start.4 = (bf16[512,768]{1,0:T(8,128)(2,1)S(1)}, bf16[512,768]{1,0:T(8,128)(2,1)}, u32[]{:S(2)}) copy-start(bf16[512,768]{1,0:T(8,128)(2,1)} %get-tuple-element.80.after) | copy-start | bytes 2359300
  115.2 32.6 %collective-permute-start.20 = (bf16[512,768]{1,0:T(8,128)(2,1)}, bf16[512,768]{1,0:T(8,128)(2,1)S(1)}, u32[]{:S(2)}, u32[]{:S(2)}) collective-permute-start(bf16[512,768]{1,0:T(8,128)(2,1)} %get-tuple-element.80.after), channel_id=1, source_target_pairs={{0,1},{1,0},{2,3},{3,2},{4,5},{5,4},{6,7},{7,6},{8,9},{9,8},{10,11... | collective-permute-start | bytes 2359304 | tf_op jit(solution)/shard_map/ppermute | solution.py:425
  115.3 11.6 %collective-permute-start.22 = (bf16[208,768]{1,0:T(8,128)(2,1)}, bf16[208,768]{1,0:T(8,128)(2,1)S(1)}, u32[]{:S(2)}, u32[]{:S(2)}) collective-permute-start(bf16[208,768]{1,0:T(8,128)(2,1)} %get-tuple-element.84), channel_id=1, source_target_pairs={{0,4},{4,8},{8,12},{12,0},{1,5},{5,9},{9,13},{13,1},{2,6},{6,10},{... | collective-permute-start | bytes 958472 | tf_op jit(solution)/shard_map/ppermute | solution.py:425
  115.7 19.5 %collective-permute-start.23 = (bf16[208,768]{1,0:T(8,128)(2,1)}, bf16[208,768]{1,0:T(8,128)(2,1)S(1)}, u32[]{:S(2)}, u32[]{:S(2)}) collective-permute-start(bf16[208,768]{1,0:T(8,128)(2,1)} %get-tuple-element.85), channel_id=1, source_target_pairs={{0,8},{4,12},{8,0},{12,4},{1,9},{5,13},{9,1},{13,5},{2,10},{6,14},... | collective-permute-start | bytes 958472 | tf_op jit(solution)/shard_map/ppermute | solution.py:425
  118.8 17.2 %collective-permute-start.24 = (bf16[208,768]{1,0:T(8,128)(2,1)}, bf16[208,768]{1,0:T(8,128)(2,1)S(1)}, u32[]{:S(2)}, u32[]{:S(2)}) collective-permute-start(bf16[208,768]{1,0:T(8,128)(2,1)} %get-tuple-element.86), channel_id=1, source_target_pairs={{0,12},{4,0},{8,4},{12,8},{1,13},{5,1},{9,5},{13,9},{2,14},{6,2},{... | collective-permute-start | bytes 958472 | tf_op jit(solution)/shard_map/ppermute | solution.py:425
  137.9 6.4 %collective-permute-start.25 = (bf16[64,768]{1,0:T(8,128)(2,1)S(1)}, bf16[64,768]{1,0:T(8,128)(2,1)S(1)}, u32[]{:S(2)}, u32[]{:S(2)}) collective-permute-start(bf16[64,768]{1,0:T(8,128)(2,1)S(1)} %get-tuple-element.88), channel_id=1, source_target_pairs={{0,16},{16,32},{32,48},{48,0},{1,17},{17,33},{33,49},{49,1},{2,18}... | collective-permute-start | bytes 294920 | tf_op jit(solution)/shard_map/ppermute | solution.py:425
  140.4 6.1 %collective-permute-start.26 = (bf16[64,768]{1,0:T(8,128)(2,1)S(1)}, bf16[64,768]{1,0:T(8,128)(2,1)S(1)}, u32[]{:S(2)}, u32[]{:S(2)}) collective-permute-start(bf16[64,768]{1,0:T(8,128)(2,1)S(1)} %get-tuple-element.89), channel_id=1, source_target_pairs={{0,32},{16,48},{32,0},{48,16},{1,33},{17,49},{33,1},{49,17},{2,34}... | collective-permute-start | bytes 294920 | tf_op jit(solution)/shard_map/ppermute | solution.py:425
  141.8 4.8 %collective-permute-start.27 = (bf16[64,768]{1,0:T(8,128)(2,1)S(1)}, bf16[64,768]{1,0:T(8,128)(2,1)S(1)}, u32[]{:S(2)}, u32[]{:S(2)}) collective-permute-start(bf16[64,768]{1,0:T(8,128)(2,1)S(1)} %get-tuple-element.90), channel_id=1, source_target_pairs={{0,48},{16,0},{32,16},{48,32},{1,49},{17,1},{33,17},{49,33},{2,50}... | collective-permute-start | bytes 294920 | tf_op jit(solution)/shard_map/ppermute | solution.py:425
  147.2 26.7 %copy-start = (bf16[256,768]{1,0:T(8,128)(2,1)S(1)}, bf16[256,768]{1,0:T(8,128)(2,1)}, u32[]{:S(2)}) copy-start(bf16[256,768]{1,0:T(8,128)(2,1)} %tok.5) | copy-start | bytes 1179652
  147.2 26.7 %copy-start.1 = (bf16[256,768]{1,0:T(8,128)(2,1)S(1)}, bf16[256,768]{1,0:T(8,128)(2,1)}, u32[]{:S(2)}) copy-start(bf16[256,768]{1,0:T(8,128)(2,1)} %cot.5) | copy-start | bytes 1179652
  147.3 26.7 %copy-start.20 = (f32[768]{0:T(1024)S(1)}, f32[768]{0:T(1024)}, u32[]{:S(2)}) copy-start(f32[768]{0:T(1024)} %b_dense.1) | copy-start | bytes 9220
  147.3 5.7 %collective-permute-start.28 = (bf16[64,768]{1,0:T(8,128)(2,1)S(1)}, bf16[64,768]{1,0:T(8,128)(2,1)S(1)}, u32[]{:S(2)}, u32[]{:S(2)}) collective-permute-start(bf16[64,768]{1,0:T(8,128)(2,1)S(1)} %shard_map.272), channel_id=1, source_target_pairs={{0,64},{64,0},{1,65},{65,1},{2,66},{66,2},{3,67},{67,3},{4,68},{68... | collective-permute-start | bytes 294920 | tf_op jit(solution)/shard_map/ppermute | solution.py:425
  147.9 26.0 %collective-permute-start.21 = (bf16[512,768]{1,0:T(8,128)(2,1)S(1)}, bf16[512,768]{1,0:T(8,128)(2,1)S(1)}, u32[]{:S(2)}, u32[]{:S(2)}) collective-permute-start(bf16[512,768]{1,0:T(8,128)(2,1)S(1)} %add_convert_fusion.e0), channel_id=1, source_target_pairs={{0,2},{2,0},{1,3},{3,1},{4,6},{6,4},{5,7},{7,5},{8,10},{10,8},{9,1... | collective-permute-start | bytes 2359304 | tf_op jit(solution)/shard_map/ppermute | solution.py:425
  153.1 7.2 %collective-permute-start.31 = (bf16[48,768]{1,0:T(8,128)(2,1)S(1)}, bf16[48,768]{1,0:T(8,128)(2,1)S(1)}, u32[]{:S(2)}, u32[]{:S(2)}) collective-permute-start(bf16[48,768]{1,0:T(8,128)(2,1)S(1)} %slice.59.b0), channel_id=1, source_target_pairs={{0,16},{16,32},{32,48},{48,0},{1,17},{17,33},{33,49},{49,1},{2,18}... | collective-permute-start | bytes 221192 | tf_op jit(solution)/shard_map/ppermute | solution.py:425
  154.3 8.7 %collective-permute-start.30 = (bf16[48,768]{1,0:T(8,128)(2,1)S(1)}, bf16[48,768]{1,0:T(8,128)(2,1)S(1)}, u32[]{:S(2)}, u32[]{:S(2)}) collective-permute-start(bf16[48,768]{1,0:T(8,128)(2,1)S(1)} %slice.59.b0), channel_id=1, source_target_pairs={{0,32},{16,48},{32,0},{48,16},{1,33},{17,49},{33,1},{49,17},{2,34}... | collective-permute-start | bytes 221192 | tf_op jit(solution)/shard_map/ppermute | solution.py:425
  157.2 5.8 %collective-permute-start.29 = (bf16[48,768]{1,0:T(8,128)(2,1)S(1)}, bf16[48,768]{1,0:T(8,128)(2,1)S(1)}, u32[]{:S(2)}, u32[]{:S(2)}) collective-permute-start(bf16[48,768]{1,0:T(8,128)(2,1)S(1)} %slice.59.b0), channel_id=1, source_target_pairs={{0,48},{16,0},{32,16},{48,32},{1,49},{17,1},{33,17},{49,33},{2,50}... | collective-permute-start | bytes 221192 | tf_op jit(solution)/shard_map/ppermute | solution.py:425
  157.7 10.2 %collective-permute-start.36 = (f32[8,768]{1,0:T(8,128)S(1)}, f32[8,768]{1,0:T(8,128)S(1)}, u32[]{:S(2)}, u32[]{:S(2)}) collective-permute-start(f32[8,768]{1,0:T(8,128)S(1)} %slice.45), channel_id=1, source_target_pairs={{0,1},{1,0},{2,3},{3,2},{4,5},{5,4},{6,7},{7,6},{8,9},{9,8},{10,11... | collective-permute-start | bytes 73736 | tf_op jit(solution)/shard_map/ppermute | solution.py:425
  163.6 12.0 %collective-permute-start.34 = (bf16[4,48,768]{2,1,0:T(8,128)(2,1)S(1)}, bf16[4,48,768]{2,1,0:T(8,128)(2,1)S(1)}, u32[]{:S(2)}, u32[]{:S(2)}) collective-permute-start(bf16[4,48,768]{2,1,0:T(8,128)(2,1)S(1)} %shard_map.273.p0), channel_id=1, source_target_pairs={{0,4},{4,8},{8,12},{12,0},{1,5},{5,9},{9,13},{13,1},{2,6},{6,10},{... | collective-permute-start | bytes 884744 | tf_op jit(solution)/shard_map/ppermute | solution.py:425
  164.9 13.6 %collective-permute-start.33 = (bf16[4,48,768]{2,1,0:T(8,128)(2,1)S(1)}, bf16[4,48,768]{2,1,0:T(8,128)(2,1)S(1)}, u32[]{:S(2)}, u32[]{:S(2)}) collective-permute-start(bf16[4,48,768]{2,1,0:T(8,128)(2,1)S(1)} %shard_map.273.p0), channel_id=1, source_target_pairs={{0,8},{4,12},{8,0},{12,4},{1,9},{5,13},{9,1},{13,5},{2,10},{6,14},... | collective-permute-start | bytes 884744 | tf_op jit(solution)/shard_map/ppermute | solution.py:425
  167.9 10.7 %collective-permute-start.32 = (bf16[4,48,768]{2,1,0:T(8,128)(2,1)S(1)}, bf16[4,48,768]{2,1,0:T(8,128)(2,1)S(1)}, u32[]{:S(2)}, u32[]{:S(2)}) collective-permute-start(bf16[4,48,768]{2,1,0:T(8,128)(2,1)S(1)} %shard_map.273.p0), channel_id=1, source_target_pairs={{0,12},{4,0},{8,4},{12,8},{1,13},{5,1},{9,5},{13,9},{2,14},{6,2},{... | collective-permute-start | bytes 884744 | tf_op jit(solution)/shard_map/ppermute | solution.py:425
  167.9 5.4 %collective-permute-start.37 = (f32[8,768]{1,0:T(8,128)S(1)}, f32[8,768]{1,0:T(8,128)S(1)}, u32[]{:S(2)}, u32[]{:S(2)}) collective-permute-start(f32[8,768]{1,0:T(8,128)S(1)} %slice_add_fusion), channel_id=1, source_target_pairs={{0,2},{2,0},{1,3},{3,1},{4,6},{6,4},{5,7},{7,5},{8,10},{10,8},{9,1... | collective-permute-start | bytes 73736 | tf_op jit(solution)/shard_map/ppermute | solution.py:425
  (21 other events, 177.1 us)
Sparse Core Ops, SparseCore 0:
  15.2 85.5 reduce-scatter.1
  115.3 48.2 all-gather.1

commit v7 on v6

--- a/solution.py
+++ b/solution.py
@@ -387,17 +387,25 @@
 
 
 def assemble_kernel(coords, p0, p1, p2, p3, mlp, gq, gd, gu, gdn):
-    gu[...] = mlp[0:768, :].astype(F32)
-    gdn[...] = mlp[768:1536, :].astype(F32)
+    step = pl.program_id(0)
+
+    @pl.when(step < 2)
+    def _():
+        gu[...] = mlp[...].astype(F32)
+
+    @pl.when(step >= 2)
+    def _():
+        gdn[...] = mlp[...].astype(F32)
+
     for slot, ref in enumerate((p0, p1, p2, p3)):
         piece = (coords[2] + slot) % 4
 
-        @pl.when(piece < 3)
+        @pl.when((step == 0) & (piece < 3))
         def _(ref=ref, piece=piece):
             for block in range(4):
                 gq[piece, 48 * block : 48 * block + 48, :] = ref[block].astype(F32)
 
-        @pl.when(piece == 3)
+        @pl.when((step == 0) & (piece == 3))
         def _(ref=ref):
             for block in range(4):
                 gd[48 * block : 48 * block + 48, :] = ref[block].astype(F32)
@@ -549,13 +557,27 @@
         (coords, block, *[hop(block, "z", -j) for j in (1, 2, 3)]),
         1,
     )
-    grad_turned, grad_w_dense, grad_w_up, grad_w_down = call(
+    half = (384, 768)
+    piece_spec = pl.BlockSpec((4, 48, 768), lambda i: (0, 0, 0))
+    grad_turned, grad_w_dense, grad_w_up, grad_w_down = pl.pallas_call(
         assemble_kernel,
-        [((3, 192, 768), F32), ((192, 768), F32), ((768, 768), F32), ((768, 768), F32)],
-        (coords, quarter, *[hop(quarter, "y", -j) for j in (1, 2, 3)], grads_mlp),
-        1,
-        mib=60,
-    )
+        grid=(4,),
+        out_shape=[
+            jax.ShapeDtypeStruct(shape, F32)
+            for shape in ((3, 192, 768), (192, 768), (768, 768), (768, 768))
+        ],
+        in_specs=[pl.BlockSpec(memory_space=pltpu.SMEM)]
+        + [piece_spec] * 4
+        + [pl.BlockSpec(half, lambda i: (i, 0))],
+        out_specs=[
+            pl.BlockSpec((3, 192, 768), lambda i: (0, 0, 0)),
+            pl.BlockSpec((192, 768), lambda i: (0, 0)),
+            pl.BlockSpec(half, lambda i: (jnp.minimum(i, 1), 0)),
+            pl.BlockSpec(half, lambda i: (jnp.maximum(i, 2) - 2, 0)),
+        ],
+        compiler_params=pltpu.CompilerParams(vmem_limit_bytes=60 << 20),
+        cost_estimate=pl.CostEstimate(flops=0, bytes_accessed=1024, transcendentals=0),
+    )(coords, quarter, *[hop(quarter, "y", -j) for j in (1, 2, 3)], grads_mlp)
     grad_tokens, output = call(
         token_kernel,
         [((256, 768), BF)] * 2,

time: 193 us -> 193 us (level)
    pallas_call x0 -> x1, Pallas kernels: none -> 6.19 us  [on_device(): pl.pallas_call(assemble_kernel, grid=(4,), out_shape=[jax.ShapeDtypeStruc...]
    pallas_call x14 -> x13, Pallas kernels: 63 us -> 57.5 us  [call(): pl.pallas_call(kernel, out_shape=shapes, in_specs=[smem] * scalars + [vme...]
where the time goes in v7:
time: 193 us
  Pallas kernels  63.7 us (33%)
  starting transfers between devices  59.4 us (31%)
  waiting for transfers between devices  45.9 us (24%)
  between operations  14.5 us (8%)
  local copies, waits for them, and re-layouts  8.58 us (4%)
    ppermute x38, starting transfers between devices, hop(): return lax.ppermute(x, axis, [(i, (i + step) % n) for i in range(n)])  59.3 us
    pallas_call x13, Pallas kernels, call(): pl.pallas_call(kernel, out_shape=shapes, in_specs=[smem] * scalars + [vme...  57.5 us
    ppermute x38, waiting for transfers between devices, hop(): return lax.ppermute(x, axis, [(i, (i + step) % n) for i in range(n)])  45.9 us
    unnamed x59, local copies, waits for them, and re-layouts  6.73 us
    pallas_call x1, Pallas kernels, on_device(): pl.pallas_call(assemble_kernel, grid=(4,), out_shape=[jax.ShapeDtypeStruc...  6.19 us
  transfers between devices with their start and end apart: 40, of which 17 were waited for; matrix products, arithmetic and copies ran while one was open for 1% of the time, Pallas kernels for 26%

profile of v7, /device:TPU:0, one launch (start us, length us, event | category | flops | bytes accessed | tf_op | source)
XLA Modules:
  0.0 193.0 jit_solution(11835946810267093239)
XLA Ops:
  7.8 7.2 %shard_map.263 = (bf16[256,384]{1,0:T(8,128)(2,1)}, bf16[256,384]{1,0:T(8,128)(2,1)}, bf16[256,768]{1,0:T(8,128)(2,1)}, bf16[1536,768]{1,0:T(8,128)(2,1)}, f32[8...) custom-call(s32[3]{0:T(128)} %pad_add_fusion.coords, s32[64]{0:T(128)} %order.9, ...), custom_call_target="tpu_custom_call" | custom-call | bytes 1024 | tf_op jit(solution)/shard_map/pallas_call | solution.py:418
  16.0 1.6 collective-permute-start.3
  17.6 1.9 collective-permute-start.6
  19.5 2.1 %collective-permute-start.4 = (bf16[256,384]{1,0:T(8,128)(2,1)S(1)}, bf16[256,384]{1,0:T(8,128)(2,1)S(1)}, u32[]{:S(2)}, u32[]{:S(2)}) collective-permute-start(bf16[256,384]{1,0:T(8,128)(2,1)S(1)} %copy-done.7), channel_id=1, source_target_pairs={{0,48},{16,0},{32,16},{48,32},{1,49},{17,1},{33,17},{49,33},{2,50}... | collective-permute-start | bytes 589832 | tf_op jit(solution)/shard_map/ppermute | solution.py:433
  21.6 1.6 collective-permute-start.2
  23.2 3.6 %collective-permute-start.5 = (bf16[256,384]{1,0:T(8,128)(2,1)S(1)}, bf16[256,384]{1,0:T(8,128)(2,1)S(1)}, u32[]{:S(2)}, u32[]{:S(2)}) collective-permute-start(bf16[256,384]{1,0:T(8,128)(2,1)S(1)} %collective-permute-done.3.refs_5_.refs_6_), channel_id=1, source_target_pairs={{0,48},{16,0},{32,16},{48,32},{1,49},{17,1},{33,17},{49,33},{2,50}... | collective-permute-start | bytes 589832 | tf_op jit(solution)/shard_map/ppermute | solution.py:433
  26.7 3.2 %collective-permute-start.1 = (bf16[256,384]{1,0:T(8,128)(2,1)S(1)}, bf16[256,384]{1,0:T(8,128)(2,1)S(1)}, u32[]{:S(2)}, u32[]{:S(2)}) collective-permute-start(bf16[256,384]{1,0:T(8,128)(2,1)S(1)} %copy-done.2), channel_id=1, source_target_pairs={{0,8},{4,12},{8,0},{12,4},{1,9},{5,13},{9,1},{13,5},{2,10},{6,14},... | collective-permute-start | bytes 589832 | tf_op jit(solution)/shard_map/ppermute | solution.py:433
  29.9 1.0 collective-permute-start
  31.1 3.4 %collective-permute-start.8 = (bf16[256,384]{1,0:T(8,128)(2,1)S(1)}, bf16[256,384]{1,0:T(8,128)(2,1)S(1)}, u32[]{:S(2)}, u32[]{:S(2)}) collective-permute-start(bf16[256,384]{1,0:T(8,128)(2,1)S(1)} %collective-permute-done.5.refs_7_.refs_6_), channel_id=1, source_target_pairs={{0,48},{16,0},{32,16},{48,32},{1,49},{17,1},{33,17},{49,33},{2,50}... | collective-permute-start | bytes 589832 | tf_op jit(solution)/shard_map/ppermute | solution.py:433
  35.4 4.6 %collective-permute-done.refs_1_.refs_5_.refs_2_ = bf16[256,384]{1,0:T(8,128)(2,1)S(1)} collective-permute-done((bf16[256,384]{1,0:T(8,128)(2,1)S(1)}, bf16[256,384]{1,0:T(8,128)(2,1)S(1)}, u32[]{:S(2)}, u32[]{:S(2)}) %collective-permute-start) | collective-permute-done | bytes 196640 | tf_op jit(solution)/shard_map/ppermute | solution.py:433
  40.0 3.4 %collective-permute-done.7.refs_8_ = bf16[256,384]{1,0:T(8,128)(2,1)S(1)} collective-permute-done((bf16[256,384]{1,0:T(8,128)(2,1)S(1)}, bf16[256,384]{1,0:T(8,128)(2,1)S(1)}, u32[]{:S(2)}, u32[]{:S(2)}) %collective-permute-start.7) | collective-permute-done | bytes 196640 | tf_op jit(solution)/shard_map/ppermute | solution.py:433
  43.4 13.2 %shard_map.264 = (bf16[192,256]{1,0:T(8,128)(2,1)S(1)}, bf16[192,256]{1,0:T(8,128)(2,1)S(1)}, bf16[192,256]{1,0:T(8,128)(2,1)S(1)}, bf16[192,256]{1,0:T(8,128)(2,1)S(1)}, f32[4,8,256]{2,1,0:T(8,128)S(1)}) custom-call(s32[3]{0:T(128)S(1)} %copy-done.17, s32[64]{0:T(128)S(1)} %copy-done.19, bf16[256,384]{1,0:T(8,128)(2,1)S(1)} %copy-done.2, ...), custom_call_target="tpu_custom_call" | custom-call | bytes 1024 | tf_op jit(solution)/shard_map/pallas_call | solution.py:418
  56.6 1.5 collective-permute-start.12
  58.8 2.4 %collective-permute-start.10 = (f32[4,8,256]{2,1,0:T(8,128)S(1)}, f32[4,8,256]{2,1,0:T(8,128)S(1)}, u32[]{:S(2)}, u32[]{:S(2)}) collective-permute-start(f32[4,8,256]{2,1,0:T(8,128)S(1)} %get-tuple-element.59.refs_0_.s0), channel_id=1, source_target_pairs={{0,12},{4,0},{8,4},{12,8},{1,13},{5,1},{9,5},{13,9},{2,14},{6,2},{... | collective-permute-start | bytes 98312 | tf_op jit(solution)/shard_map/ppermute | solution.py:433
  61.9 1.7 collective-permute-done.11.refs_2_.s2
  63.6 6.9 %shard_map.265 = (f32[4,8,256]{2,1,0:T(8,128)S(1)}, bf16[2,256,384]{2,1,0:T(8,128)(2,1)S(1)}, f32[4,192,256]{2,1,0:T(8,128)S(1)}) custom-call(s32[3]{0:T(128)S(1)} %copy-done.17, s32[64]{0:T(128)S(1)} %copy-done.19, f32[4,8,256]{2,1,0:T(8,128)S(1)} %get-tuple-element.59.refs_0_.s0, f32[4,8,256]{2,1,0:T(8,128)S(1)} %collective-permute-done.10.refs_1_.s1, ...), custom_call_target="tpu_custom_call" | custom-call | bytes 1024 | tf_op jit(solution)/shard_map/pallas_call | solution.py:418
  70.6 13.1 %shard_map.266 = (bf16[2,256,384]{2,1,0:T(8,128)(2,1)S(1)}, bf16[2,256,384]{2,1,0:T(8,128)(2,1)S(1)}, f32[4,192,256]{2,1,0:T(8,128)S(1)}) custom-call(s32[3]{0:T(128)S(1)} %copy-done.17, s32[64]{0:T(128)S(1)} %copy-done.19, f32[4,8,256]{2,1,0:T(8,128)S(1)} %get-tuple-element.60.refs_0_, bf16[256,384]{1,0:T(8,128)(2,1)S(1)} %copy-done.2, ...), custom_call_target="tpu_custom_call" | custom-call | bytes 1024 | tf_op jit(solution)/shard_map/pallas_call | solution.py:418
  83.7 1.6 collective-permute-start.17
  85.3 1.7 collective-permute-start.18
  87.0 6.9 %shard_map.267 = (bf16[2,256,384]{2,1,0:T(8,128)(2,1)S(1)}, bf16[192,256]{1,0:T(8,128)(2,1)S(1)}, bf16[384,256]{1,0:T(8,128)(2,1)S(1)}, bf16[384,256]{1,0:T(8,128)(2,1)S(1)}, bf16[384,256]{1,0:T(8,128)(2,1)S(1)}) custom-call(s32[3]{0:T(128)S(1)} %copy-done.17, s32[64]{0:T(128)S(1)} %copy-done.19, f32[4,8,256]{2,1,0:T(8,128)S(1)} %get-tuple-element.60.refs_0_, ...), custom_call_target="tpu_custom_call" | custom-call | bytes 1024 | tf_op jit(solution)/shard_map/pallas_call | solution.py:418
  95.2 1.0 collective-permute-start.19
  96.2 1.9 %collective-permute-start.14 = (bf16[384,256]{1,0:T(8,128)(2,1)S(1)}, bf16[384,256]{1,0:T(8,128)(2,1)S(1)}, u32[]{:S(2)}, u32[]{:S(2)}) collective-permute-start(bf16[384,256]{1,0:T(8,128)(2,1)S(1)} %get-tuple-element.68), channel_id=1, source_target_pairs={{0,4},{4,8},{8,12},{12,0},{1,5},{5,9},{9,13},{13,1},{2,6},{6,10},{... | collective-permute-start | bytes 589832 | tf_op jit(solution)/shard_map/ppermute | solution.py:433
  98.2 3.0 %collective-permute-start.15 = (bf16[384,256]{1,0:T(8,128)(2,1)S(1)}, bf16[384,256]{1,0:T(8,128)(2,1)S(1)}, u32[]{:S(2)}, u32[]{:S(2)}) collective-permute-start(bf16[384,256]{1,0:T(8,128)(2,1)S(1)} %get-tuple-element.69), channel_id=1, source_target_pairs={{0,8},{4,12},{8,0},{12,4},{1,9},{5,13},{9,1},{13,5},{2,10},{6,14},... | collective-permute-start | bytes 589832 | tf_op jit(solution)/shard_map/ppermute | solution.py:433
  102.2 2.0 %collective-permute-start.35 = (bf16[96,768]{1,0:T(8,128)(2,1)S(1)}, bf16[96,768]{1,0:T(8,128)(2,1)S(1)}, u32[]{:S(2)}, u32[]{:S(2)}) collective-permute-start(bf16[96,768]{1,0:T(8,128)(2,1)S(1)} %shard_map.274.x), channel_id=1, source_target_pairs={{0,64},{64,0},{1,65},{65,1},{2,66},{66,2},{3,67},{67,3},{4,68},{68... | collective-permute-start | bytes 442376 | tf_op jit(solution)/shard_map/ppermute | solution.py:433
  104.2 2.8 %collective-permute-done.15.dq2 = bf16[384,256]{1,0:T(8,128)(2,1)S(1)} collective-permute-done((bf16[384,256]{1,0:T(8,128)(2,1)S(1)}, bf16[384,256]{1,0:T(8,128)(2,1)S(1)}, u32[]{:S(2)}, u32[]{:S(2)}) %collective-permute-start.15) | collective-permute-done | bytes 196640 | tf_op jit(solution)/shard_map/ppermute | solution.py:433
  107.7 5.6 %shard_map.269 = (bf16[208,768]{1,0:T(8,128)(2,1)}, bf16[208,768]{1,0:T(8,128)(2,1)}, bf16[208,768]{1,0:T(8,128)(2,1)}, bf16[208,768]{1,0:T(8,128)(2,1)}, bf16[512,768]{1,0:T(8,128)(2,1)}) custom-call(s32[3]{0:T(128)} %pad_add_fusion.coords, bf16[256,768]{1,0:T(8,128)(2,1)} %tok.5, bf16[256,768]{1,0:T(8,128)(2,1)} %cot.5, ...), custom_call_target="tpu_custom_call" | custom-call | bytes 1024 | tf_op jit(solution)/shard_map/pallas_call | solution.py:418
  113.3 1.1 copy-done.3
  115.7 3.0 %collective-permute-start.23 = (bf16[208,768]{1,0:T(8,128)(2,1)}, bf16[208,768]{1,0:T(8,128)(2,1)S(1)}, u32[]{:S(2)}, u32[]{:S(2)}) collective-permute-start(bf16[208,768]{1,0:T(8,128)(2,1)} %get-tuple-element.85), channel_id=1, source_target_pairs={{0,8},{4,12},{8,0},{12,4},{1,9},{5,13},{9,1},{13,5},{2,10},{6,14},... | collective-permute-start | bytes 958472 | tf_op jit(solution)/shard_map/ppermute | solution.py:433
  119.4 7.5 %collective-permute-done.22.p1 = bf16[208,768]{1,0:T(8,128)(2,1)S(1)} collective-permute-done((bf16[208,768]{1,0:T(8,128)(2,1)}, bf16[208,768]{1,0:T(8,128)(2,1)S(1)}, u32[]{:S(2)}, u32[]{:S(2)}) %collective-permute-start.22) | collective-permute-done | bytes 319520 | tf_op jit(solution)/shard_map/ppermute | solution.py:433
  126.9 8.4 %collective-permute-done.23.p2 = bf16[208,768]{1,0:T(8,128)(2,1)S(1)} collective-permute-done((bf16[208,768]{1,0:T(8,128)(2,1)}, bf16[208,768]{1,0:T(8,128)(2,1)S(1)}, u32[]{:S(2)}, u32[]{:S(2)}) %collective-permute-start.23) | collective-permute-done | bytes 319520 | tf_op jit(solution)/shard_map/ppermute | solution.py:433
  137.9 2.5 %collective-permute-start.25 = (bf16[64,768]{1,0:T(8,128)(2,1)S(1)}, bf16[64,768]{1,0:T(8,128)(2,1)S(1)}, u32[]{:S(2)}, u32[]{:S(2)}) collective-permute-start(bf16[64,768]{1,0:T(8,128)(2,1)S(1)} %get-tuple-element.88), channel_id=1, source_target_pairs={{0,16},{16,32},{32,48},{48,0},{1,17},{17,33},{33,49},{49,1},{2,18}... | collective-permute-start | bytes 294920 | tf_op jit(solution)/shard_map/ppermute | solution.py:433
  140.4 1.4 collective-permute-start.26
  141.8 1.4 collective-permute-start.27
  143.2 1.1 collective-permute-done.25.b1
  144.3 2.2 %collective-permute-done.26.b2 = bf16[64,768]{1,0:T(8,128)(2,1)S(1)} collective-permute-done((bf16[64,768]{1,0:T(8,128)(2,1)S(1)}, bf16[64,768]{1,0:T(8,128)(2,1)S(1)}, u32[]{:S(2)}, u32[]{:S(2)}) %collective-permute-start.26) | collective-permute-done | bytes 98336 | tf_op jit(solution)/shard_map/ppermute | solution.py:433
  147.9 3.1 %collective-permute-start.21 = (bf16[512,768]{1,0:T(8,128)(2,1)S(1)}, bf16[512,768]{1,0:T(8,128)(2,1)S(1)}, u32[]{:S(2)}, u32[]{:S(2)}) collective-permute-start(bf16[512,768]{1,0:T(8,128)(2,1)S(1)} %add_convert_fusion.e0), channel_id=1, source_target_pairs={{0,2},{2,0},{1,3},{3,1},{4,6},{6,4},{5,7},{7,5},{8,10},{10,8},{9,1... | collective-permute-start | bytes 2359304 | tf_op jit(solution)/shard_map/ppermute | solution.py:433
  151.1 1.9 %collective-permute-done.28 = bf16[64,768]{1,0:T(8,128)(2,1)S(1)} collective-permute-done((bf16[64,768]{1,0:T(8,128)(2,1)S(1)}, bf16[64,768]{1,0:T(8,128)(2,1)S(1)}, u32[]{:S(2)}, u32[]{:S(2)}) %collective-permute-start.28) | collective-permute-done | bytes 98336 | tf_op jit(solution)/shard_map/ppermute | solution.py:433
  153.1 1.2 collective-permute-start.31
  154.3 2.9 %collective-permute-start.30 = (bf16[48,768]{1,0:T(8,128)(2,1)S(1)}, bf16[48,768]{1,0:T(8,128)(2,1)S(1)}, u32[]{:S(2)}, u32[]{:S(2)}) collective-permute-start(bf16[48,768]{1,0:T(8,128)(2,1)S(1)} %slice.59.b0), channel_id=1, source_target_pairs={{0,32},{16,48},{32,0},{48,16},{1,33},{17,49},{33,1},{49,17},{2,34}... | collective-permute-start | bytes 221192 | tf_op jit(solution)/shard_map/ppermute | solution.py:433
  158.3 2.0 %collective-permute-done.31.b3 = bf16[48,768]{1,0:T(8,128)(2,1)S(1)} collective-permute-done((bf16[48,768]{1,0:T(8,128)(2,1)S(1)}, bf16[48,768]{1,0:T(8,128)(2,1)S(1)}, u32[]{:S(2)}, u32[]{:S(2)}) %collective-permute-start.31) | collective-permute-done | bytes 73760 | tf_op jit(solution)/shard_map/ppermute | solution.py:433
  160.3 2.7 %collective-permute-done.30.b2 = bf16[48,768]{1,0:T(8,128)(2,1)S(1)} collective-permute-done((bf16[48,768]{1,0:T(8,128)(2,1)S(1)}, bf16[48,768]{1,0:T(8,128)(2,1)S(1)}, u32[]{:S(2)}, u32[]{:S(2)}) %collective-permute-start.30) | collective-permute-done | bytes 73760 | tf_op jit(solution)/shard_map/ppermute | solution.py:433
  163.6 1.3 collective-permute-start.34
  164.9 2.9 %collective-permute-start.33 = (bf16[4,48,768]{2,1,0:T(8,128)(2,1)S(1)}, bf16[4,48,768]{2,1,0:T(8,128)(2,1)S(1)}, u32[]{:S(2)}, u32[]{:S(2)}) collective-permute-start(bf16[4,48,768]{2,1,0:T(8,128)(2,1)S(1)} %shard_map.273.p0), channel_id=1, source_target_pairs={{0,8},{4,12},{8,0},{12,4},{1,9},{5,13},{9,1},{13,5},{2,10},{6,14},... | collective-permute-start | bytes 884744 | tf_op jit(solution)/shard_map/ppermute | solution.py:433
  167.9 3.1 %collective-permute-start.37 = (f32[8,768]{1,0:T(8,128)S(1)}, f32[8,768]{1,0:T(8,128)S(1)}, u32[]{:S(2)}, u32[]{:S(2)}) collective-permute-start(f32[8,768]{1,0:T(8,128)S(1)} %slice_add_fusion), channel_id=1, source_target_pairs={{0,2},{2,0},{1,3},{3,1},{4,6},{6,4},{5,7},{7,5},{8,10},{10,8},{9,1... | collective-permute-start | bytes 73736 | tf_op jit(solution)/shard_map/ppermute | solution.py:433
  171.5 1.7 collective-permute-done.37
  173.9 1.7 shard_map.270
  175.6 2.9 %collective-permute-done.33.p2 = bf16[4,48,768]{2,1,0:T(8,128)(2,1)S(1)} collective-permute-done((bf16[4,48,768]{2,1,0:T(8,128)(2,1)S(1)}, bf16[4,48,768]{2,1,0:T(8,128)(2,1)S(1)}, u32[]{:S(2)}, u32[]{:S(2)}) %collective-permute-start.33) | collective-permute-done | bytes 294944 | tf_op jit(solution)/shard_map/ppermute | solution.py:433
  179.3 6.2 %shard_map.276 = (f32[3,192,768]{2,1,0:T(8,128)}, f32[192,768]{1,0:T(8,128)}, f32[768,768]{1,0:T(8,128)}, f32[768,768]{1,0:T(8,128)}) custom-call(s32[3]{0:T(128)} %pad_add_fusion.coords, bf16[4,48,768]{2,1,0:T(8,128)(2,1)} %copy-done.5, bf16[4,48,768]{2,1,0:T(8,128)(2,1)} %copy-done.24, bf16[4,48,768]{2,1,0:T(8,128)(2,1)} %copy-done.23, ...), custom_call_target="tpu_custom_call" | custom-call | bytes 1024 | tf_op jit(solution)/shard_map/pallas_call | solution.py:562
  (117 shorter events, 17.4 us)
Async XLA Ops:
  7.2 94.1 %reduce-scatter.2.cloned.1.call-start = ((), (), s32[]{:S(2)}) async-start(), calls=%async_computation.1 | async-start | bytes 2506752 | tf_op jit(solution)/shard_map/reduce_scatter | solution.py:470
  15.1 28.3 %copy-start.17 = (s32[3]{0:T(128)S(1)}, s32[3]{0:T(128)}, u32[]{:S(2)}) copy-start(s32[3]{0:T(128)} %pad_add_fusion.coords) | copy-start | bytes 40
  15.1 28.3 %copy-start.19 = (s32[64]{0:T(128)S(1)}, s32[64]{0:T(128)}, u32[]{:S(2)}) copy-start(s32[64]{0:T(128)} %order.9) | copy-start | bytes 772
  15.1 163.4 %all-gather.2.cloned.1.call-start = ((), (), s32[]{:S(2)}) async-start(), calls=%async_computation.2 | async-start | bytes 2506752 | tf_op jit(solution)/shard_map/all_gather | solution.py:532
  16.0 7.2 %collective-permute-start.3 = (bf16[256,384]{1,0:T(8,128)(2,1)S(1)}, bf16[256,384]{1,0:T(8,128)(2,1)S(1)}, u32[]{:S(2)}, u32[]{:S(2)}) collective-permute-start(bf16[256,384]{1,0:T(8,128)(2,1)S(1)} %copy-done.7), channel_id=1, source_target_pairs={{0,64},{64,0},{1,65},{65,1},{2,66},{66,2},{3,67},{67,3},{4,68},{68... | collective-permute-start | bytes 589832 | tf_op jit(solution)/shard_map/ppermute | solution.py:433
  17.6 12.4 %collective-permute-start.6 = (bf16[256,384]{1,0:T(8,128)(2,1)S(1)}, bf16[256,384]{1,0:T(8,128)(2,1)S(1)}, u32[]{:S(2)}, u32[]{:S(2)}) collective-permute-start(bf16[256,384]{1,0:T(8,128)(2,1)S(1)} %copy-done.7), channel_id=1, source_target_pairs={{0,16},{16,32},{32,48},{48,0},{1,17},{17,33},{33,49},{49,1},{2,18}... | collective-permute-start | bytes 589832 | tf_op jit(solution)/shard_map/ppermute | solution.py:433
  19.5 11.5 %collective-permute-start.4 = (bf16[256,384]{1,0:T(8,128)(2,1)S(1)}, bf16[256,384]{1,0:T(8,128)(2,1)S(1)}, u32[]{:S(2)}, u32[]{:S(2)}) collective-permute-start(bf16[256,384]{1,0:T(8,128)(2,1)S(1)} %copy-done.7), channel_id=1, source_target_pairs={{0,48},{16,0},{32,16},{48,32},{1,49},{17,1},{33,17},{49,33},{2,50}... | collective-permute-start | bytes 589832 | tf_op jit(solution)/shard_map/ppermute | solution.py:433
  21.6 9.4 %collective-permute-start.2 = (bf16[256,384]{1,0:T(8,128)(2,1)S(1)}, bf16[256,384]{1,0:T(8,128)(2,1)S(1)}, u32[]{:S(2)}, u32[]{:S(2)}) collective-permute-start(bf16[256,384]{1,0:T(8,128)(2,1)S(1)} %copy-done.2), channel_id=1, source_target_pairs={{0,4},{4,8},{8,12},{12,0},{1,5},{5,9},{9,13},{13,1},{2,6},{6,10},{... | collective-permute-start | bytes 589832 | tf_op jit(solution)/shard_map/ppermute | solution.py:433
  23.2 7.9 %collective-permute-start.5 = (bf16[256,384]{1,0:T(8,128)(2,1)S(1)}, bf16[256,384]{1,0:T(8,128)(2,1)S(1)}, u32[]{:S(2)}, u32[]{:S(2)}) collective-permute-start(bf16[256,384]{1,0:T(8,128)(2,1)S(1)} %collective-permute-done.3.refs_5_.refs_6_), channel_id=1, source_target_pairs={{0,48},{16,0},{32,16},{48,32},{1,49},{17,1},{33,17},{49,33},{2,50}... | collective-permute-start | bytes 589832 | tf_op jit(solution)/shard_map/ppermute | solution.py:433
  26.7 8.7 %collective-permute-start.1 = (bf16[256,384]{1,0:T(8,128)(2,1)S(1)}, bf16[256,384]{1,0:T(8,128)(2,1)S(1)}, u32[]{:S(2)}, u32[]{:S(2)}) collective-permute-start(bf16[256,384]{1,0:T(8,128)(2,1)S(1)} %copy-done.2), channel_id=1, source_target_pairs={{0,8},{4,12},{8,0},{12,4},{1,9},{5,13},{9,1},{13,5},{2,10},{6,14},... | collective-permute-start | bytes 589832 | tf_op jit(solution)/shard_map/ppermute | solution.py:433
  29.9 10.0 %collective-permute-start = (bf16[256,384]{1,0:T(8,128)(2,1)S(1)}, bf16[256,384]{1,0:T(8,128)(2,1)S(1)}, u32[]{:S(2)}, u32[]{:S(2)}) collective-permute-start(bf16[256,384]{1,0:T(8,128)(2,1)S(1)} %copy-done.2), channel_id=1, source_target_pairs={{0,12},{4,0},{8,4},{12,8},{1,13},{5,1},{9,5},{13,9},{2,14},{6,2},{... | collective-permute-start | bytes 589832 | tf_op jit(solution)/shard_map/ppermute | solution.py:433
  31.0 12.4 %collective-permute-start.9 = (bf16[256,384]{1,0:T(8,128)(2,1)S(1)}, bf16[256,384]{1,0:T(8,128)(2,1)S(1)}, u32[]{:S(2)}, u32[]{:S(2)}) collective-permute-start(bf16[256,384]{1,0:T(8,128)(2,1)S(1)} %collective-permute-done.3.refs_5_.refs_6_), channel_id=1, source_target_pairs={{0,16},{16,32},{32,48},{48,0},{1,17},{17,33},{33,49},{49,1},{2,18}... | collective-permute-start | bytes 589832 | tf_op jit(solution)/shard_map/ppermute | solution.py:433
  31.0 12.4 %collective-permute-start.7 = (bf16[256,384]{1,0:T(8,128)(2,1)S(1)}, bf16[256,384]{1,0:T(8,128)(2,1)S(1)}, u32[]{:S(2)}, u32[]{:S(2)}) collective-permute-start(bf16[256,384]{1,0:T(8,128)(2,1)S(1)} %collective-permute-done.6.refs_10_.refs_7_), channel_id=1, source_target_pairs={{0,16},{16,32},{32,48},{48,0},{1,17},{17,33},{33,49},{49,1},{2,18}... | collective-permute-start | bytes 589832 | tf_op jit(solution)/shard_map/ppermute | solution.py:433
  31.1 12.3 %collective-permute-start.8 = (bf16[256,384]{1,0:T(8,128)(2,1)S(1)}, bf16[256,384]{1,0:T(8,128)(2,1)S(1)}, u32[]{:S(2)}, u32[]{:S(2)}) collective-permute-start(bf16[256,384]{1,0:T(8,128)(2,1)S(1)} %collective-permute-done.5.refs_7_.refs_6_), channel_id=1, source_target_pairs={{0,48},{16,0},{32,16},{48,32},{1,49},{17,1},{33,17},{49,33},{2,50}... | collective-permute-start | bytes 589832 | tf_op jit(solution)/shard_map/ppermute | solution.py:433
  56.6 27.1 %copy-start.11 = (f32[4,8,256]{2,1,0:T(8,128)}, f32[4,8,256]{2,1,0:T(8,128)S(1)}, u32[]{:S(2)}) copy-start(f32[4,8,256]{2,1,0:T(8,128)S(1)} %get-tuple-element.59.refs_0_.s0) | copy-start | bytes 98308
  56.6 5.3 %collective-permute-start.12 = (f32[4,8,256]{2,1,0:T(8,128)S(1)}, f32[4,8,256]{2,1,0:T(8,128)S(1)}, u32[]{:S(2)}, u32[]{:S(2)}) collective-permute-start(f32[4,8,256]{2,1,0:T(8,128)S(1)} %get-tuple-element.59.refs_0_.s0), channel_id=1, source_target_pairs={{0,4},{4,8},{8,12},{12,0},{1,5},{5,9},{9,13},{13,1},{2,6},{6,10},{... | collective-permute-start | bytes 98312 | tf_op jit(solution)/shard_map/ppermute | solution.py:433
  58.1 5.5 %collective-permute-start.11 = (f32[4,8,256]{2,1,0:T(8,128)S(1)}, f32[4,8,256]{2,1,0:T(8,128)S(1)}, u32[]{:S(2)}, u32[]{:S(2)}) collective-permute-start(f32[4,8,256]{2,1,0:T(8,128)S(1)} %get-tuple-element.59.refs_0_.s0), channel_id=1, source_target_pairs={{0,8},{4,12},{8,0},{12,4},{1,9},{5,13},{9,1},{13,5},{2,10},{6,14},... | collective-permute-start | bytes 98312 | tf_op jit(solution)/shard_map/ppermute | solution.py:433
  58.8 4.9 %collective-permute-start.10 = (f32[4,8,256]{2,1,0:T(8,128)S(1)}, f32[4,8,256]{2,1,0:T(8,128)S(1)}, u32[]{:S(2)}, u32[]{:S(2)}) collective-permute-start(f32[4,8,256]{2,1,0:T(8,128)S(1)} %get-tuple-element.59.refs_0_.s0), channel_id=1, source_target_pairs={{0,12},{4,0},{8,4},{12,8},{1,13},{5,1},{9,5},{13,9},{2,14},{6,2},{... | collective-permute-start | bytes 98312 | tf_op jit(solution)/shard_map/ppermute | solution.py:433
  70.5 16.5 %collective-permute-start.13 = (bf16[2,256,384]{2,1,0:T(8,128)(2,1)S(1)}, bf16[2,256,384]{2,1,0:T(8,128)(2,1)S(1)}, u32[]{:S(2)}, u32[]{:S(2)}) collective-permute-start(bf16[2,256,384]{2,1,0:T(8,128)(2,1)S(1)} %get-tuple-element.66), channel_id=1, source_target_pairs={{0,32},{16,48},{32,0},{48,16},{1,33},{17,49},{33,1},{49,17},{2,34}... | collective-permute-start | bytes 1179656 | tf_op jit(solution)/shard_map/ppermute | solution.py:433
  83.7 10.2 %collective-permute-start.17 = (bf16[2,256,384]{2,1,0:T(8,128)(2,1)S(1)}, bf16[2,256,384]{2,1,0:T(8,128)(2,1)S(1)}, u32[]{:S(2)}, u32[]{:S(2)}) collective-permute-start(bf16[2,256,384]{2,1,0:T(8,128)(2,1)S(1)} %get-tuple-element.72), channel_id=1, source_target_pairs={{0,16},{16,32},{32,48},{48,0},{1,17},{17,33},{33,49},{49,1},{2,18}... | collective-permute-start | bytes 1179656 | tf_op jit(solution)/shard_map/ppermute | solution.py:433
  85.3 9.0 %collective-permute-start.18 = (bf16[2,256,384]{2,1,0:T(8,128)(2,1)S(1)}, bf16[2,256,384]{2,1,0:T(8,128)(2,1)S(1)}, u32[]{:S(2)}, u32[]{:S(2)}) collective-permute-start(bf16[2,256,384]{2,1,0:T(8,128)(2,1)S(1)} %get-tuple-element.73), channel_id=1, source_target_pairs={{0,48},{16,0},{32,16},{48,32},{1,49},{17,1},{33,17},{49,33},{2,50}... | collective-permute-start | bytes 1179656 | tf_op jit(solution)/shard_map/ppermute | solution.py:433
  95.2 6.0 %collective-permute-start.19 = (bf16[256,384]{1,0:T(8,128)(2,1)S(1)}, bf16[256,384]{1,0:T(8,128)(2,1)S(1)}, u32[]{:S(2)}, u32[]{:S(2)}) collective-permute-start(bf16[256,384]{1,0:T(8,128)(2,1)S(1)} %get-tuple-element.75), channel_id=1, source_target_pairs={{0,64},{64,0},{1,65},{65,1},{2,66},{66,2},{3,67},{67,3},{4,68},{68... | collective-permute-start | bytes 589832 | tf_op jit(solution)/shard_map/ppermute | solution.py:433
  96.2 8.0 %collective-permute-start.14 = (bf16[384,256]{1,0:T(8,128)(2,1)S(1)}, bf16[384,256]{1,0:T(8,128)(2,1)S(1)}, u32[]{:S(2)}, u32[]{:S(2)}) collective-permute-start(bf16[384,256]{1,0:T(8,128)(2,1)S(1)} %get-tuple-element.68), channel_id=1, source_target_pairs={{0,4},{4,8},{8,12},{12,0},{1,5},{5,9},{9,13},{13,1},{2,6},{6,10},{... | collective-permute-start | bytes 589832 | tf_op jit(solution)/shard_map/ppermute | solution.py:433
  98.2 8.8 %collective-permute-start.15 = (bf16[384,256]{1,0:T(8,128)(2,1)S(1)}, bf16[384,256]{1,0:T(8,128)(2,1)S(1)}, u32[]{:S(2)}, u32[]{:S(2)}) collective-permute-start(bf16[384,256]{1,0:T(8,128)(2,1)S(1)} %get-tuple-element.69), channel_id=1, source_target_pairs={{0,8},{4,12},{8,0},{12,4},{1,9},{5,13},{9,1},{13,5},{2,10},{6,14},... | collective-permute-start | bytes 589832 | tf_op jit(solution)/shard_map/ppermute | solution.py:433
  101.2 5.8 %collective-permute-start.16 = (bf16[384,256]{1,0:T(8,128)(2,1)S(1)}, bf16[384,256]{1,0:T(8,128)(2,1)S(1)}, u32[]{:S(2)}, u32[]{:S(2)}) collective-permute-start(bf16[384,256]{1,0:T(8,128)(2,1)S(1)} %get-tuple-element.70), channel_id=1, source_target_pairs={{0,12},{4,0},{8,4},{12,8},{1,13},{5,1},{9,5},{13,9},{2,14},{6,2},{... | collective-permute-start | bytes 589832 | tf_op jit(solution)/shard_map/ppermute | solution.py:433
  102.2 11.0 %collective-permute-start.35 = (bf16[96,768]{1,0:T(8,128)(2,1)S(1)}, bf16[96,768]{1,0:T(8,128)(2,1)S(1)}, u32[]{:S(2)}, u32[]{:S(2)}) collective-permute-start(bf16[96,768]{1,0:T(8,128)(2,1)S(1)} %shard_map.274.x), channel_id=1, source_target_pairs={{0,64},{64,0},{1,65},{65,1},{2,66},{66,2},{3,67},{67,3},{4,68},{68... | collective-permute-start | bytes 442376 | tf_op jit(solution)/shard_map/ppermute | solution.py:433
  107.7 28.3 %copy-start.18 = (s32[3]{0:T(128)S(1)}, s32[3]{0:T(128)}, u32[]{:S(2)}) copy-start(s32[3]{0:T(128)} %pad_add_fusion.coords) | copy-start | bytes 40
  114.4 33.3 %copy-start.4 = (bf16[512,768]{1,0:T(8,128)(2,1)S(1)}, bf16[512,768]{1,0:T(8,128)(2,1)}, u32[]{:S(2)}) copy-start(bf16[512,768]{1,0:T(8,128)(2,1)} %get-tuple-element.80.after) | copy-start | bytes 2359300
  115.2 32.6 %collective-permute-start.20 = (bf16[512,768]{1,0:T(8,128)(2,1)}, bf16[512,768]{1,0:T(8,128)(2,1)S(1)}, u32[]{:S(2)}, u32[]{:S(2)}) collective-permute-start(bf16[512,768]{1,0:T(8,128)(2,1)} %get-tuple-element.80.after), channel_id=1, source_target_pairs={{0,1},{1,0},{2,3},{3,2},{4,5},{5,4},{6,7},{7,6},{8,9},{9,8},{10,11... | collective-permute-start | bytes 2359304 | tf_op jit(solution)/shard_map/ppermute | solution.py:433
  115.3 11.6 %collective-permute-start.22 = (bf16[208,768]{1,0:T(8,128)(2,1)}, bf16[208,768]{1,0:T(8,128)(2,1)S(1)}, u32[]{:S(2)}, u32[]{:S(2)}) collective-permute-start(bf16[208,768]{1,0:T(8,128)(2,1)} %get-tuple-element.84), channel_id=1, source_target_pairs={{0,4},{4,8},{8,12},{12,0},{1,5},{5,9},{9,13},{13,1},{2,6},{6,10},{... | collective-permute-start | bytes 958472 | tf_op jit(solution)/shard_map/ppermute | solution.py:433
  115.7 19.5 %collective-permute-start.23 = (bf16[208,768]{1,0:T(8,128)(2,1)}, bf16[208,768]{1,0:T(8,128)(2,1)S(1)}, u32[]{:S(2)}, u32[]{:S(2)}) collective-permute-start(bf16[208,768]{1,0:T(8,128)(2,1)} %get-tuple-element.85), channel_id=1, source_target_pairs={{0,8},{4,12},{8,0},{12,4},{1,9},{5,13},{9,1},{13,5},{2,10},{6,14},... | collective-permute-start | bytes 958472 | tf_op jit(solution)/shard_map/ppermute | solution.py:433
  118.8 17.2 %collective-permute-start.24 = (bf16[208,768]{1,0:T(8,128)(2,1)}, bf16[208,768]{1,0:T(8,128)(2,1)S(1)}, u32[]{:S(2)}, u32[]{:S(2)}) collective-permute-start(bf16[208,768]{1,0:T(8,128)(2,1)} %get-tuple-element.86), channel_id=1, source_target_pairs={{0,12},{4,0},{8,4},{12,8},{1,13},{5,1},{9,5},{13,9},{2,14},{6,2},{... | collective-permute-start | bytes 958472 | tf_op jit(solution)/shard_map/ppermute | solution.py:433
  137.9 6.4 %collective-permute-start.25 = (bf16[64,768]{1,0:T(8,128)(2,1)S(1)}, bf16[64,768]{1,0:T(8,128)(2,1)S(1)}, u32[]{:S(2)}, u32[]{:S(2)}) collective-permute-start(bf16[64,768]{1,0:T(8,128)(2,1)S(1)} %get-tuple-element.88), channel_id=1, source_target_pairs={{0,16},{16,32},{32,48},{48,0},{1,17},{17,33},{33,49},{49,1},{2,18}... | collective-permute-start | bytes 294920 | tf_op jit(solution)/shard_map/ppermute | solution.py:433
  140.4 6.1 %collective-permute-start.26 = (bf16[64,768]{1,0:T(8,128)(2,1)S(1)}, bf16[64,768]{1,0:T(8,128)(2,1)S(1)}, u32[]{:S(2)}, u32[]{:S(2)}) collective-permute-start(bf16[64,768]{1,0:T(8,128)(2,1)S(1)} %get-tuple-element.89), channel_id=1, source_target_pairs={{0,32},{16,48},{32,0},{48,16},{1,33},{17,49},{33,1},{49,17},{2,34}... | collective-permute-start | bytes 294920 | tf_op jit(solution)/shard_map/ppermute | solution.py:433
  141.8 4.8 %collective-permute-start.27 = (bf16[64,768]{1,0:T(8,128)(2,1)S(1)}, bf16[64,768]{1,0:T(8,128)(2,1)S(1)}, u32[]{:S(2)}, u32[]{:S(2)}) collective-permute-start(bf16[64,768]{1,0:T(8,128)(2,1)S(1)} %get-tuple-element.90), channel_id=1, source_target_pairs={{0,48},{16,0},{32,16},{48,32},{1,49},{17,1},{33,17},{49,33},{2,50}... | collective-permute-start | bytes 294920 | tf_op jit(solution)/shard_map/ppermute | solution.py:433
  147.2 26.7 %copy-start = (bf16[256,768]{1,0:T(8,128)(2,1)S(1)}, bf16[256,768]{1,0:T(8,128)(2,1)}, u32[]{:S(2)}) copy-start(bf16[256,768]{1,0:T(8,128)(2,1)} %tok.5) | copy-start | bytes 1179652
  147.2 26.7 %copy-start.1 = (bf16[256,768]{1,0:T(8,128)(2,1)S(1)}, bf16[256,768]{1,0:T(8,128)(2,1)}, u32[]{:S(2)}) copy-start(bf16[256,768]{1,0:T(8,128)(2,1)} %cot.5) | copy-start | bytes 1179652
  147.3 5.7 %collective-permute-start.28 = (bf16[64,768]{1,0:T(8,128)(2,1)S(1)}, bf16[64,768]{1,0:T(8,128)(2,1)S(1)}, u32[]{:S(2)}, u32[]{:S(2)}) collective-permute-start(bf16[64,768]{1,0:T(8,128)(2,1)S(1)} %shard_map.272), channel_id=1, source_target_pairs={{0,64},{64,0},{1,65},{65,1},{2,66},{66,2},{3,67},{67,3},{4,68},{68... | collective-permute-start | bytes 294920 | tf_op jit(solution)/shard_map/ppermute | solution.py:433
  147.9 26.0 %collective-permute-start.21 = (bf16[512,768]{1,0:T(8,128)(2,1)S(1)}, bf16[512,768]{1,0:T(8,128)(2,1)S(1)}, u32[]{:S(2)}, u32[]{:S(2)}) collective-permute-start(bf16[512,768]{1,0:T(8,128)(2,1)S(1)} %add_convert_fusion.e0), channel_id=1, source_target_pairs={{0,2},{2,0},{1,3},{3,1},{4,6},{6,4},{5,7},{7,5},{8,10},{10,8},{9,1... | collective-permute-start | bytes 2359304 | tf_op jit(solution)/shard_map/ppermute | solution.py:433
  153.1 7.2 %collective-permute-start.31 = (bf16[48,768]{1,0:T(8,128)(2,1)S(1)}, bf16[48,768]{1,0:T(8,128)(2,1)S(1)}, u32[]{:S(2)}, u32[]{:S(2)}) collective-permute-start(bf16[48,768]{1,0:T(8,128)(2,1)S(1)} %slice.59.b0), channel_id=1, source_target_pairs={{0,16},{16,32},{32,48},{48,0},{1,17},{17,33},{33,49},{49,1},{2,18}... | collective-permute-start | bytes 221192 | tf_op jit(solution)/shard_map/ppermute | solution.py:433
  154.3 8.7 %collective-permute-start.30 = (bf16[48,768]{1,0:T(8,128)(2,1)S(1)}, bf16[48,768]{1,0:T(8,128)(2,1)S(1)}, u32[]{:S(2)}, u32[]{:S(2)}) collective-permute-start(bf16[48,768]{1,0:T(8,128)(2,1)S(1)} %slice.59.b0), channel_id=1, source_target_pairs={{0,32},{16,48},{32,0},{48,16},{1,33},{17,49},{33,1},{49,17},{2,34}... | collective-permute-start | bytes 221192 | tf_op jit(solution)/shard_map/ppermute | solution.py:433
  157.2 5.8 %collective-permute-start.29 = (bf16[48,768]{1,0:T(8,128)(2,1)S(1)}, bf16[48,768]{1,0:T(8,128)(2,1)S(1)}, u32[]{:S(2)}, u32[]{:S(2)}) collective-permute-start(bf16[48,768]{1,0:T(8,128)(2,1)S(1)} %slice.59.b0), channel_id=1, source_target_pairs={{0,48},{16,0},{32,16},{48,32},{1,49},{17,1},{33,17},{49,33},{2,50}... | collective-permute-start | bytes 221192 | tf_op jit(solution)/shard_map/ppermute | solution.py:433
  157.7 10.2 %collective-permute-start.36 = (f32[8,768]{1,0:T(8,128)S(1)}, f32[8,768]{1,0:T(8,128)S(1)}, u32[]{:S(2)}, u32[]{:S(2)}) collective-permute-start(f32[8,768]{1,0:T(8,128)S(1)} %slice.45), channel_id=1, source_target_pairs={{0,1},{1,0},{2,3},{3,2},{4,5},{5,4},{6,7},{7,6},{8,9},{9,8},{10,11... | collective-permute-start | bytes 73736 | tf_op jit(solution)/shard_map/ppermute | solution.py:433
  158.3 27.2 %copy-start.28 = (f32[768]{0:T(1024)}, f32[768]{0:T(1024)S(1)}, u32[]{:S(2)}) copy-start(f32[768]{0:T(1024)S(1)} %get-tuple-element.125) | copy-start | bytes 9220
  163.6 12.0 %collective-permute-start.34 = (bf16[4,48,768]{2,1,0:T(8,128)(2,1)S(1)}, bf16[4,48,768]{2,1,0:T(8,128)(2,1)S(1)}, u32[]{:S(2)}, u32[]{:S(2)}) collective-permute-start(bf16[4,48,768]{2,1,0:T(8,128)(2,1)S(1)} %shard_map.273.p0), channel_id=1, source_target_pairs={{0,4},{4,8},{8,12},{12,0},{1,5},{5,9},{9,13},{13,1},{2,6},{6,10},{... | collective-permute-start | bytes 884744 | tf_op jit(solution)/shard_map/ppermute | solution.py:433
  164.9 13.6 %collective-permute-start.33 = (bf16[4,48,768]{2,1,0:T(8,128)(2,1)S(1)}, bf16[4,48,768]{2,1,0:T(8,128)(2,1)S(1)}, u32[]{:S(2)}, u32[]{:S(2)}) collective-permute-start(bf16[4,48,768]{2,1,0:T(8,128)(2,1)S(1)} %shard_map.273.p0), channel_id=1, source_target_pairs={{0,8},{4,12},{8,0},{12,4},{1,9},{5,13},{9,1},{13,5},{2,10},{6,14},... | collective-permute-start | bytes 884744 | tf_op jit(solution)/shard_map/ppermute | solution.py:433
  167.9 10.7 %collective-permute-start.32 = (bf16[4,48,768]{2,1,0:T(8,128)(2,1)S(1)}, bf16[4,48,768]{2,1,0:T(8,128)(2,1)S(1)}, u32[]{:S(2)}, u32[]{:S(2)}) collective-permute-start(bf16[4,48,768]{2,1,0:T(8,128)(2,1)S(1)} %shard_map.273.p0), channel_id=1, source_target_pairs={{0,12},{4,0},{8,4},{12,8},{1,13},{5,1},{9,5},{13,9},{2,14},{6,2},{... | collective-permute-start | bytes 884744 | tf_op jit(solution)/shard_map/ppermute | solution.py:433
  167.9 5.4 %collective-permute-start.37 = (f32[8,768]{1,0:T(8,128)S(1)}, f32[8,768]{1,0:T(8,128)S(1)}, u32[]{:S(2)}, u32[]{:S(2)}) collective-permute-start(f32[8,768]{1,0:T(8,128)S(1)} %slice_add_fusion), channel_id=1, source_target_pairs={{0,2},{2,0},{1,3},{3,1},{4,6},{6,4},{5,7},{7,5},{8,10},{10,8},{9,1... | collective-permute-start | bytes 73736 | tf_op jit(solution)/shard_map/ppermute | solution.py:433
  (21 other events, 177.2 us)
Sparse Core Ops, SparseCore 0:
  15.2 85.5 reduce-scatter.1
  115.3 48.2 all-gather.1
